TPU v7x, 32 devices: a whole 2x2x4 slice. The times are simulated.
32 devices in a mesh: gx: 4 (over z), gy: 8 (over y, x, core).
Axes of the slice: x: 2, y: 2, z: 4, core: 2. Of those that a mesh axis runs over, the one named last changes fastest.
Arguments:
- heat_source: float32 [8, 64, 6144], P(None, 'gx', 'gy'), may hold values from -90 to 90
- density: float32 [64, 6144], P('gx', 'gy'), may hold values from 0.3 to 1
Outputs:
- solution_field: float32 [8, 64, 6144], P(None, 'gx', 'gy')
- residual: float32 [8, 64, 6144], P(None, 'gx', 'gy')
All inputs are finite; a program needn't handle non-finite values.
Results may differ from a plain program's by a relative error of at most 0.0003.
Values sent between devices are 32-bit elements; how exact they have to be, the bound alone decides.
No kernel may reach another device: no remote copies, remote signals or barrier semaphores. Data moves between devices by JAX's collectives and lax.ppermute only.
A program may use at most 64 MiB of HBM per device.

v0:
```python
import jax
import jax.numpy as jnp
import numpy as np
from jax import lax
from jax.sharding import PartitionSpec as P

NZ = 96
ITERS = 2


KMIN = 0.001


def from_behind(shard, axis, by):
    length = lax.axis_size(axis)
    pairs = [(i, i + by) for i in range(length) if 0 <= i + by < length]
    return lax.ppermute(shard, axis, pairs)


def with_halo(block, sides, width):
    for axis, dim in sides:
        count = lax.axis_size(axis)
        forward = [(i, i + 1) for i in range(count - 1)]
        backward = [(target, source) for source, target in forward]
        low = lax.ppermute(
            lax.slice_in_dim(block, block.shape[dim] - width, None, axis=dim), axis, forward
        )
        high = lax.ppermute(lax.slice_in_dim(block, 0, width, axis=dim), axis, backward)
        block = jnp.concatenate([low, block, high], axis=dim)
    return block


def stiffness():
    table = np.zeros((8, 8), np.float32)
    levels = [4.0, 0.0, -1.0, -1.0]
    for first in range(8):
        for second in range(8):
            differ = first ^ second
            apart = (differ & 1) + (differ >> 1 & 1) + (differ >> 2 & 1)
            table[first, second] = levels[apart] / 12.0
    return table


def corners():
    return [(corner >> 2 & 1, corner >> 1 & 1, corner & 1) for corner in range(8)]


def conductance(density):
    return KMIN + (1.0 - KMIN) * (density * density * density)


def upper_masks(length):
    keep_z = (jnp.arange(length) % NZ < NZ - 1).astype(jnp.float32)
    ones = jnp.ones((length,), jnp.float32)
    picked = [keep_z if off_z else ones for off_x, off_y, off_z in corners()]
    return jnp.stack(picked)[:, None, None, :]


def spread_nodes(elems, rows, out_len):
    padded = jnp.pad(elems, ((0, 0), (0, 0), (0, 0), (1, 0)))
    summed = None
    for corner, (off_x, off_y, off_z) in enumerate(corners()):
        start_at = (1 - off_y) * NZ - off_z + 1
        piece = padded[corner, :, 1 - off_x : 1 - off_x + rows, start_at : start_at + out_len]
        summed = piece if summed is None else summed + piece
    return summed


def block_apply(extended, conduct_blk, rows, cols, k_elem):
    elem_len = (cols + 1) * NZ
    masks = upper_masks(elem_len)
    extended = jnp.pad(extended, ((0, 0), (0, 0), (0, 1)))
    corner_vals = (
        jnp.stack(
            [
                extended[
                    :, off_x : off_x + rows + 1, off_y * NZ + off_z : off_y * NZ + off_z + elem_len
                ]
                for off_x, off_y, off_z in corners()
            ]
        )
        * masks
    )
    elems = (
        jnp.einsum("nm,mlag->nlag", k_elem, corner_vals, precision=lax.Precision.HIGHEST)
        * conduct_blk
        * masks
    )
    return spread_nodes(elems, rows, cols * NZ)


def node_weights(conduct_blk, rows, cols, k_elem):
    elem_len = (cols + 1) * NZ
    masks = upper_masks(elem_len)
    weights = jnp.broadcast_to(conduct_blk * k_elem[0, 0], (8, 1, rows + 1, elem_len)) * masks
    return spread_nodes(weights, rows, cols * NZ)


def local_sums(first, second):
    return jnp.sum(first * second, axis=(1, 2))


def paired_dots(residual, scaled, applied):
    return lax.psum((local_sums(residual, scaled), local_sums(applied, scaled)), ("gx", "gy"))


def per_device(heat_source, density):
    load_count, x_cells, flat_len = heat_source.shape
    y_cells = flat_len // NZ
    conduct = conductance(density)
    k_elem = jnp.asarray(stiffness())
    row_in = from_behind(conduct[x_cells - 1 :], "gx", 1)
    conduct_x = jnp.concatenate([row_in, conduct], 0).reshape(x_cells + 1, y_cells, NZ)
    col_in = from_behind(conduct_x[:, y_cells - 1 :], "gy", 1)
    conduct_e = jnp.concatenate([col_in, conduct_x], 1).reshape(x_cells + 1, (y_cells + 1) * NZ)

    def operate(field, cycle):
        blocks = field.reshape(load_count, x_cells, y_cells, NZ)
        extended = with_halo(blocks, (("gx", 1), ("gy", 2)), 1)
        extended = extended.reshape(load_count, x_cells + 2, (y_cells + 2) * NZ)
        return (block_apply(extended, conduct_e, x_cells, y_cells, k_elem), cycle)

    precond_whole = node_weights(conduct_e, x_cells, y_cells, k_elem)

    def precond_at():
        return precond_whole

    start_cycle = 0
    solution = jnp.zeros_like(heat_source)
    cycle = start_cycle
    residual = heat_source
    scaled = residual / precond_at()
    applied, applied_cycle = operate(scaled, cycle)
    gamma, delta = paired_dots(residual, scaled, applied)
    alpha = gamma / delta
    beta = jnp.zeros_like(gamma)
    direction = None
    image_dir = None
    for step in range(ITERS):
        if direction is None:
            direction = scaled
            image_dir = applied
        else:
            direction = scaled + beta[:, None, None] * direction
            image_dir = applied + beta[:, None, None] * image_dir
        solution = solution + alpha[:, None, None] * direction
        residual = residual - alpha[:, None, None] * image_dir
        cycle = applied_cycle
        if step + 1 < ITERS:
            scaled = residual / precond_at()
            applied, applied_cycle = operate(scaled, cycle)
            gamma_next, delta = paired_dots(residual, scaled, applied)
            beta = gamma_next / gamma
            alpha = gamma_next / (delta - beta * gamma_next / alpha)
            gamma = gamma_next
    return (solution, residual)


def solution(mesh):
    placed = (P(None, "gx", "gy"), P("gx", "gy"))
    return jax.shard_map(
        per_device,
        mesh=mesh,
        in_specs=placed,
        out_specs=(P(None, "gx", "gy"), P(None, "gx", "gy")),
        check_vma=False,
    )
```

profile of v0, /device:TPU:0, one launch (start us, length us, event | category | flops | bytes accessed | tf_op | source)
XLA Modules:
  0.0 159.6 jit_solution(7123603473581914169)
XLA Ops:
  0.6 0.8 fusion.39
  1.5 4.9 %collective-permute-start = (f32[1,768]{1,0:T(1,128)S(1)}, f32[1,768]{1,0:T(1,128)S(1)}, u32[]{:S(2)}, u32[]{:S(2)}) collective-permute-start(f32[1,768]{1,0:T(1,128)S(1)} %slice.234), channel_id=1, source_target_pairs={{0,8},{8,16},{16,24},{1,9},{9,17},{17,25},{2,10},{10,18},{18,26},{... | collective-permute-start | bytes 9224 | tf_op jit(solution)/shard_map/ppermute | solution.py:17
  6.4 1.3 collective-permute-done
  7.8 1.3 collective-permute-start.1
  9.2 0.7 collective-permute-done.1
  10.3 1.0 broadcast_divide_fusion.1
  11.6 4.2 %collective-permute-start.2 = (f32[8,1,8,96]{3,2,0,1:T(8,128)S(1)}, f32[8,1,8,96]{3,2,0,1:T(8,128)S(1)}, u32[]{:S(2)}, u32[]{:S(2)}) collective-permute-start(f32[8,1,8,96]{3,2,0,1:T(8,128)S(1)} %copy.58), channel_id=1, source_target_pairs={{0,8},{8,16},{16,24},{1,9},{9,17},{17,25},{2,10},{10,18},{18,26},{... | collective-permute-start | bytes 73736 | tf_op jit(solution)/shard_map/ppermute | solution.py:25
  15.8 1.3 collective-permute-start.3
  17.4 4.2 %collective-permute-done.3 = f32[8,1,8,96]{3,2,0,1:T(8,128)S(1)} collective-permute-done((f32[8,1,8,96]{3,2,0,1:T(8,128)S(1)}, f32[8,1,8,96]{3,2,0,1:T(8,128)S(1)}, u32[]{:S(2)}, u32[]{:S(2)}) %collective-permute-start.3) | collective-permute-done | bytes 24608 | tf_op jit(solution)/shard_map/ppermute | solution.py:28
  21.7 2.7 %collective-permute-start.4 = (f32[8,18,1,96]{3,2,0,1:T(1,128)S(1)}, f32[8,18,1,96]{3,2,0,1:T(1,128)S(1)}, u32[]{:S(2)}, u32[]{:S(2)}) collective-permute-start(f32[8,18,1,96]{3,2,0,1:T(1,128)S(1)} %get-tuple-element.15), channel_id=1, source_target_pairs={{0,1},{1,2},{2,3},{3,4},{4,5},{5,6},{6,7},{8,9},{9,10},{10,11},{11... | collective-permute-start | bytes 165896 | tf_op jit(solution)/shard_map/ppermute | solution.py:25
  24.4 1.3 collective-permute-start.5
  25.7 5.1 %collective-permute-done.5 = f32[8,18,1,96]{3,2,0,1:T(1,128)S(1)} collective-permute-done((f32[8,18,1,96]{3,2,0,1:T(1,128)S(1)}, f32[8,18,1,96]{3,2,0,1:T(1,128)S(1)}, u32[]{:S(2)}, u32[]{:S(2)}) %collective-permute-start.5) | collective-permute-done | bytes 55328 | tf_op jit(solution)/shard_map/ppermute | solution.py:28
  31.0 0.4 reshape.131
  31.4 0.4 copy.13
  33.4 0.4 broadcast_multiply_fusion.1
  34.1 5.8 %bitcast_multiply_fusion.1 = f32[8,8,17,864]{3,0,2,1:T(8,128)S(1)} fusion(f32[8,864]{1,0:T(8,128)S(1)} %stack.71, f32[17,864]{1,0:T(8,128)S(1)} %reshape.129, f32[8,8,1,1]{1,0,3,2:T(8,128)S(1)} %copy-done.1, f32[8,8,17,864]{3,2,1,0:T(8,128)S(1)} %broadcast_multiply_fusion.1), kind=kOutput, calls=%fused_computation.4 | convolution fusion | flops 92123136 | bytes 7606912 | tf_op jit(solution)/shard_map/nm,mlag->nlag/dot_general | solution.py:85
  39.9 5.2 %fusion.25 = f32[1,8,16,768]{3,0,2,1:T(1,128)S(1)} fusion(f32[8,8,17,864]{3,0,2,1:T(8,128)S(1)} %bitcast_multiply_fusion.1), kind=kLoop, calls=%fused_computation.54 | loop fusion | flops 688128 | bytes 6651904 | tf_op jit(solution)/shard_map/add | solution.py:65
  45.3 43.9 %all-reduce.6 = (f32[8]{0:T(128)S(1)}, f32[8]{0:T(128)S(1)}) all-reduce(f32[8]{0:T(128)S(1)} %get-tuple-element.3, f32[8]{0:T(128)S(1)} %get-tuple-element.2), channel_id=1, replica_groups=mesh['gx'=4,'gy'=8] {'gx','gy'}, use_global_device_ids=true, to_apply=%region_1.2 | all-reduce | flops 16 | bytes 128 | tf_op jit(solution)/shard_map/psum | solution.py:104
  89.7 2.2 %collective-permute-start.6 = (f32[8,1,8,96]{3,2,0,1:T(8,128)S(1)}, f32[8,1,8,96]{3,2,0,1:T(8,128)S(1)}, u32[]{:S(2)}, u32[]{:S(2)}) collective-permute-start(f32[8,1,8,96]{3,2,0,1:T(8,128)S(1)} %copy.60), channel_id=1, source_target_pairs={{0,8},{8,16},{16,24},{1,9},{9,17},{17,25},{2,10},{10,18},{18,26},{... | collective-permute-start | bytes 73736 | tf_op jit(solution)/shard_map/ppermute | solution.py:25
  91.9 1.3 collective-permute-start.7
  93.5 4.2 %collective-permute-done.7 = f32[8,1,8,96]{3,2,0,1:T(8,128)S(1)} collective-permute-done((f32[8,1,8,96]{3,2,0,1:T(8,128)S(1)}, f32[8,1,8,96]{3,2,0,1:T(8,128)S(1)}, u32[]{:S(2)}, u32[]{:S(2)}) %collective-permute-start.7) | collective-permute-done | bytes 24608 | tf_op jit(solution)/shard_map/ppermute | solution.py:28
  97.8 1.3 collective-permute-start.8
  99.1 1.3 collective-permute-start.9
  100.4 4.4 %collective-permute-done.9 = f32[8,18,1,96]{3,2,0,1:T(1,128)S(1)} collective-permute-done((f32[8,18,1,96]{3,2,0,1:T(1,128)S(1)}, f32[8,18,1,96]{3,2,0,1:T(1,128)S(1)}, u32[]{:S(2)}, u32[]{:S(2)}) %collective-permute-start.9) | collective-permute-done | bytes 55328 | tf_op jit(solution)/shard_map/ppermute | solution.py:28
  105.0 0.4 reshape.133
  105.4 0.4 copy.26
  107.3 0.4 broadcast_multiply_fusion
  107.8 6.1 %fusion = f32[8,17,864,8]{2,3,1,0:T(8,128)S(1)} fusion(f32[8,8,1,1]{1,0,3,2:T(8,128)S(1)} %copy-done.1, f32[8,8,17,864]{3,2,1,0:T(8,128)S(1)} %broadcast_multiply_fusion), kind=kOutput, calls=%fused_computation.5 | convolution fusion | flops 90243072 | bytes 7520512 | tf_op jit(solution)/shard_map/nm,mlag->nlag/dot_general | solution.py:85
  113.9 0.9 bitcast_multiply_fusion
  114.7 0.9 fusion.37
  115.6 42.8 %all-reduce.5 = (f32[8]{0:T(128)S(1)}, f32[8]{0:T(128)S(1)}) all-reduce(f32[8]{0:T(128)S(1)} %get-tuple-element.5, f32[8]{0:T(128)S(1)} %get-tuple-element.4), channel_id=1, replica_groups=mesh['gx'=4,'gy'=8] {'gx','gy'}, use_global_device_ids=true, to_apply=%region_5.6 | all-reduce | flops 16 | bytes 128 | tf_op jit(solution)/shard_map/psum | solution.py:104
  158.5 1.1 fusion.36
  (58 shorter events, 6.2 us)
Async XLA Ops:
  1.5 6.2 %collective-permute-start = (f32[1,768]{1,0:T(1,128)S(1)}, f32[1,768]{1,0:T(1,128)S(1)}, u32[]{:S(2)}, u32[]{:S(2)}) collective-permute-start(f32[1,768]{1,0:T(1,128)S(1)} %slice.234), channel_id=1, source_target_pairs={{0,8},{8,16},{16,24},{1,9},{9,17},{17,25},{2,10},{10,18},{18,26},{... | collective-permute-start | bytes 9224 | tf_op jit(solution)/shard_map/ppermute | solution.py:17
  7.8 2.1 %collective-permute-start.1 = (f32[17,1,96]{2,1,0:T(1,128)S(1)}, f32[17,1,96]{2,1,0:T(1,128)S(1)}, u32[]{:S(2)}, u32[]{:S(2)}) collective-permute-start(f32[17,1,96]{2,1,0:T(1,128)S(1)} %slice.235), channel_id=1, source_target_pairs={{0,1},{1,2},{2,3},{3,4},{4,5},{5,6},{6,7},{8,9},{9,10},{10,11},{11... | collective-permute-start | bytes 19592 | tf_op jit(solution)/shard_map/ppermute | solution.py:17
  11.6 5.8 %collective-permute-start.2 = (f32[8,1,8,96]{3,2,0,1:T(8,128)S(1)}, f32[8,1,8,96]{3,2,0,1:T(8,128)S(1)}, u32[]{:S(2)}, u32[]{:S(2)}) collective-permute-start(f32[8,1,8,96]{3,2,0,1:T(8,128)S(1)} %copy.58), channel_id=1, source_target_pairs={{0,8},{8,16},{16,24},{1,9},{9,17},{17,25},{2,10},{10,18},{18,26},{... | collective-permute-start | bytes 73736 | tf_op jit(solution)/shard_map/ppermute | solution.py:25
  15.8 5.8 %collective-permute-start.3 = (f32[8,1,8,96]{3,2,0,1:T(8,128)S(1)}, f32[8,1,8,96]{3,2,0,1:T(8,128)S(1)}, u32[]{:S(2)}, u32[]{:S(2)}) collective-permute-start(f32[8,1,8,96]{3,2,0,1:T(8,128)S(1)} %copy.59), channel_id=1, source_target_pairs={{8,0},{16,8},{24,16},{9,1},{17,9},{25,17},{10,2},{18,10},{26,18},{... | collective-permute-start | bytes 73736 | tf_op jit(solution)/shard_map/ppermute | solution.py:28
  21.7 4.0 %collective-permute-start.4 = (f32[8,18,1,96]{3,2,0,1:T(1,128)S(1)}, f32[8,18,1,96]{3,2,0,1:T(1,128)S(1)}, u32[]{:S(2)}, u32[]{:S(2)}) collective-permute-start(f32[8,18,1,96]{3,2,0,1:T(1,128)S(1)} %get-tuple-element.15), channel_id=1, source_target_pairs={{0,1},{1,2},{2,3},{3,4},{4,5},{5,6},{6,7},{8,9},{9,10},{10,11},{11... | collective-permute-start | bytes 165896 | tf_op jit(solution)/shard_map/ppermute | solution.py:25
  24.4 6.4 %collective-permute-start.5 = (f32[8,18,1,96]{3,2,0,1:T(1,128)S(1)}, f32[8,18,1,96]{3,2,0,1:T(1,128)S(1)}, u32[]{:S(2)}, u32[]{:S(2)}) collective-permute-start(f32[8,18,1,96]{3,2,0,1:T(1,128)S(1)} %get-tuple-element.16), channel_id=1, source_target_pairs={{1,0},{2,1},{3,2},{4,3},{5,4},{6,5},{7,6},{9,8},{10,9},{11,10},{12... | collective-permute-start | bytes 165896 | tf_op jit(solution)/shard_map/ppermute | solution.py:28
  33.4 0.7 copy-start.1
  34.1 11.0 %copy-start = (f32[8,16,768]{2,1,0:T(8,128)S(1)}, f32[8,16,768]{2,1,0:T(8,128)}, u32[]{:S(2)}) copy-start(f32[8,16,768]{2,1,0:T(8,128)} %param.3) | copy-start | bytes 1179652
  89.7 3.7 %collective-permute-start.6 = (f32[8,1,8,96]{3,2,0,1:T(8,128)S(1)}, f32[8,1,8,96]{3,2,0,1:T(8,128)S(1)}, u32[]{:S(2)}, u32[]{:S(2)}) collective-permute-start(f32[8,1,8,96]{3,2,0,1:T(8,128)S(1)} %copy.60), channel_id=1, source_target_pairs={{0,8},{8,16},{16,24},{1,9},{9,17},{17,25},{2,10},{10,18},{18,26},{... | collective-permute-start | bytes 73736 | tf_op jit(solution)/shard_map/ppermute | solution.py:25
  91.9 5.8 %collective-permute-start.7 = (f32[8,1,8,96]{3,2,0,1:T(8,128)S(1)}, f32[8,1,8,96]{3,2,0,1:T(8,128)S(1)}, u32[]{:S(2)}, u32[]{:S(2)}) collective-permute-start(f32[8,1,8,96]{3,2,0,1:T(8,128)S(1)} %copy.61), channel_id=1, source_target_pairs={{8,0},{16,8},{24,16},{9,1},{17,9},{25,17},{10,2},{18,10},{26,18},{... | collective-permute-start | bytes 73736 | tf_op jit(solution)/shard_map/ppermute | solution.py:28
  97.8 2.6 %collective-permute-start.8 = (f32[8,18,1,96]{3,2,0,1:T(1,128)S(1)}, f32[8,18,1,96]{3,2,0,1:T(1,128)S(1)}, u32[]{:S(2)}, u32[]{:S(2)}) collective-permute-start(f32[8,18,1,96]{3,2,0,1:T(1,128)S(1)} %get-tuple-element.13), channel_id=1, source_target_pairs={{0,1},{1,2},{2,3},{3,4},{4,5},{5,6},{6,7},{8,9},{9,10},{10,11},{11... | collective-permute-start | bytes 165896 | tf_op jit(solution)/shard_map/ppermute | solution.py:25
  99.1 5.7 %collective-permute-start.9 = (f32[8,18,1,96]{3,2,0,1:T(1,128)S(1)}, f32[8,18,1,96]{3,2,0,1:T(1,128)S(1)}, u32[]{:S(2)}, u32[]{:S(2)}) collective-permute-start(f32[8,18,1,96]{3,2,0,1:T(1,128)S(1)} %get-tuple-element.14), channel_id=1, source_target_pairs={{1,0},{2,1},{3,2},{4,3},{5,4},{6,5},{7,6},{9,8},{10,9},{11,10},{12... | collective-permute-start | bytes 165896 | tf_op jit(solution)/shard_map/ppermute | solution.py:28
where the time goes:
time: 160 us
  blocking collectives  86.8 us (54%)
  starting transfers between devices  21.7 us (14%)
  waiting for transfers between devices  20.3 us (13%)
  other arithmetic  11.9 us (7%)
  matrix products  11.9 us (7%)
  local copies, waits for them, and re-layouts  5.96 us (4%)
    psum x2, blocking collectives, paired_dots(): lax.psum((local_sums(residual, scaled), local_sums(applied, scaled)), ('g...  86.8 us
    ppermute x4, waiting for transfers between devices, with_halo(): lax.ppermute(lax.slice_in_dim(block, 0, width, axis=dim), axis, backward)  17.8 us
    dot_general x2, matrix products, block_apply(): jnp.einsum('nm,mlag->nlag', k_elem, corner_vals, precision=lax.Precision....  11.9 us
    ppermute x4, starting transfers between devices, with_halo(): lax.ppermute(lax.slice_in_dim(block, block.shape[dim] - width, None, axis...  10.3 us
    ppermute x2, starting transfers between devices, from_behind(): return lax.ppermute(shard, axis, pairs)  6.22 us
    add x2, other arithmetic, spread_nodes(): summed = piece if summed is None else summed + piece  5.33 us
    ppermute x4, starting transfers between devices, with_halo(): lax.ppermute(lax.slice_in_dim(block, 0, width, axis=dim), axis, backward)  5.17 us
  transfers between devices with their start and end apart: 10, of which 8 were waited for; matrix products, arithmetic and copies ran while one was open for 0% of the time, Pallas kernels for 0%

commit v1 on v0

v1 whole, which is shorter than its diff:
```python
import functools

import jax
import jax.numpy as jnp
from jax import lax
from jax.experimental import pallas as pl
from jax.experimental.pallas import tpu as pltpu
from jax.sharding import PartitionSpec as P

NZ = 96
KMIN = 0.001
LANES = 128
SUB = 8


def lane_ids(rows):
    return lax.broadcasted_iota(jnp.int32, (rows, LANES), 1)


def read_z(read, y, rows):
    start = y * NZ
    block, offset = start // LANES, start % LANES
    lane = lane_ids(rows)
    first = read(block)
    if offset:
        first = pltpu.roll(first, LANES - offset, 1)
    if offset + NZ > LANES:
        second = pltpu.roll(read(block + 1), LANES - offset, 1)
        first = jnp.where(lane < LANES - offset, first, second)
    return jnp.where(lane < NZ, first, 0.0)


def write_z(read_tile, block, rows):
    lane = lane_ids(rows)
    start = block * LANES
    out, at = None, start
    while at < start + LANES:
        y, z = at // NZ, at % NZ
        here = at - start
        piece = read_tile(y)
        shift = (here - z) % LANES
        if shift:
            piece = pltpu.roll(piece, shift, 1)
        out = piece if out is None else jnp.where(lane < here, out, piece)
        at += NZ - z
    return out


def pack_x_kernel(sizes, b_ref, d_ref, bt_ref, dt_ref, up_ref, down_ref):
    loads, nx, ny = sizes
    for load in range(loads):
        for x0 in range(0, nx, SUB):
            for y in range(ny):
                tile = read_z(
                    lambda t: b_ref[load, x0 : x0 + SUB, t * LANES : (t + 1) * LANES], y, SUB
                )
                bt_ref[pl.ds((x0 * ny + y) * loads + load, SUB, stride=ny * loads), :] = tile
    for x0 in range(0, nx, SUB):
        for y in range(ny):
            tile = read_z(lambda t: d_ref[x0 : x0 + SUB, t * LANES : (t + 1) * LANES], y, SUB)
            dt_ref[pl.ds(x0 * ny + y, SUB, stride=ny), :] = tile
    plane = ny * loads
    up_ref[: 2 * plane] = bt_ref[(nx - 2) * plane :]
    up_ref[2 * plane :] = dt_ref[(nx - 3) * ny :]
    down_ref[: 2 * plane] = bt_ref[: 2 * plane]
    down_ref[2 * plane :] = dt_ref[: 2 * ny]


def ext_rows(x, nx, plane, inner, low, high, low_planes, low_at, high_at):
    if x < 0:
        return low, low_at + (x + low_planes) * plane
    if x >= nx:
        return high, high_at + (x - nx) * plane
    return inner, x * plane


def pack_y_kernel(sizes, bt_ref, dt_ref, low_ref, high_ref, up_ref, down_ref):
    loads, nx, ny = sizes
    plane = ny * loads
    for x in range(-2, nx + 2):
        ref, row = ext_rows(x, nx, plane, bt_ref, low_ref, high_ref, 2, 0, 0)
        to = (x + 2) * 2 * loads
        up_ref[to : to + 2 * loads] = ref[row + (ny - 2) * loads : row + ny * loads]
        down_ref[to : to + 2 * loads] = ref[row : row + 2 * loads]
    base = (nx + 4) * 2 * loads
    for x in range(-3, nx + 2):
        ref, row = ext_rows(x, nx, ny, dt_ref, low_ref, high_ref, 3, 2 * plane, 2 * plane)
        to = base + (x + 3) * 3
        up_ref[to : to + 3] = ref[row + ny - 3 : row + ny]
        to = base + (x + 3) * 2
        down_ref[to : to + 2] = ref[row : row + 2]
    up_ref[base + (nx + 5) * 3 :] = jnp.zeros_like(up_ref[base + (nx + 5) * 3 :])
    down_ref[base + (nx + 5) * 2 :] = jnp.zeros_like(down_ref[base + (nx + 5) * 2 :])


def solve_kernel(
    sizes, bt_ref, dt_ref, xl_ref, xh_ref, yl_ref, yh_ref,
    q_ref, v_ref, inv_ref, sums_ref,
    dens, cond, invx, bx, zx, zs, wx, ws, qx, carry,
):
    loads, nx, ny = sizes
    plane = ny * loads
    base = (nx + 4) * 2 * loads
    for x in range(-3, nx + 2):
        ref, row = ext_rows(x, nx, ny, dt_ref, xl_ref, xh_ref, 3, 2 * plane, 2 * plane)
        dens[x + 3, 3 : 3 + ny, :] = ref[row : row + ny]
        at = base + (x + 3) * 3
        dens[x + 3, 0:3, :] = yl_ref[at : at + 3]
        at = base + (x + 3) * 2
        dens[x + 3, 3 + ny : 5 + ny, :] = yh_ref[at : at + 2]
    mx, my = nx + 4, ny + 4
    d = dens[...]
    conduct = jnp.where(d > 0.0, (KMIN + (1.0 - KMIN) * (d * d * d)) * (1.0 / 12.0), 0.0)
    pair = conduct[:-1] + conduct[1:]
    pair = pair[:, :-1, :] + pair[:, 1:, :]
    here = conduct[1:, 1:, :]
    for x in range(mx):
        total = 4.0 * (pair[x] + pltpu.roll(pair[x], 1, 1))
        inverse = jnp.where(here[x] > 0.0, 1.0 / total, 0.0)
        for y in range(my):
            row = inverse[y : y + 1, :]
            invx[x, y] = jnp.broadcast_to(row, (loads, LANES))
            if x < mx - 1 and y < my - 1:
                cond[x, y] = jnp.broadcast_to(here[x, y : y + 1, :], (loads, LANES))
        if 2 <= x < 2 + nx:
            inv_ref[(x - 2) * ny : (x - 1) * ny, :] = inverse[2 : 2 + ny, :]
    def stage(x, y, tile):
        bx[x, y] = tile
        scaled = tile * invx[x, y]
        zx[x, y] = scaled
        zs[x, y] = pltpu.roll(scaled, LANES - 1, 1)

    for x in range(mx):
        ref, row = ext_rows(x - 2, nx, plane, bt_ref, xl_ref, xh_ref, 2, 0, 0)
        for y in range(ny):
            at = row + y * loads
            stage(x, y + 2, ref[at : at + loads])
        for y in range(2):
            at = (x * 2 + y) * loads
            stage(x, y, yl_ref[at : at + loads])
            stage(x, y + 2 + ny, yh_ref[at : at + loads])

    def element_plane(a, a0, rows, low, low_s, first, emit):
        above_lo = above_hi = None
        left_lo = left_hi = None
        p0, p0s = low[a, a0], low_s[a, a0]
        p1, p1s = low[a + 1, a0], low_s[a + 1, a0]
        for step in range(rows):
            y = a0 + step
            r0, r0s = low[a, y + 1], low_s[a, y + 1]
            r1, r1s = low[a + 1, y + 1], low_s[a + 1, y + 1]
            c = cond[a, y]
            even = p0 + r1 + (r0s + p1s)
            odd = r0 + p1 + (p0s + r1s)
            t000 = c * (even + r1s)
            t110 = c * (even + p0s)
            t011 = c * (even + p1)
            t101 = c * (even + r0)
            t111 = c * (odd + p0)
            t001 = c * (odd + r1)
            t100 = c * (odd + r0s)
            t010 = c * (odd + p1s)
            if step and not first:
                lo = t000 + left_lo + carry[0, y]
                hi = t001 + left_hi + carry[1, y]
                emit(y, lo + pltpu.roll(hi, 1, 1))
            left_lo, left_hi = t010, t011
            if step:
                carry[0, y] = t100 + above_lo
                carry[1, y] = t101 + above_hi
            above_lo, above_hi = t110, t111
            p0, p0s, p1, p1s = r0, r0s, r1, r1s

    def first_pass(a, first):
        def emit(y, total):
            image = 1.25 * bx[a, y] - total
            weighted = image * invx[a, y]
            qx[a, y] = image
            wx[a, y] = weighted
            ws[a, y] = pltpu.roll(weighted, LANES - 1, 1)

        element_plane(a, 0, my - 1, zx, zs, first, emit)

    first_pass(0, True)

    @pl.loop(1, mx - 1)
    def _(a):
        first_pass(a, False)

    def second_pass(a, first, sums):
        sums = list(sums)

        def emit(y, total):
            image = qx[a, y]
            again = 1.25 * image - total
            row = pl.multiple_of(((a - 2) * ny + (y - 2)) * loads, SUB)
            q_ref[pl.ds(row, loads), :] = image
            v_ref[pl.ds(row, loads), :] = again
            scaled, weighted = zx[a, y], wx[a, y]
            sums[0] = sums[0] + bx[a, y] * scaled
            sums[1] = sums[1] + scaled * image
            sums[2] = sums[2] + image * weighted
            sums[3] = sums[3] + weighted * again

        element_plane(a, 1, my - 3, wx, ws, first, emit)
        return tuple(sums)

    zero = jnp.zeros((loads, LANES), jnp.float32)
    second_pass(1, True, (zero,) * 4)
    sums = lax.fori_loop(2, mx - 2, lambda a, s: second_pass(a, False, s), (zero,) * 4)
    lane = lane_ids(loads)
    packed = zero
    for place, part in enumerate(sums):
        packed = jnp.where(lane == place, jnp.sum(part, axis=1, keepdims=True), packed)
    sums_ref[...] = packed


def unpack_kernel(sizes, q_ref, v_ref, inv_ref, qo_ref, vo_ref, io_ref):
    loads, nx, ny = sizes
    for x0 in range(0, nx, SUB):
        for block in range(ny * NZ // LANES):
            lanes = slice(block * LANES, (block + 1) * LANES)
            io_ref[x0 : x0 + SUB, lanes] = write_z(
                lambda y: inv_ref[pl.ds(x0 * ny + y, SUB, stride=ny), :], block, SUB
            )
            for ref, out in ((q_ref, qo_ref), (v_ref, vo_ref)):
                for load in range(loads):
                    out[load, x0 : x0 + SUB, lanes] = write_z(
                        lambda y: ref[
                            pl.ds((x0 * ny + y) * loads + load, SUB, stride=ny * loads), :
                        ],
                        block,
                        SUB,
                    )


def shift(array, axis, by):
    length = lax.axis_size(axis)
    pairs = [(i, i + by) for i in range(length) if 0 <= i + by < length]
    return lax.ppermute(array, axis, pairs)


def prime_factors(number):
    factors, divisor = [], 2
    while number > 1:
        while number % divisor == 0:
            factors.append(divisor)
            number //= divisor
        divisor += 1
    return factors


def sum_over(array, axis):
    length = lax.axis_size(axis)
    stride = 1
    for factor in prime_factors(length):
        total = array
        for step in range(1, factor):
            pairs = []
            for i in range(length):
                digit = i // stride % factor
                pairs.append((i, i + ((digit + step) % factor - digit) * stride))
            total = total + lax.ppermute(array, axis, pairs)
        array = total
        stride *= factor
    return array


def per_device(heat_source, density):
    loads, nx, flat = heat_source.shape
    ny = flat // NZ
    sizes = (loads, nx, ny)
    plane = ny * loads
    f32 = jnp.float32

    def shape(*dims):
        return jax.ShapeDtypeStruct(dims, f32)

    def scratch(*dims):
        return pltpu.VMEM(dims, f32)

    params = pltpu.CompilerParams(vmem_limit_bytes=48 * 1024 * 1024)
    bt, dt, x_up, x_down = pl.pallas_call(
        functools.partial(pack_x_kernel, sizes),
        out_shape=(
            shape(nx * plane, LANES),
            shape(nx * ny, LANES),
            shape(2 * plane + 3 * ny, LANES),
            shape(2 * plane + 2 * ny, LANES),
        ),
        compiler_params=params,
    )(heat_source, density)
    x_low, x_high = shift(x_up, "gx", 1), shift(x_down, "gx", -1)
    tail = lambda width: (nx + 4) * 2 * loads + -(-(nx + 5) * width // SUB) * SUB
    y_up, y_down = pl.pallas_call(
        functools.partial(pack_y_kernel, sizes),
        out_shape=(shape(tail(3), LANES), shape(tail(2), LANES)),
        compiler_params=params,
    )(bt, dt, x_low, x_high)
    y_low, y_high = shift(y_up, "gy", 1), shift(y_down, "gy", -1)
    mx, my = nx + 4, ny + 4
    q_t, v_t, inv_t, sums = pl.pallas_call(
        functools.partial(solve_kernel, sizes),
        out_shape=(
            shape(nx * plane, LANES),
            shape(nx * plane, LANES),
            shape(nx * ny, LANES),
            shape(loads, LANES),
        ),
        scratch_shapes=[
            scratch(mx + 1, my + 1, LANES),
            scratch(mx - 1, my - 1, loads, LANES),
        ]
        + [scratch(mx, my, loads, LANES)] * 7
        + [scratch(2, my, loads, LANES)],
        compiler_params=params,
    )(bt, dt, x_low, x_high, y_low, y_high)
    totals = sum_over(sum_over(sums, "gx"), "gy")
    image, again, inverse = pl.pallas_call(
        functools.partial(unpack_kernel, sizes),
        out_shape=(shape(*heat_source.shape), shape(*heat_source.shape), shape(nx, flat)),
        compiler_params=params,
    )(q_t, v_t, inv_t)
    rz, direct, square, last = (totals[:, place] for place in range(4))
    alpha = rz / direct
    rz_next = alpha * alpha * square - rz
    beta = rz_next / rz
    grown = 1.0 + beta
    alpha_next = rz_next / (
        grown * grown * direct - 2.0 * alpha * grown * square + alpha * alpha * last
    )
    first = (alpha + alpha_next * grown)[:, None, None]
    second = (alpha_next * alpha)[:, None, None]
    solution_field = (first * heat_source - second * image) * inverse
    residual = heat_source - first * image + second * again
    return solution_field, residual


def solution(mesh):
    placed = (P(None, "gx", "gy"), P("gx", "gy"))
    return jax.shard_map(
        per_device,
        mesh=mesh,
        in_specs=placed,
        out_specs=(P(None, "gx", "gy"), P(None, "gx", "gy")),
        check_vma=False,
    )
```

time: 160 us -> 46.6 us (0.29)
  blocking collectives: 86.8 us -> 0 us
  matrix products: 11.9 us -> 0 us
  other arithmetic: 11.9 us -> 1.1 us
  Pallas kernels: 0 us -> 6.62 us
  waiting for transfers between devices: 20.3 us -> 15.8 us
  local copies, waits for them, and re-layouts: 5.96 us -> 2.01 us
    psum x2 -> x0, blocking collectives: 86.8 us -> none  [paired_dots(): lax.psum((local_sums(residual, scaled), local_sums(applied, scaled)), ('g...]
    dot_general x2 -> x0, matrix products: 11.9 us -> none  [block_apply(): jnp.einsum('nm,mlag->nlag', k_elem, corner_vals, precision=lax.Precision....]
    pallas_call x0 -> x4, Pallas kernels: none -> 6.62 us  [the longest x1 5.33 us: per_device(): pl.pallas_call(functools.partial(solve_kernel, sizes), out_shape=(shape(n...]
    add x3 -> x8, other arithmetic: 6.14 us -> 1.09 us  [the longest x1 1.05 us: per_device(): residual = heat_source - first * image + second * again]
    ppermute x10 -> x9, waiting for transfers between devices: 20.3 us -> 15.8 us  [the longest x4 8.69 us: shift(): return lax.ppermute(array, axis, pairs)]
    reshape x8 -> x0, local copies, waits for them, and re-layouts: 2.15 us -> none  [the longest x4 1.44 us: operate(): extended = extended.reshape(load_count, x_cells + 2, (y_cells + 2) * NZ)]
    mul x5 -> x1, other arithmetic: 1.79 us -> 0.01 us  [per_device(): second = (alpha_next * alpha)[:, None, None]]
    ppermute x10 -> x9, starting transfers between devices: 21.7 us -> 20.1 us  [the longest x5 11.3 us: sum_over(): total = total + lax.ppermute(array, axis, pairs)]
  transfers between devices with their start and end apart: 10 -> 9, of which waited for: 8 -> 7; matrix products, arithmetic and copies ran while one was open for 0% -> 0% of each run, Pallas kernels for 0% -> 2%
where the time goes in v1:
time: 46.6 us; the launch traced here: 46.4 us
  starting transfers between devices  20.1 us (43%)
  waiting for transfers between devices  15.8 us (34%)
  Pallas kernels  6.62 us (14%)
  local copies, waits for them, and re-layouts  2.01 us (4%)
  other arithmetic  1.1 us (2%)
  between operations  0.72 us (2%)
    ppermute x5, starting transfers between devices, sum_over(): total = total + lax.ppermute(array, axis, pairs)  11.3 us
    ppermute x4, starting transfers between devices, shift(): return lax.ppermute(array, axis, pairs)  8.82 us
    ppermute x4, waiting for transfers between devices, shift(): return lax.ppermute(array, axis, pairs)  8.69 us
    ppermute x5, waiting for transfers between devices, sum_over(): total = total + lax.ppermute(array, axis, pairs)  7.14 us
    pallas_call x1, Pallas kernels, per_device(): pl.pallas_call(functools.partial(solve_kernel, sizes), out_shape=(shape(n...  5.33 us
    unnamed x6, local copies, waits for them, and re-layouts  1.79 us
    add x1, other arithmetic, per_device(): residual = heat_source - first * image + second * again  1.05 us
  transfers between devices with their start and end apart: 9, of which 7 were waited for; matrix products, arithmetic and copies ran while one was open for 0% of the time, Pallas kernels for 2%

profile of v1, /device:TPU:0, one launch (start us, length us, event | category | flops | bytes accessed | tf_op | source)
XLA Modules:
  0.0 46.4 jit_solution(3449905738389713808)
XLA Ops:
  0.6 0.0 copy-start
  0.6 1.0 %copy-done = f32[8,16,768]{2,1,0:T(8,128)S(1)} copy-done((f32[8,16,768]{2,1,0:T(8,128)S(1)}, f32[8,16,768]{2,1,0:T(8,128)}, u32[]{:S(2)}) %copy-start) | copy-done | bytes 393240
  1.6 0.0 copy-start.2
  1.6 0.8 %copy-done.2 = f32[16,768]{1,0:T(8,128)S(1)} copy-done((f32[16,768]{1,0:T(8,128)S(1)}, f32[16,768]{1,0:T(8,128)}, u32[]{:S(2)}) %copy-start.2) | copy-done | bytes 49176
  2.4 0.5 shard_map.41
  2.9 4.9 %collective-permute-start = (f32[152,128]{1,0:T(8,128)S(1)}, f32[152,128]{1,0:T(8,128)S(1)}, u32[]{:S(2)}, u32[]{:S(2)}) collective-permute-start(f32[152,128]{1,0:T(8,128)S(1)} %get-tuple-element.17), channel_id=1, source_target_pairs={{0,8},{8,16},{16,24},{1,9},{9,17},{17,25},{2,10},{10,18},{18,26},{... | collective-permute-start | bytes 233480 | tf_op jit(solution)/shard_map/ppermute | solution.py:240
  7.8 1.3 %collective-permute-start.1 = (f32[144,128]{1,0:T(8,128)S(1)}, f32[144,128]{1,0:T(8,128)S(1)}, u32[]{:S(2)}, u32[]{:S(2)}) collective-permute-start(f32[144,128]{1,0:T(8,128)S(1)} %get-tuple-element.18), channel_id=1, source_target_pairs={{8,0},{16,8},{24,16},{9,1},{17,9},{25,17},{10,2},{18,10},{26,18},{... | collective-permute-start | bytes 221192 | tf_op jit(solution)/shard_map/ppermute | solution.py:240
  9.1 4.9 %collective-permute-done.1.high_ref.xh_ref = f32[144,128]{1,0:T(8,128)S(1)} collective-permute-done((f32[144,128]{1,0:T(8,128)S(1)}, f32[144,128]{1,0:T(8,128)S(1)}, u32[]{:S(2)}, u32[]{:S(2)}) %collective-permute-start.1) | collective-permute-done | bytes 73760 | tf_op jit(solution)/shard_map/ppermute | solution.py:240
  14.1 0.0 collective-permute-done.low_ref.xl_ref
  14.1 1.3 %collective-permute-start.2 = (f32[384,128]{1,0:T(8,128)S(1)}, f32[384,128]{1,0:T(8,128)S(1)}, u32[]{:S(2)}, u32[]{:S(2)}) collective-permute-start(f32[384,128]{1,0:T(8,128)S(1)} %get-tuple-element.19), channel_id=1, source_target_pairs={{0,1},{1,2},{2,3},{3,4},{4,5},{5,6},{6,7},{8,9},{9,10},{10,11},{11... | collective-permute-start | bytes 589832 | tf_op jit(solution)/shard_map/ppermute | solution.py:240
  15.4 1.3 %collective-permute-start.3 = (f32[368,128]{1,0:T(8,128)S(1)}, f32[368,128]{1,0:T(8,128)S(1)}, u32[]{:S(2)}, u32[]{:S(2)}) collective-permute-start(f32[368,128]{1,0:T(8,128)S(1)} %get-tuple-element.20), channel_id=1, source_target_pairs={{1,0},{2,1},{3,2},{4,3},{5,4},{6,5},{7,6},{9,8},{10,9},{11,10},{12... | collective-permute-start | bytes 565256 | tf_op jit(solution)/shard_map/ppermute | solution.py:240
  16.7 3.7 %collective-permute-done.3.yh_ref = f32[368,128]{1,0:T(8,128)S(1)} collective-permute-done((f32[368,128]{1,0:T(8,128)S(1)}, f32[368,128]{1,0:T(8,128)S(1)}, u32[]{:S(2)}, u32[]{:S(2)}) %collective-permute-start.3) | collective-permute-done | bytes 188448 | tf_op jit(solution)/shard_map/ppermute | solution.py:240
  20.5 0.0 collective-permute-done.2.yl_ref
  20.5 5.3 %shard_map.43 = (f32[1024,128]{1,0:T(8,128)S(1)}, f32[1024,128]{1,0:T(8,128)S(1)}, f32[128,128]{1,0:T(8,128)S(1)}, f32[8,128]{1,0:T(8,128)S(1)}) custom-call(f32[1024,128]{1,0:T(8,128)S(1)} %get-tuple-element.15.bt_ref, f32[128,128]{1,0:T(8,128)S(1)} %get-tuple-element.16.dt_ref, f32[152,128]{1,0:T(8,128)S(1)} %collective-permute-done.low_ref.xl_ref, ...), custom_call_target="tpu_custom_call" | custom-call | tf_op jit(solution)/shard_map/pallas_call | solution.py:302
  25.8 1.6 %collective-permute-start.4 = (f32[8,128]{1,0:T(8,128)S(1)}, f32[8,128]{1,0:T(8,128)S(1)}, u32[]{:S(2)}, u32[]{:S(2)}) collective-permute-start(f32[8,128]{1,0:T(8,128)S(1)} %get-tuple-element.21), channel_id=1, source_target_pairs={{0,8},{8,0},{16,24},{24,16},{1,9},{9,1},{17,25},{25,17},{2,10},{10... | collective-permute-start | bytes 12296 | tf_op jit(solution)/shard_map/ppermute | solution.py:263
  27.4 2.0 %collective-permute-done.4 = f32[8,128]{1,0:T(8,128)S(1)} collective-permute-done((f32[8,128]{1,0:T(8,128)S(1)}, f32[8,128]{1,0:T(8,128)S(1)}, u32[]{:S(2)}, u32[]{:S(2)}) %collective-permute-start.4) | collective-permute-done | bytes 4128 | tf_op jit(solution)/shard_map/ppermute | solution.py:263
  29.4 2.6 %collective-permute-start.5 = (f32[8,128]{1,0:T(8,128)S(1)}, f32[8,128]{1,0:T(8,128)S(1)}, u32[]{:S(2)}, u32[]{:S(2)}) collective-permute-start(f32[8,128]{1,0:T(8,128)S(1)} %add.45), channel_id=1, source_target_pairs={{0,16},{8,24},{16,0},{24,8},{1,17},{9,25},{17,1},{25,9},{2,18},{10... | collective-permute-start | bytes 12296 | tf_op jit(solution)/shard_map/ppermute | solution.py:263
  32.0 1.9 %collective-permute-done.5 = f32[8,128]{1,0:T(8,128)S(1)} collective-permute-done((f32[8,128]{1,0:T(8,128)S(1)}, f32[8,128]{1,0:T(8,128)S(1)}, u32[]{:S(2)}, u32[]{:S(2)}) %collective-permute-start.5) | collective-permute-done | bytes 4128 | tf_op jit(solution)/shard_map/ppermute | solution.py:263
  33.9 1.8 %collective-permute-start.6 = (f32[8,128]{1,0:T(8,128)S(1)}, f32[8,128]{1,0:T(8,128)S(1)}, u32[]{:S(2)}, u32[]{:S(2)}) collective-permute-start(f32[8,128]{1,0:T(8,128)S(1)} %add.46), channel_id=1, source_target_pairs={{0,1},{1,0},{2,3},{3,2},{4,5},{5,4},{6,7},{7,6},{8,9},{9,8},{10,11... | collective-permute-start | bytes 12296 | tf_op jit(solution)/shard_map/ppermute | solution.py:263
  35.7 0.8 %collective-permute-done.6 = f32[8,128]{1,0:T(8,128)S(1)} collective-permute-done((f32[8,128]{1,0:T(8,128)S(1)}, f32[8,128]{1,0:T(8,128)S(1)}, u32[]{:S(2)}, u32[]{:S(2)}) %collective-permute-start.6) | collective-permute-done | bytes 4128 | tf_op jit(solution)/shard_map/ppermute | solution.py:263
  36.5 2.4 %collective-permute-start.7 = (f32[8,128]{1,0:T(8,128)S(1)}, f32[8,128]{1,0:T(8,128)S(1)}, u32[]{:S(2)}, u32[]{:S(2)}) collective-permute-start(f32[8,128]{1,0:T(8,128)S(1)} %add.47), channel_id=1, source_target_pairs={{0,2},{1,3},{2,0},{3,1},{4,6},{5,7},{6,4},{7,5},{8,10},{9,11},{10,... | collective-permute-start | bytes 12296 | tf_op jit(solution)/shard_map/ppermute | solution.py:263
  38.9 1.6 %collective-permute-done.7 = f32[8,128]{1,0:T(8,128)S(1)} collective-permute-done((f32[8,128]{1,0:T(8,128)S(1)}, f32[8,128]{1,0:T(8,128)S(1)}, u32[]{:S(2)}, u32[]{:S(2)}) %collective-permute-start.7) | collective-permute-done | bytes 4128 | tf_op jit(solution)/shard_map/ppermute | solution.py:263
  40.5 2.9 %collective-permute-start.8 = (f32[8,128]{1,0:T(8,128)S(1)}, f32[8,128]{1,0:T(8,128)S(1)}, u32[]{:S(2)}, u32[]{:S(2)}) collective-permute-start(f32[8,128]{1,0:T(8,128)S(1)} %add.48), channel_id=1, source_target_pairs={{0,4},{1,5},{2,6},{3,7},{4,0},{5,1},{6,2},{7,3},{8,12},{9,13},{10,... | collective-permute-start | bytes 12296 | tf_op jit(solution)/shard_map/ppermute | solution.py:263
  43.4 0.0 copy-start.1
  43.4 0.8 %shard_map.44 = (f32[8,16,768]{2,1,0:T(8,128)S(1)}, f32[8,16,768]{2,1,0:T(8,128)S(1)}, f32[16,768]{1,0:T(8,128)S(1)}) custom-call(f32[1024,128]{1,0:T(8,128)S(1)} %get-tuple-element.22.q_ref, f32[1024,128]{1,0:T(8,128)S(1)} %get-tuple-element.23.v_ref, f32[128,128]{1,0:T(8,128)S(1)} %get-tuple-element.24.inv_ref), custom_call_target="tpu_custom_call" | custom-call | tf_op jit(solution)/shard_map/pallas_call | solution.py:319
  44.2 0.8 %collective-permute-done.8 = f32[8,128]{1,0:T(8,128)S(1)} collective-permute-done((f32[8,128]{1,0:T(8,128)S(1)}, f32[8,128]{1,0:T(8,128)S(1)}, u32[]{:S(2)}, u32[]{:S(2)}) %collective-permute-start.8) | collective-permute-done | bytes 4128 | tf_op jit(solution)/shard_map/ppermute | solution.py:263
  45.0 0.2 slice_reduce_fusion.2
  45.3 0.0 copy-done.1
  45.3 1.1 %multiply_add_fusion = (f32[8,16,768]{2,1,0:T(8,128)}, f32[8,16,768]{2,1,0:T(8,128)}) fusion(f32[8,16,768]{2,1,0:T(8,128)S(1)} %get-tuple-element.27, f32[8,16,768]{2,1,0:T(8,128)S(1)} %copy-done.1, f32[8,16,768]{2,1,0:T(8,128)S(1)} %get-tuple-element.25, f32[8]{0:T(128)S(1)} %mul.142, f32[8]{0:T(128)S(1)} %get-tuple-element.32, f32[16,768]{1,0:T(8,128)S(1)} %get-tuple-element.26), kind=kLoop, calls=%fused_computation | loop fusion | flops 786432 | bytes 2015296 | tf_op jit(solution)/shard_map/add | solution.py:335
  (9 shorter events, 0.1 us)
Async XLA Ops:
  0.6 1.0 %copy-start = (f32[8,16,768]{2,1,0:T(8,128)S(1)}, f32[8,16,768]{2,1,0:T(8,128)}, u32[]{:S(2)}) copy-start(f32[8,16,768]{2,1,0:T(8,128)} %b_ref.1) | copy-start | bytes 1179652
  1.6 0.8 %copy-start.2 = (f32[16,768]{1,0:T(8,128)S(1)}, f32[16,768]{1,0:T(8,128)}, u32[]{:S(2)}) copy-start(f32[16,768]{1,0:T(8,128)} %d_ref.1) | copy-start | bytes 147460
  2.9 11.2 %collective-permute-start = (f32[152,128]{1,0:T(8,128)S(1)}, f32[152,128]{1,0:T(8,128)S(1)}, u32[]{:S(2)}, u32[]{:S(2)}) collective-permute-start(f32[152,128]{1,0:T(8,128)S(1)} %get-tuple-element.17), channel_id=1, source_target_pairs={{0,8},{8,16},{16,24},{1,9},{9,17},{17,25},{2,10},{10,18},{18,26},{... | collective-permute-start | bytes 233480 | tf_op jit(solution)/shard_map/ppermute | solution.py:240
  7.8 6.2 %collective-permute-start.1 = (f32[144,128]{1,0:T(8,128)S(1)}, f32[144,128]{1,0:T(8,128)S(1)}, u32[]{:S(2)}, u32[]{:S(2)}) collective-permute-start(f32[144,128]{1,0:T(8,128)S(1)} %get-tuple-element.18), channel_id=1, source_target_pairs={{8,0},{16,8},{24,16},{9,1},{17,9},{25,17},{10,2},{18,10},{26,18},{... | collective-permute-start | bytes 221192 | tf_op jit(solution)/shard_map/ppermute | solution.py:240
  14.1 6.4 %collective-permute-start.2 = (f32[384,128]{1,0:T(8,128)S(1)}, f32[384,128]{1,0:T(8,128)S(1)}, u32[]{:S(2)}, u32[]{:S(2)}) collective-permute-start(f32[384,128]{1,0:T(8,128)S(1)} %get-tuple-element.19), channel_id=1, source_target_pairs={{0,1},{1,2},{2,3},{3,4},{4,5},{5,6},{6,7},{8,9},{9,10},{10,11},{11... | collective-permute-start | bytes 589832 | tf_op jit(solution)/shard_map/ppermute | solution.py:240
  15.4 5.0 %collective-permute-start.3 = (f32[368,128]{1,0:T(8,128)S(1)}, f32[368,128]{1,0:T(8,128)S(1)}, u32[]{:S(2)}, u32[]{:S(2)}) collective-permute-start(f32[368,128]{1,0:T(8,128)S(1)} %get-tuple-element.20), channel_id=1, source_target_pairs={{1,0},{2,1},{3,2},{4,3},{5,4},{6,5},{7,6},{9,8},{10,9},{11,10},{12... | collective-permute-start | bytes 565256 | tf_op jit(solution)/shard_map/ppermute | solution.py:240
  25.8 3.6 %collective-permute-start.4 = (f32[8,128]{1,0:T(8,128)S(1)}, f32[8,128]{1,0:T(8,128)S(1)}, u32[]{:S(2)}, u32[]{:S(2)}) collective-permute-start(f32[8,128]{1,0:T(8,128)S(1)} %get-tuple-element.21), channel_id=1, source_target_pairs={{0,8},{8,0},{16,24},{24,16},{1,9},{9,1},{17,25},{25,17},{2,10},{10... | collective-permute-start | bytes 12296 | tf_op jit(solution)/shard_map/ppermute | solution.py:263
  29.4 4.5 %collective-permute-start.5 = (f32[8,128]{1,0:T(8,128)S(1)}, f32[8,128]{1,0:T(8,128)S(1)}, u32[]{:S(2)}, u32[]{:S(2)}) collective-permute-start(f32[8,128]{1,0:T(8,128)S(1)} %add.45), channel_id=1, source_target_pairs={{0,16},{8,24},{16,0},{24,8},{1,17},{9,25},{17,1},{25,9},{2,18},{10... | collective-permute-start | bytes 12296 | tf_op jit(solution)/shard_map/ppermute | solution.py:263
  33.9 2.6 %collective-permute-start.6 = (f32[8,128]{1,0:T(8,128)S(1)}, f32[8,128]{1,0:T(8,128)S(1)}, u32[]{:S(2)}, u32[]{:S(2)}) collective-permute-start(f32[8,128]{1,0:T(8,128)S(1)} %add.46), channel_id=1, source_target_pairs={{0,1},{1,0},{2,3},{3,2},{4,5},{5,4},{6,7},{7,6},{8,9},{9,8},{10,11... | collective-permute-start | bytes 12296 | tf_op jit(solution)/shard_map/ppermute | solution.py:263
  36.5 4.0 %collective-permute-start.7 = (f32[8,128]{1,0:T(8,128)S(1)}, f32[8,128]{1,0:T(8,128)S(1)}, u32[]{:S(2)}, u32[]{:S(2)}) collective-permute-start(f32[8,128]{1,0:T(8,128)S(1)} %add.47), channel_id=1, source_target_pairs={{0,2},{1,3},{2,0},{3,1},{4,6},{5,7},{6,4},{7,5},{8,10},{9,11},{10,... | collective-permute-start | bytes 12296 | tf_op jit(solution)/shard_map/ppermute | solution.py:263
  40.5 4.5 %collective-permute-start.8 = (f32[8,128]{1,0:T(8,128)S(1)}, f32[8,128]{1,0:T(8,128)S(1)}, u32[]{:S(2)}, u32[]{:S(2)}) collective-permute-start(f32[8,128]{1,0:T(8,128)S(1)} %add.48), channel_id=1, source_target_pairs={{0,4},{1,5},{2,6},{3,7},{4,0},{5,1},{6,2},{7,3},{8,12},{9,13},{10,... | collective-permute-start | bytes 12296 | tf_op jit(solution)/shard_map/ppermute | solution.py:263
  43.4 1.9 %copy-start.1 = (f32[8,16,768]{2,1,0:T(8,128)S(1)}, f32[8,16,768]{2,1,0:T(8,128)}, u32[]{:S(2)}) copy-start(f32[8,16,768]{2,1,0:T(8,128)} %b_ref.1) | copy-start | bytes 1179652

commit v2 on v1

--- a/solution.py
+++ b/solution.py
@@ -315,7 +315,10 @@
         + [scratch(2, my, loads, LANES)],
         compiler_params=params,
     )(bt, dt, x_low, x_high, y_low, y_high)
-    totals = sum_over(sum_over(sums, "gx"), "gy")
+    count = lax.axis_size("gx") * lax.axis_size("gy")
+    spread = jnp.broadcast_to(sums[:, :4].reshape(1, -1), (count, 4 * loads))
+    spread = lax.all_to_all(spread, ("gx", "gy"), 0, 0, tiled=True)
+    totals = jnp.sum(spread, axis=0).reshape(loads, 4)
     image, again, inverse = pl.pallas_call(
         functools.partial(unpack_kernel, sizes),
         out_shape=(shape(*heat_source.shape), shape(*heat_source.shape), shape(nx, flat)),

time: 46.6 us -> 43.8 us (0.940)
  starting transfers between devices: 20.1 us -> 17.3 us
  waiting for transfers between devices: 15.8 us -> 15 us
  local copies, waits for them, and re-layouts: 2.01 us -> 2.8 us
    ppermute x5 -> x0, starting transfers between devices: 11.3 us -> none  [sum_over(): total = total + lax.ppermute(array, axis, pairs)]
    all_to_all x0 -> x1, starting transfers between devices: none -> 8.46 us  [per_device(): spread = lax.all_to_all(spread, ('gx', 'gy'), 0, 0, tiled=True)]
    ppermute x5 -> x0, waiting for transfers between devices: 7.14 us -> none  [sum_over(): total = total + lax.ppermute(array, axis, pairs)]
    all_to_all x0 -> x1, waiting for transfers between devices: none -> 6.26 us  [per_device(): spread = lax.all_to_all(spread, ('gx', 'gy'), 0, 0, tiled=True)]
    broadcast_in_dim x0 -> x2, local copies, waits for them, and re-layouts: none -> 0.71 us  [per_device(): spread = jnp.broadcast_to(sums[:, :4].reshape(1, -1), (count, 4 * loads))]
  transfers between devices with their start and end apart: 9 -> 5, of which waited for: 7 -> 3; matrix products, arithmetic and copies ran while one was open for 0% -> 0% of each run, Pallas kernels for 2% -> 2%
where the time goes in v2:
time: 43.8 us; the launch traced here: 43.5 us
  starting transfers between devices  17.3 us (39%)
  waiting for transfers between devices  15 us (34%)
  Pallas kernels  6.63 us (15%)
  local copies, waits for them, and re-layouts  2.8 us (6%)
  other arithmetic  1.1 us (3%)
  between operations  0.73 us (2%)
    ppermute x4, starting transfers between devices, shift(): return lax.ppermute(array, axis, pairs)  8.82 us
    ppermute x4, waiting for transfers between devices, shift(): return lax.ppermute(array, axis, pairs)  8.69 us
    all_to_all x1, starting transfers between devices, per_device(): spread = lax.all_to_all(spread, ('gx', 'gy'), 0, 0, tiled=True)  8.46 us
    all_to_all x1, waiting for transfers between devices, per_device(): spread = lax.all_to_all(spread, ('gx', 'gy'), 0, 0, tiled=True)  6.26 us
    pallas_call x1, Pallas kernels, per_device(): pl.pallas_call(functools.partial(solve_kernel, sizes), out_shape=(shape(n...  5.33 us
    unnamed x6, local copies, waits for them, and re-layouts  1.8 us
    add x1, other arithmetic, per_device(): residual = heat_source - first * image + second * again  1.05 us
  transfers between devices with their start and end apart: 5, of which 3 were waited for; matrix products, arithmetic and copies ran while one was open for 0% of the time, Pallas kernels for 2%

profile of v2, /device:TPU:0, one launch (start us, length us, event | category | flops | bytes accessed | tf_op | source)
XLA Modules:
  0.0 43.5 jit_solution(14140976874086071720)
XLA Ops:
  0.6 0.0 copy-start
  0.6 1.0 %copy-done = f32[8,16,768]{2,1,0:T(8,128)S(1)} copy-done((f32[8,16,768]{2,1,0:T(8,128)S(1)}, f32[8,16,768]{2,1,0:T(8,128)}, u32[]{:S(2)}) %copy-start) | copy-done | bytes 393240
  1.6 0.0 copy-start.2
  1.6 0.8 %copy-done.2 = f32[16,768]{1,0:T(8,128)S(1)} copy-done((f32[16,768]{1,0:T(8,128)S(1)}, f32[16,768]{1,0:T(8,128)}, u32[]{:S(2)}) %copy-start.2) | copy-done | bytes 49176
  2.4 0.5 %shard_map.41 = (f32[1024,128]{1,0:T(8,128)S(1)}, f32[128,128]{1,0:T(8,128)S(1)}, f32[152,128]{1,0:T(8,128)S(1)}, f32[144,128]{1,0:T(8,128)S(1)}) custom-call(f32[8,16,768]{2,1,0:T(8,128)S(1)} %copy-done, f32[16,768]{1,0:T(8,128)S(1)} %copy-done.2), custom_call_target="tpu_custom_call" | custom-call | tf_op jit(solution)/shard_map/pallas_call | solution.py:283
  2.9 4.9 %collective-permute-start = (f32[152,128]{1,0:T(8,128)S(1)}, f32[152,128]{1,0:T(8,128)S(1)}, u32[]{:S(2)}, u32[]{:S(2)}) collective-permute-start(f32[152,128]{1,0:T(8,128)S(1)} %get-tuple-element.17), channel_id=1, source_target_pairs={{0,8},{8,16},{16,24},{1,9},{9,17},{17,25},{2,10},{10,18},{18,26},{... | collective-permute-start | bytes 233480 | tf_op jit(solution)/shard_map/ppermute | solution.py:240
  7.8 1.3 %collective-permute-start.1 = (f32[144,128]{1,0:T(8,128)S(1)}, f32[144,128]{1,0:T(8,128)S(1)}, u32[]{:S(2)}, u32[]{:S(2)}) collective-permute-start(f32[144,128]{1,0:T(8,128)S(1)} %get-tuple-element.18), channel_id=1, source_target_pairs={{8,0},{16,8},{24,16},{9,1},{17,9},{25,17},{10,2},{18,10},{26,18},{... | collective-permute-start | bytes 221192 | tf_op jit(solution)/shard_map/ppermute | solution.py:240
  9.1 4.9 %collective-permute-done.1.high_ref.xh_ref = f32[144,128]{1,0:T(8,128)S(1)} collective-permute-done((f32[144,128]{1,0:T(8,128)S(1)}, f32[144,128]{1,0:T(8,128)S(1)}, u32[]{:S(2)}, u32[]{:S(2)}) %collective-permute-start.1) | collective-permute-done | bytes 73760 | tf_op jit(solution)/shard_map/ppermute | solution.py:240
  14.1 0.0 collective-permute-done.low_ref.xl_ref
  14.1 1.3 %collective-permute-start.2 = (f32[384,128]{1,0:T(8,128)S(1)}, f32[384,128]{1,0:T(8,128)S(1)}, u32[]{:S(2)}, u32[]{:S(2)}) collective-permute-start(f32[384,128]{1,0:T(8,128)S(1)} %get-tuple-element.19), channel_id=1, source_target_pairs={{0,1},{1,2},{2,3},{3,4},{4,5},{5,6},{6,7},{8,9},{9,10},{10,11},{11... | collective-permute-start | bytes 589832 | tf_op jit(solution)/shard_map/ppermute | solution.py:240
  15.4 1.3 %collective-permute-start.3 = (f32[368,128]{1,0:T(8,128)S(1)}, f32[368,128]{1,0:T(8,128)S(1)}, u32[]{:S(2)}, u32[]{:S(2)}) collective-permute-start(f32[368,128]{1,0:T(8,128)S(1)} %get-tuple-element.20), channel_id=1, source_target_pairs={{1,0},{2,1},{3,2},{4,3},{5,4},{6,5},{7,6},{9,8},{10,9},{11,10},{12... | collective-permute-start | bytes 565256 | tf_op jit(solution)/shard_map/ppermute | solution.py:240
  16.7 3.7 %collective-permute-done.3.yh_ref = f32[368,128]{1,0:T(8,128)S(1)} collective-permute-done((f32[368,128]{1,0:T(8,128)S(1)}, f32[368,128]{1,0:T(8,128)S(1)}, u32[]{:S(2)}, u32[]{:S(2)}) %collective-permute-start.3) | collective-permute-done | bytes 188448 | tf_op jit(solution)/shard_map/ppermute | solution.py:240
  20.5 0.0 collective-permute-done.2.yl_ref
  20.5 5.3 %shard_map.43 = (f32[1024,128]{1,0:T(8,128)S(1)}, f32[1024,128]{1,0:T(8,128)S(1)}, f32[128,128]{1,0:T(8,128)S(1)}, f32[8,128]{1,0:T(8,128)S(1)}) custom-call(f32[1024,128]{1,0:T(8,128)S(1)} %get-tuple-element.15.bt_ref, f32[128,128]{1,0:T(8,128)S(1)} %get-tuple-element.16.dt_ref, f32[152,128]{1,0:T(8,128)S(1)} %collective-permute-done.low_ref.xl_ref, ...), custom_call_target="tpu_custom_call" | custom-call | tf_op jit(solution)/shard_map/pallas_call | solution.py:302
  25.8 0.1 broadcast_in_dim.4
  25.9 0.6 %broadcast_in_dim.5 = f32[32,1,32]{2,1,0:T(1,128)} broadcast(f32[32]{0:T(128)S(1)} %broadcast_in_dim.4), dimensions={2} | broadcast | bytes 4224 | tf_op jit(solution)/shard_map/broadcast_in_dim | solution.py:319
  26.5 8.5 %all-to-all-start = ((f32[32,1,32]{2,1,0:T(1,128)}), f32[32,1,32]{2,1,0:T(1,128)S(1)}, u32[]{:S(2)}, u32[]{:S(2)}) async-start(f32[32,1,32]{2,1,0:T(1,128)} %broadcast_in_dim.5), calls=%async_computation | async-start | bytes 32768 | tf_op jit(solution)/shard_map/all_to_all | solution.py:320
  35.0 0.0 copy-start.1
  35.0 0.8 %shard_map.44 = (f32[8,16,768]{2,1,0:T(8,128)S(1)}, f32[8,16,768]{2,1,0:T(8,128)S(1)}, f32[16,768]{1,0:T(8,128)S(1)}) custom-call(f32[1024,128]{1,0:T(8,128)S(1)} %get-tuple-element.22.q_ref, f32[1024,128]{1,0:T(8,128)S(1)} %get-tuple-element.23.v_ref, f32[128,128]{1,0:T(8,128)S(1)} %get-tuple-element.24.inv_ref), custom_call_target="tpu_custom_call" | custom-call | tf_op jit(solution)/shard_map/pallas_call | solution.py:322
  35.8 6.3 %all-to-all-done = f32[32,1,32]{2,1,0:T(1,128)S(1)} async-done(((f32[32,1,32]{2,1,0:T(1,128)}), f32[32,1,32]{2,1,0:T(1,128)S(1)}, u32[]{:S(2)}, u32[]{:S(2)}) %all-to-all-start) | async-done | bytes 4128 | tf_op jit(solution)/shard_map/all_to_all | solution.py:320
  42.1 0.1 reshape.83
  42.2 0.2 slice_reduce_fusion.2
  42.4 0.0 copy-done.1
  42.4 1.1 %multiply_add_fusion = (f32[8,16,768]{2,1,0:T(8,128)}, f32[8,16,768]{2,1,0:T(8,128)}) fusion(f32[8,16,768]{2,1,0:T(8,128)S(1)} %get-tuple-element.27, f32[8,16,768]{2,1,0:T(8,128)S(1)} %copy-done.1, f32[8,16,768]{2,1,0:T(8,128)S(1)} %get-tuple-element.25, f32[8]{0:T(128)S(1)} %mul.142, f32[8]{0:T(128)S(1)} %get-tuple-element.32, f32[16,768]{1,0:T(8,128)S(1)} %get-tuple-element.26), kind=kLoop, calls=%fused_computation | loop fusion | flops 786432 | bytes 2015296 | tf_op jit(solution)/shard_map/add | solution.py:338
  (5 shorter events, 0.1 us)
Async XLA Ops:
  0.6 1.0 %copy-start = (f32[8,16,768]{2,1,0:T(8,128)S(1)}, f32[8,16,768]{2,1,0:T(8,128)}, u32[]{:S(2)}) copy-start(f32[8,16,768]{2,1,0:T(8,128)} %b_ref.1) | copy-start | bytes 1179652
  1.6 0.8 %copy-start.2 = (f32[16,768]{1,0:T(8,128)S(1)}, f32[16,768]{1,0:T(8,128)}, u32[]{:S(2)}) copy-start(f32[16,768]{1,0:T(8,128)} %d_ref.1) | copy-start | bytes 147460
  2.9 11.2 %collective-permute-start = (f32[152,128]{1,0:T(8,128)S(1)}, f32[152,128]{1,0:T(8,128)S(1)}, u32[]{:S(2)}, u32[]{:S(2)}) collective-permute-start(f32[152,128]{1,0:T(8,128)S(1)} %get-tuple-element.17), channel_id=1, source_target_pairs={{0,8},{8,16},{16,24},{1,9},{9,17},{17,25},{2,10},{10,18},{18,26},{... | collective-permute-start | bytes 233480 | tf_op jit(solution)/shard_map/ppermute | solution.py:240
  7.8 6.2 %collective-permute-start.1 = (f32[144,128]{1,0:T(8,128)S(1)}, f32[144,128]{1,0:T(8,128)S(1)}, u32[]{:S(2)}, u32[]{:S(2)}) collective-permute-start(f32[144,128]{1,0:T(8,128)S(1)} %get-tuple-element.18), channel_id=1, source_target_pairs={{8,0},{16,8},{24,16},{9,1},{17,9},{25,17},{10,2},{18,10},{26,18},{... | collective-permute-start | bytes 221192 | tf_op jit(solution)/shard_map/ppermute | solution.py:240
  14.1 6.4 %collective-permute-start.2 = (f32[384,128]{1,0:T(8,128)S(1)}, f32[384,128]{1,0:T(8,128)S(1)}, u32[]{:S(2)}, u32[]{:S(2)}) collective-permute-start(f32[384,128]{1,0:T(8,128)S(1)} %get-tuple-element.19), channel_id=1, source_target_pairs={{0,1},{1,2},{2,3},{3,4},{4,5},{5,6},{6,7},{8,9},{9,10},{10,11},{11... | collective-permute-start | bytes 589832 | tf_op jit(solution)/shard_map/ppermute | solution.py:240
  15.4 5.0 %collective-permute-start.3 = (f32[368,128]{1,0:T(8,128)S(1)}, f32[368,128]{1,0:T(8,128)S(1)}, u32[]{:S(2)}, u32[]{:S(2)}) collective-permute-start(f32[368,128]{1,0:T(8,128)S(1)} %get-tuple-element.20), channel_id=1, source_target_pairs={{1,0},{2,1},{3,2},{4,3},{5,4},{6,5},{7,6},{9,8},{10,9},{11,10},{12... | collective-permute-start | bytes 565256 | tf_op jit(solution)/shard_map/ppermute | solution.py:240
  26.5 15.5 %all-to-all-start = ((f32[32,1,32]{2,1,0:T(1,128)}), f32[32,1,32]{2,1,0:T(1,128)S(1)}, u32[]{:S(2)}, u32[]{:S(2)}) async-start(f32[32,1,32]{2,1,0:T(1,128)} %broadcast_in_dim.5), calls=%async_computation | async-start | bytes 32768 | tf_op jit(solution)/shard_map/all_to_all | solution.py:320
  35.0 7.4 %copy-start.1 = (f32[8,16,768]{2,1,0:T(8,128)S(1)}, f32[8,16,768]{2,1,0:T(8,128)}, u32[]{:S(2)}) copy-start(f32[8,16,768]{2,1,0:T(8,128)} %b_ref.1) | copy-start | bytes 1179652

commit v3 on v1

--- a/solution.py
+++ b/solution.py
@@ -315,7 +315,7 @@
         + [scratch(2, my, loads, LANES)],
         compiler_params=params,
     )(bt, dt, x_low, x_high, y_low, y_high)
-    totals = sum_over(sum_over(sums, "gx"), "gy")
+    totals = jnp.sum(lax.all_gather(sums, ("gx", "gy")), axis=0)
     image, again, inverse = pl.pallas_call(
         functools.partial(unpack_kernel, sizes),
         out_shape=(shape(*heat_source.shape), shape(*heat_source.shape), shape(nx, flat)),

time: 46.6 us -> 71 us (1.52)
  blocking collectives: 0 us -> 42.5 us
  starting transfers between devices: 20.1 us -> 8.82 us
  waiting for transfers between devices: 15.8 us -> 8.69 us
    all_gather x0 -> x1, blocking collectives: none -> 42.5 us  [per_device(): totals = jnp.sum(lax.all_gather(sums, ('gx', 'gy')), axis=0)]
    ppermute x5 -> x0, starting transfers between devices: 11.3 us -> none  [sum_over(): total = total + lax.ppermute(array, axis, pairs)]
    ppermute x5 -> x0, waiting for transfers between devices: 7.14 us -> none  [sum_over(): total = total + lax.ppermute(array, axis, pairs)]
  transfers between devices with their start and end apart: 9 -> 4, of which waited for: 7 -> 2; matrix products, arithmetic and copies ran while one was open for 0% -> 0% of each run, Pallas kernels for 2% -> 0%
where the time goes in v3:
time: 71 us; the launch traced here: 70.7 us
  blocking collectives  42.5 us (60%)
  starting transfers between devices  8.82 us (12%)
  waiting for transfers between devices  8.69 us (12%)
  Pallas kernels  6.62 us (9%)
  local copies, waits for them, and re-layouts  2.2 us (3%)
  other arithmetic  1.11 us (2%)
  between operations  0.71 us (1%)
    all_gather x1, blocking collectives, per_device(): totals = jnp.sum(lax.all_gather(sums, ('gx', 'gy')), axis=0)  42.5 us
    ppermute x4, starting transfers between devices, shift(): return lax.ppermute(array, axis, pairs)  8.82 us
    ppermute x4, waiting for transfers between devices, shift(): return lax.ppermute(array, axis, pairs)  8.69 us
    pallas_call x1, Pallas kernels, per_device(): pl.pallas_call(functools.partial(solve_kernel, sizes), out_shape=(shape(n...  5.33 us
    unnamed x6, local copies, waits for them, and re-layouts  1.98 us
  transfers between devices with their start and end apart: 4, of which 2 were waited for; matrix products, arithmetic and copies ran while one was open for 0% of the time, Pallas kernels for 0%

profile of v3, /device:TPU:0, one launch (start us, length us, event | category | flops | bytes accessed | tf_op | source)
XLA Modules:
  0.0 70.7 jit_solution(8972087451704534133)
XLA Ops:
  0.6 0.0 copy-start
  0.6 1.0 %copy-done = f32[8,16,768]{2,1,0:T(8,128)S(1)} copy-done((f32[8,16,768]{2,1,0:T(8,128)S(1)}, f32[8,16,768]{2,1,0:T(8,128)}, u32[]{:S(2)}) %copy-start) | copy-done | bytes 393240
  1.6 0.0 copy-start.2
  1.6 0.8 %copy-done.2 = f32[16,768]{1,0:T(8,128)S(1)} copy-done((f32[16,768]{1,0:T(8,128)S(1)}, f32[16,768]{1,0:T(8,128)}, u32[]{:S(2)}) %copy-start.2) | copy-done | bytes 49176
  2.4 0.5 shard_map.41
  2.9 4.9 %collective-permute-start = (f32[152,128]{1,0:T(8,128)S(1)}, f32[152,128]{1,0:T(8,128)S(1)}, u32[]{:S(2)}, u32[]{:S(2)}) collective-permute-start(f32[152,128]{1,0:T(8,128)S(1)} %get-tuple-element.17), channel_id=1, source_target_pairs={{0,8},{8,16},{16,24},{1,9},{9,17},{17,25},{2,10},{10,18},{18,26},{... | collective-permute-start | bytes 233480 | tf_op jit(solution)/shard_map/ppermute | solution.py:240
  7.8 1.3 %collective-permute-start.1 = (f32[144,128]{1,0:T(8,128)S(1)}, f32[144,128]{1,0:T(8,128)S(1)}, u32[]{:S(2)}, u32[]{:S(2)}) collective-permute-start(f32[144,128]{1,0:T(8,128)S(1)} %get-tuple-element.18), channel_id=1, source_target_pairs={{8,0},{16,8},{24,16},{9,1},{17,9},{25,17},{10,2},{18,10},{26,18},{... | collective-permute-start | bytes 221192 | tf_op jit(solution)/shard_map/ppermute | solution.py:240
  9.1 4.9 %collective-permute-done.1.high_ref.xh_ref = f32[144,128]{1,0:T(8,128)S(1)} collective-permute-done((f32[144,128]{1,0:T(8,128)S(1)}, f32[144,128]{1,0:T(8,128)S(1)}, u32[]{:S(2)}, u32[]{:S(2)}) %collective-permute-start.1) | collective-permute-done | bytes 73760 | tf_op jit(solution)/shard_map/ppermute | solution.py:240
  14.1 0.0 collective-permute-done.low_ref.xl_ref
  14.1 1.3 %collective-permute-start.2 = (f32[384,128]{1,0:T(8,128)S(1)}, f32[384,128]{1,0:T(8,128)S(1)}, u32[]{:S(2)}, u32[]{:S(2)}) collective-permute-start(f32[384,128]{1,0:T(8,128)S(1)} %get-tuple-element.19), channel_id=1, source_target_pairs={{0,1},{1,2},{2,3},{3,4},{4,5},{5,6},{6,7},{8,9},{9,10},{10,11},{11... | collective-permute-start | bytes 589832 | tf_op jit(solution)/shard_map/ppermute | solution.py:240
  15.4 1.3 %collective-permute-start.3 = (f32[368,128]{1,0:T(8,128)S(1)}, f32[368,128]{1,0:T(8,128)S(1)}, u32[]{:S(2)}, u32[]{:S(2)}) collective-permute-start(f32[368,128]{1,0:T(8,128)S(1)} %get-tuple-element.20), channel_id=1, source_target_pairs={{1,0},{2,1},{3,2},{4,3},{5,4},{6,5},{7,6},{9,8},{10,9},{11,10},{12... | collective-permute-start | bytes 565256 | tf_op jit(solution)/shard_map/ppermute | solution.py:240
  16.7 3.7 %collective-permute-done.3.yh_ref = f32[368,128]{1,0:T(8,128)S(1)} collective-permute-done((f32[368,128]{1,0:T(8,128)S(1)}, f32[368,128]{1,0:T(8,128)S(1)}, u32[]{:S(2)}, u32[]{:S(2)}) %collective-permute-start.3) | collective-permute-done | bytes 188448 | tf_op jit(solution)/shard_map/ppermute | solution.py:240
  20.5 0.0 collective-permute-done.2.yl_ref
  20.5 5.3 %shard_map.43 = (f32[1024,128]{1,0:T(8,128)S(1)}, f32[1024,128]{1,0:T(8,128)S(1)}, f32[128,128]{1,0:T(8,128)S(1)}, f32[8,128]{1,0:T(8,128)S(1)}) custom-call(f32[1024,128]{1,0:T(8,128)S(1)} %get-tuple-element.15.bt_ref, f32[128,128]{1,0:T(8,128)S(1)} %get-tuple-element.16.dt_ref, f32[152,128]{1,0:T(8,128)S(1)} %collective-permute-done.low_ref.xl_ref, ...), custom_call_target="tpu_custom_call" | custom-call | tf_op jit(solution)/shard_map/pallas_call | solution.py:302
  25.8 42.5 %all-gather = f32[256,128]{1,0:T(8,128)S(1)} all-gather(f32[8,128]{1,0:T(8,128)S(1)} %get-tuple-element.21), channel_id=2, replica_groups=mesh['gx'=4,'gy'=8] {'gx','gy'}, dimensions={0}, use_global_device_ids=true | all-gather | bytes 135168 | tf_op jit(solution)/shard_map/all_gather | solution.py:318
  68.3 0.2 slice_reduce_fusion.2
  68.6 0.0 copy-start.1
  68.6 0.8 %shard_map.44 = (f32[8,16,768]{2,1,0:T(8,128)S(1)}, f32[8,16,768]{2,1,0:T(8,128)S(1)}, f32[16,768]{1,0:T(8,128)S(1)}) custom-call(f32[1024,128]{1,0:T(8,128)S(1)} %get-tuple-element.22.q_ref, f32[1024,128]{1,0:T(8,128)S(1)} %get-tuple-element.23.v_ref, f32[128,128]{1,0:T(8,128)S(1)} %get-tuple-element.24.inv_ref), custom_call_target="tpu_custom_call" | custom-call | tf_op jit(solution)/shard_map/pallas_call | solution.py:319
  69.4 0.2 copy-done.1
  69.6 1.1 %multiply_add_fusion = (f32[8,16,768]{2,1,0:T(8,128)}, f32[8,16,768]{2,1,0:T(8,128)}) fusion(f32[8,16,768]{2,1,0:T(8,128)S(1)} %get-tuple-element.27, f32[8,16,768]{2,1,0:T(8,128)S(1)} %copy-done.1, f32[8,16,768]{2,1,0:T(8,128)S(1)} %get-tuple-element.25, f32[8]{0:T(128)S(1)} %mul.142, f32[8]{0:T(128)S(1)} %get-tuple-element.32, f32[16,768]{1,0:T(8,128)S(1)} %get-tuple-element.26), kind=kLoop, calls=%fused_computation | loop fusion | flops 786432 | bytes 2015296 | tf_op jit(solution)/shard_map/add | solution.py:335
  (5 shorter events, 0.1 us)
Async XLA Ops:
  0.6 1.0 %copy-start = (f32[8,16,768]{2,1,0:T(8,128)S(1)}, f32[8,16,768]{2,1,0:T(8,128)}, u32[]{:S(2)}) copy-start(f32[8,16,768]{2,1,0:T(8,128)} %b_ref.1) | copy-start | bytes 1179652
  1.6 0.8 %copy-start.2 = (f32[16,768]{1,0:T(8,128)S(1)}, f32[16,768]{1,0:T(8,128)}, u32[]{:S(2)}) copy-start(f32[16,768]{1,0:T(8,128)} %d_ref.1) | copy-start | bytes 147460
  2.9 11.2 %collective-permute-start = (f32[152,128]{1,0:T(8,128)S(1)}, f32[152,128]{1,0:T(8,128)S(1)}, u32[]{:S(2)}, u32[]{:S(2)}) collective-permute-start(f32[152,128]{1,0:T(8,128)S(1)} %get-tuple-element.17), channel_id=1, source_target_pairs={{0,8},{8,16},{16,24},{1,9},{9,17},{17,25},{2,10},{10,18},{18,26},{... | collective-permute-start | bytes 233480 | tf_op jit(solution)/shard_map/ppermute | solution.py:240
  7.8 6.2 %collective-permute-start.1 = (f32[144,128]{1,0:T(8,128)S(1)}, f32[144,128]{1,0:T(8,128)S(1)}, u32[]{:S(2)}, u32[]{:S(2)}) collective-permute-start(f32[144,128]{1,0:T(8,128)S(1)} %get-tuple-element.18), channel_id=1, source_target_pairs={{8,0},{16,8},{24,16},{9,1},{17,9},{25,17},{10,2},{18,10},{26,18},{... | collective-permute-start | bytes 221192 | tf_op jit(solution)/shard_map/ppermute | solution.py:240
  14.1 6.4 %collective-permute-start.2 = (f32[384,128]{1,0:T(8,128)S(1)}, f32[384,128]{1,0:T(8,128)S(1)}, u32[]{:S(2)}, u32[]{:S(2)}) collective-permute-start(f32[384,128]{1,0:T(8,128)S(1)} %get-tuple-element.19), channel_id=1, source_target_pairs={{0,1},{1,2},{2,3},{3,4},{4,5},{5,6},{6,7},{8,9},{9,10},{10,11},{11... | collective-permute-start | bytes 589832 | tf_op jit(solution)/shard_map/ppermute | solution.py:240
  15.4 5.0 %collective-permute-start.3 = (f32[368,128]{1,0:T(8,128)S(1)}, f32[368,128]{1,0:T(8,128)S(1)}, u32[]{:S(2)}, u32[]{:S(2)}) collective-permute-start(f32[368,128]{1,0:T(8,128)S(1)} %get-tuple-element.20), channel_id=1, source_target_pairs={{1,0},{2,1},{3,2},{4,3},{5,4},{6,5},{7,6},{9,8},{10,9},{11,10},{12... | collective-permute-start | bytes 565256 | tf_op jit(solution)/shard_map/ppermute | solution.py:240
  68.6 1.0 %copy-start.1 = (f32[8,16,768]{2,1,0:T(8,128)S(1)}, f32[8,16,768]{2,1,0:T(8,128)}, u32[]{:S(2)}) copy-start(f32[8,16,768]{2,1,0:T(8,128)} %b_ref.1) | copy-start | bytes 1179652

commit v4 on v0

v4 whole, which is shorter than its diff:
```python
import functools

import jax
import jax.numpy as jnp
from jax import lax
from jax.experimental import pallas as pl
from jax.experimental.pallas import tpu as pltpu
from jax.sharding import PartitionSpec as P

NZ = 96
KMIN = 0.001
LANES = 128
SUB = 8


def packed_count(tiles):
    return -(-tiles * NZ // LANES)


def lane_ids(rows):
    return lax.broadcasted_iota(jnp.int32, (rows, LANES), 1)


def unpack_tile(read, index, rows):
    start = index * NZ
    block, offset = start // LANES, start % LANES
    lane = lane_ids(rows)
    first = read(block)
    if offset:
        first = pltpu.roll(first, LANES - offset, 1)
    if offset + NZ > LANES:
        second = pltpu.roll(read(block + 1), LANES - offset, 1)
        first = jnp.where(lane < LANES - offset, first, second)
    return jnp.where(lane < NZ, first, 0.0)


def pack_block(read_tile, tiles, block, rows):
    lane = lane_ids(rows)
    start = block * LANES
    out, at = None, start
    while at < start + LANES and at // NZ < tiles:
        index, z = at // NZ, at % NZ
        here = at - start
        piece = read_tile(index)
        shift = (here - z) % LANES
        if shift:
            piece = pltpu.roll(piece, shift, 1)
        out = piece if out is None else jnp.where(lane < here, out, piece)
        at += NZ - z
    return out


def pack_tiles(out_ref, at, rows, tiles, read_tile):
    for block in range(packed_count(tiles)):
        out_ref[at + block * rows : at + (block + 1) * rows, :] = pack_block(
            read_tile, tiles, block, rows
        )


def unpack_tiles(ref, at, rows, tiles, write):
    for index in range(tiles):
        write(
            index,
            unpack_tile(lambda t: ref[at + t * rows : at + (t + 1) * rows, :], index, rows),
        )


class Sizes:
    def __init__(self, loads, nx, ny):
        self.loads, self.nx, self.ny = loads, nx, ny
        self.plane = ny * loads
        self.x_dens = packed_count(2 * ny) * loads
        self.x_rows = self.x_dens + 3 * ny
        self.y_dens = packed_count(2 * nx) * loads
        self.y_rows = self.y_dens + 3 * nx
        self.c_dens = packed_count(8) * loads
        self.c_rows = self.c_dens + -(-18 // SUB) * SUB
        self.pitch = -(-(ny + 6) // SUB) * SUB


def is_even(axis):
    return lax.rem(lax.axis_index(axis), 2) == 0


def pick(even, if_even, if_odd):
    return jnp.where(even, if_even, if_odd)


def pack_kernel(s, b_hbm, d_hbm, bt_ref, dt_ref, x1_ref, x2_ref, yb_ref, b_ref, d_ref, sems):
    loads, nx, ny = s.loads, s.nx, s.ny
    d_copy = pltpu.make_async_copy(d_hbm, d_ref, sems.at[loads])
    d_copy.start()
    copies = []
    for load in range(loads):
        copies.append(pltpu.make_async_copy(b_hbm.at[load], b_ref.at[load], sems.at[load]))
        copies[-1].start()
    d_copy.wait()
    for x0 in range(0, nx, SUB):
        for y in range(ny):
            tile = unpack_tile(
                lambda t: d_ref[x0 : x0 + SUB, t * LANES : (t + 1) * LANES], y, SUB
            )
            dt_ref[pl.ds(x0 * ny + y, SUB, stride=ny), :] = tile
    for load in range(loads):
        copies[load].wait()
        for x0 in range(0, nx, SUB):
            for y in range(ny):
                tile = unpack_tile(
                    lambda t: b_ref[load, x0 : x0 + SUB, t * LANES : (t + 1) * LANES], y, SUB
                )
                bt_ref[pl.ds((x0 * ny + y) * loads + load, SUB, stride=ny * loads), :] = tile
    even_x, even_y = is_even("gx"), is_even("gy")

    def tile_at(x, y):
        return bt_ref[pl.ds(pl.multiple_of((x * ny + y) * loads, SUB), loads), :]

    for ref, even in ((x1_ref, even_x), (x2_ref, jnp.logical_not(even_x))):
        x0 = pick(even, nx - 2, 0)
        pack_tiles(ref, 0, loads, 2 * ny, lambda i: tile_at(x0 + i // ny, i % ny))
        rows = pl.ds(pl.multiple_of(pick(even, nx - 3, 0) * ny, SUB), 3 * ny)
        ref[s.x_dens :, :] = dt_ref[rows, :]
    pack_face(s, jnp.logical_not(even_y), bt_ref, dt_ref, yb_ref)


def pack_face(s, upper, bt_ref, dt_ref, out_ref):
    loads, nx, ny = s.loads, s.nx, s.ny
    y0 = pick(upper, ny - 2, 0)

    def tile_at(i):
        return bt_ref[
            pl.ds(pl.multiple_of((i // 2 * ny + y0 + i % 2) * loads, SUB), loads), :
        ]

    pack_tiles(out_ref, 0, loads, 2 * nx, tile_at)
    y0 = pick(upper, ny - 3, 0)
    for dy in range(3):
        for x0 in range(0, nx, SUB):
            at = s.y_dens + dy * nx + x0
            out_ref[at : at + SUB, :] = dt_ref[pl.ds(x0 * ny + y0 + dy, SUB, stride=ny), :]


def corner_kernel(s, bt_ref, dt_ref, x1_ref, x2_ref, xt_ref, ya_ref, yc_ref):
    loads, ny = s.loads, s.ny
    for side, ref in enumerate((x1_ref, x2_ref)):

        def write(index, tile):
            at = (side * 2 * ny + index) * loads
            xt_ref[at : at + loads, :] = tile

        unpack_tiles(ref, 0, loads, 2 * ny, write)
    even_y = is_even("gy")
    pack_face(s, even_y, bt_ref, dt_ref, ya_ref)
    for out_ref, base, upper in (
        (ya_ref, s.y_rows, even_y),
        (yc_ref, 0, jnp.logical_not(even_y)),
    ):
        y0 = pick(upper, ny - 2, 0)

        def tile_at(i):
            return xt_ref[
                pl.ds(pl.multiple_of((i // 2 * ny + y0 + i % 2) * loads, SUB), loads), :
            ]

        pack_tiles(out_ref, base, loads, 8, tile_at)
        y0 = pick(upper, ny - 3, 0)
        at = base + s.c_dens
        for ref in (x1_ref, x2_ref):
            for t in range(3):
                for dy in range(3):
                    row = s.x_dens + t * ny + y0 + dy
                    out_ref[at : at + 1, :] = ref[pl.ds(row, 1), :]
                    at += 1
        end = base + s.c_rows
        out_ref[at:end, :] = jnp.zeros((end - at, LANES), jnp.float32)


def solve_kernel(
    s, bt_ref, dt_ref, xt_ref, x1_ref, x2_ref, yb_ref, ya_ref, yc_ref,
    q_ref, v_ref, inv_ref, sums_ref,
    dens, cond, invx, bx, zx, zs, wx, ws, qx, carry,
):
    loads, nx, ny, pitch = s.loads, s.nx, s.ny, s.pitch
    even_x, even_y = is_even("gx"), is_even("gy")
    xs = (pick(even_x, nx + 2, 0), pick(even_x, 0, nx + 2))
    ys = (pick(even_y, ny + 2, 0), pick(even_y, 0, ny + 2))
    xd = (pick(even_x, nx + 3, 0), pick(even_x, 0, nx + 3))
    yd = (pick(even_y, ny + 3, 0), pick(even_y, 0, ny + 3))
    faces = ((ya_ref, 0, ya_ref, s.y_rows), (yb_ref, 0, yc_ref, 0))

    for x in range(nx):
        dens[(x + 3) * pitch + 3 : (x + 3) * pitch + 3 + ny, :] = dt_ref[x * ny : (x + 1) * ny, :]
    for side, ref in enumerate((x1_ref, x2_ref)):
        for t in range(3):
            at = s.x_dens + t * ny
            to = pl.multiple_of((xd[side] + t) * pitch, SUB)
            plane = jnp.concatenate(
                [jnp.zeros((3, LANES), jnp.float32), ref[at : at + ny, :],
                 jnp.zeros((pitch - 3 - ny, LANES), jnp.float32)], axis=0
            )
            dens[pl.ds(to, pitch), :] = plane
    for side, (face, _, corner, corner_at) in enumerate(faces):
        for dy in range(3):
            for x0 in range(0, nx, SUB):
                at = s.y_dens + dy * nx + x0
                to = (x0 + 3) * pitch + yd[side] + dy
                dens[pl.ds(to, SUB, stride=pitch), :] = face[at : at + SUB, :]
        at = corner_at + s.c_dens
        for x_side in range(2):
            for t in range(3):
                for dy in range(3):
                    to = (xd[x_side] + t) * pitch + yd[side] + dy
                    dens[pl.ds(to, 1), :] = corner[at : at + 1, :]
                    at += 1

    mx, my = nx + 4, ny + 4

    def conduct_of(x):
        d = dens[x * pitch : (x + 1) * pitch, :]
        return jnp.where(d > 0.0, (KMIN + (1.0 - KMIN) * (d * d * d)) * (1.0 / 12.0), 0.0)

    before = conduct_of(0)
    for x in range(mx):
        after = conduct_of(x + 1)
        pair = before + after
        pair = pair[: pitch - 1] + pair[1:]
        here = after[1:]
        total = 4.0 * (pair + pltpu.roll(pair, 1, 1))
        inverse = jnp.where(here > 0.0, 1.0 / total, 0.0)
        for y in range(my):
            invx[x, y] = jnp.broadcast_to(inverse[y : y + 1, :], (loads, LANES))
            if x < mx - 1 and y < my - 1:
                cond[x, y] = jnp.broadcast_to(here[y : y + 1, :], (loads, LANES))
        if 2 <= x < 2 + nx:
            inv_ref[(x - 2) * ny : (x - 1) * ny, :] = inverse[2 : 2 + ny, :]
        before = after

    def stage(x, y, tile):
        bx[x, y] = tile
        scaled = tile * invx[x, y]
        zx[x, y] = scaled
        zs[x, y] = pltpu.roll(scaled, LANES - 1, 1)

    for x in range(nx):
        for y in range(ny):
            at = (x * ny + y) * loads
            stage(x + 2, y + 2, bt_ref[at : at + loads, :])
    for side in range(2):
        for dx in range(2):
            for y in range(ny):
                at = ((side * 2 + dx) * ny + y) * loads
                stage(xs[side] + dx, y + 2, xt_ref[at : at + loads, :])
    for side, (face, face_at, corner, corner_at) in enumerate(faces):
        unpack_tiles(
            face, face_at, loads, 2 * nx,
            lambda i, tile: stage(i // 2 + 2, ys[side] + i % 2, tile),
        )
        unpack_tiles(
            corner, corner_at, loads, 8,
            lambda i, tile: stage(xs[i // 4] + i // 2 % 2, ys[side] + i % 2, tile),
        )

    def element_planes(a, count, y0, columns, field, field_up, emit):
        left = [(field[a + u, y0], field_up[a + u, y0]) for u in range(count + 1)]
        old = [None] * count
        for step in range(columns):
            y = y0 + step
            right = [(field[a + u, y + 1], field_up[a + u, y + 1]) for u in range(count + 1)]
            above = (carry[0, y], carry[1, y]) if step and emit else None
            for u in range(count):
                (p0, p0s), (p1, p1s) = left[u], left[u + 1]
                (r0, r0s), (r1, r1s) = right[u], right[u + 1]
                c = cond[a + u, y]
                even = (p0 + r1) + (r0s + p1s)
                odd = (r0 + p1) + (p0s + r1s)
                lower = None
                if emit:
                    lower = (c * (odd + p1s), c * (even + p1))
                upper = (c * (even + p0s), c * (odd + p0))
                if step and emit:
                    low = (c * (even + r1s) + old[u][0][0]) + above[0]
                    high = (c * (odd + r1) + old[u][0][1]) + above[1]
                    emit(u, a + u, y, p0, low + pltpu.roll(high, 1, 1))
                if step:
                    above = (
                        c * (odd + r0s) + old[u][1][0],
                        c * (even + r0) + old[u][1][1],
                    )
                old[u] = (lower, upper)
            if step:
                carry[0, y], carry[1, y] = above
            left = right

    def first_emit(u, x, y, node, total):
        image = 1.25 * bx[x, y] - total
        weighted = image * invx[x, y]
        qx[x, y] = image
        wx[x, y] = weighted
        ws[x, y] = pltpu.roll(weighted, LANES - 1, 1)

    width = 2 if nx % 2 == 0 else 1
    element_planes(0, 1, 0, my - 1, zx, zs, None)

    @pl.loop(0, (nx + 2) // width)
    def _(i):
        element_planes(1 + i * width, width, 0, my - 1, zx, zs, first_emit)

    element_planes(1, 1, 1, ny + 1, wx, ws, None)

    def second(i, sums):
        sums = list(sums)

        def emit(u, x, y, weighted, total):
            image, source, scaled = qx[x, y], bx[x, y], zx[x, y]
            again = 1.25 * image - total
            row = pl.multiple_of(((x - 2) * ny + (y - 2)) * loads, SUB)
            q_ref[pl.ds(row, loads), :] = image
            v_ref[pl.ds(row, loads), :] = again
            change = scaled - weighted
            sums[0] = sums[0] + source * scaled
            sums[1] = sums[1] + source * change
            sums[2] = sums[2] + (source - image) * change
            sums[3] = sums[3] + (image - again) * change

        element_planes(2 + i * width, width, 1, ny + 1, wx, ws, emit)
        return tuple(sums)

    zero = jnp.zeros((loads, LANES), jnp.float32)
    sums = lax.fori_loop(0, nx // width, second, (zero,) * 4)
    lane = lane_ids(loads)
    load = lax.broadcasted_iota(jnp.int32, (loads, LANES), 0)
    packed = zero
    for place, part in enumerate(sums):
        total = jnp.sum(part, axis=1, keepdims=True)
        packed = packed + jnp.where(lane == place * loads + load, total, 0.0)
    row = jnp.sum(packed, axis=0, keepdims=True)
    sums_ref[...] = jnp.broadcast_to(row[None], sums_ref.shape)


def unpack_kernel(s, q_ref, v_ref, inv_ref, qo_ref, vo_ref, io_ref):
    loads, nx, ny = s.loads, s.nx, s.ny
    for x0 in range(0, nx, SUB):
        for block in range(packed_count(ny)):
            lanes = slice(block * LANES, (block + 1) * LANES)
            io_ref[x0 : x0 + SUB, lanes] = pack_block(
                lambda y: inv_ref[pl.ds(x0 * ny + y, SUB, stride=ny), :], ny, block, SUB
            )
            for ref, out in ((q_ref, qo_ref), (v_ref, vo_ref)):
                for load in range(loads):
                    out[load, x0 : x0 + SUB, lanes] = pack_block(
                        lambda y: ref[
                            pl.ds((x0 * ny + y) * loads + load, SUB, stride=ny * loads), :
                        ],
                        ny,
                        block,
                        SUB,
                    )


def finish_kernel(s, parts_ref, b_ref, q_ref, v_ref, inv_ref, x_hbm, r_hbm, x_ref, r_ref, sems):
    loads = s.loads
    totals = jnp.sum(parts_ref[...], axis=0)

    def part(place):
        return pltpu.roll(totals, (LANES - place * loads) % LANES, 1) if place else totals

    rz, near, square, last = (part(place) for place in range(4))
    direct = rz - near
    alpha = rz / direct
    short = -near / direct
    rz_next = short * short * rz + 2.0 * alpha * short * near + alpha * alpha * square
    beta = rz_next / rz
    grown = short + beta
    curved = (
        grown * grown * direct
        + 2.0 * alpha * grown * (near - square)
        + alpha * alpha * last
    )
    alpha_next = rz_next / curved
    first_row = alpha + alpha_next * (1.0 + beta)
    second_row = alpha_next * alpha
    inverse = inv_ref[...]
    copies = []
    for load in range(loads):
        first = first_row[:, load : load + 1]
        second = second_row[:, load : load + 1]
        source, image = b_ref[load], q_ref[load]
        x_ref[load] = (first * source - second * image) * inverse
        copies.append(pltpu.make_async_copy(x_ref.at[load], x_hbm.at[load], sems.at[0, load]))
        copies[-1].start()
        r_ref[load] = source - first * image + second * v_ref[load]
        copies.append(pltpu.make_async_copy(r_ref.at[load], r_hbm.at[load], sems.at[1, load]))
        copies[-1].start()
    for copy in copies:
        copy.wait()


def swap(array, axis, start):
    pairs = []
    for i in range(start, lax.axis_size(axis) - 1, 2):
        pairs += [(i, i + 1), (i + 1, i)]
    return lax.ppermute(array, axis, pairs)


def per_device(heat_source, density):
    loads, nx, flat = heat_source.shape
    ny = flat // NZ
    s = Sizes(loads, nx, ny)
    nodes = nx * ny * loads
    devices = lax.axis_size("gx") * lax.axis_size("gy")

    def shape(*dims):
        return jax.ShapeDtypeStruct(dims, jnp.float32)

    def scratch(*dims):
        return pltpu.VMEM(dims, jnp.float32)

    def call(kernel, out_shape, **more):
        params = pltpu.CompilerParams(vmem_limit_bytes=48 * 1024 * 1024)
        return pl.pallas_call(
            functools.partial(kernel, s), out_shape=out_shape, compiler_params=params, **more
        )

    hbm = pl.BlockSpec(memory_space=pl.ANY)
    bt, dt, x1, x2, yb = call(
        pack_kernel,
        (
            shape(nodes, LANES),
            shape(nx * ny, LANES),
            shape(s.x_rows, LANES),
            shape(s.x_rows, LANES),
            shape(s.y_rows, LANES),
        ),
        in_specs=[hbm, hbm],
        scratch_shapes=[
            scratch(loads, nx, flat),
            scratch(nx, flat),
            pltpu.SemaphoreType.DMA((loads + 1,)),
        ],
    )(heat_source, density)
    x1, x2 = swap(x1, "gx", 0), swap(x2, "gx", 1)
    yb = swap(yb, "gy", 1)
    xt, ya, yc = call(
        corner_kernel,
        (
            shape(4 * ny * loads, LANES),
            shape(s.y_rows + s.c_rows, LANES),
            shape(s.c_rows, LANES),
        ),
    )(bt, dt, x1, x2)
    ya, yc = swap(ya, "gy", 0), swap(yc, "gy", 1)
    mx, my = nx + 4, ny + 4
    field = scratch(mx, my, loads, LANES)
    q_t, v_t, inv_t, sums = call(
        solve_kernel,
        (
            shape(nodes, LANES),
            shape(nodes, LANES),
            shape(nx * ny, LANES),
            shape(devices, 1, LANES),
        ),
        scratch_shapes=[scratch((nx + 6) * s.pitch, LANES)]
        + [field] * 8
        + [scratch(2, my, loads, LANES)],
    )(bt, dt, xt, x1, x2, yb, ya, yc)
    parts = lax.all_to_all(sums, ("gx", "gy"), 0, 0, tiled=True)
    whole = shape(loads, nx, flat)
    image, again, inverse = call(unpack_kernel, (whole, whole, shape(nx, flat)))(q_t, v_t, inv_t)
    return call(
        finish_kernel,
        (whole, whole),
        out_specs=(hbm, hbm),
        scratch_shapes=[
            scratch(loads, nx, flat),
            scratch(loads, nx, flat),
            pltpu.SemaphoreType.DMA((2, loads)),
        ],
    )(parts, heat_source, image, again, inverse)


def solution(mesh):
    placed = (P(None, "gx", "gy"), P("gx", "gy"))
    return jax.shard_map(
        per_device,
        mesh=mesh,
        in_specs=placed,
        out_specs=(P(None, "gx", "gy"), P(None, "gx", "gy")),
        check_vma=False,
    )
```

time: 160 us -> 41.5 us (0.26)
  blocking collectives: 86.8 us -> 0 us
  waiting for transfers between devices: 20.3 us -> 7.82 us
  matrix products: 11.9 us -> 0 us
  other arithmetic: 11.9 us -> 0 us
  Pallas kernels: 0 us -> 9.75 us
  local copies, waits for them, and re-layouts: 5.96 us -> 1.8 us
    psum x2 -> x0, blocking collectives: 86.8 us -> none  [paired_dots(): lax.psum((local_sums(residual, scaled), local_sums(applied, scaled)), ('g...]
    ppermute x10 -> x5, waiting for transfers between devices: 20.3 us -> 1.56 us  [swap(): return lax.ppermute(array, axis, pairs)]
    ppermute x10 -> x5, starting transfers between devices: 21.7 us -> 5.14 us  [swap(): return lax.ppermute(array, axis, pairs)]
    all_to_all x0 -> x1, starting transfers between devices: none -> 16 us  [per_device(): parts = lax.all_to_all(sums, ('gx', 'gy'), 0, 0, tiled=True)]
    dot_general x2 -> x0, matrix products: 11.9 us -> none  [block_apply(): jnp.einsum('nm,mlag->nlag', k_elem, corner_vals, precision=lax.Precision....]
    pallas_call x0 -> x5, Pallas kernels: none -> 9.75 us  [the longest x1 5.73 us: per_device(): call(solve_kernel, (shape(nodes, LANES), shape(nodes, LANES), shape(nx *...]
    all_to_all x0 -> x1, waiting for transfers between devices: none -> 6.26 us  [per_device(): parts = lax.all_to_all(sums, ('gx', 'gy'), 0, 0, tiled=True)]
    add x3 -> x0, other arithmetic: 6.14 us -> none  [the longest x2 5.33 us: spread_nodes(): summed = piece if summed is None else summed + piece]
  transfers between devices with their start and end apart: 10 -> 6, of which waited for: 8 -> 2; matrix products, arithmetic and copies ran while one was open for 0% -> 0% of each run, Pallas kernels for 0% -> 2%
where the time goes in v4:
time: 41.5 us; the launch traced here: 41.3 us
  starting transfers between devices  21.2 us (51%)
  Pallas kernels  9.75 us (23%)
  waiting for transfers between devices  7.82 us (19%)
  local copies, waits for them, and re-layouts  1.8 us (4%)
  between operations  0.72 us (2%)
    all_to_all x1, starting transfers between devices, per_device(): parts = lax.all_to_all(sums, ('gx', 'gy'), 0, 0, tiled=True)  16 us
    all_to_all x1, waiting for transfers between devices, per_device(): parts = lax.all_to_all(sums, ('gx', 'gy'), 0, 0, tiled=True)  6.26 us
    pallas_call x1, Pallas kernels, per_device(): call(solve_kernel, (shape(nodes, LANES), shape(nodes, LANES), shape(nx *...  5.73 us
    ppermute x5, starting transfers between devices, swap(): return lax.ppermute(array, axis, pairs)  5.14 us
    pallas_call x1, Pallas kernels, per_device(): call(pack_kernel, (shape(nodes, LANES), shape(nx * ny, LANES), shape(s.x_...  1.82 us
    unnamed x6, local copies, waits for them, and re-layouts  1.8 us
    ppermute x5, waiting for transfers between devices, swap(): return lax.ppermute(array, axis, pairs)  1.56 us
    pallas_call x1, Pallas kernels, per_device(): call(finish_kernel, (whole, whole), out_specs=(hbm, hbm), scratch_shapes=...  1.21 us
  transfers between devices with their start and end apart: 6, of which 2 were waited for; matrix products, arithmetic and copies ran while one was open for 0% of the time, Pallas kernels for 2%

profile of v4, /device:TPU:0, one launch (start us, length us, event | category | flops | bytes accessed | tf_op | source)
XLA Modules:
  0.0 41.3 jit_solution(3073070522182309761)
XLA Ops:
  0.6 0.0 copy-start
  0.6 1.0 %copy-done = f32[8,16,768]{2,1,0:T(8,128)S(1)} copy-done((f32[8,16,768]{2,1,0:T(8,128)S(1)}, f32[8,16,768]{2,1,0:T(8,128)}, u32[]{:S(2)}) %copy-start) | copy-done | bytes 393240
  1.6 0.0 copy-start.2
  1.6 0.8 %copy-done.2 = f32[16,768]{1,0:T(8,128)S(1)} copy-done((f32[16,768]{1,0:T(8,128)S(1)}, f32[16,768]{1,0:T(8,128)}, u32[]{:S(2)}) %copy-start.2) | copy-done | bytes 49176
  2.4 1.8 %shard_map.41 = (f32[1024,128]{1,0:T(8,128)S(1)}, f32[128,128]{1,0:T(8,128)S(1)}, f32[120,128]{1,0:T(8,128)S(1)}, f32[120,128]{1,0:T(8,128)S(1)}, f32[240,128]{1,0:T(8,128)S(1)}) custom-call(f32[8,16,768]{2,1,0:T(8,128)S(1)} %copy-done, f32[16,768]{1,0:T(8,128)S(1)} %copy-done.2), custom_call_target="tpu_custom_call" | custom-call | tf_op jit(solution)/shard_map/pallas_call | solution.py:424
  4.3 3.1 %collective-permute-start = (f32[120,128]{1,0:T(8,128)S(1)}, f32[120,128]{1,0:T(8,128)S(1)}, u32[]{:S(2)}, u32[]{:S(2)}) collective-permute-start(f32[120,128]{1,0:T(8,128)S(1)} %get-tuple-element.19), channel_id=1, source_target_pairs={{0,8},{8,0},{16,24},{24,16},{1,9},{9,1},{17,25},{25,17},{2,10},{10... | collective-permute-start | bytes 184328 | tf_op jit(solution)/shard_map/ppermute | solution.py:401
  7.3 0.7 %collective-permute-start.1 = (f32[120,128]{1,0:T(8,128)S(1)}, f32[120,128]{1,0:T(8,128)S(1)}, u32[]{:S(2)}, u32[]{:S(2)}) collective-permute-start(f32[120,128]{1,0:T(8,128)S(1)} %get-tuple-element.20), channel_id=1, source_target_pairs={{8,16},{16,8},{9,17},{17,9},{10,18},{18,10},{11,19},{19,11},{12,20... | collective-permute-start | bytes 184328 | tf_op jit(solution)/shard_map/ppermute | solution.py:401
  8.0 1.5 %collective-permute-done.x1_ref = f32[120,128]{1,0:T(8,128)S(1)} collective-permute-done((f32[120,128]{1,0:T(8,128)S(1)}, f32[120,128]{1,0:T(8,128)S(1)}, u32[]{:S(2)}, u32[]{:S(2)}) %collective-permute-start) | collective-permute-done | bytes 61472 | tf_op jit(solution)/shard_map/ppermute | solution.py:401
  9.5 0.0 collective-permute-done.1.x2_ref
  9.5 0.2 shard_map.42
  9.7 0.1 collective-permute-start.3
  9.8 0.7 %collective-permute-start.2 = (f32[240,128]{1,0:T(8,128)S(1)}, f32[240,128]{1,0:T(8,128)S(1)}, u32[]{:S(2)}, u32[]{:S(2)}) collective-permute-start(f32[240,128]{1,0:T(8,128)S(1)} %get-tuple-element.22), channel_id=1, source_target_pairs={{1,2},{2,1},{3,4},{4,3},{5,6},{6,5},{9,10},{10,9},{11,12},{12,11},... | collective-permute-start | bytes 368648 | tf_op jit(solution)/shard_map/ppermute | solution.py:401
  10.5 0.7 %collective-permute-start.4 = (f32[72,128]{1,0:T(8,128)S(1)}, f32[72,128]{1,0:T(8,128)S(1)}, u32[]{:S(2)}, u32[]{:S(2)}) collective-permute-start(f32[72,128]{1,0:T(8,128)S(1)} %get-tuple-element.24), channel_id=1, source_target_pairs={{1,2},{2,1},{3,4},{4,3},{5,6},{6,5},{9,10},{10,9},{11,12},{12,11},... | collective-permute-start | bytes 110600 | tf_op jit(solution)/shard_map/ppermute | solution.py:401
  11.2 0.0 collective-permute-done.4.yc_ref
  11.2 0.0 collective-permute-done.2.yb_ref
  11.2 0.0 collective-permute-done.3.ya_ref
  11.2 5.7 %shard_map.43 = (f32[1024,128]{1,0:T(8,128)S(1)}, f32[1024,128]{1,0:T(8,128)S(1)}, f32[128,128]{1,0:T(8,128)S(1)}, f32[32,1,128]{2,1,0:T(1,128)}) custom-call(f32[1024,128]{1,0:T(8,128)S(1)} %get-tuple-element.17.bt_ref, f32[128,128]{1,0:T(8,128)S(1)} %get-tuple-element.18.dt_ref, f32[256,128]{1,0:T(8,128)S(1)} %get-tuple-element.21.xt_ref, ...), custom_call_target="tpu_custom_call" | custom-call | tf_op jit(solution)/shard_map/pallas_call | solution.py:453
  16.9 16.0 %all-to-all-start = ((f32[32,1,128]{2,1,0:T(1,128)}), f32[32,1,128]{2,1,0:T(1,128)S(1)}, u32[]{:S(2)}, u32[]{:S(2)}) async-start(f32[32,1,128]{2,1,0:T(1,128)} %get-tuple-element.25), calls=%async_computation | async-start | bytes 32768 | tf_op jit(solution)/shard_map/all_to_all | solution.py:465
  33.0 0.0 copy-start.1
  33.0 0.8 %shard_map.44 = (f32[8,16,768]{2,1,0:T(8,128)S(1)}, f32[8,16,768]{2,1,0:T(8,128)S(1)}, f32[16,768]{1,0:T(8,128)S(1)}) custom-call(f32[1024,128]{1,0:T(8,128)S(1)} %get-tuple-element.26.q_ref, f32[1024,128]{1,0:T(8,128)S(1)} %get-tuple-element.27.v_ref, f32[128,128]{1,0:T(8,128)S(1)} %get-tuple-element.28.inv_ref), custom_call_target="tpu_custom_call" | custom-call | tf_op jit(solution)/shard_map/pallas_call | solution.py:467
  33.8 6.3 %all-to-all-done.parts_ref = f32[32,1,128]{2,1,0:T(1,128)S(1)} async-done(((f32[32,1,128]{2,1,0:T(1,128)}), f32[32,1,128]{2,1,0:T(1,128)S(1)}, u32[]{:S(2)}, u32[]{:S(2)}) %all-to-all-start) | async-done | bytes 16416 | tf_op jit(solution)/shard_map/all_to_all | solution.py:465
  40.0 0.0 copy-done.1
  40.1 1.2 %shard_map.45 = (f32[8,16,768]{2,1,0:T(8,128)}, f32[8,16,768]{2,1,0:T(8,128)}) custom-call(f32[32,1,128]{2,1,0:T(1,128)S(1)} %all-to-all-done.parts_ref, f32[8,16,768]{2,1,0:T(8,128)S(1)} %copy-done.1, f32[8,16,768]{2,1,0:T(8,128)S(1)} %get-tuple-element.29.q_ref, f32[8,16,768]{2,1,0:T(8,128)S(1)} %get-tuple-element.30.v_ref, ...), custom_call_target="tpu_custom_call" | custom-call | tf_op jit(solution)/shard_map/pallas_call | solution.py:468
Async XLA Ops:
  0.6 1.0 %copy-start = (f32[8,16,768]{2,1,0:T(8,128)S(1)}, f32[8,16,768]{2,1,0:T(8,128)}, u32[]{:S(2)}) copy-start(f32[8,16,768]{2,1,0:T(8,128)} %b_ref.1) | copy-start | bytes 1179652
  1.6 0.8 %copy-start.2 = (f32[16,768]{1,0:T(8,128)S(1)}, f32[16,768]{1,0:T(8,128)}, u32[]{:S(2)}) copy-start(f32[16,768]{1,0:T(8,128)} %d_hbm.1) | copy-start | bytes 147460
  4.3 5.3 %collective-permute-start = (f32[120,128]{1,0:T(8,128)S(1)}, f32[120,128]{1,0:T(8,128)S(1)}, u32[]{:S(2)}, u32[]{:S(2)}) collective-permute-start(f32[120,128]{1,0:T(8,128)S(1)} %get-tuple-element.19), channel_id=1, source_target_pairs={{0,8},{8,0},{16,24},{24,16},{1,9},{9,1},{17,25},{25,17},{2,10},{10... | collective-permute-start | bytes 184328 | tf_op jit(solution)/shard_map/ppermute | solution.py:401
  7.3 2.2 %collective-permute-start.1 = (f32[120,128]{1,0:T(8,128)S(1)}, f32[120,128]{1,0:T(8,128)S(1)}, u32[]{:S(2)}, u32[]{:S(2)}) collective-permute-start(f32[120,128]{1,0:T(8,128)S(1)} %get-tuple-element.20), channel_id=1, source_target_pairs={{8,16},{16,8},{9,17},{17,9},{10,18},{18,10},{11,19},{19,11},{12,20... | collective-permute-start | bytes 184328 | tf_op jit(solution)/shard_map/ppermute | solution.py:401
  9.7 1.5 %collective-permute-start.3 = (f32[312,128]{1,0:T(8,128)S(1)}, f32[312,128]{1,0:T(8,128)S(1)}, u32[]{:S(2)}, u32[]{:S(2)}) collective-permute-start(f32[312,128]{1,0:T(8,128)S(1)} %get-tuple-element.23), channel_id=1, source_target_pairs={{0,1},{1,0},{2,3},{3,2},{4,5},{5,4},{6,7},{7,6},{8,9},{9,8},{10,11... | collective-permute-start | bytes 479240 | tf_op jit(solution)/shard_map/ppermute | solution.py:401
  9.8 1.4 %collective-permute-start.2 = (f32[240,128]{1,0:T(8,128)S(1)}, f32[240,128]{1,0:T(8,128)S(1)}, u32[]{:S(2)}, u32[]{:S(2)}) collective-permute-start(f32[240,128]{1,0:T(8,128)S(1)} %get-tuple-element.22), channel_id=1, source_target_pairs={{1,2},{2,1},{3,4},{4,3},{5,6},{6,5},{9,10},{10,9},{11,12},{12,11},... | collective-permute-start | bytes 368648 | tf_op jit(solution)/shard_map/ppermute | solution.py:401
  10.5 0.7 %collective-permute-start.4 = (f32[72,128]{1,0:T(8,128)S(1)}, f32[72,128]{1,0:T(8,128)S(1)}, u32[]{:S(2)}, u32[]{:S(2)}) collective-permute-start(f32[72,128]{1,0:T(8,128)S(1)} %get-tuple-element.24), channel_id=1, source_target_pairs={{1,2},{2,1},{3,4},{4,3},{5,6},{6,5},{9,10},{10,9},{11,12},{12,11},... | collective-permute-start | bytes 110600 | tf_op jit(solution)/shard_map/ppermute | solution.py:401
  16.9 23.1 %all-to-all-start = ((f32[32,1,128]{2,1,0:T(1,128)}), f32[32,1,128]{2,1,0:T(1,128)S(1)}, u32[]{:S(2)}, u32[]{:S(2)}) async-start(f32[32,1,128]{2,1,0:T(1,128)} %get-tuple-element.25), calls=%async_computation | async-start | bytes 32768 | tf_op jit(solution)/shard_map/all_to_all | solution.py:465
  33.0 7.1 %copy-start.1 = (f32[8,16,768]{2,1,0:T(8,128)S(1)}, f32[8,16,768]{2,1,0:T(8,128)}, u32[]{:S(2)}) copy-start(f32[8,16,768]{2,1,0:T(8,128)} %b_ref.1) | copy-start | bytes 1179652

commit v5 on v4

--- a/solution.py
+++ b/solution.py
@@ -406,7 +406,6 @@
     ny = flat // NZ
     s = Sizes(loads, nx, ny)
     nodes = nx * ny * loads
-    devices = lax.axis_size("gx") * lax.axis_size("gy")
 
     def shape(*dims):
         return jax.ShapeDtypeStruct(dims, jnp.float32)
@@ -456,13 +455,15 @@
             shape(nodes, LANES),
             shape(nodes, LANES),
             shape(nx * ny, LANES),
-            shape(devices, 1, LANES),
+            shape(lax.axis_size("gy"), 1, LANES),
         ),
         scratch_shapes=[scratch((nx + 6) * s.pitch, LANES)]
         + [field] * 8
         + [scratch(2, my, loads, LANES)],
     )(bt, dt, xt, x1, x2, yb, ya, yc)
-    parts = lax.all_to_all(sums, ("gx", "gy"), 0, 0, tiled=True)
+    parts = jnp.sum(lax.all_to_all(sums, "gy", 0, 0, tiled=True), axis=0, keepdims=True)
+    parts = jnp.broadcast_to(parts, (lax.axis_size("gx"), 1, LANES))
+    parts = lax.all_to_all(parts, "gx", 0, 0, tiled=True)
     whole = shape(loads, nx, flat)
     image, again, inverse = call(unpack_kernel, (whole, whole, shape(nx, flat)))(q_t, v_t, inv_t)
     return call(

time: 41.5 us -> 47.2 us (1.14)
  blocking collectives: 0 us -> 15.9 us
  starting transfers between devices: 21.2 us -> 12.4 us
  waiting for transfers between devices: 7.82 us -> 6.23 us
  Pallas kernels: 9.75 us -> 9.11 us
  local copies, waits for them, and re-layouts: 1.8 us -> 2.38 us
    all_to_all x0 -> x1, blocking collectives: none -> 15.9 us  [per_device(): lax.all_to_all(sums, 'gy', 0, 0, tiled=True)]
    all_to_all x1, starting transfers between devices: 16 us -> 7.31 us  [per_device(): parts = lax.all_to_all(parts, 'gx', 0, 0, tiled=True)]
    all_to_all x1, waiting for transfers between devices: 6.26 us -> 4.67 us  [per_device(): parts = lax.all_to_all(parts, 'gx', 0, 0, tiled=True)]
    pallas_call x1, Pallas kernels: 5.73 us -> 5.12 us  [per_device(): call(solve_kernel, (shape(nodes, LANES), shape(nodes, LANES), shape(nx *...]
    broadcast_in_dim x0 -> x1, local copies, waits for them, and re-layouts: none -> 0.58 us  [per_device(): parts = jnp.broadcast_to(parts, (lax.axis_size('gx'), 1, LANES))]
where the time goes in v5:
time: 47.2 us; the launch traced here: 46.8 us
  blocking collectives  15.9 us (34%)
  starting transfers between devices  12.4 us (26%)
  Pallas kernels  9.11 us (19%)
  waiting for transfers between devices  6.23 us (13%)
  local copies, waits for them, and re-layouts  2.38 us (5%)
  between operations  0.71 us (2%)
    all_to_all x1, blocking collectives, per_device(): lax.all_to_all(sums, 'gy', 0, 0, tiled=True)  15.9 us
    all_to_all x1, starting transfers between devices, per_device(): parts = lax.all_to_all(parts, 'gx', 0, 0, tiled=True)  7.31 us
    ppermute x5, starting transfers between devices, swap(): return lax.ppermute(array, axis, pairs)  5.14 us
    pallas_call x1, Pallas kernels, per_device(): call(solve_kernel, (shape(nodes, LANES), shape(nodes, LANES), shape(nx *...  5.12 us
    all_to_all x1, waiting for transfers between devices, per_device(): parts = lax.all_to_all(parts, 'gx', 0, 0, tiled=True)  4.67 us
    pallas_call x1, Pallas kernels, per_device(): call(pack_kernel, (shape(nodes, LANES), shape(nx * ny, LANES), shape(s.x_...  1.82 us
    unnamed x6, local copies, waits for them, and re-layouts  1.79 us
    ppermute x5, waiting for transfers between devices, swap(): return lax.ppermute(array, axis, pairs)  1.56 us
  transfers between devices with their start and end apart: 6, of which 2 were waited for; matrix products, arithmetic and copies ran while one was open for 0% of the time, Pallas kernels for 2%

profile of v5, /device:TPU:0, one launch (start us, length us, event | category | flops | bytes accessed | tf_op | source)
XLA Modules:
  0.0 46.8 jit_solution(4382389287137035491)
XLA Ops:
  0.6 0.0 copy-start
  0.6 1.0 %copy-done = f32[8,16,768]{2,1,0:T(8,128)S(1)} copy-done((f32[8,16,768]{2,1,0:T(8,128)S(1)}, f32[8,16,768]{2,1,0:T(8,128)}, u32[]{:S(2)}) %copy-start) | copy-done | bytes 393240
  1.6 0.0 copy-start.2
  1.6 0.8 %copy-done.2 = f32[16,768]{1,0:T(8,128)S(1)} copy-done((f32[16,768]{1,0:T(8,128)S(1)}, f32[16,768]{1,0:T(8,128)}, u32[]{:S(2)}) %copy-start.2) | copy-done | bytes 49176
  2.4 1.8 %shard_map.41 = (f32[1024,128]{1,0:T(8,128)S(1)}, f32[128,128]{1,0:T(8,128)S(1)}, f32[120,128]{1,0:T(8,128)S(1)}, f32[120,128]{1,0:T(8,128)S(1)}, f32[240,128]{1,0:T(8,128)S(1)}) custom-call(f32[8,16,768]{2,1,0:T(8,128)S(1)} %copy-done, f32[16,768]{1,0:T(8,128)S(1)} %copy-done.2), custom_call_target="tpu_custom_call" | custom-call | tf_op jit(solution)/shard_map/pallas_call | solution.py:423
  4.3 3.1 %collective-permute-start = (f32[120,128]{1,0:T(8,128)S(1)}, f32[120,128]{1,0:T(8,128)S(1)}, u32[]{:S(2)}, u32[]{:S(2)}) collective-permute-start(f32[120,128]{1,0:T(8,128)S(1)} %get-tuple-element.19), channel_id=1, source_target_pairs={{0,8},{8,0},{16,24},{24,16},{1,9},{9,1},{17,25},{25,17},{2,10},{10... | collective-permute-start | bytes 184328 | tf_op jit(solution)/shard_map/ppermute | solution.py:401
  7.3 0.7 %collective-permute-start.1 = (f32[120,128]{1,0:T(8,128)S(1)}, f32[120,128]{1,0:T(8,128)S(1)}, u32[]{:S(2)}, u32[]{:S(2)}) collective-permute-start(f32[120,128]{1,0:T(8,128)S(1)} %get-tuple-element.20), channel_id=1, source_target_pairs={{8,16},{16,8},{9,17},{17,9},{10,18},{18,10},{11,19},{19,11},{12,20... | collective-permute-start | bytes 184328 | tf_op jit(solution)/shard_map/ppermute | solution.py:401
  8.0 1.5 %collective-permute-done.x1_ref = f32[120,128]{1,0:T(8,128)S(1)} collective-permute-done((f32[120,128]{1,0:T(8,128)S(1)}, f32[120,128]{1,0:T(8,128)S(1)}, u32[]{:S(2)}, u32[]{:S(2)}) %collective-permute-start) | collective-permute-done | bytes 61472 | tf_op jit(solution)/shard_map/ppermute | solution.py:401
  9.5 0.0 collective-permute-done.1.x2_ref
  9.5 0.2 shard_map.42
  9.7 0.1 collective-permute-start.3
  9.8 0.7 %collective-permute-start.2 = (f32[240,128]{1,0:T(8,128)S(1)}, f32[240,128]{1,0:T(8,128)S(1)}, u32[]{:S(2)}, u32[]{:S(2)}) collective-permute-start(f32[240,128]{1,0:T(8,128)S(1)} %get-tuple-element.22), channel_id=1, source_target_pairs={{1,2},{2,1},{3,4},{4,3},{5,6},{6,5},{9,10},{10,9},{11,12},{12,11},... | collective-permute-start | bytes 368648 | tf_op jit(solution)/shard_map/ppermute | solution.py:401
  10.5 0.7 %collective-permute-start.4 = (f32[72,128]{1,0:T(8,128)S(1)}, f32[72,128]{1,0:T(8,128)S(1)}, u32[]{:S(2)}, u32[]{:S(2)}) collective-permute-start(f32[72,128]{1,0:T(8,128)S(1)} %get-tuple-element.24), channel_id=1, source_target_pairs={{1,2},{2,1},{3,4},{4,3},{5,6},{6,5},{9,10},{10,9},{11,12},{12,11},... | collective-permute-start | bytes 110600 | tf_op jit(solution)/shard_map/ppermute | solution.py:401
  11.2 0.0 collective-permute-done.4.yc_ref
  11.2 0.0 collective-permute-done.2.yb_ref
  11.2 0.0 collective-permute-done.3.ya_ref
  11.2 5.1 %shard_map.43 = (f32[1024,128]{1,0:T(8,128)S(1)}, f32[1024,128]{1,0:T(8,128)S(1)}, f32[128,128]{1,0:T(8,128)S(1)}, f32[8,1,128]{2,1,0:T(1,128)S(1)}) custom-call(f32[1024,128]{1,0:T(8,128)S(1)} %get-tuple-element.17.bt_ref, f32[128,128]{1,0:T(8,128)S(1)} %get-tuple-element.18.dt_ref, f32[256,128]{1,0:T(8,128)S(1)} %get-tuple-element.21.xt_ref, ...), custom_call_target="tpu_custom_call" | custom-call | tf_op jit(solution)/shard_map/pallas_call | solution.py:452
  16.3 15.9 %all_to_all.10 = f32[8,1,128]{2,1,0:T(1,128)S(1)} all-to-all(f32[8,1,128]{2,1,0:T(1,128)S(1)} %get-tuple-element.25), channel_id=1, replica_groups=mesh['gx'=4,'gy'=8] {'gy'}, dimensions={0} | all-to-all | bytes 8192 | tf_op jit(solution)/shard_map/all_to_all | solution.py:464
  32.3 0.6 %broadcast_in_dim.2 = f32[4,1,128]{2,1,0:T(1,128)} broadcast(f32[128]{0:T(128)S(1)} %reduce_sum.9), dimensions={2} | broadcast | bytes 2560 | tf_op jit(solution)/shard_map/broadcast_in_dim | solution.py:465
  32.9 7.3 %all-to-all-start.1 = ((f32[4,1,128]{2,1,0:T(1,128)}), f32[4,1,128]{2,1,0:T(1,128)S(1)}, u32[]{:S(2)}, u32[]{:S(2)}) async-start(f32[4,1,128]{2,1,0:T(1,128)} %broadcast_in_dim.2), calls=%async_computation.1 | async-start | bytes 4096 | tf_op jit(solution)/shard_map/all_to_all | solution.py:466
  40.2 0.0 copy-start.1
  40.2 0.8 %shard_map.44 = (f32[8,16,768]{2,1,0:T(8,128)S(1)}, f32[8,16,768]{2,1,0:T(8,128)S(1)}, f32[16,768]{1,0:T(8,128)S(1)}) custom-call(f32[1024,128]{1,0:T(8,128)S(1)} %get-tuple-element.26.q_ref, f32[1024,128]{1,0:T(8,128)S(1)} %get-tuple-element.27.v_ref, f32[128,128]{1,0:T(8,128)S(1)} %get-tuple-element.28.inv_ref), custom_call_target="tpu_custom_call" | custom-call | tf_op jit(solution)/shard_map/pallas_call | solution.py:468
  41.0 4.7 %all-to-all-done.1.parts_ref = f32[4,1,128]{2,1,0:T(1,128)S(1)} async-done(((f32[4,1,128]{2,1,0:T(1,128)}), f32[4,1,128]{2,1,0:T(1,128)S(1)}, u32[]{:S(2)}, u32[]{:S(2)}) %all-to-all-start.1) | async-done | bytes 2080 | tf_op jit(solution)/shard_map/all_to_all | solution.py:466
  45.6 0.0 copy-done.1
  45.6 1.2 %shard_map.45 = (f32[8,16,768]{2,1,0:T(8,128)}, f32[8,16,768]{2,1,0:T(8,128)}) custom-call(f32[4,1,128]{2,1,0:T(1,128)S(1)} %all-to-all-done.1.parts_ref, f32[8,16,768]{2,1,0:T(8,128)S(1)} %copy-done.1, f32[8,16,768]{2,1,0:T(8,128)S(1)} %get-tuple-element.29.q_ref, f32[8,16,768]{2,1,0:T(8,128)S(1)} %get-tuple-element.30.v_ref, ...), custom_call_target="tpu_custom_call" | custom-call | tf_op jit(solution)/shard_map/pallas_call | solution.py:469
  (1 shorter events, 0.0 us)
Async XLA Ops:
  0.6 1.0 %copy-start = (f32[8,16,768]{2,1,0:T(8,128)S(1)}, f32[8,16,768]{2,1,0:T(8,128)}, u32[]{:S(2)}) copy-start(f32[8,16,768]{2,1,0:T(8,128)} %b_ref.1) | copy-start | bytes 1179652
  1.6 0.8 %copy-start.2 = (f32[16,768]{1,0:T(8,128)S(1)}, f32[16,768]{1,0:T(8,128)}, u32[]{:S(2)}) copy-start(f32[16,768]{1,0:T(8,128)} %d_hbm.1) | copy-start | bytes 147460
  4.3 5.3 %collective-permute-start = (f32[120,128]{1,0:T(8,128)S(1)}, f32[120,128]{1,0:T(8,128)S(1)}, u32[]{:S(2)}, u32[]{:S(2)}) collective-permute-start(f32[120,128]{1,0:T(8,128)S(1)} %get-tuple-element.19), channel_id=1, source_target_pairs={{0,8},{8,0},{16,24},{24,16},{1,9},{9,1},{17,25},{25,17},{2,10},{10... | collective-permute-start | bytes 184328 | tf_op jit(solution)/shard_map/ppermute | solution.py:401
  7.3 2.2 %collective-permute-start.1 = (f32[120,128]{1,0:T(8,128)S(1)}, f32[120,128]{1,0:T(8,128)S(1)}, u32[]{:S(2)}, u32[]{:S(2)}) collective-permute-start(f32[120,128]{1,0:T(8,128)S(1)} %get-tuple-element.20), channel_id=1, source_target_pairs={{8,16},{16,8},{9,17},{17,9},{10,18},{18,10},{11,19},{19,11},{12,20... | collective-permute-start | bytes 184328 | tf_op jit(solution)/shard_map/ppermute | solution.py:401
  9.7 1.5 %collective-permute-start.3 = (f32[312,128]{1,0:T(8,128)S(1)}, f32[312,128]{1,0:T(8,128)S(1)}, u32[]{:S(2)}, u32[]{:S(2)}) collective-permute-start(f32[312,128]{1,0:T(8,128)S(1)} %get-tuple-element.23), channel_id=1, source_target_pairs={{0,1},{1,0},{2,3},{3,2},{4,5},{5,4},{6,7},{7,6},{8,9},{9,8},{10,11... | collective-permute-start | bytes 479240 | tf_op jit(solution)/shard_map/ppermute | solution.py:401
  9.8 1.4 %collective-permute-start.2 = (f32[240,128]{1,0:T(8,128)S(1)}, f32[240,128]{1,0:T(8,128)S(1)}, u32[]{:S(2)}, u32[]{:S(2)}) collective-permute-start(f32[240,128]{1,0:T(8,128)S(1)} %get-tuple-element.22), channel_id=1, source_target_pairs={{1,2},{2,1},{3,4},{4,3},{5,6},{6,5},{9,10},{10,9},{11,12},{12,11},... | collective-permute-start | bytes 368648 | tf_op jit(solution)/shard_map/ppermute | solution.py:401
  10.5 0.7 %collective-permute-start.4 = (f32[72,128]{1,0:T(8,128)S(1)}, f32[72,128]{1,0:T(8,128)S(1)}, u32[]{:S(2)}, u32[]{:S(2)}) collective-permute-start(f32[72,128]{1,0:T(8,128)S(1)} %get-tuple-element.24), channel_id=1, source_target_pairs={{1,2},{2,1},{3,4},{4,3},{5,6},{6,5},{9,10},{10,9},{11,12},{12,11},... | collective-permute-start | bytes 110600 | tf_op jit(solution)/shard_map/ppermute | solution.py:401
  32.9 12.8 %all-to-all-start.1 = ((f32[4,1,128]{2,1,0:T(1,128)}), f32[4,1,128]{2,1,0:T(1,128)S(1)}, u32[]{:S(2)}, u32[]{:S(2)}) async-start(f32[4,1,128]{2,1,0:T(1,128)} %broadcast_in_dim.2), calls=%async_computation.1 | async-start | bytes 4096 | tf_op jit(solution)/shard_map/all_to_all | solution.py:466
  40.2 5.5 %copy-start.1 = (f32[8,16,768]{2,1,0:T(8,128)S(1)}, f32[8,16,768]{2,1,0:T(8,128)}, u32[]{:S(2)}) copy-start(f32[8,16,768]{2,1,0:T(8,128)} %b_ref.1) | copy-start | bytes 1179652

commit v6 on v4

v6 whole, which is shorter than its diff:
```python
import functools

import jax
import jax.numpy as jnp
from jax import lax
from jax.experimental import pallas as pl
from jax.experimental.pallas import tpu as pltpu
from jax.sharding import PartitionSpec as P

NZ = 96
KMIN = 0.001
LANES = 128
SUB = 8


def packed_count(tiles):
    return -(-tiles * NZ // LANES)


def lane_ids(rows):
    return lax.broadcasted_iota(jnp.int32, (rows, LANES), 1)


def unpack_tile(read, index, rows):
    start = index * NZ
    block, offset = start // LANES, start % LANES
    lane = lane_ids(rows)
    first = read(block)
    if offset:
        first = pltpu.roll(first, LANES - offset, 1)
    if offset + NZ > LANES:
        second = pltpu.roll(read(block + 1), LANES - offset, 1)
        first = jnp.where(lane < LANES - offset, first, second)
    return jnp.where(lane < NZ, first, 0.0)


def pack_block(read_tile, tiles, block, rows):
    lane = lane_ids(rows)
    start = block * LANES
    out, at = None, start
    while at < start + LANES and at // NZ < tiles:
        index, z = at // NZ, at % NZ
        here = at - start
        piece = read_tile(index)
        shift = (here - z) % LANES
        if shift:
            piece = pltpu.roll(piece, shift, 1)
        out = piece if out is None else jnp.where(lane < here, out, piece)
        at += NZ - z
    return out


def pack_tiles(out_ref, at, rows, tiles, read_tile):
    for block in range(packed_count(tiles)):
        out_ref[at + block * rows : at + (block + 1) * rows, :] = pack_block(
            read_tile, tiles, block, rows
        )


def unpack_tiles(ref, at, rows, tiles, write):
    for index in range(tiles):
        write(
            index,
            unpack_tile(lambda t: ref[at + t * rows : at + (t + 1) * rows, :], index, rows),
        )


class Sizes:
    def __init__(self, loads, nx, ny):
        self.loads, self.nx, self.ny = loads, nx, ny
        self.mx, self.my = nx + 4, ny + 4
        self.pitch = -(-(ny + 6) // SUB) * SUB
        self.y_dens = packed_count(2 * nx) * loads
        self.y_rows = self.y_dens + 3 * nx
        self.x_dens = packed_count(2 * self.my) * loads
        self.x_rows = self.x_dens + 3 * self.pitch


class Tiles:
    def __init__(self, ref, columns, loads):
        self.ref, self.columns, self.loads = ref, columns, loads

    def rows(self, at):
        start = (at[0] * self.columns + at[1]) * self.loads
        if not isinstance(start, int):
            start = pl.multiple_of(start, SUB)
        return pl.ds(start, self.loads)

    def __getitem__(self, at):
        return self.ref[self.rows(at), :]

    def __setitem__(self, at, tile):
        self.ref[self.rows(at), :] = tile


class Joined:
    def __init__(self, first, second, own):
        self.first, self.second, self.own = first, second, own

    def __getitem__(self, at):
        return (self.first if at[0] in self.own else self.second)[at]

    def __setitem__(self, at, tile):
        self.first[at] = tile


def is_even(axis):
    return lax.rem(lax.axis_index(axis), 2) == 0


def pick(even, if_even, if_odd):
    return jnp.where(even, if_even, if_odd)


def pack_kernel(s, b_hbm, d_hbm, bt_ref, dt_ref, y1_ref, y2_ref, b_ref, d_ref, sems):
    loads, nx, ny = s.loads, s.nx, s.ny
    d_copy = pltpu.make_async_copy(d_hbm, d_ref, sems.at[loads])
    d_copy.start()
    copies = []
    for load in range(loads):
        copies.append(pltpu.make_async_copy(b_hbm.at[load], b_ref.at[load], sems.at[load]))
        copies[-1].start()
    d_copy.wait()
    for x0 in range(0, nx, SUB):
        for y in range(ny):
            tile = unpack_tile(
                lambda t: d_ref[x0 : x0 + SUB, t * LANES : (t + 1) * LANES], y, SUB
            )
            dt_ref[pl.ds(x0 * ny + y, SUB, stride=ny), :] = tile
    for load in range(loads):
        copies[load].wait()
        for x0 in range(0, nx, SUB):
            for y in range(ny):
                tile = unpack_tile(
                    lambda t: b_ref[load, x0 : x0 + SUB, t * LANES : (t + 1) * LANES], y, SUB
                )
                bt_ref[pl.ds((x0 * ny + y) * loads + load, SUB, stride=ny * loads), :] = tile
    even_y = is_even("gy")
    pack_face(s, even_y, bt_ref, dt_ref, y1_ref)
    pack_face(s, jnp.logical_not(even_y), bt_ref, dt_ref, y2_ref)


def pack_face(s, upper, bt_ref, dt_ref, out_ref):
    loads, nx, ny = s.loads, s.nx, s.ny
    tiles = Tiles(bt_ref, ny, loads)
    y0 = pick(upper, ny - 2, 0)
    pack_tiles(out_ref, 0, loads, 2 * nx, lambda i: tiles[i // 2, y0 + i % 2])
    y0 = pick(upper, ny - 3, 0)
    for dy in range(3):
        for x0 in range(0, nx, SUB):
            at = s.y_dens + dy * nx + x0
            out_ref[at : at + SUB, :] = dt_ref[pl.ds(x0 * ny + y0 + dy, SUB, stride=ny), :]


def pack_x_kernel(s, bt_ref, dt_ref, y1_ref, y2_ref, dens_ref, x1_ref, x2_ref, edge_ref):
    loads, nx, ny, my, pitch = s.loads, s.nx, s.ny, s.my, s.pitch
    even_x, even_y = is_even("gx"), is_even("gy")
    ys = (pick(even_y, ny + 2, 0), pick(even_y, 0, ny + 2))
    yd = (pick(even_y, ny + 3, 0), pick(even_y, 0, ny + 3))
    for x in range(nx):
        at = x * pitch
        dens_ref[at + 3 : at + 3 + ny, :] = dt_ref[x * ny : (x + 1) * ny, :]
        dens_ref[at + ny + 6 : at + pitch, :] = jnp.zeros((pitch - ny - 6, LANES), jnp.float32)
    for side, ref in enumerate((y1_ref, y2_ref)):
        for dy in range(3):
            for x0 in range(0, nx, SUB):
                at = s.y_dens + dy * nx + x0
                to = x0 * pitch + yd[side] + dy
                dens_ref[pl.ds(to, SUB, stride=pitch), :] = ref[at : at + SUB, :]
    inner, edge = Tiles(bt_ref, ny, loads), Tiles(edge_ref, my, loads)
    for place, x in enumerate((0, 1, nx - 2, nx - 1)):
        for y in range(ny):
            edge[place, y + 2] = inner[x, y]
        for side, ref in enumerate((y1_ref, y2_ref)):
            for dy in range(2):
                edge[place, ys[side] + dy] = unpack_tile(
                    lambda t: ref[t * loads : (t + 1) * loads, :], 2 * x + dy, loads
                )
    for ref, upper in ((x1_ref, even_x), (x2_ref, jnp.logical_not(even_x))):
        place = pick(upper, 2, 0)
        pack_tiles(ref, 0, loads, 2 * my, lambda i: edge[place + i // my, i % my])
        rows = pl.ds(pl.multiple_of(pick(upper, nx - 3, 0) * pitch, SUB), 3 * pitch)
        ref[s.x_dens :, :] = dens_ref[rows, :]


def conduct_of(dens):
    return jnp.where(
        dens > 0.0, (KMIN + (1.0 - KMIN) * (dens * dens * dens)) * (1.0 / 12.0), 0.0
    )


def inverse_of(s, before, after):
    pair = before + after
    pair = pair[: s.pitch - 1] + pair[1:]
    total = 4.0 * (pair + pltpu.roll(pair, 1, 1))
    return jnp.where(after[1:] > 0.0, 1.0 / total, 0.0)


def spread_rows(s, field, x, values, columns):
    for y in range(columns):
        field[x, y] = jnp.broadcast_to(values[y : y + 1, :], (s.loads, LANES))


def up(tile):
    return pltpu.roll(tile, LANES - 1, 1)


def element_planes(cond, carry, a, count, y0, columns, field, field_up, emit, keep=True):
    left = [(field[a + u, y0], field_up[a + u, y0]) for u in range(count + 1)]
    old = [None] * count
    for step in range(columns):
        y = y0 + step
        right = [(field[a + u, y + 1], field_up[a + u, y + 1]) for u in range(count + 1)]
        above = (carry[0, y], carry[1, y]) if step and emit else None
        for u in range(count):
            (p0, p0s), (p1, p1s) = left[u], left[u + 1]
            (r0, r0s), (r1, r1s) = right[u], right[u + 1]
            c = cond[a + u, y]
            even = (p0 + r1) + (r0s + p1s)
            odd = (r0 + p1) + (p0s + r1s)
            pass_on = keep or u + 1 < count
            lower = upper = None
            if emit:
                lower = (c * (odd + p1s), c * (even + p1))
            if pass_on:
                upper = (c * (even + p0s), c * (odd + p0))
            if step and emit:
                low = (c * (even + r1s) + old[u][0][0]) + above[0]
                high = (c * (odd + r1) + old[u][0][1]) + above[1]
                emit(u, a + u, y, p0, low + pltpu.roll(high, 1, 1))
            if step and pass_on:
                above = (
                    c * (odd + r0s) + old[u][1][0],
                    c * (even + r0) + old[u][1][1],
                )
            old[u] = (lower, upper)
        if step and keep:
            carry[0, y], carry[1, y] = above
        left = right


def first_emit(bx, invx, qx, wx, ws):
    def emit(u, x, y, node, total):
        image = 1.25 * bx[x, y] - total
        weighted = image * invx[x, y]
        qx[x, y] = image
        wx[x, y] = weighted
        ws[x, y] = up(weighted)

    return emit


def second_emit(bx, zx, qx, vx, sums):
    def emit(u, x, y, weighted, total):
        image, source, scaled = qx[x, y], bx[x, y], zx[x, y]
        again = 1.25 * image - total
        vx[x, y] = again
        change = scaled - weighted
        sums[0] = sums[0] + source * scaled
        sums[1] = sums[1] + source * change
        sums[2] = sums[2] + (source - image) * change
        sums[3] = sums[3] + (image - again) * change

    return emit


def over_planes(start, stop, body, state):
    pairs = (stop - start) // 2
    state = lax.fori_loop(0, pairs, lambda i, st: body(start + 2 * i, 2, st), state)
    if (stop - start) % 2:
        state = body(stop - 1, 1, state)
    return state


def inner_kernel(
    s, bt_ref, dens_ref, y1_ref, y2_ref,
    cond, invx, bx, zx, zs, qx, wx, ws, vx, carry1, carry2, sums_ref,
):
    loads, nx, ny, my, pitch = s.loads, s.nx, s.ny, s.my, s.pitch
    cond, invx, bx, zx, zs, qx, wx, ws, vx, carry1, carry2 = (
        Tiles(ref, my, loads) for ref in (cond, invx, bx, zx, zs, qx, wx, ws, vx, carry1, carry2)
    )
    even_y = is_even("gy")
    ys = (pick(even_y, ny + 2, 0), pick(even_y, 0, ny + 2))
    before = None
    for x in range(nx):
        after = conduct_of(dens_ref[x * pitch : (x + 1) * pitch, :])
        spread_rows(s, cond, x + 2, after[1:], my - 1)
        if x:
            spread_rows(s, invx, x + 2, inverse_of(s, before, after), my)
        before = after

    def stage(x, y, tile):
        bx[x + 2, y] = tile
        if x:
            scaled = tile * invx[x + 2, y]
            zx[x + 2, y] = scaled
            zs[x + 2, y] = up(scaled)

    inner = Tiles(bt_ref, ny, loads)
    for x in range(nx):
        for y in range(ny):
            stage(x, y + 2, inner[x, y])
    for side, ref in enumerate((y1_ref, y2_ref)):
        unpack_tiles(
            ref, 0, loads, 2 * nx, lambda i, tile: stage(i // 2, ys[side] + i % 2, tile)
        )

    element_planes(cond, carry1, 3, 1, 0, my - 1, zx, zs, None)

    def first(a, count, state):
        emit = first_emit(bx, invx, qx, wx, ws)
        element_planes(cond, carry1, a, count, 0, my - 1, zx, zs, emit)
        return state

    over_planes(4, nx + 1, first, 0)
    element_planes(cond, carry2, 4, 1, 1, my - 3, wx, ws, None)

    def second(a, count, sums):
        sums = list(sums)
        emit = second_emit(bx, zx, qx, vx, sums)
        element_planes(cond, carry2, a, count, 1, my - 3, wx, ws, emit)
        return tuple(sums)

    zero = jnp.zeros((loads, LANES), jnp.float32)
    sums = over_planes(5, nx, second, (zero,) * 4)
    for place, part in enumerate(sums):
        sums_ref[place * loads : (place + 1) * loads, :] = part


def outer_kernel(
    s, dens_ref, x1_ref, x2_ref,
    cond1, invx1, bx1, zx1, zs1, qx1, wx1, ws1, carry1, carry2, sums1,
    q_out, v_out, inv_out, sums_ref,
    low_ref, high_ref, cond2, invx2, bx2, zx2, zs2, qx2, wx2, ws2, vx2, carry3,
):
    loads, nx, ny, mx, my, pitch = s.loads, s.nx, s.ny, s.mx, s.my, s.pitch
    even_x = is_even("gx")

    @pl.when(even_x)
    def _():
        low_ref[...] = x2_ref[...]
        high_ref[...] = x1_ref[...]

    @pl.when(jnp.logical_not(even_x))
    def _():
        low_ref[...] = x1_ref[...]
        high_ref[...] = x2_ref[...]

    def tiles(ref):
        return Tiles(ref, my, loads)

    def joined(first, second, own):
        return Joined(tiles(first), tiles(second), own)

    outside = (0, 1, nx + 2, nx + 3)
    scaled_own = outside + (2,)
    image_own = (1, 2, 3, nx + 1, nx + 2)
    cond, invx = joined(cond2, cond1, outside), joined(invx2, invx1, scaled_own)
    bx = joined(bx2, bx1, outside)
    zx, zs = joined(zx2, zx1, scaled_own), joined(zs2, zs1, scaled_own)
    qx = joined(qx2, qx1, image_own)
    wx, ws = joined(wx2, wx1, image_own), joined(ws2, ws1, image_own)
    vx, carry3 = tiles(vx2), tiles(carry3)
    carry1, carry2 = tiles(carry1), tiles(carry2)

    def conduct(ref, base, x):
        return conduct_of(ref[base + x * pitch : base + (x + 1) * pitch, :])

    low = [conduct(low_ref, s.x_dens, t) for t in range(3)] + [conduct(dens_ref, 0, 0)]
    high = [conduct(dens_ref, 0, nx - 1)] + [conduct(high_ref, s.x_dens, t) for t in range(2)]
    for x in range(3):
        inverse = inverse_of(s, low[x], low[x + 1])
        spread_rows(s, invx, x, inverse, my)
        if x < 2:
            spread_rows(s, cond, x, low[x + 1][1:], my - 1)
    inv_out[...] = inverse[2 : 2 + ny]
    for x in range(2):
        spread_rows(s, invx, nx + 2 + x, inverse_of(s, high[x], high[x + 1]), my)
    spread_rows(s, cond, nx + 2, high[1][1:], my - 1)

    def stage(x, y, tile):
        scaled = tile * invx[x, y]
        zx[x, y] = scaled
        zs[x, y] = up(scaled)

    for ref, x0 in ((low_ref, 0), (high_ref, nx + 2)):

        def write(i, tile):
            bx[x0 + i // my, i % my] = tile
            stage(x0 + i // my, i % my, tile)

        unpack_tiles(ref, 0, loads, 2 * my, write)
    for y in range(my):
        stage(2, y, bx[2, y])

    emit = first_emit(bx, invx, qx, wx, ws)
    element_planes(cond, carry3, 0, 1, 0, my - 1, zx, zs, None)
    element_planes(cond, carry3, 1, 2, 0, my - 1, zx, zs, emit)
    element_planes(cond, carry3, 3, 1, 0, my - 1, zx, zs, emit, keep=False)
    element_planes(cond, carry1, nx + 1, 2, 0, my - 1, zx, zs, emit, keep=False)
    sums = [sums1[place * loads : (place + 1) * loads, :] for place in range(4)]
    emit = second_emit(bx, zx, qx, vx, sums)
    element_planes(cond, carry3, 1, 1, 1, my - 3, wx, ws, None)
    element_planes(cond, carry3, 2, 2, 1, my - 3, wx, ws, emit)
    element_planes(cond, carry3, 4, 1, 1, my - 3, wx, ws, emit, keep=False)
    element_planes(cond, carry2, nx, 2, 1, my - 3, wx, ws, emit, keep=False)
    for field, out, planes in ((qx, q_out, image_planes(nx)), (vx, v_out, again_planes(nx))):
        out = Tiles(out, ny, loads)
        for place, x in enumerate(planes):
            for y in range(ny):
                out[place, y] = field[x, y + 2]

    lane = lane_ids(loads)
    load = lax.broadcasted_iota(jnp.int32, (loads, LANES), 0)
    packed = jnp.zeros((loads, LANES), jnp.float32)
    for place, part in enumerate(sums):
        total = jnp.sum(part, axis=1, keepdims=True)
        packed = packed + jnp.where(lane == place * loads + load, total, 0.0)
    row = jnp.sum(packed, axis=0, keepdims=True)
    sums_ref[...] = jnp.broadcast_to(row[None], sums_ref.shape)


def image_planes(nx):
    return (2, 3, nx + 1)


def again_planes(nx):
    return (2, 3, 4, nx, nx + 1)


def unpack_kernel(
    s, q1_ref, q2_ref, v1_ref, v2_ref, inv1_ref, inv2_ref, qo_ref, vo_ref, io_ref, t_ref
):
    loads, nx, ny, my = s.loads, s.nx, s.ny, s.my
    whole = Tiles(t_ref, ny, loads)
    for first, second, planes, out in (
        (q1_ref, q2_ref, image_planes(nx), qo_ref),
        (v1_ref, v2_ref, again_planes(nx), vo_ref),
    ):
        first, second = Tiles(first, my, loads), Tiles(second, ny, loads)
        for x in range(nx):
            for y in range(ny):
                if x + 2 in planes:
                    whole[x, y] = second[planes.index(x + 2), y]
                else:
                    whole[x, y] = first[x + 2, y + 2]
        for x0 in range(0, nx, SUB):
            for block in range(packed_count(ny)):
                for load in range(loads):
                    out[load, x0 : x0 + SUB, block * LANES : (block + 1) * LANES] = pack_block(
                        lambda y: t_ref[
                            pl.ds((x0 * ny + y) * loads + load, SUB, stride=ny * loads), :
                        ],
                        ny, block, SUB,
                    )
    for x0 in range(0, nx, SUB):
        for block in range(packed_count(ny)):
            io_ref[x0 : x0 + SUB, block * LANES : (block + 1) * LANES] = pack_block(
                lambda y: inv1_ref[
                    pl.ds(((x0 + 2) * my + y + 2) * loads, SUB, stride=my * loads), :
                ],
                ny, block, SUB,
            )
    for block in range(packed_count(ny)):
        io_ref[0:1, block * LANES : (block + 1) * LANES] = pack_block(
            lambda y: inv2_ref[y : y + 1, :], ny, block, 1
        )


def finish_kernel(s, parts_ref, b_ref, q_ref, v_ref, inv_ref, x_hbm, r_hbm, x_ref, r_ref, sems):
    loads = s.loads
    totals = jnp.sum(parts_ref[...], axis=0)

    def part(place):
        return pltpu.roll(totals, (LANES - place * loads) % LANES, 1) if place else totals

    rz, near, square, last = (part(place) for place in range(4))
    direct = rz - near
    alpha = rz / direct
    short = -near / direct
    rz_next = short * short * rz + 2.0 * alpha * short * near + alpha * alpha * square
    beta = rz_next / rz
    grown = short + beta
    curved = (
        grown * grown * direct
        + 2.0 * alpha * grown * (near - square)
        + alpha * alpha * last
    )
    alpha_next = rz_next / curved
    first_row = alpha + alpha_next * (1.0 + beta)
    second_row = alpha_next * alpha
    inverse = inv_ref[...]
    copies = []
    for load in range(loads):
        first = first_row[:, load : load + 1]
        second = second_row[:, load : load + 1]
        source, image = b_ref[load], q_ref[load]
        x_ref[load] = (first * source - second * image) * inverse
        copies.append(pltpu.make_async_copy(x_ref.at[load], x_hbm.at[load], sems.at[0, load]))
        copies[-1].start()
        r_ref[load] = source - first * image + second * v_ref[load]
        copies.append(pltpu.make_async_copy(r_ref.at[load], r_hbm.at[load], sems.at[1, load]))
        copies[-1].start()
    for copy in copies:
        copy.wait()


def swap(array, axis, start):
    pairs = []
    for i in range(start, lax.axis_size(axis) - 1, 2):
        pairs += [(i, i + 1), (i + 1, i)]
    return lax.ppermute(array, axis, pairs)


def per_device(heat_source, density):
    loads, nx, flat = heat_source.shape
    ny = flat // NZ
    s = Sizes(loads, nx, ny)
    nodes = nx * ny * loads
    devices = lax.axis_size("gx") * lax.axis_size("gy")

    def shape(*dims):
        return jax.ShapeDtypeStruct(dims, jnp.float32)

    def scratch(*dims):
        return pltpu.VMEM(dims, jnp.float32)

    def call(kernel, out_shape, **more):
        params = pltpu.CompilerParams(vmem_limit_bytes=48 * 1024 * 1024)
        return pl.pallas_call(
            functools.partial(kernel, s), out_shape=out_shape, compiler_params=params, **more
        )

    hbm = pl.BlockSpec(memory_space=pltpu.HBM)
    bt, dt, y1, y2 = call(
        pack_kernel,
        (
            shape(nodes, LANES),
            shape(nx * ny, LANES),
            shape(s.y_rows, LANES),
            shape(s.y_rows, LANES),
        ),
        in_specs=[hbm, hbm],
        scratch_shapes=[
            scratch(loads, nx, flat),
            scratch(nx, flat),
            pltpu.SemaphoreType.DMA((loads + 1,)),
        ],
    )(heat_source, density)
    y2, y1 = swap(y2, "gy", 1), swap(y1, "gy", 0)
    dens, x1, x2 = call(
        pack_x_kernel,
        (shape(nx * s.pitch, LANES), shape(s.x_rows, LANES), shape(s.x_rows, LANES)),
        scratch_shapes=[scratch(4 * s.my * loads, LANES)],
    )(bt, dt, y1, y2)
    x1, x2 = swap(x1, "gx", 0), swap(x2, "gx", 1)
    field = s.mx * s.my * loads
    edge = 2 * s.my * loads
    *fields, v_1, carry1, carry2, sums = call(
        inner_kernel,
        (shape(field, LANES),) * 9 + (shape(edge, LANES),) * 2 + (shape(4 * loads, LANES),),
    )(bt, dens, y1, y2)
    q_2, v_2, inv_2, sums = call(
        outer_kernel,
        (
            shape(len(image_planes(nx)) * ny * loads, LANES),
            shape(len(again_planes(nx)) * ny * loads, LANES),
            shape(ny, LANES),
            shape(devices, 1, LANES),
        ),
        scratch_shapes=[scratch(s.x_rows, LANES)] * 2
        + [scratch(field, LANES)] * 9
        + [scratch(edge, LANES)],
    )(dens, x1, x2, *fields, carry1, carry2, sums)
    parts = lax.all_to_all(sums, ("gx", "gy"), 0, 0, tiled=True)
    whole = shape(loads, nx, flat)
    image, again, inverse = call(
        unpack_kernel,
        (whole, whole, shape(nx, flat)),
        scratch_shapes=[scratch(nodes, LANES)],
    )(fields[5], q_2, v_1, v_2, fields[1], inv_2)
    return call(
        finish_kernel,
        (whole, whole),
        out_specs=(hbm, hbm),
        scratch_shapes=[
            scratch(loads, nx, flat),
            scratch(loads, nx, flat),
            pltpu.SemaphoreType.DMA((2, loads)),
        ],
    )(parts, heat_source, image, again, inverse)


def solution(mesh):
    placed = (P(None, "gx", "gy"), P("gx", "gy"))
    return jax.shard_map(
        per_device,
        mesh=mesh,
        in_specs=placed,
        out_specs=(P(None, "gx", "gy"), P(None, "gx", "gy")),
        check_vma=False,
    )
```

time: 41.5 us -> 42.9 us (1.034)
  local copies, waits for them, and re-layouts: 1.8 us -> 8.22 us
  waiting for transfers between devices: 7.82 us -> 3.66 us
  starting transfers between devices: 21.2 us -> 17.3 us
  Pallas kernels: 9.75 us -> 12.5 us
    unnamed x6 -> x26, local copies, waits for them, and re-layouts: 1.8 us -> 8.22 us
    all_to_all x1, starting transfers between devices: 16 us -> 12.5 us  [per_device(): parts = lax.all_to_all(sums, ('gx', 'gy'), 0, 0, tiled=True)]
    all_to_all x1, waiting for transfers between devices: 6.26 us -> 3.34 us  [per_device(): parts = lax.all_to_all(sums, ('gx', 'gy'), 0, 0, tiled=True)]
    pallas_call x4 -> x5, Pallas kernels: 8.54 us -> 11.3 us  [the longest x1 5.3 us: per_device(): call(inner_kernel, (shape(field, LANES),) * 9 + (shape(edge, LANES),) * 2...]
    ppermute x5 -> x4, waiting for transfers between devices: 1.56 us -> 0.32 us  [swap(): return lax.ppermute(array, axis, pairs)]
    ppermute x5 -> x4, starting transfers between devices: 5.14 us -> 4.82 us  [swap(): return lax.ppermute(array, axis, pairs)]
  transfers between devices with their start and end apart: 6 -> 5, of which waited for: 2 -> 2; matrix products, arithmetic and copies ran while one was open for 0% -> 0% of each run, Pallas kernels for 2% -> 14%
where the time goes in v6:
time: 42.9 us; the launch traced here: 42.5 us
  starting transfers between devices  17.3 us (40%)
  Pallas kernels  12.5 us (29%)
  local copies, waits for them, and re-layouts  8.22 us (19%)
  waiting for transfers between devices  3.66 us (9%)
  between operations  0.74 us (2%)
    all_to_all x1, starting transfers between devices, per_device(): parts = lax.all_to_all(sums, ('gx', 'gy'), 0, 0, tiled=True)  12.5 us
    unnamed x26, local copies, waits for them, and re-layouts  8.22 us
    pallas_call x1, Pallas kernels, per_device(): call(inner_kernel, (shape(field, LANES),) * 9 + (shape(edge, LANES),) * 2...  5.3 us
    ppermute x4, starting transfers between devices, swap(): return lax.ppermute(array, axis, pairs)  4.82 us
    all_to_all x1, waiting for transfers between devices, per_device(): parts = lax.all_to_all(sums, ('gx', 'gy'), 0, 0, tiled=True)  3.34 us
    pallas_call x1, Pallas kernels, per_device(): call(outer_kernel, (shape(len(image_planes(nx)) * ny * loads, LANES), sha...  3.26 us
    pallas_call x1, Pallas kernels, per_device(): call(pack_kernel, (shape(nodes, LANES), shape(nx * ny, LANES), shape(s.y_...  1.81 us
    pallas_call x1, Pallas kernels, per_device(): call(finish_kernel, (whole, whole), out_specs=(hbm, hbm), scratch_shapes=...  1.21 us
  transfers between devices with their start and end apart: 5, of which 2 were waited for; matrix products, arithmetic and copies ran while one was open for 0% of the time, Pallas kernels for 14%

profile of v6, /device:TPU:0, one launch (start us, length us, event | category | flops | bytes accessed | tf_op | source)
XLA Modules:
  0.0 42.5 jit_solution(14163231909170682149)
XLA Ops:
  0.6 0.0 copy-start.1
  0.6 1.0 %copy-done.1 = f32[8,16,768]{2,1,0:T(8,128)S(1)} copy-done((f32[8,16,768]{2,1,0:T(8,128)S(1)}, f32[8,16,768]{2,1,0:T(8,128)}, u32[]{:S(2)}) %copy-start.1) | copy-done | bytes 393240
  1.6 0.8 %copy-done.12 = f32[16,768]{1,0:T(8,128)S(1)} copy-done((f32[16,768]{1,0:T(8,128)S(1)}, f32[16,768]{1,0:T(8,128)}, u32[]{:S(2)}) %copy-start.12) | copy-done | bytes 49176
  2.4 1.8 %shard_map.41 = (f32[1024,128]{1,0:T(8,128)S(1)}, f32[128,128]{1,0:T(8,128)S(1)}, f32[240,128]{1,0:T(8,128)S(1)}, f32[240,128]{1,0:T(8,128)S(1)}) custom-call(f32[8,16,768]{2,1,0:T(8,128)S(1)} %copy-done.1, f32[16,768]{1,0:T(8,128)S(1)} %copy-done.12), custom_call_target="tpu_custom_call" | custom-call | tf_op jit(solution)/shard_map/pallas_call | solution.py:536
  4.2 0.5 %collective-permute-start = (f32[240,128]{1,0:T(8,128)S(1)}, f32[240,128]{1,0:T(8,128)S(1)}, u32[]{:S(2)}, u32[]{:S(2)}) collective-permute-start(f32[240,128]{1,0:T(8,128)S(1)} %get-tuple-element.30), channel_id=1, source_target_pairs={{0,1},{1,0},{2,3},{3,2},{4,5},{5,4},{6,7},{7,6},{8,9},{9,8},{10,11... | collective-permute-start | bytes 368648 | tf_op jit(solution)/shard_map/ppermute | solution.py:513
  4.8 0.7 %collective-permute-start.1 = (f32[240,128]{1,0:T(8,128)S(1)}, f32[240,128]{1,0:T(8,128)S(1)}, u32[]{:S(2)}, u32[]{:S(2)}) collective-permute-start(f32[240,128]{1,0:T(8,128)S(1)} %get-tuple-element.31), channel_id=1, source_target_pairs={{1,2},{2,1},{3,4},{4,3},{5,6},{6,5},{9,10},{10,9},{11,12},{12,11},... | collective-permute-start | bytes 368648 | tf_op jit(solution)/shard_map/ppermute | solution.py:513
  5.4 0.3 collective-permute-done.y1_ref
  5.7 0.0 collective-permute-done.1.y2_ref
  5.7 0.2 shard_map.42
  5.9 3.0 %collective-permute-start.2 = (f32[192,128]{1,0:T(8,128)S(1)}, f32[192,128]{1,0:T(8,128)S(1)}, u32[]{:S(2)}, u32[]{:S(2)}) collective-permute-start(f32[192,128]{1,0:T(8,128)S(1)} %get-tuple-element.33), channel_id=1, source_target_pairs={{0,8},{8,0},{16,24},{24,16},{1,9},{9,1},{17,25},{25,17},{2,10},{10... | collective-permute-start | bytes 294920 | tf_op jit(solution)/shard_map/ppermute | solution.py:513
  8.9 0.7 %collective-permute-start.3 = (f32[192,128]{1,0:T(8,128)S(1)}, f32[192,128]{1,0:T(8,128)S(1)}, u32[]{:S(2)}, u32[]{:S(2)}) collective-permute-start(f32[192,128]{1,0:T(8,128)S(1)} %get-tuple-element.34), channel_id=1, source_target_pairs={{8,16},{16,8},{9,17},{17,9},{10,18},{18,10},{11,19},{19,11},{12,20... | collective-permute-start | bytes 294920 | tf_op jit(solution)/shard_map/ppermute | solution.py:513
  9.6 5.3 %shard_map.43 = (f32[1920,128]{1,0:T(8,128)S(1)}, f32[1920,128]{1,0:T(8,128)S(1)}, f32[1920,128]{1,0:T(8,128)S(1)}, f32[1920,128]{1,0:T(8,128)S(1)}, f32[1920,12...) custom-call(f32[1024,128]{1,0:T(8,128)S(1)} %get-tuple-element.28.bt, ...), custom_call_target="tpu_custom_call" | custom-call | tf_op jit(solution)/shard_map/pallas_call | solution.py:560
  14.9 0.0 collective-permute-done.2.x1_ref
  14.9 0.0 collective-permute-done.3.x2_ref
  14.9 0.0 copy-start.3
  14.9 3.3 %shard_map.44 = (f32[192,128]{1,0:T(8,128)S(1)}, f32[320,128]{1,0:T(8,128)S(1)}, f32[8,128]{1,0:T(8,128)S(1)}, f32[32,1,128]{2,1,0:T(1,128)}) custom-call(f32[256,128]{1,0:T(8,128)S(1)} %get-tuple-element.32.dens_ref, f32[192,128]{1,0:T(8,128)S(1)} %collective-permute-done.2.x1_ref, f32[192,128]{1,0:T(8,128)S(1)} %collective-permute-done.3.x2_ref, ...), custom_call_target="tpu_custom_call" | custom-call | tf_op jit(solution)/shard_map/pallas_call | solution.py:564
  18.2 0.6 %copy-done.8 = f32[192,128]{1,0:T(8,128)} copy-done((f32[192,128]{1,0:T(8,128)}, f32[192,128]{1,0:T(8,128)S(1)}, u32[]{:S(2)}) %copy-start.8) | copy-done | bytes 98328
  18.8 12.5 %all-to-all-start = ((f32[32,1,128]{2,1,0:T(1,128)}), f32[32,1,128]{2,1,0:T(1,128)S(1)}, u32[]{:S(2)}, u32[]{:S(2)}) async-start(f32[32,1,128]{2,1,0:T(1,128)} %get-tuple-element.46), calls=%async_computation | async-start | bytes 32768 | tf_op jit(solution)/shard_map/all_to_all | solution.py:576
  31.3 0.0 copy-done
  31.4 0.0 copy-start.9
  31.4 0.9 %copy-done.9 = f32[192,128]{1,0:T(8,128)S(1)} copy-done((f32[192,128]{1,0:T(8,128)S(1)}, f32[192,128]{1,0:T(8,128)}, u32[]{:S(2)}) %copy-start.9) | copy-done | bytes 98328
  32.3 0.8 %shard_map.45 = (f32[8,16,768]{2,1,0:T(8,128)S(1)}, f32[8,16,768]{2,1,0:T(8,128)S(1)}, f32[16,768]{1,0:T(8,128)S(1)}) custom-call(f32[1920,128]{1,0:T(8,128)S(1)} %copy-done, f32[192,128]{1,0:T(8,128)S(1)} %copy-done.9, f32[1920,128]{1,0:T(8,128)S(1)} %copy-done.3, f32[320,128]{1,0:T(8,128)S(1)} %get-tuple-element.49.v2_ref, ...), custom_call_target="tpu_custom_call" | custom-call | tf_op jit(solution)/shard_map/pallas_call | solution.py:578
  33.0 0.0 copy-start.4
  33.0 0.7 %copy-done.4 = f32[8,16,768]{2,1,0:T(8,128)} copy-done((f32[8,16,768]{2,1,0:T(8,128)}, f32[8,16,768]{2,1,0:T(8,128)S(1)}, u32[]{:S(2)}) %copy-start.4) | copy-done | bytes 393240
  33.8 0.7 %copy-done.6 = f32[8,16,768]{2,1,0:T(8,128)} copy-done((f32[8,16,768]{2,1,0:T(8,128)}, f32[8,16,768]{2,1,0:T(8,128)S(1)}, u32[]{:S(2)}) %copy-start.6) | copy-done | bytes 393240
  34.5 0.6 %copy-done.10 = f32[16,768]{1,0:T(8,128)} copy-done((f32[16,768]{1,0:T(8,128)}, f32[16,768]{1,0:T(8,128)S(1)}, u32[]{:S(2)}) %copy-start.10) | copy-done | bytes 49176
  35.1 3.3 %all-to-all-done.parts_ref = f32[32,1,128]{2,1,0:T(1,128)S(1)} async-done(((f32[32,1,128]{2,1,0:T(1,128)}), f32[32,1,128]{2,1,0:T(1,128)S(1)}, u32[]{:S(2)}, u32[]{:S(2)}) %all-to-all-start) | async-done | bytes 16416 | tf_op jit(solution)/shard_map/all_to_all | solution.py:576
  38.5 0.0 copy-done.2
  38.5 1.0 %copy-done.5 = f32[8,16,768]{2,1,0:T(8,128)S(1)} copy-done((f32[8,16,768]{2,1,0:T(8,128)S(1)}, f32[8,16,768]{2,1,0:T(8,128)}, u32[]{:S(2)}) %copy-start.5) | copy-done | bytes 393240
  39.5 1.0 %copy-done.7 = f32[8,16,768]{2,1,0:T(8,128)S(1)} copy-done((f32[8,16,768]{2,1,0:T(8,128)S(1)}, f32[8,16,768]{2,1,0:T(8,128)}, u32[]{:S(2)}) %copy-start.7) | copy-done | bytes 393240
  40.5 0.8 %copy-done.11 = f32[16,768]{1,0:T(8,128)S(1)} copy-done((f32[16,768]{1,0:T(8,128)S(1)}, f32[16,768]{1,0:T(8,128)}, u32[]{:S(2)}) %copy-start.11) | copy-done | bytes 49176
  41.3 1.2 %shard_map.46 = (f32[8,16,768]{2,1,0:T(8,128)}, f32[8,16,768]{2,1,0:T(8,128)}) custom-call(f32[32,1,128]{2,1,0:T(1,128)S(1)} %all-to-all-done.parts_ref, f32[8,16,768]{2,1,0:T(8,128)S(1)} %copy-done.2, f32[8,16,768]{2,1,0:T(8,128)S(1)} %copy-done.5, f32[8,16,768]{2,1,0:T(8,128)S(1)} %copy-done.7, f32[16,768]{1,0:T(8,128)S(1)} %copy-done.11), custom_call_target="tpu_custom_call" | custom-call | tf_op jit(solution)/shard_map/pallas_call | solution.py:583
  (10 shorter events, 0.0 us)
Async XLA Ops:
  0.6 1.0 %copy-start.1 = (f32[8,16,768]{2,1,0:T(8,128)S(1)}, f32[8,16,768]{2,1,0:T(8,128)}, u32[]{:S(2)}) copy-start(f32[8,16,768]{2,1,0:T(8,128)} %b_ref.1) | copy-start | bytes 1179652
  1.6 0.8 %copy-start.12 = (f32[16,768]{1,0:T(8,128)S(1)}, f32[16,768]{1,0:T(8,128)}, u32[]{:S(2)}) copy-start(f32[16,768]{1,0:T(8,128)} %d_hbm.1) | copy-start | bytes 147460
  4.2 1.5 %collective-permute-start = (f32[240,128]{1,0:T(8,128)S(1)}, f32[240,128]{1,0:T(8,128)S(1)}, u32[]{:S(2)}, u32[]{:S(2)}) collective-permute-start(f32[240,128]{1,0:T(8,128)S(1)} %get-tuple-element.30), channel_id=1, source_target_pairs={{0,1},{1,0},{2,3},{3,2},{4,5},{5,4},{6,7},{7,6},{8,9},{9,8},{10,11... | collective-permute-start | bytes 368648 | tf_op jit(solution)/shard_map/ppermute | solution.py:513
  4.8 1.0 %collective-permute-start.1 = (f32[240,128]{1,0:T(8,128)S(1)}, f32[240,128]{1,0:T(8,128)S(1)}, u32[]{:S(2)}, u32[]{:S(2)}) collective-permute-start(f32[240,128]{1,0:T(8,128)S(1)} %get-tuple-element.31), channel_id=1, source_target_pairs={{1,2},{2,1},{3,4},{4,3},{5,6},{6,5},{9,10},{10,9},{11,12},{12,11},... | collective-permute-start | bytes 368648 | tf_op jit(solution)/shard_map/ppermute | solution.py:513
  5.9 9.0 %collective-permute-start.2 = (f32[192,128]{1,0:T(8,128)S(1)}, f32[192,128]{1,0:T(8,128)S(1)}, u32[]{:S(2)}, u32[]{:S(2)}) collective-permute-start(f32[192,128]{1,0:T(8,128)S(1)} %get-tuple-element.33), channel_id=1, source_target_pairs={{0,8},{8,0},{16,24},{24,16},{1,9},{9,1},{17,25},{25,17},{2,10},{10... | collective-permute-start | bytes 294920 | tf_op jit(solution)/shard_map/ppermute | solution.py:513
  8.9 6.0 %collective-permute-start.3 = (f32[192,128]{1,0:T(8,128)S(1)}, f32[192,128]{1,0:T(8,128)S(1)}, u32[]{:S(2)}, u32[]{:S(2)}) collective-permute-start(f32[192,128]{1,0:T(8,128)S(1)} %get-tuple-element.34), channel_id=1, source_target_pairs={{8,16},{16,8},{9,17},{17,9},{10,18},{18,10},{11,19},{19,11},{12,20... | collective-permute-start | bytes 294920 | tf_op jit(solution)/shard_map/ppermute | solution.py:513
  14.9 16.4 %copy-start = (f32[1920,128]{1,0:T(8,128)S(1)}, f32[1920,128]{1,0:T(8,128)}, u32[]{:S(2)}) copy-start(f32[1920,128]{1,0:T(8,128)} %get-tuple-element.40.qx1.q1_ref) | copy-start | bytes 2949124
  14.9 16.4 %copy-start.3 = (f32[1920,128]{1,0:T(8,128)S(1)}, f32[1920,128]{1,0:T(8,128)}, u32[]{:S(2)}) copy-start(f32[1920,128]{1,0:T(8,128)} %get-tuple-element.48.v1_ref) | copy-start | bytes 2949124
  18.2 0.6 %copy-start.8 = (f32[192,128]{1,0:T(8,128)}, f32[192,128]{1,0:T(8,128)S(1)}, u32[]{:S(2)}) copy-start(f32[192,128]{1,0:T(8,128)S(1)} %get-tuple-element.47.q2_ref) | copy-start | bytes 294916
  18.8 19.7 %all-to-all-start = ((f32[32,1,128]{2,1,0:T(1,128)}), f32[32,1,128]{2,1,0:T(1,128)S(1)}, u32[]{:S(2)}, u32[]{:S(2)}) async-start(f32[32,1,128]{2,1,0:T(1,128)} %get-tuple-element.46), calls=%async_computation | async-start | bytes 32768 | tf_op jit(solution)/shard_map/all_to_all | solution.py:576
  31.4 0.9 %copy-start.9 = (f32[192,128]{1,0:T(8,128)S(1)}, f32[192,128]{1,0:T(8,128)}, u32[]{:S(2)}) copy-start(f32[192,128]{1,0:T(8,128)} %copy-done.8) | copy-start | bytes 294916
  32.3 6.2 %copy-start.2 = (f32[8,16,768]{2,1,0:T(8,128)S(1)}, f32[8,16,768]{2,1,0:T(8,128)}, u32[]{:S(2)}) copy-start(f32[8,16,768]{2,1,0:T(8,128)} %b_ref.1) | copy-start | bytes 1179652
  33.0 0.7 %copy-start.4 = (f32[8,16,768]{2,1,0:T(8,128)}, f32[8,16,768]{2,1,0:T(8,128)S(1)}, u32[]{:S(2)}) copy-start(f32[8,16,768]{2,1,0:T(8,128)S(1)} %get-tuple-element.51.q_ref) | copy-start | bytes 1179652
  33.8 0.7 %copy-start.6 = (f32[8,16,768]{2,1,0:T(8,128)}, f32[8,16,768]{2,1,0:T(8,128)S(1)}, u32[]{:S(2)}) copy-start(f32[8,16,768]{2,1,0:T(8,128)S(1)} %get-tuple-element.52.v_ref) | copy-start | bytes 1179652
  34.5 0.6 %copy-start.10 = (f32[16,768]{1,0:T(8,128)}, f32[16,768]{1,0:T(8,128)S(1)}, u32[]{:S(2)}) copy-start(f32[16,768]{1,0:T(8,128)S(1)} %get-tuple-element.53.inv_ref) | copy-start | bytes 147460
  38.5 1.0 %copy-start.5 = (f32[8,16,768]{2,1,0:T(8,128)S(1)}, f32[8,16,768]{2,1,0:T(8,128)}, u32[]{:S(2)}) copy-start(f32[8,16,768]{2,1,0:T(8,128)} %copy-done.4) | copy-start | bytes 1179652
  39.5 1.0 %copy-start.7 = (f32[8,16,768]{2,1,0:T(8,128)S(1)}, f32[8,16,768]{2,1,0:T(8,128)}, u32[]{:S(2)}) copy-start(f32[8,16,768]{2,1,0:T(8,128)} %copy-done.6) | copy-start | bytes 1179652
  40.5 0.8 %copy-start.11 = (f32[16,768]{1,0:T(8,128)S(1)}, f32[16,768]{1,0:T(8,128)}, u32[]{:S(2)}) copy-start(f32[16,768]{1,0:T(8,128)} %copy-done.10) | copy-start | bytes 147460

commit v7 on v6

--- a/solution.py
+++ b/solution.py
@@ -93,15 +93,32 @@
         self.ref[self.rows(at), :] = tile
 
 
+class Rows:
+    def __init__(self, ref, pitch, loads):
+        self.ref, self.pitch, self.loads = ref, pitch, loads
+
+    def __getitem__(self, at):
+        row = self.ref[pl.ds(at[0] * self.pitch + at[1], 1), :]
+        return jnp.broadcast_to(row, (self.loads, LANES))
+
+    def put(self, x, values):
+        self.ref[x * self.pitch : x * self.pitch + values.shape[0], :] = values
+
+
 class Joined:
     def __init__(self, first, second, own):
         self.first, self.second, self.own = first, second, own
 
     def __getitem__(self, at):
-        return (self.first if at[0] in self.own else self.second)[at]
+        if at[0] in self.own:
+            return self.first[self.own.index(at[0]), at[1]]
+        return self.second[at]
 
     def __setitem__(self, at, tile):
-        self.first[at] = tile
+        self.first[self.own.index(at[0]), at[1]] = tile
+
+    def put(self, x, values):
+        self.first.put(self.own.index(x), values)
 
 
 def is_even(axis):
@@ -112,15 +129,8 @@
     return jnp.where(even, if_even, if_odd)
 
 
-def pack_kernel(s, b_hbm, d_hbm, bt_ref, dt_ref, y1_ref, y2_ref, b_ref, d_ref, sems):
+def pack_kernel(s, b_ref, d_ref, bt_ref, dt_ref, y1_ref, y2_ref):
     loads, nx, ny = s.loads, s.nx, s.ny
-    d_copy = pltpu.make_async_copy(d_hbm, d_ref, sems.at[loads])
-    d_copy.start()
-    copies = []
-    for load in range(loads):
-        copies.append(pltpu.make_async_copy(b_hbm.at[load], b_ref.at[load], sems.at[load]))
-        copies[-1].start()
-    d_copy.wait()
     for x0 in range(0, nx, SUB):
         for y in range(ny):
             tile = unpack_tile(
@@ -128,7 +138,6 @@
             )
             dt_ref[pl.ds(x0 * ny + y, SUB, stride=ny), :] = tile
     for load in range(loads):
-        copies[load].wait()
         for x0 in range(0, nx, SUB):
             for y in range(ny):
                 tile = unpack_tile(
@@ -196,38 +205,51 @@
     return jnp.where(after[1:] > 0.0, 1.0 / total, 0.0)
 
 
-def spread_rows(s, field, x, values, columns):
-    for y in range(columns):
-        field[x, y] = jnp.broadcast_to(values[y : y + 1, :], (s.loads, LANES))
-
-
 def up(tile):
     return pltpu.roll(tile, LANES - 1, 1)
 
 
-def element_planes(cond, carry, a, count, y0, columns, field, field_up, emit, keep=True):
-    left = [(field[a + u, y0], field_up[a + u, y0]) for u in range(count + 1)]
-    old = [None] * count
+def element_planes(cond, carry, a, count, y0, columns, field, emitter, keep=True):
+    def loads_of(step):
+        y = y0 + step
+        right = [field[a + u, y + 1] for u in range(count + 1)]
+        conduct = [cond[a + u, y] for u in range(count)]
+        above = extra = None
+        if step and emitter:
+            above = (carry[0, y], carry[1, y])
+            extra = [emitter.fetch(a + u, y) for u in range(count)]
+        return right, conduct, above, extra
+
+    left = [(tile, up(tile)) for tile in [field[a + u, y0] for u in range(count + 1)]]
+    ahead = loads_of(0)
+    old, waiting = [None] * count, []
     for step in range(columns):
         y = y0 + step
-        right = [(field[a + u, y + 1], field_up[a + u, y + 1]) for u in range(count + 1)]
-        above = (carry[0, y], carry[1, y]) if step and emit else None
+        right, conduct, above, extra = ahead
+        if step + 1 < columns:
+            ahead = loads_of(step + 1)
+        if len(waiting) > 1:
+            for into, at, tile in waiting.pop(0):
+                into[at] = tile
+        stores = []
+        right = [(tile, up(tile)) for tile in right]
         for u in range(count):
             (p0, p0s), (p1, p1s) = left[u], left[u + 1]
             (r0, r0s), (r1, r1s) = right[u], right[u + 1]
-            c = cond[a + u, y]
+            c = conduct[u]
             even = (p0 + r1) + (r0s + p1s)
             odd = (r0 + p1) + (p0s + r1s)
             pass_on = keep or u + 1 < count
             lower = upper = None
-            if emit:
+            if emitter:
                 lower = (c * (odd + p1s), c * (even + p1))
             if pass_on:
                 upper = (c * (even + p0s), c * (odd + p0))
-            if step and emit:
+            if step and emitter:
                 low = (c * (even + r1s) + old[u][0][0]) + above[0]
                 high = (c * (odd + r1) + old[u][0][1]) + above[1]
-                emit(u, a + u, y, p0, low + pltpu.roll(high, 1, 1))
+                total = low + pltpu.roll(high, 1, 1)
+                stores += emitter.finish(a + u, y, p0, total, extra[u])
             if step and pass_on:
                 above = (
                     c * (odd + r0s) + old[u][1][0],
@@ -235,33 +257,44 @@
                 )
             old[u] = (lower, upper)
         if step and keep:
-            carry[0, y], carry[1, y] = above
+            stores += [(carry, (0, y), above[0]), (carry, (1, y), above[1])]
+        waiting.append(stores)
         left = right
-
-
-def first_emit(bx, invx, qx, wx, ws):
-    def emit(u, x, y, node, total):
-        image = 1.25 * bx[x, y] - total
-        weighted = image * invx[x, y]
-        qx[x, y] = image
-        wx[x, y] = weighted
-        ws[x, y] = up(weighted)
-
-    return emit
-
-
-def second_emit(bx, zx, qx, vx, sums):
-    def emit(u, x, y, weighted, total):
-        image, source, scaled = qx[x, y], bx[x, y], zx[x, y]
+    for stores in waiting:
+        for into, at, tile in stores:
+            into[at] = tile
+
+
+class First:
+    def __init__(self, bx, invx, qx, wx):
+        self.bx, self.invx, self.qx, self.wx = bx, invx, qx, wx
+
+    def fetch(self, x, y):
+        return self.bx[x, y], self.invx[x, y]
+
+    def finish(self, x, y, node, total, extra):
+        source, inverse = extra
+        image = 1.25 * source - total
+        return [(self.qx, (x, y), image), (self.wx, (x, y), image * inverse)]
+
+
+class Second:
+    def __init__(self, bx, zx, qx, vx, sums):
+        self.bx, self.zx, self.qx, self.vx, self.sums = bx, zx, qx, vx, sums
+
+    def fetch(self, x, y):
+        return self.bx[x, y], self.zx[x, y], self.qx[x, y]
+
+    def finish(self, x, y, weighted, total, extra):
+        source, scaled, image = extra
         again = 1.25 * image - total
-        vx[x, y] = again
         change = scaled - weighted
+        sums = self.sums
         sums[0] = sums[0] + source * scaled
         sums[1] = sums[1] + source * change
         sums[2] = sums[2] + (source - image) * change
         sums[3] = sums[3] + (image - again) * change
-
-    return emit
+        return [(self.vx, (x, y), again)]
 
 
 def over_planes(start, stop, body, state):
@@ -274,28 +307,27 @@
 
 def inner_kernel(
     s, bt_ref, dens_ref, y1_ref, y2_ref,
-    cond, invx, bx, zx, zs, qx, wx, ws, vx, carry1, carry2, sums_ref,
+    cond, invx, bx, zx, qx, wx, vx, carry1, carry2, sums_ref,
 ):
     loads, nx, ny, my, pitch = s.loads, s.nx, s.ny, s.my, s.pitch
-    cond, invx, bx, zx, zs, qx, wx, ws, vx, carry1, carry2 = (
-        Tiles(ref, my, loads) for ref in (cond, invx, bx, zx, zs, qx, wx, ws, vx, carry1, carry2)
+    bx, zx, qx, wx, vx, carry1, carry2 = (
+        Tiles(ref, my, loads) for ref in (bx, zx, qx, wx, vx, carry1, carry2)
     )
+    cond, invx = Rows(cond, pitch, loads), Rows(invx, pitch, loads)
     even_y = is_even("gy")
     ys = (pick(even_y, ny + 2, 0), pick(even_y, 0, ny + 2))
     before = None
     for x in range(nx):
         after = conduct_of(dens_ref[x * pitch : (x + 1) * pitch, :])
-        spread_rows(s, cond, x + 2, after[1:], my - 1)
+        cond.put(x + 2, after[1:])
         if x:
-            spread_rows(s, invx, x + 2, inverse_of(s, before, after), my)
+            invx.put(x + 2, inverse_of(s, before, after))
         before = after
 
     def stage(x, y, tile):
         bx[x + 2, y] = tile
         if x:
-            scaled = tile * invx[x + 2, y]
-            zx[x + 2, y] = scaled
-            zs[x + 2, y] = up(scaled)
+            zx[x + 2, y] = tile * invx[x + 2, y]
 
     inner = Tiles(bt_ref, ny, loads)
     for x in range(nx):
@@ -306,20 +338,18 @@
             ref, 0, loads, 2 * nx, lambda i, tile: stage(i // 2, ys[side] + i % 2, tile)
         )
 
-    element_planes(cond, carry1, 3, 1, 0, my - 1, zx, zs, None)
+    element_planes(cond, carry1, 3, 1, 0, my - 1, zx, None)
 
     def first(a, count, state):
-        emit = first_emit(bx, invx, qx, wx, ws)
-        element_planes(cond, carry1, a, count, 0, my - 1, zx, zs, emit)
+        element_planes(cond, carry1, a, count, 0, my - 1, zx, First(bx, invx, qx, wx))
         return state
 
     over_planes(4, nx + 1, first, 0)
-    element_planes(cond, carry2, 4, 1, 1, my - 3, wx, ws, None)
+    element_planes(cond, carry2, 4, 1, 1, my - 3, wx, None)
 
     def second(a, count, sums):
         sums = list(sums)
-        emit = second_emit(bx, zx, qx, vx, sums)
-        element_planes(cond, carry2, a, count, 1, my - 3, wx, ws, emit)
+        element_planes(cond, carry2, a, count, 1, my - 3, wx, Second(bx, zx, qx, vx, sums))
         return tuple(sums)
 
     zero = jnp.zeros((loads, LANES), jnp.float32)
@@ -330,9 +360,9 @@
 
 def outer_kernel(
     s, dens_ref, x1_ref, x2_ref,
-    cond1, invx1, bx1, zx1, zs1, qx1, wx1, ws1, carry1, carry2, sums1,
+    cond1, invx1, bx1, zx1, qx1, wx1, carry1, carry2, sums1,
     q_out, v_out, inv_out, sums_ref,
-    low_ref, high_ref, cond2, invx2, bx2, zx2, zs2, qx2, wx2, ws2, vx2, carry3,
+    low_ref, high_ref, cond2, invx2, bx2, zx2, qx2, wx2, vx2, carry3,
 ):
     loads, nx, ny, mx, my, pitch = s.loads, s.nx, s.ny, s.mx, s.my, s.pitch
     even_x = is_even("gx")
@@ -347,22 +377,20 @@
         low_ref[...] = x1_ref[...]
         high_ref[...] = x2_ref[...]
 
-    def tiles(ref):
-        return Tiles(ref, my, loads)
-
     def joined(first, second, own):
-        return Joined(tiles(first), tiles(second), own)
+        return Joined(Tiles(first, my, loads), Tiles(second, my, loads), own)
+
+    def joined_rows(first, second, own):
+        return Joined(Rows(first, pitch, loads), Rows(second, pitch, loads), own)
 
     outside = (0, 1, nx + 2, nx + 3)
     scaled_own = outside + (2,)
     image_own = (1, 2, 3, nx + 1, nx + 2)
-    cond, invx = joined(cond2, cond1, outside), joined(invx2, invx1, scaled_own)
-    bx = joined(bx2, bx1, outside)
-    zx, zs = joined(zx2, zx1, scaled_own), joined(zs2, zs1, scaled_own)
-    qx = joined(qx2, qx1, image_own)
-    wx, ws = joined(wx2, wx1, image_own), joined(ws2, ws1, image_own)
-    vx, carry3 = tiles(vx2), tiles(carry3)
-    carry1, carry2 = tiles(carry1), tiles(carry2)
+    cond, invx = joined_rows(cond2, cond1, outside), joined_rows(invx2, invx1, scaled_own)
+    bx, zx = joined(bx2, bx1, outside), joined(zx2, zx1, scaled_own)
+    qx, wx = joined(qx2, qx1, image_own), joined(wx2, wx1, image_own)
+    vx = joined(vx2, vx2, again_planes(nx))
+    carry1, carry2, carry3 = (Tiles(ref, my, loads) for ref in (carry1, carry2, carry3))
 
     def conduct(ref, base, x):
         return conduct_of(ref[base + x * pitch : base + (x + 1) * pitch, :])
@@ -371,40 +399,36 @@
     high = [conduct(dens_ref, 0, nx - 1)] + [conduct(high_ref, s.x_dens, t) for t in range(2)]
     for x in range(3):
         inverse = inverse_of(s, low[x], low[x + 1])
-        spread_rows(s, invx, x, inverse, my)
+        invx.put(x, inverse)
         if x < 2:
-            spread_rows(s, cond, x, low[x + 1][1:], my - 1)
+            cond.put(x, low[x + 1][1:])
     inv_out[...] = inverse[2 : 2 + ny]
     for x in range(2):
-        spread_rows(s, invx, nx + 2 + x, inverse_of(s, high[x], high[x + 1]), my)
-    spread_rows(s, cond, nx + 2, high[1][1:], my - 1)
-
-    def stage(x, y, tile):
-        scaled = tile * invx[x, y]
-        zx[x, y] = scaled
-        zs[x, y] = up(scaled)
+        invx.put(nx + 2 + x, inverse_of(s, high[x], high[x + 1]))
+    cond.put(nx + 2, high[1][1:])
 
     for ref, x0 in ((low_ref, 0), (high_ref, nx + 2)):
 
         def write(i, tile):
-            bx[x0 + i // my, i % my] = tile
-            stage(x0 + i // my, i % my, tile)
+            at = x0 + i // my, i % my
+            bx[at] = tile
+            zx[at] = tile * invx[at]
 
         unpack_tiles(ref, 0, loads, 2 * my, write)
     for y in range(my):
-        stage(2, y, bx[2, y])
-
-    emit = first_emit(bx, invx, qx, wx, ws)
-    element_planes(cond, carry3, 0, 1, 0, my - 1, zx, zs, None)
-    element_planes(cond, carry3, 1, 2, 0, my - 1, zx, zs, emit)
-    element_planes(cond, carry3, 3, 1, 0, my - 1, zx, zs, emit, keep=False)
-    element_planes(cond, carry1, nx + 1, 2, 0, my - 1, zx, zs, emit, keep=False)
+        zx[2, y] = bx[2, y] * invx[2, y]
+
+    emitter = First(bx, invx, qx, wx)
+    element_planes(cond, carry3, 0, 1, 0, my - 1, zx, None)
+    element_planes(cond, carry3, 1, 2, 0, my - 1, zx, emitter)
+    element_planes(cond, carry3, 3, 1, 0, my - 1, zx, emitter, keep=False)
+    element_planes(cond, carry1, nx + 1, 2, 0, my - 1, zx, emitter, keep=False)
     sums = [sums1[place * loads : (place + 1) * loads, :] for place in range(4)]
-    emit = second_emit(bx, zx, qx, vx, sums)
-    element_planes(cond, carry3, 1, 1, 1, my - 3, wx, ws, None)
-    element_planes(cond, carry3, 2, 2, 1, my - 3, wx, ws, emit)
-    element_planes(cond, carry3, 4, 1, 1, my - 3, wx, ws, emit, keep=False)
-    element_planes(cond, carry2, nx, 2, 1, my - 3, wx, ws, emit, keep=False)
+    emitter = Second(bx, zx, qx, vx, sums)
+    element_planes(cond, carry3, 1, 1, 1, my - 3, wx, None)
+    element_planes(cond, carry3, 2, 2, 1, my - 3, wx, emitter)
+    element_planes(cond, carry3, 4, 1, 1, my - 3, wx, emitter, keep=False)
+    element_planes(cond, carry2, nx, 2, 1, my - 3, wx, emitter, keep=False)
     for field, out, planes in ((qx, q_out, image_planes(nx)), (vx, v_out, again_planes(nx))):
         out = Tiles(out, ny, loads)
         for place, x in enumerate(planes):
@@ -458,7 +482,7 @@
         for block in range(packed_count(ny)):
             io_ref[x0 : x0 + SUB, block * LANES : (block + 1) * LANES] = pack_block(
                 lambda y: inv1_ref[
-                    pl.ds(((x0 + 2) * my + y + 2) * loads, SUB, stride=my * loads), :
+                    pl.ds((x0 + 2) * s.pitch + y + 2, SUB, stride=s.pitch), :
                 ],
                 ny, block, SUB,
             )
@@ -527,7 +551,7 @@
         return pltpu.VMEM(dims, jnp.float32)
 
     def call(kernel, out_shape, **more):
-        params = pltpu.CompilerParams(vmem_limit_bytes=48 * 1024 * 1024)
+        params = pltpu.CompilerParams(vmem_limit_bytes=20 * 1024 * 1024)
         return pl.pallas_call(
             functools.partial(kernel, s), out_shape=out_shape, compiler_params=params, **more
         )
@@ -541,12 +565,6 @@
             shape(s.y_rows, LANES),
             shape(s.y_rows, LANES),
         ),
-        in_specs=[hbm, hbm],
-        scratch_shapes=[
-            scratch(loads, nx, flat),
-            scratch(nx, flat),
-            pltpu.SemaphoreType.DMA((loads + 1,)),
-        ],
     )(heat_source, density)
     y2, y1 = swap(y2, "gy", 1), swap(y1, "gy", 0)
     dens, x1, x2 = call(
@@ -555,11 +573,11 @@
         scratch_shapes=[scratch(4 * s.my * loads, LANES)],
     )(bt, dt, y1, y2)
     x1, x2 = swap(x1, "gx", 0), swap(x2, "gx", 1)
-    field = s.mx * s.my * loads
-    edge = 2 * s.my * loads
-    *fields, v_1, carry1, carry2, sums = call(
-        inner_kernel,
-        (shape(field, LANES),) * 9 + (shape(edge, LANES),) * 2 + (shape(4 * loads, LANES),),
+    plane = s.my * loads
+    rows, field = shape(s.mx * s.pitch, LANES), shape(s.mx * plane, LANES)
+    edge = shape(2 * plane, LANES)
+    cond, inv_1, bx, zx, q_1, w_1, v_1, carry1, carry2, sums = call(
+        inner_kernel, (rows,) * 2 + (field,) * 5 + (edge,) * 2 + (shape(4 * loads, LANES),)
     )(bt, dens, y1, y2)
     q_2, v_2, inv_2, sums = call(
         outer_kernel,
@@ -570,16 +588,17 @@
             shape(devices, 1, LANES),
         ),
         scratch_shapes=[scratch(s.x_rows, LANES)] * 2
-        + [scratch(field, LANES)] * 9
-        + [scratch(edge, LANES)],
-    )(dens, x1, x2, *fields, carry1, carry2, sums)
+        + [scratch(5 * s.pitch, LANES)] * 2
+        + [scratch(5 * plane, LANES)] * 5
+        + [scratch(2 * plane, LANES)],
+    )(dens, x1, x2, cond, inv_1, bx, zx, q_1, w_1, carry1, carry2, sums)
     parts = lax.all_to_all(sums, ("gx", "gy"), 0, 0, tiled=True)
     whole = shape(loads, nx, flat)
     image, again, inverse = call(
         unpack_kernel,
         (whole, whole, shape(nx, flat)),
         scratch_shapes=[scratch(nodes, LANES)],
-    )(fields[5], q_2, v_1, v_2, fields[1], inv_2)
+    )(q_1, q_2, v_1, v_2, inv_1, inv_2)
     return call(
         finish_kernel,
         (whole, whole),

time: 42.9 us -> 35.6 us (0.83)
  Pallas kernels: 12.5 us -> 6.94 us
  local copies, waits for them, and re-layouts: 8.22 us -> 3.32 us
  waiting for transfers between devices: 3.66 us -> 5.73 us
  starting transfers between devices: 17.3 us -> 18.6 us
    unnamed x26 -> x10, local copies, waits for them, and re-layouts: 8.22 us -> 3.32 us
    pallas_call x1, Pallas kernels: 5.3 us -> 2.77 us  [per_device(): call(inner_kernel, (rows,) * 2 + (field,) * 5 + (edge,) * 2 + (shape(4 *...]
    all_to_all x1, waiting for transfers between devices: 3.34 us -> 5.41 us  [per_device(): parts = lax.all_to_all(sums, ('gx', 'gy'), 0, 0, tiled=True)]
    pallas_call x1, Pallas kernels: 3.26 us -> 1.48 us  [per_device(): call(outer_kernel, (shape(len(image_planes(nx)) * ny * loads, LANES), sha...]
    pallas_call x1, Pallas kernels: 1.81 us -> 0.55 us  [per_device(): call(pack_kernel, (shape(nodes, LANES), shape(nx * ny, LANES), shape(s.y_...]
    all_to_all x1, starting transfers between devices: 12.5 us -> 13.7 us  [per_device(): parts = lax.all_to_all(sums, ('gx', 'gy'), 0, 0, tiled=True)]
  transfers between devices with their start and end apart: 5 -> 5, of which waited for: 2 -> 2; matrix products, arithmetic and copies ran while one was open for 0% -> 0% of each run, Pallas kernels for 14% -> 10%
where the time goes in v7:
time: 35.6 us; the launch traced here: 35.3 us
  starting transfers between devices  18.6 us (52%)
  Pallas kernels  6.94 us (19%)
  waiting for transfers between devices  5.73 us (16%)
  local copies, waits for them, and re-layouts  3.32 us (9%)
  between operations  0.72 us (2%)
    all_to_all x1, starting transfers between devices, per_device(): parts = lax.all_to_all(sums, ('gx', 'gy'), 0, 0, tiled=True)  13.7 us
    all_to_all x1, waiting for transfers between devices, per_device(): parts = lax.all_to_all(sums, ('gx', 'gy'), 0, 0, tiled=True)  5.41 us
    ppermute x4, starting transfers between devices, swap(): return lax.ppermute(array, axis, pairs)  4.82 us
    unnamed x10, local copies, waits for them, and re-layouts  3.32 us
    pallas_call x1, Pallas kernels, per_device(): call(inner_kernel, (rows,) * 2 + (field,) * 5 + (edge,) * 2 + (shape(4 *...  2.77 us
    pallas_call x1, Pallas kernels, per_device(): call(outer_kernel, (shape(len(image_planes(nx)) * ny * loads, LANES), sha...  1.48 us
    pallas_call x1, Pallas kernels, per_device(): call(finish_kernel, (whole, whole), out_specs=(hbm, hbm), scratch_shapes=...  1.21 us
    pallas_call x1, Pallas kernels, per_device(): call(unpack_kernel, (whole, whole, shape(nx, flat)), scratch_shapes=[scra...  0.76 us
  transfers between devices with their start and end apart: 5, of which 2 were waited for; matrix products, arithmetic and copies ran while one was open for 0% of the time, Pallas kernels for 10%

profile of v7, /device:TPU:0, one launch (start us, length us, event | category | flops | bytes accessed | tf_op | source)
XLA Modules:
  0.0 35.3 jit_solution(14113261896532617863)
XLA Ops:
  0.6 0.0 copy-start
  0.6 1.0 %copy-done = f32[8,16,768]{2,1,0:T(8,128)S(1)} copy-done((f32[8,16,768]{2,1,0:T(8,128)S(1)}, f32[8,16,768]{2,1,0:T(8,128)}, u32[]{:S(2)}) %copy-start) | copy-done | bytes 393240
  1.6 0.0 copy-start.4
  1.6 0.8 %copy-done.4 = f32[16,768]{1,0:T(8,128)S(1)} copy-done((f32[16,768]{1,0:T(8,128)S(1)}, f32[16,768]{1,0:T(8,128)}, u32[]{:S(2)}) %copy-start.4) | copy-done | bytes 49176
  2.4 0.5 %shard_map.41 = (f32[1024,128]{1,0:T(8,128)S(1)}, f32[128,128]{1,0:T(8,128)S(1)}, f32[240,128]{1,0:T(8,128)S(1)}, f32[240,128]{1,0:T(8,128)S(1)}) custom-call(f32[8,16,768]{2,1,0:T(8,128)S(1)} %copy-done, f32[16,768]{1,0:T(8,128)S(1)} %copy-done.4), custom_call_target="tpu_custom_call" | custom-call | tf_op jit(solution)/shard_map/pallas_call | solution.py:560
  3.0 0.5 %collective-permute-start = (f32[240,128]{1,0:T(8,128)S(1)}, f32[240,128]{1,0:T(8,128)S(1)}, u32[]{:S(2)}, u32[]{:S(2)}) collective-permute-start(f32[240,128]{1,0:T(8,128)S(1)} %get-tuple-element.28), channel_id=1, source_target_pairs={{0,1},{1,0},{2,3},{3,2},{4,5},{5,4},{6,7},{7,6},{8,9},{9,8},{10,11... | collective-permute-start | bytes 368648 | tf_op jit(solution)/shard_map/ppermute | solution.py:537
  3.5 0.7 %collective-permute-start.1 = (f32[240,128]{1,0:T(8,128)S(1)}, f32[240,128]{1,0:T(8,128)S(1)}, u32[]{:S(2)}, u32[]{:S(2)}) collective-permute-start(f32[240,128]{1,0:T(8,128)S(1)} %get-tuple-element.29), channel_id=1, source_target_pairs={{1,2},{2,1},{3,4},{4,3},{5,6},{6,5},{9,10},{10,9},{11,12},{12,11},... | collective-permute-start | bytes 368648 | tf_op jit(solution)/shard_map/ppermute | solution.py:537
  4.2 0.3 collective-permute-done.y1_ref
  4.5 0.0 collective-permute-done.1.y2_ref
  4.5 0.2 shard_map.42
  4.7 3.0 %collective-permute-start.2 = (f32[192,128]{1,0:T(8,128)S(1)}, f32[192,128]{1,0:T(8,128)S(1)}, u32[]{:S(2)}, u32[]{:S(2)}) collective-permute-start(f32[192,128]{1,0:T(8,128)S(1)} %get-tuple-element.31), channel_id=1, source_target_pairs={{0,8},{8,0},{16,24},{24,16},{1,9},{9,1},{17,25},{25,17},{2,10},{10... | collective-permute-start | bytes 294920 | tf_op jit(solution)/shard_map/ppermute | solution.py:537
  7.7 0.7 %collective-permute-start.3 = (f32[192,128]{1,0:T(8,128)S(1)}, f32[192,128]{1,0:T(8,128)S(1)}, u32[]{:S(2)}, u32[]{:S(2)}) collective-permute-start(f32[192,128]{1,0:T(8,128)S(1)} %get-tuple-element.32), channel_id=1, source_target_pairs={{8,16},{16,8},{9,17},{17,9},{10,18},{18,10},{11,19},{19,11},{12,20... | collective-permute-start | bytes 294920 | tf_op jit(solution)/shard_map/ppermute | solution.py:537
  8.3 2.8 %shard_map.43 = (f32[320,128]{1,0:T(8,128)S(1)}, f32[320,128]{1,0:T(8,128)S(1)}, f32[1920,128]{1,0:T(8,128)S(1)}, f32[1920,128]{1,0:T(8,128)S(1)}, f32[1920,128]...) custom-call(f32[1024,128]{1,0:T(8,128)S(1)} %get-tuple-element.26.bt, ...), custom_call_target="tpu_custom_call" | custom-call | tf_op jit(solution)/shard_map/pallas_call | solution.py:579
  11.1 0.0 collective-permute-done.2.x1_ref
  11.1 0.0 collective-permute-done.3.x2_ref
  11.1 1.5 %shard_map.44 = (f32[192,128]{1,0:T(8,128)S(1)}, f32[320,128]{1,0:T(8,128)S(1)}, f32[8,128]{1,0:T(8,128)S(1)}, f32[32,1,128]{2,1,0:T(1,128)}) custom-call(f32[256,128]{1,0:T(8,128)S(1)} %get-tuple-element.30.dens_ref, f32[192,128]{1,0:T(8,128)S(1)} %collective-permute-done.2.x1_ref, f32[192,128]{1,0:T(8,128)S(1)} %collective-permute-done.3.x2_ref, ...), custom_call_target="tpu_custom_call" | custom-call | tf_op jit(solution)/shard_map/pallas_call | solution.py:582
  12.6 0.0 copy-start.2
  12.6 0.6 %copy-done.2 = f32[192,128]{1,0:T(8,128)} copy-done((f32[192,128]{1,0:T(8,128)}, f32[192,128]{1,0:T(8,128)S(1)}, u32[]{:S(2)}) %copy-start.2) | copy-done | bytes 98328
  13.2 13.7 %all-to-all-start = ((f32[32,1,128]{2,1,0:T(1,128)}), f32[32,1,128]{2,1,0:T(1,128)S(1)}, u32[]{:S(2)}, u32[]{:S(2)}) async-start(f32[32,1,128]{2,1,0:T(1,128)} %get-tuple-element.42), calls=%async_computation | async-start | bytes 32768 | tf_op jit(solution)/shard_map/all_to_all | solution.py:595
  27.0 0.0 copy-start.3
  27.0 0.9 %copy-done.3 = f32[192,128]{1,0:T(8,128)S(1)} copy-done((f32[192,128]{1,0:T(8,128)S(1)}, f32[192,128]{1,0:T(8,128)}, u32[]{:S(2)}) %copy-start.3) | copy-done | bytes 98328
  27.9 0.0 copy-start.1
  27.9 0.8 %shard_map.45 = (f32[8,16,768]{2,1,0:T(8,128)S(1)}, f32[8,16,768]{2,1,0:T(8,128)S(1)}, f32[16,768]{1,0:T(8,128)S(1)}) custom-call(f32[1920,128]{1,0:T(8,128)S(1)} %get-tuple-element.37.qx1.q1_ref, f32[192,128]{1,0:T(8,128)S(1)} %copy-done.3, f32[1920,128]{1,0:T(8,128)S(1)} %get-tuple-element.44.v1_ref, f32[320,128]{1,0:T(8,128)S(1)} %get-tuple-element.45.v2_ref, ...), custom_call_target="tpu_custom_call" | custom-call | tf_op jit(solution)/shard_map/pallas_call | solution.py:597
  28.6 5.4 %all-to-all-done.parts_ref = f32[32,1,128]{2,1,0:T(1,128)S(1)} async-done(((f32[32,1,128]{2,1,0:T(1,128)}), f32[32,1,128]{2,1,0:T(1,128)S(1)}, u32[]{:S(2)}, u32[]{:S(2)}) %all-to-all-start) | async-done | bytes 16416 | tf_op jit(solution)/shard_map/all_to_all | solution.py:595
  34.1 0.0 copy-done.1
  34.1 1.2 %shard_map.46 = (f32[8,16,768]{2,1,0:T(8,128)}, f32[8,16,768]{2,1,0:T(8,128)}) custom-call(f32[32,1,128]{2,1,0:T(1,128)S(1)} %all-to-all-done.parts_ref, f32[8,16,768]{2,1,0:T(8,128)S(1)} %copy-done.1, f32[8,16,768]{2,1,0:T(8,128)S(1)} %get-tuple-element.47.q_ref, f32[8,16,768]{2,1,0:T(8,128)S(1)} %get-tuple-element.48.v_ref, ...), custom_call_target="tpu_custom_call" | custom-call | tf_op jit(solution)/shard_map/pallas_call | solution.py:602
Async XLA Ops:
  0.6 1.0 %copy-start = (f32[8,16,768]{2,1,0:T(8,128)S(1)}, f32[8,16,768]{2,1,0:T(8,128)}, u32[]{:S(2)}) copy-start(f32[8,16,768]{2,1,0:T(8,128)} %b_ref.3) | copy-start | bytes 1179652
  1.6 0.8 %copy-start.4 = (f32[16,768]{1,0:T(8,128)S(1)}, f32[16,768]{1,0:T(8,128)}, u32[]{:S(2)}) copy-start(f32[16,768]{1,0:T(8,128)} %d_ref.1) | copy-start | bytes 147460
  3.0 1.5 %collective-permute-start = (f32[240,128]{1,0:T(8,128)S(1)}, f32[240,128]{1,0:T(8,128)S(1)}, u32[]{:S(2)}, u32[]{:S(2)}) collective-permute-start(f32[240,128]{1,0:T(8,128)S(1)} %get-tuple-element.28), channel_id=1, source_target_pairs={{0,1},{1,0},{2,3},{3,2},{4,5},{5,4},{6,7},{7,6},{8,9},{9,8},{10,11... | collective-permute-start | bytes 368648 | tf_op jit(solution)/shard_map/ppermute | solution.py:537
  3.5 1.0 %collective-permute-start.1 = (f32[240,128]{1,0:T(8,128)S(1)}, f32[240,128]{1,0:T(8,128)S(1)}, u32[]{:S(2)}, u32[]{:S(2)}) collective-permute-start(f32[240,128]{1,0:T(8,128)S(1)} %get-tuple-element.29), channel_id=1, source_target_pairs={{1,2},{2,1},{3,4},{4,3},{5,6},{6,5},{9,10},{10,9},{11,12},{12,11},... | collective-permute-start | bytes 368648 | tf_op jit(solution)/shard_map/ppermute | solution.py:537
  4.7 6.4 %collective-permute-start.2 = (f32[192,128]{1,0:T(8,128)S(1)}, f32[192,128]{1,0:T(8,128)S(1)}, u32[]{:S(2)}, u32[]{:S(2)}) collective-permute-start(f32[192,128]{1,0:T(8,128)S(1)} %get-tuple-element.31), channel_id=1, source_target_pairs={{0,8},{8,0},{16,24},{24,16},{1,9},{9,1},{17,25},{25,17},{2,10},{10... | collective-permute-start | bytes 294920 | tf_op jit(solution)/shard_map/ppermute | solution.py:537
  7.7 3.4 %collective-permute-start.3 = (f32[192,128]{1,0:T(8,128)S(1)}, f32[192,128]{1,0:T(8,128)S(1)}, u32[]{:S(2)}, u32[]{:S(2)}) collective-permute-start(f32[192,128]{1,0:T(8,128)S(1)} %get-tuple-element.32), channel_id=1, source_target_pairs={{8,16},{16,8},{9,17},{17,9},{10,18},{18,10},{11,19},{19,11},{12,20... | collective-permute-start | bytes 294920 | tf_op jit(solution)/shard_map/ppermute | solution.py:537
  12.6 0.6 %copy-start.2 = (f32[192,128]{1,0:T(8,128)}, f32[192,128]{1,0:T(8,128)S(1)}, u32[]{:S(2)}) copy-start(f32[192,128]{1,0:T(8,128)S(1)} %get-tuple-element.43.q2_ref) | copy-start | bytes 294916
  13.2 20.8 %all-to-all-start = ((f32[32,1,128]{2,1,0:T(1,128)}), f32[32,1,128]{2,1,0:T(1,128)S(1)}, u32[]{:S(2)}, u32[]{:S(2)}) async-start(f32[32,1,128]{2,1,0:T(1,128)} %get-tuple-element.42), calls=%async_computation | async-start | bytes 32768 | tf_op jit(solution)/shard_map/all_to_all | solution.py:595
  27.0 0.9 %copy-start.3 = (f32[192,128]{1,0:T(8,128)S(1)}, f32[192,128]{1,0:T(8,128)}, u32[]{:S(2)}) copy-start(f32[192,128]{1,0:T(8,128)} %copy-done.2) | copy-start | bytes 294916
  27.9 6.2 %copy-start.1 = (f32[8,16,768]{2,1,0:T(8,128)S(1)}, f32[8,16,768]{2,1,0:T(8,128)}, u32[]{:S(2)}) copy-start(f32[8,16,768]{2,1,0:T(8,128)} %b_ref.3) | copy-start | bytes 1179652

commit v8 on v7

--- a/solution.py
+++ b/solution.py
@@ -129,24 +129,34 @@
     return jnp.where(even, if_even, if_odd)
 
 
-def pack_kernel(s, b_ref, d_ref, bt_ref, dt_ref, y1_ref, y2_ref):
+def pack_kernel(s, b_hbm, d_hbm, bt_ref, dt_ref, y2_ref, b_ref, d_ref, sems):
     loads, nx, ny = s.loads, s.nx, s.ny
+    d_copy = pltpu.make_async_copy(d_hbm, d_ref, sems.at[loads])
+    copies = []
+    for load in range(loads):
+        copies.append(pltpu.make_async_copy(b_hbm.at[load], b_ref.at[load], sems.at[load]))
+        copies[-1].start()
+    d_copy.start()
+    for load in range(loads):
+        copies[load].wait()
+        for x0 in range(0, nx, SUB):
+            for y in range(ny):
+                tile = unpack_tile(
+                    lambda t: b_ref[load, x0 : x0 + SUB, t * LANES : (t + 1) * LANES], y, SUB
+                )
+                bt_ref[pl.ds((x0 * ny + y) * loads + load, SUB, stride=ny * loads), :] = tile
+    d_copy.wait()
     for x0 in range(0, nx, SUB):
         for y in range(ny):
             tile = unpack_tile(
                 lambda t: d_ref[x0 : x0 + SUB, t * LANES : (t + 1) * LANES], y, SUB
             )
             dt_ref[pl.ds(x0 * ny + y, SUB, stride=ny), :] = tile
-    for load in range(loads):
-        for x0 in range(0, nx, SUB):
-            for y in range(ny):
-                tile = unpack_tile(
-                    lambda t: b_ref[load, x0 : x0 + SUB, t * LANES : (t + 1) * LANES], y, SUB
-                )
-                bt_ref[pl.ds((x0 * ny + y) * loads + load, SUB, stride=ny * loads), :] = tile
-    even_y = is_even("gy")
-    pack_face(s, even_y, bt_ref, dt_ref, y1_ref)
-    pack_face(s, jnp.logical_not(even_y), bt_ref, dt_ref, y2_ref)
+    pack_face(s, jnp.logical_not(is_even("gy")), bt_ref, dt_ref, y2_ref)
+
+
+def pack_near_kernel(s, bt_ref, dt_ref, y1_ref):
+    pack_face(s, is_even("gy"), bt_ref, dt_ref, y1_ref)
 
 
 def pack_face(s, upper, bt_ref, dt_ref, out_ref):
@@ -161,7 +171,7 @@
             out_ref[at : at + SUB, :] = dt_ref[pl.ds(x0 * ny + y0 + dy, SUB, stride=ny), :]
 
 
-def pack_x_kernel(s, bt_ref, dt_ref, y1_ref, y2_ref, dens_ref, x1_ref, x2_ref, edge_ref):
+def pack_x_kernel(s, bt_ref, dt_ref, y2_ref, y1_ref, dens_ref, x1_ref, x2_ref, edge_ref):
     loads, nx, ny, my, pitch = s.loads, s.nx, s.ny, s.my, s.pitch
     even_x, even_y = is_even("gx"), is_even("gy")
     ys = (pick(even_y, ny + 2, 0), pick(even_y, 0, ny + 2))
@@ -305,14 +315,12 @@
     return state
 
 
-def inner_kernel(
+def image_kernel(
     s, bt_ref, dens_ref, y1_ref, y2_ref,
-    cond, invx, bx, zx, qx, wx, vx, carry1, carry2, sums_ref,
+    cond, invx, bx, zx, qx, wx, carry1,
 ):
     loads, nx, ny, my, pitch = s.loads, s.nx, s.ny, s.my, s.pitch
-    bx, zx, qx, wx, vx, carry1, carry2 = (
-        Tiles(ref, my, loads) for ref in (bx, zx, qx, wx, vx, carry1, carry2)
-    )
+    bx, zx, qx, wx, carry1 = (Tiles(ref, my, loads) for ref in (bx, zx, qx, wx, carry1))
     cond, invx = Rows(cond, pitch, loads), Rows(invx, pitch, loads)
     even_y = is_even("gy")
     ys = (pick(even_y, ny + 2, 0), pick(even_y, 0, ny + 2))
@@ -345,6 +353,12 @@
         return state
 
     over_planes(4, nx + 1, first, 0)
+
+
+def again_kernel(s, cond, bx, zx, qx, wx, vx, carry2, sums_ref):
+    loads, nx, my = s.loads, s.nx, s.my
+    bx, zx, qx, wx, vx, carry2 = (Tiles(ref, my, loads) for ref in (bx, zx, qx, wx, vx, carry2))
+    cond = Rows(cond, s.pitch, loads)
     element_planes(cond, carry2, 4, 1, 1, my - 3, wx, None)
 
     def second(a, count, sums):
@@ -360,7 +374,7 @@
 
 def outer_kernel(
     s, dens_ref, x1_ref, x2_ref,
-    cond1, invx1, bx1, zx1, qx1, wx1, carry1, carry2, sums1,
+    cond1, invx1, bx1, zx1, qx1, wx1, vx1, carry1, carry2, sums1,
     q_out, v_out, inv_out, sums_ref,
     low_ref, high_ref, cond2, invx2, bx2, zx2, qx2, wx2, vx2, carry3,
 ):
@@ -389,7 +403,7 @@
     cond, invx = joined_rows(cond2, cond1, outside), joined_rows(invx2, invx1, scaled_own)
     bx, zx = joined(bx2, bx1, outside), joined(zx2, zx1, scaled_own)
     qx, wx = joined(qx2, qx1, image_own), joined(wx2, wx1, image_own)
-    vx = joined(vx2, vx2, again_planes(nx))
+    vx = joined(vx2, vx1, again_planes(nx))
     carry1, carry2, carry3 = (Tiles(ref, my, loads) for ref in (carry1, carry2, carry3))
 
     def conduct(ref, base, x):
@@ -429,11 +443,11 @@
     element_planes(cond, carry3, 2, 2, 1, my - 3, wx, emitter)
     element_planes(cond, carry3, 4, 1, 1, my - 3, wx, emitter, keep=False)
     element_planes(cond, carry2, nx, 2, 1, my - 3, wx, emitter, keep=False)
-    for field, out, planes in ((qx, q_out, image_planes(nx)), (vx, v_out, again_planes(nx))):
+    for field, out in ((qx, q_out), (vx, v_out)):
         out = Tiles(out, ny, loads)
-        for place, x in enumerate(planes):
+        for x in range(nx):
             for y in range(ny):
-                out[place, y] = field[x, y + 2]
+                out[x, y] = field[x + 2, y + 2]
 
     lane = lane_ids(loads)
     load = lax.broadcasted_iota(jnp.int32, (loads, LANES), 0)
@@ -445,42 +459,24 @@
     sums_ref[...] = jnp.broadcast_to(row[None], sums_ref.shape)
 
 
-def image_planes(nx):
-    return (2, 3, nx + 1)
-
-
 def again_planes(nx):
     return (2, 3, 4, nx, nx + 1)
 
 
-def unpack_kernel(
-    s, q1_ref, q2_ref, v1_ref, v2_ref, inv1_ref, inv2_ref, qo_ref, vo_ref, io_ref, t_ref
-):
-    loads, nx, ny, my = s.loads, s.nx, s.ny, s.my
-    whole = Tiles(t_ref, ny, loads)
-    for first, second, planes, out in (
-        (q1_ref, q2_ref, image_planes(nx), qo_ref),
-        (v1_ref, v2_ref, again_planes(nx), vo_ref),
-    ):
-        first, second = Tiles(first, my, loads), Tiles(second, ny, loads)
-        for x in range(nx):
-            for y in range(ny):
-                if x + 2 in planes:
-                    whole[x, y] = second[planes.index(x + 2), y]
-                else:
-                    whole[x, y] = first[x + 2, y + 2]
-        for x0 in range(0, nx, SUB):
-            for block in range(packed_count(ny)):
+def unpack_kernel(s, q_ref, v_ref, inv1_ref, inv2_ref, qo_ref, vo_ref, io_ref):
+    loads, nx, ny = s.loads, s.nx, s.ny
+    for x0 in range(0, nx, SUB):
+        for block in range(packed_count(ny)):
+            lanes = slice(block * LANES, (block + 1) * LANES)
+            for ref, out in ((q_ref, qo_ref), (v_ref, vo_ref)):
                 for load in range(loads):
-                    out[load, x0 : x0 + SUB, block * LANES : (block + 1) * LANES] = pack_block(
-                        lambda y: t_ref[
+                    out[load, x0 : x0 + SUB, lanes] = pack_block(
+                        lambda y: ref[
                             pl.ds((x0 * ny + y) * loads + load, SUB, stride=ny * loads), :
                         ],
                         ny, block, SUB,
                     )
-    for x0 in range(0, nx, SUB):
-        for block in range(packed_count(ny)):
-            io_ref[x0 : x0 + SUB, block * LANES : (block + 1) * LANES] = pack_block(
+            io_ref[x0 : x0 + SUB, lanes] = pack_block(
                 lambda y: inv1_ref[
                     pl.ds((x0 + 2) * s.pitch + y + 2, SUB, stride=s.pitch), :
                 ],
@@ -557,33 +553,44 @@
         )
 
     hbm = pl.BlockSpec(memory_space=pltpu.HBM)
-    bt, dt, y1, y2 = call(
+    face = shape(s.y_rows, LANES)
+    bt, dt, y2 = call(
         pack_kernel,
-        (
-            shape(nodes, LANES),
-            shape(nx * ny, LANES),
-            shape(s.y_rows, LANES),
-            shape(s.y_rows, LANES),
-        ),
-    )(heat_source, density)
-    y2, y1 = swap(y2, "gy", 1), swap(y1, "gy", 0)
+        (shape(nodes, LANES), shape(nx * ny, LANES), face),
+        in_specs=[hbm, hbm],
+        scratch_shapes=[
+            scratch(loads, nx, flat),
+            scratch(nx, flat),
+            pltpu.SemaphoreType.DMA((loads + 1,)),
+        ],
+    )(
+        pltpu.with_memory_space_constraint(heat_source, pltpu.HBM),
+        pltpu.with_memory_space_constraint(density, pltpu.HBM),
+    )
+    y2 = swap(y2, "gy", 1)
+    y1 = swap(call(pack_near_kernel, face)(bt, dt), "gy", 0)
     dens, x1, x2 = call(
         pack_x_kernel,
         (shape(nx * s.pitch, LANES), shape(s.x_rows, LANES), shape(s.x_rows, LANES)),
         scratch_shapes=[scratch(4 * s.my * loads, LANES)],
-    )(bt, dt, y1, y2)
-    x1, x2 = swap(x1, "gx", 0), swap(x2, "gx", 1)
+    )(bt, dt, y2, y1)
+    x1 = swap(x1, "gx", 0)
     plane = s.my * loads
     rows, field = shape(s.mx * s.pitch, LANES), shape(s.mx * plane, LANES)
     edge = shape(2 * plane, LANES)
-    cond, inv_1, bx, zx, q_1, w_1, v_1, carry1, carry2, sums = call(
-        inner_kernel, (rows,) * 2 + (field,) * 5 + (edge,) * 2 + (shape(4 * loads, LANES),)
+    cond, inv_1, bx, zx, q_1, w_1, carry1 = call(
+        image_kernel, (rows,) * 2 + (field,) * 4 + (edge,)
     )(bt, dens, y1, y2)
-    q_2, v_2, inv_2, sums = call(
+    x2, w_1 = lax.optimization_barrier((x2, w_1))
+    x2 = swap(x2, "gx", 1)
+    v_1, carry2, sums = call(again_kernel, (field, edge, shape(4 * loads, LANES)))(
+        cond, bx, zx, q_1, w_1
+    )
+    q_t, v_t, inv_2, sums = call(
         outer_kernel,
         (
-            shape(len(image_planes(nx)) * ny * loads, LANES),
-            shape(len(again_planes(nx)) * ny * loads, LANES),
+            shape(nodes, LANES),
+            shape(nodes, LANES),
             shape(ny, LANES),
             shape(devices, 1, LANES),
         ),
@@ -591,14 +598,12 @@
         + [scratch(5 * s.pitch, LANES)] * 2
         + [scratch(5 * plane, LANES)] * 5
         + [scratch(2 * plane, LANES)],
-    )(dens, x1, x2, cond, inv_1, bx, zx, q_1, w_1, carry1, carry2, sums)
+    )(dens, x1, x2, cond, inv_1, bx, zx, q_1, w_1, v_1, carry1, carry2, sums)
     parts = lax.all_to_all(sums, ("gx", "gy"), 0, 0, tiled=True)
     whole = shape(loads, nx, flat)
-    image, again, inverse = call(
-        unpack_kernel,
-        (whole, whole, shape(nx, flat)),
-        scratch_shapes=[scratch(nodes, LANES)],
-    )(q_1, q_2, v_1, v_2, inv_1, inv_2)
+    image, again, inverse = call(unpack_kernel, (whole, whole, shape(nx, flat)))(
+        q_t, v_t, inv_1, inv_2
+    )
     return call(
         finish_kernel,
         (whole, whole),

time: 35.6 us -> 36.3 us (1.020)
  local copies, waits for them, and re-layouts: 3.32 us -> 0.01 us
  Pallas kernels: 6.94 us -> 8.71 us
  starting transfers between devices: 18.6 us -> 20.1 us
  waiting for transfers between devices: 5.73 us -> 6.55 us
    unnamed x10 -> x2, local copies, waits for them, and re-layouts: 3.32 us -> 0.01 us
    pallas_call x4 -> x6, Pallas kernels: 5.55 us -> 7.31 us  [the longest x1 1.97 us: per_device(): call(pack_kernel, (shape(nodes, LANES), shape(nx * ny, LANES), face), in_...]
    all_to_all x1, starting transfers between devices: 13.7 us -> 15.3 us  [per_device(): parts = lax.all_to_all(sums, ('gx', 'gy'), 0, 0, tiled=True)]
    all_to_all x1, waiting for transfers between devices: 5.41 us -> 6.23 us  [per_device(): parts = lax.all_to_all(sums, ('gx', 'gy'), 0, 0, tiled=True)]
where the time goes in v8:
time: 36.3 us; the launch traced here: 36.1 us
  starting transfers between devices  20.1 us (55%)
  Pallas kernels  8.71 us (24%)
  waiting for transfers between devices  6.55 us (18%)
  between operations  0.72 us (2%)
    all_to_all x1, starting transfers between devices, per_device(): parts = lax.all_to_all(sums, ('gx', 'gy'), 0, 0, tiled=True)  15.3 us
    all_to_all x1, waiting for transfers between devices, per_device(): parts = lax.all_to_all(sums, ('gx', 'gy'), 0, 0, tiled=True)  6.23 us
    ppermute x4, starting transfers between devices, swap(): return lax.ppermute(array, axis, pairs)  4.83 us
    pallas_call x1, Pallas kernels, per_device(): call(pack_kernel, (shape(nodes, LANES), shape(nx * ny, LANES), face), in_...  1.97 us
    pallas_call x1, Pallas kernels, per_device(): call(image_kernel, (rows,) * 2 + (field,) * 4 + (edge,))(bt, dens, y1, y2)  1.68 us
    pallas_call x1, Pallas kernels, per_device(): call(outer_kernel, (shape(nodes, LANES), shape(nodes, LANES), shape(ny, L...  1.51 us
    pallas_call x1, Pallas kernels, per_device(): call(again_kernel, (field, edge, shape(4 * loads, LANES)))  1.21 us
    pallas_call x1, Pallas kernels, per_device(): call(finish_kernel, (whole, whole), out_specs=(hbm, hbm), scratch_shapes=...  1.21 us
  transfers between devices with their start and end apart: 5, of which 2 were waited for; matrix products, arithmetic and copies ran while one was open for 0% of the time, Pallas kernels for 10%

profile of v8, /device:TPU:0, one launch (start us, length us, event | category | flops | bytes accessed | tf_op | source)
XLA Modules:
  0.0 36.1 jit_solution(2137796503773518663)
XLA Ops:
  0.6 2.0 %shard_map.41 = (f32[1024,128]{1,0:T(8,128)S(1)}, f32[128,128]{1,0:T(8,128)S(1)}, f32[240,128]{1,0:T(8,128)S(1)}) custom-call(f32[8,16,768]{2,1,0:T(8,128)} %b_ref.1, f32[16,768]{1,0:T(8,128)} %d_hbm.1), custom_call_target="tpu_custom_call" | custom-call | tf_op jit(solution)/shard_map/pallas_call | solution.py:557
  2.6 0.1 shard_map.42
  2.7 0.5 %collective-permute-start.1 = (f32[240,128]{1,0:T(8,128)S(1)}, f32[240,128]{1,0:T(8,128)S(1)}, u32[]{:S(2)}, u32[]{:S(2)}) collective-permute-start(f32[240,128]{1,0:T(8,128)S(1)} %shard_map.42), channel_id=1, source_target_pairs={{0,1},{1,0},{2,3},{3,2},{4,5},{5,4},{6,7},{7,6},{8,9},{9,8},{10,11... | collective-permute-start | bytes 368648 | tf_op jit(solution)/shard_map/ppermute | solution.py:533
  3.3 0.7 %collective-permute-start = (f32[240,128]{1,0:T(8,128)S(1)}, f32[240,128]{1,0:T(8,128)S(1)}, u32[]{:S(2)}, u32[]{:S(2)}) collective-permute-start(f32[240,128]{1,0:T(8,128)S(1)} %get-tuple-element.29), channel_id=1, source_target_pairs={{1,2},{2,1},{3,4},{4,3},{5,6},{6,5},{9,10},{10,9},{11,12},{12,11},... | collective-permute-start | bytes 368648 | tf_op jit(solution)/shard_map/ppermute | solution.py:533
  3.9 0.3 collective-permute-done.1.y1_ref
  4.2 0.0 collective-permute-done.y2_ref
  4.2 0.2 shard_map.43
  4.4 3.0 %collective-permute-start.2 = (f32[192,128]{1,0:T(8,128)S(1)}, f32[192,128]{1,0:T(8,128)S(1)}, u32[]{:S(2)}, u32[]{:S(2)}) collective-permute-start(f32[192,128]{1,0:T(8,128)S(1)} %get-tuple-element.31), channel_id=1, source_target_pairs={{0,8},{8,0},{16,24},{24,16},{1,9},{9,1},{17,25},{25,17},{2,10},{10... | collective-permute-start | bytes 294920 | tf_op jit(solution)/shard_map/ppermute | solution.py:533
  7.4 1.7 %shard_map.44 = (f32[320,128]{1,0:T(8,128)S(1)}, f32[320,128]{1,0:T(8,128)S(1)}, f32[1920,128]{1,0:T(8,128)S(1)}, f32[1920,128]{1,0:T(8,128)S(1)}, f32[1920,128]...) custom-call(f32[1024,128]{1,0:T(8,128)S(1)} %get-tuple-element.27.bt_ref, ...), custom_call_target="tpu_custom_call" | custom-call | tf_op jit(solution)/shard_map/pallas_call | solution.py:581
  9.1 0.7 %collective-permute-start.3 = (f32[192,128]{1,0:T(8,128)S(1)}, f32[192,128]{1,0:T(8,128)S(1)}, u32[]{:S(2)}, u32[]{:S(2)}) collective-permute-start(f32[192,128]{1,0:T(8,128)S(1)} %get-tuple-element.34), channel_id=1, source_target_pairs={{8,16},{16,8},{9,17},{17,9},{10,18},{18,10},{11,19},{19,11},{12,20... | collective-permute-start | bytes 294920 | tf_op jit(solution)/shard_map/ppermute | solution.py:533
  9.8 1.2 %shard_map.45 = (f32[1920,128]{1,0:T(8,128)S(1)}, f32[192,128]{1,0:T(8,128)S(1)}, f32[32,128]{1,0:T(8,128)S(1)}) custom-call(f32[320,128]{1,0:T(8,128)S(1)} %get-tuple-element.35.cond.cond1, f32[1920,128]{1,0:T(8,128)S(1)} %get-tuple-element.37.bx.bx1, f32[1920,128]{1,0:T(8,128)S(1)} %get-tuple-element.38.zx.zx1, f32[1920,128]{1,0:T(8,128)S(1)} %get-tuple-element.39.qx.qx1, ...), custom_call_target="tpu_custom_call" | custom-call | tf_op jit(solution)/shard_map/pallas_call | solution.py:586
  11.0 0.0 collective-permute-done.2.x1_ref
  11.0 0.0 collective-permute-done.3.x2_ref
  11.0 1.5 %shard_map.46 = (f32[1024,128]{1,0:T(8,128)S(1)}, f32[1024,128]{1,0:T(8,128)S(1)}, f32[8,128]{1,0:T(8,128)S(1)}, f32[32,1,128]{2,1,0:T(1,128)}) custom-call(f32[256,128]{1,0:T(8,128)S(1)} %get-tuple-element.30.dens_ref, f32[192,128]{1,0:T(8,128)S(1)} %collective-permute-done.2.x1_ref, f32[192,128]{1,0:T(8,128)S(1)} %collective-permute-done.3.x2_ref, ...), custom_call_target="tpu_custom_call" | custom-call | tf_op jit(solution)/shard_map/pallas_call | solution.py:589
  12.5 15.3 %all-to-all-start = ((f32[32,1,128]{2,1,0:T(1,128)}), f32[32,1,128]{2,1,0:T(1,128)S(1)}, u32[]{:S(2)}, u32[]{:S(2)}) async-start(f32[32,1,128]{2,1,0:T(1,128)} %get-tuple-element.45), calls=%async_computation | async-start | bytes 32768 | tf_op jit(solution)/shard_map/all_to_all | solution.py:602
  27.8 0.0 copy-start
  27.8 0.8 %shard_map.47 = (f32[8,16,768]{2,1,0:T(8,128)S(1)}, f32[8,16,768]{2,1,0:T(8,128)S(1)}, f32[16,768]{1,0:T(8,128)S(1)}) custom-call(f32[1024,128]{1,0:T(8,128)S(1)} %get-tuple-element.46.q_ref, f32[1024,128]{1,0:T(8,128)S(1)} %get-tuple-element.47.v_ref, f32[320,128]{1,0:T(8,128)S(1)} %get-tuple-element.36.invx1.inv1_ref, f32[8,128]{1,0:T(8,128)S(1)} %get-tuple-element.48.inv2_ref), custom_call_target="tpu_custom_call" | custom-call | tf_op jit(solution)/shard_map/pallas_call | solution.py:604
  28.7 6.2 %all-to-all-done.parts_ref = f32[32,1,128]{2,1,0:T(1,128)S(1)} async-done(((f32[32,1,128]{2,1,0:T(1,128)}), f32[32,1,128]{2,1,0:T(1,128)S(1)}, u32[]{:S(2)}, u32[]{:S(2)}) %all-to-all-start) | async-done | bytes 16416 | tf_op jit(solution)/shard_map/all_to_all | solution.py:602
  34.9 0.0 copy-done
  34.9 1.2 %shard_map.48 = (f32[8,16,768]{2,1,0:T(8,128)}, f32[8,16,768]{2,1,0:T(8,128)}) custom-call(f32[32,1,128]{2,1,0:T(1,128)S(1)} %all-to-all-done.parts_ref, f32[8,16,768]{2,1,0:T(8,128)S(1)} %copy-done, f32[8,16,768]{2,1,0:T(8,128)S(1)} %get-tuple-element.49.q_ref, f32[8,16,768]{2,1,0:T(8,128)S(1)} %get-tuple-element.50.v_ref, ...), custom_call_target="tpu_custom_call" | custom-call | tf_op jit(solution)/shard_map/pallas_call | solution.py:607
Async XLA Ops:
  2.7 1.5 %collective-permute-start.1 = (f32[240,128]{1,0:T(8,128)S(1)}, f32[240,128]{1,0:T(8,128)S(1)}, u32[]{:S(2)}, u32[]{:S(2)}) collective-permute-start(f32[240,128]{1,0:T(8,128)S(1)} %shard_map.42), channel_id=1, source_target_pairs={{0,1},{1,0},{2,3},{3,2},{4,5},{5,4},{6,7},{7,6},{8,9},{9,8},{10,11... | collective-permute-start | bytes 368648 | tf_op jit(solution)/shard_map/ppermute | solution.py:533
  3.3 1.0 %collective-permute-start = (f32[240,128]{1,0:T(8,128)S(1)}, f32[240,128]{1,0:T(8,128)S(1)}, u32[]{:S(2)}, u32[]{:S(2)}) collective-permute-start(f32[240,128]{1,0:T(8,128)S(1)} %get-tuple-element.29), channel_id=1, source_target_pairs={{1,2},{2,1},{3,4},{4,3},{5,6},{6,5},{9,10},{10,9},{11,12},{12,11},... | collective-permute-start | bytes 368648 | tf_op jit(solution)/shard_map/ppermute | solution.py:533
  4.4 6.6 %collective-permute-start.2 = (f32[192,128]{1,0:T(8,128)S(1)}, f32[192,128]{1,0:T(8,128)S(1)}, u32[]{:S(2)}, u32[]{:S(2)}) collective-permute-start(f32[192,128]{1,0:T(8,128)S(1)} %get-tuple-element.31), channel_id=1, source_target_pairs={{0,8},{8,0},{16,24},{24,16},{1,9},{9,1},{17,25},{25,17},{2,10},{10... | collective-permute-start | bytes 294920 | tf_op jit(solution)/shard_map/ppermute | solution.py:533
  9.1 1.9 %collective-permute-start.3 = (f32[192,128]{1,0:T(8,128)S(1)}, f32[192,128]{1,0:T(8,128)S(1)}, u32[]{:S(2)}, u32[]{:S(2)}) collective-permute-start(f32[192,128]{1,0:T(8,128)S(1)} %get-tuple-element.34), channel_id=1, source_target_pairs={{8,16},{16,8},{9,17},{17,9},{10,18},{18,10},{11,19},{19,11},{12,20... | collective-permute-start | bytes 294920 | tf_op jit(solution)/shard_map/ppermute | solution.py:533
  12.5 22.4 %all-to-all-start = ((f32[32,1,128]{2,1,0:T(1,128)}), f32[32,1,128]{2,1,0:T(1,128)S(1)}, u32[]{:S(2)}, u32[]{:S(2)}) async-start(f32[32,1,128]{2,1,0:T(1,128)} %get-tuple-element.45), calls=%async_computation | async-start | bytes 32768 | tf_op jit(solution)/shard_map/all_to_all | solution.py:602
  27.8 7.1 %copy-start = (f32[8,16,768]{2,1,0:T(8,128)S(1)}, f32[8,16,768]{2,1,0:T(8,128)}, u32[]{:S(2)}) copy-start(f32[8,16,768]{2,1,0:T(8,128)} %b_ref.1) | copy-start | bytes 1179652

commit v9 on v8

--- a/solution.py
+++ b/solution.py
@@ -66,8 +66,9 @@
 
 
 class Sizes:
-    def __init__(self, loads, nx, ny):
+    def __init__(self, loads, nx, ny, count_x, count_y):
         self.loads, self.nx, self.ny = loads, nx, ny
+        self.count_x, self.count_y = count_x, count_y
         self.mx, self.my = nx + 4, ny + 4
         self.pitch = -(-(ny + 6) // SUB) * SUB
         self.y_dens = packed_count(2 * nx) * loads
@@ -123,6 +124,13 @@
 
 def is_even(axis):
     return lax.rem(lax.axis_index(axis), 2) == 0
+
+
+def is_alone(axis, count, start):
+    place = lax.axis_index(axis)
+    last = (count - start) % 2
+    alone = place < start
+    return jnp.logical_or(alone, place == count - 1) if last else alone
 
 
 def pick(even, if_even, if_odd):
@@ -181,11 +189,14 @@
         dens_ref[at + 3 : at + 3 + ny, :] = dt_ref[x * ny : (x + 1) * ny, :]
         dens_ref[at + ny + 6 : at + pitch, :] = jnp.zeros((pitch - ny - 6, LANES), jnp.float32)
     for side, ref in enumerate((y1_ref, y2_ref)):
+        alone = is_alone("gy", s.count_y, side)
         for dy in range(3):
             for x0 in range(0, nx, SUB):
                 at = s.y_dens + dy * nx + x0
                 to = x0 * pitch + yd[side] + dy
-                dens_ref[pl.ds(to, SUB, stride=pitch), :] = ref[at : at + SUB, :]
+                dens_ref[pl.ds(to, SUB, stride=pitch), :] = jnp.where(
+                    alone, 0.0, ref[at : at + SUB, :]
+                )
     inner, edge = Tiles(bt_ref, ny, loads), Tiles(edge_ref, my, loads)
     for place, x in enumerate((0, 1, nx - 2, nx - 1)):
         for y in range(ny):
@@ -381,15 +392,20 @@
     loads, nx, ny, mx, my, pitch = s.loads, s.nx, s.ny, s.mx, s.my, s.pitch
     even_x = is_even("gx")
 
+    def take(into, ref, start):
+        into[: s.x_dens, :] = ref[: s.x_dens, :]
+        dens = ref[s.x_dens :, :]
+        into[s.x_dens :, :] = jnp.where(is_alone("gx", s.count_x, start), 0.0, dens)
+
     @pl.when(even_x)
     def _():
-        low_ref[...] = x2_ref[...]
-        high_ref[...] = x1_ref[...]
+        take(low_ref, x2_ref, 1)
+        take(high_ref, x1_ref, 0)
 
     @pl.when(jnp.logical_not(even_x))
     def _():
-        low_ref[...] = x1_ref[...]
-        high_ref[...] = x2_ref[...]
+        take(low_ref, x1_ref, 0)
+        take(high_ref, x2_ref, 1)
 
     def joined(first, second, own):
         return Joined(Tiles(first, my, loads), Tiles(second, my, loads), own)
@@ -527,16 +543,17 @@
 
 
 def swap(array, axis, start):
-    pairs = []
-    for i in range(start, lax.axis_size(axis) - 1, 2):
-        pairs += [(i, i + 1), (i + 1, i)]
-    return lax.ppermute(array, axis, pairs)
+    count = lax.axis_size(axis)
+    target = list(range(count))
+    for i in range(start, count - 1, 2):
+        target[i], target[i + 1] = i + 1, i
+    return lax.ppermute(array, axis, list(enumerate(target)))
 
 
 def per_device(heat_source, density):
     loads, nx, flat = heat_source.shape
     ny = flat // NZ
-    s = Sizes(loads, nx, ny)
+    s = Sizes(loads, nx, ny, lax.axis_size("gx"), lax.axis_size("gy"))
     nodes = nx * ny * loads
     devices = lax.axis_size("gx") * lax.axis_size("gy")
 

time: 36.3 us -> 36.3 us (level)
  no operation moved by 1% of the time
where the time goes in v9:
time: 36.3 us; the launch traced here: 36.1 us
  starting transfers between devices  20.1 us (55%)
  Pallas kernels  8.7 us (24%)
  waiting for transfers between devices  6.55 us (18%)
  between operations  0.72 us (2%)
    all_to_all x1, starting transfers between devices, per_device(): parts = lax.all_to_all(sums, ('gx', 'gy'), 0, 0, tiled=True)  15.3 us
    all_to_all x1, waiting for transfers between devices, per_device(): parts = lax.all_to_all(sums, ('gx', 'gy'), 0, 0, tiled=True)  6.23 us
    ppermute x4, starting transfers between devices, swap(): return lax.ppermute(array, axis, list(enumerate(target)))  4.84 us
    pallas_call x1, Pallas kernels, per_device(): call(pack_kernel, (shape(nodes, LANES), shape(nx * ny, LANES), face), in_...  1.97 us
    pallas_call x1, Pallas kernels, per_device(): call(image_kernel, (rows,) * 2 + (field,) * 4 + (edge,))(bt, dens, y1, y2)  1.68 us
    pallas_call x1, Pallas kernels, per_device(): call(outer_kernel, (shape(nodes, LANES), shape(nodes, LANES), shape(ny, L...  1.51 us
    pallas_call x1, Pallas kernels, per_device(): call(again_kernel, (field, edge, shape(4 * loads, LANES)))  1.21 us
    pallas_call x1, Pallas kernels, per_device(): call(finish_kernel, (whole, whole), out_specs=(hbm, hbm), scratch_shapes=...  1.21 us
  transfers between devices with their start and end apart: 5, of which 2 were waited for; matrix products, arithmetic and copies ran while one was open for 0% of the time, Pallas kernels for 10%

profile of v9, /device:TPU:0, one launch (start us, length us, event | category | flops | bytes accessed | tf_op | source)
XLA Modules:
  0.0 36.1 jit_solution(13468390840868958096)
XLA Ops:
  0.6 2.0 %shard_map.41 = (f32[1024,128]{1,0:T(8,128)S(1)}, f32[128,128]{1,0:T(8,128)S(1)}, f32[240,128]{1,0:T(8,128)S(1)}) custom-call(f32[8,16,768]{2,1,0:T(8,128)} %b_ref.1, f32[16,768]{1,0:T(8,128)} %d_hbm.1), custom_call_target="tpu_custom_call" | custom-call | tf_op jit(solution)/shard_map/pallas_call | solution.py:574
  2.6 0.1 shard_map.42
  2.7 0.5 %collective-permute-start.1 = (f32[240,128]{1,0:T(8,128)S(1)}, f32[240,128]{1,0:T(8,128)S(1)}, u32[]{:S(2)}, u32[]{:S(2)}) collective-permute-start(f32[240,128]{1,0:T(8,128)S(1)} %shard_map.42), channel_id=1, source_target_pairs={{0,1},{1,0},{2,3},{3,2},{4,5},{5,4},{6,7},{7,6},{8,9},{9,8},{10,11... | collective-permute-start | bytes 368648 | tf_op jit(solution)/shard_map/ppermute | solution.py:550
  3.3 0.7 %collective-permute-start = (f32[240,128]{1,0:T(8,128)S(1)}, f32[240,128]{1,0:T(8,128)S(1)}, u32[]{:S(2)}, u32[]{:S(2)}) collective-permute-start(f32[240,128]{1,0:T(8,128)S(1)} %get-tuple-element.29), channel_id=1, source_target_pairs={{0,0},{1,2},{2,1},{3,4},{4,3},{5,6},{6,5},{7,7},{8,8},{9,10},{10,9... | collective-permute-start | bytes 368648 | tf_op jit(solution)/shard_map/ppermute | solution.py:550
  3.9 0.3 collective-permute-done.1.y1_ref
  4.2 0.0 collective-permute-done.y2_ref
  4.2 0.2 shard_map.43
  4.4 3.0 %collective-permute-start.2 = (f32[192,128]{1,0:T(8,128)S(1)}, f32[192,128]{1,0:T(8,128)S(1)}, u32[]{:S(2)}, u32[]{:S(2)}) collective-permute-start(f32[192,128]{1,0:T(8,128)S(1)} %get-tuple-element.31), channel_id=1, source_target_pairs={{0,8},{8,0},{16,24},{24,16},{1,9},{9,1},{17,25},{25,17},{2,10},{10... | collective-permute-start | bytes 294920 | tf_op jit(solution)/shard_map/ppermute | solution.py:550
  7.4 1.7 %shard_map.44 = (f32[320,128]{1,0:T(8,128)S(1)}, f32[320,128]{1,0:T(8,128)S(1)}, f32[1920,128]{1,0:T(8,128)S(1)}, f32[1920,128]{1,0:T(8,128)S(1)}, f32[1920,128]...) custom-call(f32[1024,128]{1,0:T(8,128)S(1)} %get-tuple-element.27.bt_ref, ...), custom_call_target="tpu_custom_call" | custom-call | tf_op jit(solution)/shard_map/pallas_call | solution.py:598
  9.1 0.7 %collective-permute-start.3 = (f32[192,128]{1,0:T(8,128)S(1)}, f32[192,128]{1,0:T(8,128)S(1)}, u32[]{:S(2)}, u32[]{:S(2)}) collective-permute-start(f32[192,128]{1,0:T(8,128)S(1)} %get-tuple-element.34), channel_id=1, source_target_pairs={{0,0},{8,16},{16,8},{24,24},{1,1},{9,17},{17,9},{25,25},{2,2},{10,... | collective-permute-start | bytes 294920 | tf_op jit(solution)/shard_map/ppermute | solution.py:550
  9.8 1.2 %shard_map.45 = (f32[1920,128]{1,0:T(8,128)S(1)}, f32[192,128]{1,0:T(8,128)S(1)}, f32[32,128]{1,0:T(8,128)S(1)}) custom-call(f32[320,128]{1,0:T(8,128)S(1)} %get-tuple-element.35.cond.cond1, f32[1920,128]{1,0:T(8,128)S(1)} %get-tuple-element.37.bx.bx1, f32[1920,128]{1,0:T(8,128)S(1)} %get-tuple-element.38.zx.zx1, f32[1920,128]{1,0:T(8,128)S(1)} %get-tuple-element.39.qx.qx1, ...), custom_call_target="tpu_custom_call" | custom-call | tf_op jit(solution)/shard_map/pallas_call | solution.py:603
  11.0 0.0 collective-permute-done.2.x1_ref
  11.0 0.0 collective-permute-done.3.x2_ref
  11.0 1.5 %shard_map.46 = (f32[1024,128]{1,0:T(8,128)S(1)}, f32[1024,128]{1,0:T(8,128)S(1)}, f32[8,128]{1,0:T(8,128)S(1)}, f32[32,1,128]{2,1,0:T(1,128)}) custom-call(f32[256,128]{1,0:T(8,128)S(1)} %get-tuple-element.30.dens_ref, f32[192,128]{1,0:T(8,128)S(1)} %collective-permute-done.2.x1_ref, f32[192,128]{1,0:T(8,128)S(1)} %collective-permute-done.3.x2_ref, ...), custom_call_target="tpu_custom_call" | custom-call | tf_op jit(solution)/shard_map/pallas_call | solution.py:606
  12.5 15.3 %all-to-all-start = ((f32[32,1,128]{2,1,0:T(1,128)}), f32[32,1,128]{2,1,0:T(1,128)S(1)}, u32[]{:S(2)}, u32[]{:S(2)}) async-start(f32[32,1,128]{2,1,0:T(1,128)} %get-tuple-element.45), calls=%async_computation | async-start | bytes 32768 | tf_op jit(solution)/shard_map/all_to_all | solution.py:619
  27.8 0.0 copy-start
  27.8 0.8 %shard_map.47 = (f32[8,16,768]{2,1,0:T(8,128)S(1)}, f32[8,16,768]{2,1,0:T(8,128)S(1)}, f32[16,768]{1,0:T(8,128)S(1)}) custom-call(f32[1024,128]{1,0:T(8,128)S(1)} %get-tuple-element.46.q_ref, f32[1024,128]{1,0:T(8,128)S(1)} %get-tuple-element.47.v_ref, f32[320,128]{1,0:T(8,128)S(1)} %get-tuple-element.36.invx1.inv1_ref, f32[8,128]{1,0:T(8,128)S(1)} %get-tuple-element.48.inv2_ref), custom_call_target="tpu_custom_call" | custom-call | tf_op jit(solution)/shard_map/pallas_call | solution.py:621
  28.7 6.2 %all-to-all-done.parts_ref = f32[32,1,128]{2,1,0:T(1,128)S(1)} async-done(((f32[32,1,128]{2,1,0:T(1,128)}), f32[32,1,128]{2,1,0:T(1,128)S(1)}, u32[]{:S(2)}, u32[]{:S(2)}) %all-to-all-start) | async-done | bytes 16416 | tf_op jit(solution)/shard_map/all_to_all | solution.py:619
  34.9 0.0 copy-done
  34.9 1.2 %shard_map.48 = (f32[8,16,768]{2,1,0:T(8,128)}, f32[8,16,768]{2,1,0:T(8,128)}) custom-call(f32[32,1,128]{2,1,0:T(1,128)S(1)} %all-to-all-done.parts_ref, f32[8,16,768]{2,1,0:T(8,128)S(1)} %copy-done, f32[8,16,768]{2,1,0:T(8,128)S(1)} %get-tuple-element.49.q_ref, f32[8,16,768]{2,1,0:T(8,128)S(1)} %get-tuple-element.50.v_ref, ...), custom_call_target="tpu_custom_call" | custom-call | tf_op jit(solution)/shard_map/pallas_call | solution.py:624
Async XLA Ops:
  2.7 1.5 %collective-permute-start.1 = (f32[240,128]{1,0:T(8,128)S(1)}, f32[240,128]{1,0:T(8,128)S(1)}, u32[]{:S(2)}, u32[]{:S(2)}) collective-permute-start(f32[240,128]{1,0:T(8,128)S(1)} %shard_map.42), channel_id=1, source_target_pairs={{0,1},{1,0},{2,3},{3,2},{4,5},{5,4},{6,7},{7,6},{8,9},{9,8},{10,11... | collective-permute-start | bytes 368648 | tf_op jit(solution)/shard_map/ppermute | solution.py:550
  3.3 1.0 %collective-permute-start = (f32[240,128]{1,0:T(8,128)S(1)}, f32[240,128]{1,0:T(8,128)S(1)}, u32[]{:S(2)}, u32[]{:S(2)}) collective-permute-start(f32[240,128]{1,0:T(8,128)S(1)} %get-tuple-element.29), channel_id=1, source_target_pairs={{0,0},{1,2},{2,1},{3,4},{4,3},{5,6},{6,5},{7,7},{8,8},{9,10},{10,9... | collective-permute-start | bytes 368648 | tf_op jit(solution)/shard_map/ppermute | solution.py:550
  4.4 6.6 %collective-permute-start.2 = (f32[192,128]{1,0:T(8,128)S(1)}, f32[192,128]{1,0:T(8,128)S(1)}, u32[]{:S(2)}, u32[]{:S(2)}) collective-permute-start(f32[192,128]{1,0:T(8,128)S(1)} %get-tuple-element.31), channel_id=1, source_target_pairs={{0,8},{8,0},{16,24},{24,16},{1,9},{9,1},{17,25},{25,17},{2,10},{10... | collective-permute-start | bytes 294920 | tf_op jit(solution)/shard_map/ppermute | solution.py:550
  9.1 1.9 %collective-permute-start.3 = (f32[192,128]{1,0:T(8,128)S(1)}, f32[192,128]{1,0:T(8,128)S(1)}, u32[]{:S(2)}, u32[]{:S(2)}) collective-permute-start(f32[192,128]{1,0:T(8,128)S(1)} %get-tuple-element.34), channel_id=1, source_target_pairs={{0,0},{8,16},{16,8},{24,24},{1,1},{9,17},{17,9},{25,25},{2,2},{10,... | collective-permute-start | bytes 294920 | tf_op jit(solution)/shard_map/ppermute | solution.py:550
  12.5 22.4 %all-to-all-start = ((f32[32,1,128]{2,1,0:T(1,128)}), f32[32,1,128]{2,1,0:T(1,128)S(1)}, u32[]{:S(2)}, u32[]{:S(2)}) async-start(f32[32,1,128]{2,1,0:T(1,128)} %get-tuple-element.45), calls=%async_computation | async-start | bytes 32768 | tf_op jit(solution)/shard_map/all_to_all | solution.py:619
  27.8 7.1 %copy-start = (f32[8,16,768]{2,1,0:T(8,128)S(1)}, f32[8,16,768]{2,1,0:T(8,128)}, u32[]{:S(2)}) copy-start(f32[8,16,768]{2,1,0:T(8,128)} %b_ref.1) | copy-start | bytes 1179652

commit v10 on v8

--- a/solution.py
+++ b/solution.py
@@ -11,6 +11,21 @@
 KMIN = 0.001
 LANES = 128
 SUB = 8
+
+
+class Batch:
+    def __init__(self, size=12):
+        self.size, self.held = size, []
+
+    def add(self, into, at, tile):
+        self.held.append((into, at, tile))
+        if len(self.held) >= self.size:
+            self.flush()
+
+    def flush(self):
+        for into, at, tile in self.held:
+            into[at] = tile
+        self.held = []
 
 
 def packed_count(tiles):
@@ -51,18 +66,20 @@
 
 
 def pack_tiles(out_ref, at, rows, tiles, read_tile):
+    batch = Batch()
     for block in range(packed_count(tiles)):
-        out_ref[at + block * rows : at + (block + 1) * rows, :] = pack_block(
-            read_tile, tiles, block, rows
-        )
+        place = slice(at + block * rows, at + (block + 1) * rows), slice(None)
+        batch.add(out_ref, place, pack_block(read_tile, tiles, block, rows))
+    batch.flush()
 
 
 def unpack_tiles(ref, at, rows, tiles, write):
+    batch = Batch()
     for index in range(tiles):
-        write(
-            index,
-            unpack_tile(lambda t: ref[at + t * rows : at + (t + 1) * rows, :], index, rows),
-        )
+        tile = unpack_tile(lambda t: ref[at + t * rows : at + (t + 1) * rows, :], index, rows)
+        for store in write(index, tile):
+            batch.add(*store)
+    batch.flush()
 
 
 class Sizes:
@@ -139,19 +156,24 @@
     d_copy.start()
     for load in range(loads):
         copies[load].wait()
+        batch = Batch(16)
         for x0 in range(0, nx, SUB):
             for y in range(ny):
                 tile = unpack_tile(
                     lambda t: b_ref[load, x0 : x0 + SUB, t * LANES : (t + 1) * LANES], y, SUB
                 )
-                bt_ref[pl.ds((x0 * ny + y) * loads + load, SUB, stride=ny * loads), :] = tile
+                rows = pl.ds((x0 * ny + y) * loads + load, SUB, stride=ny * loads)
+                batch.add(bt_ref, (rows, slice(None)), tile)
+        batch.flush()
     d_copy.wait()
+    batch = Batch(16)
     for x0 in range(0, nx, SUB):
         for y in range(ny):
             tile = unpack_tile(
                 lambda t: d_ref[x0 : x0 + SUB, t * LANES : (t + 1) * LANES], y, SUB
             )
-            dt_ref[pl.ds(x0 * ny + y, SUB, stride=ny), :] = tile
+            batch.add(dt_ref, (pl.ds(x0 * ny + y, SUB, stride=ny), slice(None)), tile)
+    batch.flush()
     pack_face(s, jnp.logical_not(is_even("gy")), bt_ref, dt_ref, y2_ref)
 
 
@@ -165,10 +187,13 @@
     y0 = pick(upper, ny - 2, 0)
     pack_tiles(out_ref, 0, loads, 2 * nx, lambda i: tiles[i // 2, y0 + i % 2])
     y0 = pick(upper, ny - 3, 0)
+    batch = Batch()
     for dy in range(3):
         for x0 in range(0, nx, SUB):
             at = s.y_dens + dy * nx + x0
-            out_ref[at : at + SUB, :] = dt_ref[pl.ds(x0 * ny + y0 + dy, SUB, stride=ny), :]
+            tile = dt_ref[pl.ds(x0 * ny + y0 + dy, SUB, stride=ny), :]
+            batch.add(out_ref, (slice(at, at + SUB), slice(None)), tile)
+    batch.flush()
 
 
 def pack_x_kernel(s, bt_ref, dt_ref, y2_ref, y1_ref, dens_ref, x1_ref, x2_ref, edge_ref):
@@ -187,14 +212,17 @@
                 to = x0 * pitch + yd[side] + dy
                 dens_ref[pl.ds(to, SUB, stride=pitch), :] = ref[at : at + SUB, :]
     inner, edge = Tiles(bt_ref, ny, loads), Tiles(edge_ref, my, loads)
+    batch = Batch()
     for place, x in enumerate((0, 1, nx - 2, nx - 1)):
         for y in range(ny):
-            edge[place, y + 2] = inner[x, y]
+            batch.add(edge, (place, y + 2), inner[x, y])
         for side, ref in enumerate((y1_ref, y2_ref)):
             for dy in range(2):
-                edge[place, ys[side] + dy] = unpack_tile(
+                tile = unpack_tile(
                     lambda t: ref[t * loads : (t + 1) * loads, :], 2 * x + dy, loads
                 )
+                batch.add(edge, (place, ys[side] + dy), tile)
+    batch.flush()
     for ref, upper in ((x1_ref, even_x), (x2_ref, jnp.logical_not(even_x))):
         place = pick(upper, 2, 0)
         pack_tiles(ref, 0, loads, 2 * my, lambda i: edge[place + i // my, i % my])
@@ -315,12 +343,14 @@
     return state
 
 
-def image_kernel(
+def inner_kernel(
     s, bt_ref, dens_ref, y1_ref, y2_ref,
-    cond, invx, bx, zx, qx, wx, carry1,
+    cond, invx, bx, zx, qx, wx, vx, carry1, carry2, sums_ref,
 ):
     loads, nx, ny, my, pitch = s.loads, s.nx, s.ny, s.my, s.pitch
-    bx, zx, qx, wx, carry1 = (Tiles(ref, my, loads) for ref in (bx, zx, qx, wx, carry1))
+    bx, zx, qx, wx, vx, carry1, carry2 = (
+        Tiles(ref, my, loads) for ref in (bx, zx, qx, wx, vx, carry1, carry2)
+    )
     cond, invx = Rows(cond, pitch, loads), Rows(invx, pitch, loads)
     even_y = is_even("gy")
     ys = (pick(even_y, ny + 2, 0), pick(even_y, 0, ny + 2))
@@ -333,14 +363,18 @@
         before = after
 
     def stage(x, y, tile):
-        bx[x + 2, y] = tile
+        stores = [(bx, (x + 2, y), tile)]
         if x:
-            zx[x + 2, y] = tile * invx[x + 2, y]
+            stores.append((zx, (x + 2, y), tile * invx[x + 2, y]))
+        return stores
 
     inner = Tiles(bt_ref, ny, loads)
+    batch = Batch(16)
     for x in range(nx):
         for y in range(ny):
-            stage(x, y + 2, inner[x, y])
+            for store in stage(x, y + 2, inner[x, y]):
+                batch.add(*store)
+    batch.flush()
     for side, ref in enumerate((y1_ref, y2_ref)):
         unpack_tiles(
             ref, 0, loads, 2 * nx, lambda i, tile: stage(i // 2, ys[side] + i % 2, tile)
@@ -353,12 +387,6 @@
         return state
 
     over_planes(4, nx + 1, first, 0)
-
-
-def again_kernel(s, cond, bx, zx, qx, wx, vx, carry2, sums_ref):
-    loads, nx, my = s.loads, s.nx, s.my
-    bx, zx, qx, wx, vx, carry2 = (Tiles(ref, my, loads) for ref in (bx, zx, qx, wx, vx, carry2))
-    cond = Rows(cond, s.pitch, loads)
     element_planes(cond, carry2, 4, 1, 1, my - 3, wx, None)
 
     def second(a, count, sums):
@@ -425,12 +453,13 @@
 
         def write(i, tile):
             at = x0 + i // my, i % my
-            bx[at] = tile
-            zx[at] = tile * invx[at]
+            return [(bx, at, tile), (zx, at, tile * invx[at])]
 
         unpack_tiles(ref, 0, loads, 2 * my, write)
+    batch = Batch()
     for y in range(my):
-        zx[2, y] = bx[2, y] * invx[2, y]
+        batch.add(zx, (2, y), bx[2, y] * invx[2, y])
+    batch.flush()
 
     emitter = First(bx, invx, qx, wx)
     element_planes(cond, carry3, 0, 1, 0, my - 1, zx, None)
@@ -445,9 +474,11 @@
     element_planes(cond, carry2, nx, 2, 1, my - 3, wx, emitter, keep=False)
     for field, out in ((qx, q_out), (vx, v_out)):
         out = Tiles(out, ny, loads)
+        batch = Batch()
         for x in range(nx):
             for y in range(ny):
-                out[x, y] = field[x + 2, y + 2]
+                batch.add(out, (x, y), field[x + 2, y + 2])
+        batch.flush()
 
     lane = lane_ids(loads)
     load = lax.broadcasted_iota(jnp.int32, (loads, LANES), 0)
@@ -465,23 +496,29 @@
 
 def unpack_kernel(s, q_ref, v_ref, inv1_ref, inv2_ref, qo_ref, vo_ref, io_ref):
     loads, nx, ny = s.loads, s.nx, s.ny
+    batch = Batch()
     for x0 in range(0, nx, SUB):
-        for block in range(packed_count(ny)):
-            lanes = slice(block * LANES, (block + 1) * LANES)
-            for ref, out in ((q_ref, qo_ref), (v_ref, vo_ref)):
-                for load in range(loads):
-                    out[load, x0 : x0 + SUB, lanes] = pack_block(
+        for ref, out in ((q_ref, qo_ref), (v_ref, vo_ref)):
+            for load in range(loads):
+                for block in range(packed_count(ny)):
+                    tile = pack_block(
                         lambda y: ref[
                             pl.ds((x0 * ny + y) * loads + load, SUB, stride=ny * loads), :
                         ],
                         ny, block, SUB,
                     )
-            io_ref[x0 : x0 + SUB, lanes] = pack_block(
+                    lanes = slice(block * LANES, (block + 1) * LANES)
+                    batch.add(out, (load, slice(x0, x0 + SUB), lanes), tile)
+        for block in range(packed_count(ny)):
+            tile = pack_block(
                 lambda y: inv1_ref[
                     pl.ds((x0 + 2) * s.pitch + y + 2, SUB, stride=s.pitch), :
                 ],
                 ny, block, SUB,
             )
+            lanes = slice(block * LANES, (block + 1) * LANES)
+            batch.add(io_ref, (slice(x0, x0 + SUB), lanes), tile)
+    batch.flush()
     for block in range(packed_count(ny)):
         io_ref[0:1, block * LANES : (block + 1) * LANES] = pack_block(
             lambda y: inv2_ref[y : y + 1, :], ny, block, 1
@@ -574,18 +611,13 @@
         (shape(nx * s.pitch, LANES), shape(s.x_rows, LANES), shape(s.x_rows, LANES)),
         scratch_shapes=[scratch(4 * s.my * loads, LANES)],
     )(bt, dt, y2, y1)
-    x1 = swap(x1, "gx", 0)
+    x1, x2 = swap(x1, "gx", 0), swap(x2, "gx", 1)
     plane = s.my * loads
     rows, field = shape(s.mx * s.pitch, LANES), shape(s.mx * plane, LANES)
     edge = shape(2 * plane, LANES)
-    cond, inv_1, bx, zx, q_1, w_1, carry1 = call(
-        image_kernel, (rows,) * 2 + (field,) * 4 + (edge,)
+    cond, inv_1, bx, zx, q_1, w_1, v_1, carry1, carry2, sums = call(
+        inner_kernel, (rows,) * 2 + (field,) * 5 + (edge,) * 2 + (shape(4 * loads, LANES),)
     )(bt, dens, y1, y2)
-    x2, w_1 = lax.optimization_barrier((x2, w_1))
-    x2 = swap(x2, "gx", 1)
-    v_1, carry2, sums = call(again_kernel, (field, edge, shape(4 * loads, LANES)))(
-        cond, bx, zx, q_1, w_1
-    )
     q_t, v_t, inv_2, sums = call(
         outer_kernel,
         (

time: 36.3 us -> 34.5 us (0.950)
  starting transfers between devices: 20.1 us -> 18.6 us
  Pallas kernels: 8.71 us -> 8.26 us
    all_to_all x1, starting transfers between devices: 15.3 us -> 13.7 us  [per_device(): parts = lax.all_to_all(sums, ('gx', 'gy'), 0, 0, tiled=True)]
    pallas_call x2 -> x1, Pallas kernels: 2.89 us -> 2.77 us  [per_device(): call(inner_kernel, (rows,) * 2 + (field,) * 5 + (edge,) * 2 + (shape(4 *...]
where the time goes in v10:
time: 34.5 us; the launch traced here: 34.3 us
  starting transfers between devices  18.6 us (54%)
  Pallas kernels  8.26 us (24%)
  waiting for transfers between devices  6.76 us (20%)
  between operations  0.7 us (2%)
    all_to_all x1, starting transfers between devices, per_device(): parts = lax.all_to_all(sums, ('gx', 'gy'), 0, 0, tiled=True)  13.7 us
    all_to_all x1, waiting for transfers between devices, per_device(): parts = lax.all_to_all(sums, ('gx', 'gy'), 0, 0, tiled=True)  6.44 us
    ppermute x4, starting transfers between devices, swap(): return lax.ppermute(array, axis, pairs)  4.83 us
    pallas_call x1, Pallas kernels, per_device(): call(inner_kernel, (rows,) * 2 + (field,) * 5 + (edge,) * 2 + (shape(4 *...  2.77 us
    pallas_call x1, Pallas kernels, per_device(): call(pack_kernel, (shape(nodes, LANES), shape(nx * ny, LANES), face), in_...  1.9 us
    pallas_call x1, Pallas kernels, per_device(): call(outer_kernel, (shape(nodes, LANES), shape(nodes, LANES), shape(ny, L...  1.48 us
    pallas_call x1, Pallas kernels, per_device(): call(finish_kernel, (whole, whole), out_specs=(hbm, hbm), scratch_shapes=...  1.21 us
  transfers between devices with their start and end apart: 5, of which 2 were waited for; matrix products, arithmetic and copies ran while one was open for 0% of the time, Pallas kernels for 10%

profile of v10, /device:TPU:0, one launch (start us, length us, event | category | flops | bytes accessed | tf_op | source)
XLA Modules:
  0.0 34.3 jit_solution(3526464977127303315)
XLA Ops:
  0.6 1.9 %shard_map.41 = (f32[1024,128]{1,0:T(8,128)S(1)}, f32[128,128]{1,0:T(8,128)S(1)}, f32[240,128]{1,0:T(8,128)S(1)}) custom-call(f32[8,16,768]{2,1,0:T(8,128)} %b_ref.1, f32[16,768]{1,0:T(8,128)} %d_hbm.1), custom_call_target="tpu_custom_call" | custom-call | tf_op jit(solution)/shard_map/pallas_call | solution.py:594
  2.5 0.1 shard_map.42
  2.7 0.5 %collective-permute-start.1 = (f32[240,128]{1,0:T(8,128)S(1)}, f32[240,128]{1,0:T(8,128)S(1)}, u32[]{:S(2)}, u32[]{:S(2)}) collective-permute-start(f32[240,128]{1,0:T(8,128)S(1)} %shard_map.42), channel_id=1, source_target_pairs={{0,1},{1,0},{2,3},{3,2},{4,5},{5,4},{6,7},{7,6},{8,9},{9,8},{10,11... | collective-permute-start | bytes 368648 | tf_op jit(solution)/shard_map/ppermute | solution.py:570
  3.2 0.7 %collective-permute-start = (f32[240,128]{1,0:T(8,128)S(1)}, f32[240,128]{1,0:T(8,128)S(1)}, u32[]{:S(2)}, u32[]{:S(2)}) collective-permute-start(f32[240,128]{1,0:T(8,128)S(1)} %get-tuple-element.27), channel_id=1, source_target_pairs={{1,2},{2,1},{3,4},{4,3},{5,6},{6,5},{9,10},{10,9},{11,12},{12,11},... | collective-permute-start | bytes 368648 | tf_op jit(solution)/shard_map/ppermute | solution.py:570
  3.8 0.3 collective-permute-done.1.y1_ref
  4.1 0.0 collective-permute-done.y2_ref
  4.2 0.2 shard_map.43
  4.3 3.0 %collective-permute-start.2 = (f32[192,128]{1,0:T(8,128)S(1)}, f32[192,128]{1,0:T(8,128)S(1)}, u32[]{:S(2)}, u32[]{:S(2)}) collective-permute-start(f32[192,128]{1,0:T(8,128)S(1)} %get-tuple-element.29), channel_id=1, source_target_pairs={{0,8},{8,0},{16,24},{24,16},{1,9},{9,1},{17,25},{25,17},{2,10},{10... | collective-permute-start | bytes 294920 | tf_op jit(solution)/shard_map/ppermute | solution.py:570
  7.3 0.7 %collective-permute-start.3 = (f32[192,128]{1,0:T(8,128)S(1)}, f32[192,128]{1,0:T(8,128)S(1)}, u32[]{:S(2)}, u32[]{:S(2)}) collective-permute-start(f32[192,128]{1,0:T(8,128)S(1)} %get-tuple-element.30), channel_id=1, source_target_pairs={{8,16},{16,8},{9,17},{17,9},{10,18},{18,10},{11,19},{19,11},{12,20... | collective-permute-start | bytes 294920 | tf_op jit(solution)/shard_map/ppermute | solution.py:570
  8.0 2.8 %shard_map.44 = (f32[320,128]{1,0:T(8,128)S(1)}, f32[320,128]{1,0:T(8,128)S(1)}, f32[1920,128]{1,0:T(8,128)S(1)}, f32[1920,128]{1,0:T(8,128)S(1)}, f32[1920,128]...) custom-call(f32[1024,128]{1,0:T(8,128)S(1)} %get-tuple-element.25.bt, ...), custom_call_target="tpu_custom_call" | custom-call | tf_op jit(solution)/shard_map/pallas_call | solution.py:618
  10.8 0.0 collective-permute-done.2.x1_ref
  10.8 0.0 collective-permute-done.3.x2_ref
  10.8 1.5 %shard_map.45 = (f32[1024,128]{1,0:T(8,128)S(1)}, f32[1024,128]{1,0:T(8,128)S(1)}, f32[8,128]{1,0:T(8,128)S(1)}, f32[32,1,128]{2,1,0:T(1,128)}) custom-call(f32[256,128]{1,0:T(8,128)S(1)} %get-tuple-element.28.dens_ref, f32[192,128]{1,0:T(8,128)S(1)} %collective-permute-done.2.x1_ref, f32[192,128]{1,0:T(8,128)S(1)} %collective-permute-done.3.x2_ref, ...), custom_call_target="tpu_custom_call" | custom-call | tf_op jit(solution)/shard_map/pallas_call | solution.py:621
  12.3 13.7 %all-to-all-start = ((f32[32,1,128]{2,1,0:T(1,128)}), f32[32,1,128]{2,1,0:T(1,128)S(1)}, u32[]{:S(2)}, u32[]{:S(2)}) async-start(f32[32,1,128]{2,1,0:T(1,128)} %get-tuple-element.41), calls=%async_computation | async-start | bytes 32768 | tf_op jit(solution)/shard_map/all_to_all | solution.py:634
  26.0 0.0 copy-start
  26.0 0.6 %shard_map.46 = (f32[8,16,768]{2,1,0:T(8,128)S(1)}, f32[8,16,768]{2,1,0:T(8,128)S(1)}, f32[16,768]{1,0:T(8,128)S(1)}) custom-call(f32[1024,128]{1,0:T(8,128)S(1)} %get-tuple-element.42.q_ref, f32[1024,128]{1,0:T(8,128)S(1)} %get-tuple-element.43.v_ref, f32[320,128]{1,0:T(8,128)S(1)} %get-tuple-element.32.invx1.inv1_ref, f32[8,128]{1,0:T(8,128)S(1)} %get-tuple-element.44.inv2_ref), custom_call_target="tpu_custom_call" | custom-call | tf_op jit(solution)/shard_map/pallas_call | solution.py:636
  26.6 6.4 %all-to-all-done.parts_ref = f32[32,1,128]{2,1,0:T(1,128)S(1)} async-done(((f32[32,1,128]{2,1,0:T(1,128)}), f32[32,1,128]{2,1,0:T(1,128)S(1)}, u32[]{:S(2)}, u32[]{:S(2)}) %all-to-all-start) | async-done | bytes 16416 | tf_op jit(solution)/shard_map/all_to_all | solution.py:634
  33.1 0.0 copy-done
  33.1 1.2 %shard_map.47 = (f32[8,16,768]{2,1,0:T(8,128)}, f32[8,16,768]{2,1,0:T(8,128)}) custom-call(f32[32,1,128]{2,1,0:T(1,128)S(1)} %all-to-all-done.parts_ref, f32[8,16,768]{2,1,0:T(8,128)S(1)} %copy-done, f32[8,16,768]{2,1,0:T(8,128)S(1)} %get-tuple-element.45.q_ref, f32[8,16,768]{2,1,0:T(8,128)S(1)} %get-tuple-element.46.v_ref, ...), custom_call_target="tpu_custom_call" | custom-call | tf_op jit(solution)/shard_map/pallas_call | solution.py:639
Async XLA Ops:
  2.7 1.5 %collective-permute-start.1 = (f32[240,128]{1,0:T(8,128)S(1)}, f32[240,128]{1,0:T(8,128)S(1)}, u32[]{:S(2)}, u32[]{:S(2)}) collective-permute-start(f32[240,128]{1,0:T(8,128)S(1)} %shard_map.42), channel_id=1, source_target_pairs={{0,1},{1,0},{2,3},{3,2},{4,5},{5,4},{6,7},{7,6},{8,9},{9,8},{10,11... | collective-permute-start | bytes 368648 | tf_op jit(solution)/shard_map/ppermute | solution.py:570
  3.2 1.0 %collective-permute-start = (f32[240,128]{1,0:T(8,128)S(1)}, f32[240,128]{1,0:T(8,128)S(1)}, u32[]{:S(2)}, u32[]{:S(2)}) collective-permute-start(f32[240,128]{1,0:T(8,128)S(1)} %get-tuple-element.27), channel_id=1, source_target_pairs={{1,2},{2,1},{3,4},{4,3},{5,6},{6,5},{9,10},{10,9},{11,12},{12,11},... | collective-permute-start | bytes 368648 | tf_op jit(solution)/shard_map/ppermute | solution.py:570
  4.3 6.4 %collective-permute-start.2 = (f32[192,128]{1,0:T(8,128)S(1)}, f32[192,128]{1,0:T(8,128)S(1)}, u32[]{:S(2)}, u32[]{:S(2)}) collective-permute-start(f32[192,128]{1,0:T(8,128)S(1)} %get-tuple-element.29), channel_id=1, source_target_pairs={{0,8},{8,0},{16,24},{24,16},{1,9},{9,1},{17,25},{25,17},{2,10},{10... | collective-permute-start | bytes 294920 | tf_op jit(solution)/shard_map/ppermute | solution.py:570
  7.3 3.5 %collective-permute-start.3 = (f32[192,128]{1,0:T(8,128)S(1)}, f32[192,128]{1,0:T(8,128)S(1)}, u32[]{:S(2)}, u32[]{:S(2)}) collective-permute-start(f32[192,128]{1,0:T(8,128)S(1)} %get-tuple-element.30), channel_id=1, source_target_pairs={{8,16},{16,8},{9,17},{17,9},{10,18},{18,10},{11,19},{19,11},{12,20... | collective-permute-start | bytes 294920 | tf_op jit(solution)/shard_map/ppermute | solution.py:570
  12.3 20.8 %all-to-all-start = ((f32[32,1,128]{2,1,0:T(1,128)}), f32[32,1,128]{2,1,0:T(1,128)S(1)}, u32[]{:S(2)}, u32[]{:S(2)}) async-start(f32[32,1,128]{2,1,0:T(1,128)} %get-tuple-element.41), calls=%async_computation | async-start | bytes 32768 | tf_op jit(solution)/shard_map/all_to_all | solution.py:634
  26.0 7.1 %copy-start = (f32[8,16,768]{2,1,0:T(8,128)S(1)}, f32[8,16,768]{2,1,0:T(8,128)}, u32[]{:S(2)}) copy-start(f32[8,16,768]{2,1,0:T(8,128)} %b_ref.1) | copy-start | bytes 1179652

commit v11 on v10

--- a/solution.py
+++ b/solution.py
@@ -148,14 +148,27 @@
 
 def pack_kernel(s, b_hbm, d_hbm, bt_ref, dt_ref, y2_ref, b_ref, d_ref, sems):
     loads, nx, ny = s.loads, s.nx, s.ny
-    d_copy = pltpu.make_async_copy(d_hbm, d_ref, sems.at[loads])
+    d_copy = pltpu.make_async_copy(d_hbm, d_ref, sems.at[0])
+    d_copy.start()
+    parts = 2 if loads % 2 == 0 else 1
+    each = loads // parts
     copies = []
+    for part in range(parts):
+        some = pl.ds(part * each, each)
+        copies.append(pltpu.make_async_copy(b_hbm.at[some], b_ref.at[some], sems.at[part + 1]))
+        copies[-1].start()
+    d_copy.wait()
+    batch = Batch(16)
+    for x0 in range(0, nx, SUB):
+        for y in range(ny):
+            tile = unpack_tile(
+                lambda t: d_ref[x0 : x0 + SUB, t * LANES : (t + 1) * LANES], y, SUB
+            )
+            batch.add(dt_ref, (pl.ds(x0 * ny + y, SUB, stride=ny), slice(None)), tile)
+    batch.flush()
     for load in range(loads):
-        copies.append(pltpu.make_async_copy(b_hbm.at[load], b_ref.at[load], sems.at[load]))
-        copies[-1].start()
-    d_copy.start()
-    for load in range(loads):
-        copies[load].wait()
+        if load % each == 0:
+            copies[load // each].wait()
         batch = Batch(16)
         for x0 in range(0, nx, SUB):
             for y in range(ny):
@@ -165,15 +178,6 @@
                 rows = pl.ds((x0 * ny + y) * loads + load, SUB, stride=ny * loads)
                 batch.add(bt_ref, (rows, slice(None)), tile)
         batch.flush()
-    d_copy.wait()
-    batch = Batch(16)
-    for x0 in range(0, nx, SUB):
-        for y in range(ny):
-            tile = unpack_tile(
-                lambda t: d_ref[x0 : x0 + SUB, t * LANES : (t + 1) * LANES], y, SUB
-            )
-            batch.add(dt_ref, (pl.ds(x0 * ny + y, SUB, stride=ny), slice(None)), tile)
-    batch.flush()
     pack_face(s, jnp.logical_not(is_even("gy")), bt_ref, dt_ref, y2_ref)
 
 
@@ -196,7 +200,21 @@
     batch.flush()
 
 
-def pack_x_kernel(s, bt_ref, dt_ref, y2_ref, y1_ref, dens_ref, x1_ref, x2_ref, edge_ref):
+def open_y_kernel(s, y_ref, t_ref):
+    tiles = Tiles(t_ref, 2, s.loads)
+    unpack_tiles(
+        y_ref, 0, s.loads, 2 * s.nx, lambda i, tile: [(tiles, (i // 2, i % 2), tile)]
+    )
+
+
+def open_x_kernel(s, x_ref, t_ref):
+    tiles = Tiles(t_ref, s.my, s.loads)
+    unpack_tiles(
+        x_ref, 0, s.loads, 2 * s.my, lambda i, tile: [(tiles, (i // s.my, i % s.my), tile)]
+    )
+
+
+def pack_x_kernel(s, bt_ref, dt_ref, y2_ref, t2_ref, y1_ref, dens_ref, x1_ref, x2_ref, edge_ref):
     loads, nx, ny, my, pitch = s.loads, s.nx, s.ny, s.my, s.pitch
     even_x, even_y = is_even("gx"), is_even("gy")
     ys = (pick(even_y, ny + 2, 0), pick(even_y, 0, ny + 2))
@@ -212,16 +230,17 @@
                 to = x0 * pitch + yd[side] + dy
                 dens_ref[pl.ds(to, SUB, stride=pitch), :] = ref[at : at + SUB, :]
     inner, edge = Tiles(bt_ref, ny, loads), Tiles(edge_ref, my, loads)
+    far = Tiles(t2_ref, 2, loads)
     batch = Batch()
     for place, x in enumerate((0, 1, nx - 2, nx - 1)):
         for y in range(ny):
             batch.add(edge, (place, y + 2), inner[x, y])
-        for side, ref in enumerate((y1_ref, y2_ref)):
-            for dy in range(2):
-                tile = unpack_tile(
-                    lambda t: ref[t * loads : (t + 1) * loads, :], 2 * x + dy, loads
-                )
-                batch.add(edge, (place, ys[side] + dy), tile)
+        for dy in range(2):
+            tile = unpack_tile(
+                lambda t: y1_ref[t * loads : (t + 1) * loads, :], 2 * x + dy, loads
+            )
+            batch.add(edge, (place, ys[0] + dy), tile)
+            batch.add(edge, (place, ys[1] + dy), far[x, dy])
     batch.flush()
     for ref, upper in ((x1_ref, even_x), (x2_ref, jnp.logical_not(even_x))):
         place = pick(upper, 2, 0)
@@ -344,7 +363,7 @@
 
 
 def inner_kernel(
-    s, bt_ref, dens_ref, y1_ref, y2_ref,
+    s, bt_ref, dens_ref, y1_ref, t2_ref,
     cond, invx, bx, zx, qx, wx, vx, carry1, carry2, sums_ref,
 ):
     loads, nx, ny, my, pitch = s.loads, s.nx, s.ny, s.my, s.pitch
@@ -375,10 +394,16 @@
             for store in stage(x, y + 2, inner[x, y]):
                 batch.add(*store)
     batch.flush()
-    for side, ref in enumerate((y1_ref, y2_ref)):
-        unpack_tiles(
-            ref, 0, loads, 2 * nx, lambda i, tile: stage(i // 2, ys[side] + i % 2, tile)
-        )
+    unpack_tiles(
+        y1_ref, 0, loads, 2 * nx, lambda i, tile: stage(i // 2, ys[0] + i % 2, tile)
+    )
+    far = Tiles(t2_ref, 2, loads)
+    batch = Batch(16)
+    for x in range(nx):
+        for dy in range(2):
+            for store in stage(x, ys[1] + dy, far[x, dy]):
+                batch.add(*store)
+    batch.flush()
 
     element_planes(cond, carry1, 3, 1, 0, my - 1, zx, None)
 
@@ -401,23 +426,32 @@
 
 
 def outer_kernel(
-    s, dens_ref, x1_ref, x2_ref,
+    s, dens_ref, x1_ref, x2_ref, t2_ref,
     cond1, invx1, bx1, zx1, qx1, wx1, vx1, carry1, carry2, sums1,
     q_out, v_out, inv_out, sums_ref,
-    low_ref, high_ref, cond2, invx2, bx2, zx2, qx2, wx2, vx2, carry3,
+    low_ref, high_ref, low_d, high_d, cond2, invx2, bx2, zx2, qx2, wx2, vx2, carry3,
 ):
     loads, nx, ny, mx, my, pitch = s.loads, s.nx, s.ny, s.mx, s.my, s.pitch
     even_x = is_even("gx")
 
+    def take(near, far):
+        near_t, near_d = near
+        far_t, far_d = far
+        unpack_tiles(
+            x1_ref, 0, loads, 2 * my,
+            lambda i, tile: [(Tiles(near_t, my, loads), (i // my, i % my), tile)],
+        )
+        far_t[...] = t2_ref[...]
+        near_d[...] = x1_ref[s.x_dens :, :]
+        far_d[...] = x2_ref[s.x_dens :, :]
+
     @pl.when(even_x)
     def _():
-        low_ref[...] = x2_ref[...]
-        high_ref[...] = x1_ref[...]
+        take((high_ref, high_d), (low_ref, low_d))
 
     @pl.when(jnp.logical_not(even_x))
     def _():
-        low_ref[...] = x1_ref[...]
-        high_ref[...] = x2_ref[...]
+        take((low_ref, low_d), (high_ref, high_d))
 
     def joined(first, second, own):
         return Joined(Tiles(first, my, loads), Tiles(second, my, loads), own)
@@ -434,11 +468,11 @@
     vx = joined(vx2, vx1, again_planes(nx))
     carry1, carry2, carry3 = (Tiles(ref, my, loads) for ref in (carry1, carry2, carry3))
 
-    def conduct(ref, base, x):
-        return conduct_of(ref[base + x * pitch : base + (x + 1) * pitch, :])
-
-    low = [conduct(low_ref, s.x_dens, t) for t in range(3)] + [conduct(dens_ref, 0, 0)]
-    high = [conduct(dens_ref, 0, nx - 1)] + [conduct(high_ref, s.x_dens, t) for t in range(2)]
+    def conduct(ref, x):
+        return conduct_of(ref[x * pitch : (x + 1) * pitch, :])
+
+    low = [conduct(low_d, t) for t in range(3)] + [conduct(dens_ref, 0)]
+    high = [conduct(dens_ref, nx - 1)] + [conduct(high_d, t) for t in range(2)]
     for x in range(3):
         inverse = inverse_of(s, low[x], low[x + 1])
         invx.put(x, inverse)
@@ -449,14 +483,14 @@
         invx.put(nx + 2 + x, inverse_of(s, high[x], high[x + 1]))
     cond.put(nx + 2, high[1][1:])
 
+    batch = Batch(16)
     for ref, x0 in ((low_ref, 0), (high_ref, nx + 2)):
-
-        def write(i, tile):
-            at = x0 + i // my, i % my
-            return [(bx, at, tile), (zx, at, tile * invx[at])]
-
-        unpack_tiles(ref, 0, loads, 2 * my, write)
-    batch = Batch()
+        tiles = Tiles(ref, my, loads)
+        for dx in range(2):
+            for y in range(my):
+                tile = tiles[dx, y]
+                batch.add(bx, (x0 + dx, y), tile)
+                batch.add(zx, (x0 + dx, y), tile * invx[x0 + dx, y])
     for y in range(my):
         batch.add(zx, (2, y), bx[2, y] * invx[2, y])
     batch.flush()
@@ -598,7 +632,7 @@
         scratch_shapes=[
             scratch(loads, nx, flat),
             scratch(nx, flat),
-            pltpu.SemaphoreType.DMA((loads + 1,)),
+            pltpu.SemaphoreType.DMA((3,)),
         ],
     )(
         pltpu.with_memory_space_constraint(heat_source, pltpu.HBM),
@@ -606,18 +640,20 @@
     )
     y2 = swap(y2, "gy", 1)
     y1 = swap(call(pack_near_kernel, face)(bt, dt), "gy", 0)
+    t2 = call(open_y_kernel, shape(2 * nx * loads, LANES))(y2)
     dens, x1, x2 = call(
         pack_x_kernel,
         (shape(nx * s.pitch, LANES), shape(s.x_rows, LANES), shape(s.x_rows, LANES)),
         scratch_shapes=[scratch(4 * s.my * loads, LANES)],
-    )(bt, dt, y2, y1)
+    )(bt, dt, y2, t2, y1)
     x1, x2 = swap(x1, "gx", 0), swap(x2, "gx", 1)
     plane = s.my * loads
     rows, field = shape(s.mx * s.pitch, LANES), shape(s.mx * plane, LANES)
     edge = shape(2 * plane, LANES)
     cond, inv_1, bx, zx, q_1, w_1, v_1, carry1, carry2, sums = call(
         inner_kernel, (rows,) * 2 + (field,) * 5 + (edge,) * 2 + (shape(4 * loads, LANES),)
-    )(bt, dens, y1, y2)
+    )(bt, dens, y1, t2)
+    xt2 = call(open_x_kernel, shape(2 * plane, LANES))(x2)
     q_t, v_t, inv_2, sums = call(
         outer_kernel,
         (
@@ -626,11 +662,12 @@
             shape(ny, LANES),
             shape(devices, 1, LANES),
         ),
-        scratch_shapes=[scratch(s.x_rows, LANES)] * 2
+        scratch_shapes=[scratch(2 * plane, LANES)] * 2
+        + [scratch(3 * s.pitch, LANES)] * 2
         + [scratch(5 * s.pitch, LANES)] * 2
         + [scratch(5 * plane, LANES)] * 5
         + [scratch(2 * plane, LANES)],
-    )(dens, x1, x2, cond, inv_1, bx, zx, q_1, w_1, v_1, carry1, carry2, sums)
+    )(dens, x1, x2, xt2, cond, inv_1, bx, zx, q_1, w_1, v_1, carry1, carry2, sums)
     parts = lax.all_to_all(sums, ("gx", "gy"), 0, 0, tiled=True)
     whole = shape(loads, nx, flat)
     image, again, inverse = call(unpack_kernel, (whole, whole, shape(nx, flat)))(

time: 34.5 us -> 33.4 us (0.968)
  starting transfers between devices: 18.6 us -> 17 us
  waiting for transfers between devices: 6.76 us -> 7.31 us
    all_to_all x1, starting transfers between devices: 13.7 us -> 6.87 us  [per_device(): parts = lax.all_to_all(sums, ('gx', 'gy'), 0, 0, tiled=True)]
    ppermute x4, starting transfers between devices: 4.83 us -> 10.2 us  [swap(): return lax.ppermute(array, axis, pairs)]
    ppermute x4, waiting for transfers between devices: 0.32 us -> 0.87 us  [swap(): return lax.ppermute(array, axis, pairs)]
  transfers between devices with their start and end apart: 5 -> 5, of which waited for: 2 -> 2; matrix products, arithmetic and copies ran while one was open for 0% -> 0% of each run, Pallas kernels for 10% -> 11%
where the time goes in v11:
time: 33.4 us; the launch traced here: 33.2 us
  starting transfers between devices  17 us (51%)
  Pallas kernels  8.14 us (24%)
  waiting for transfers between devices  7.31 us (22%)
  between operations  0.72 us (2%)
    ppermute x4, starting transfers between devices, swap(): return lax.ppermute(array, axis, pairs)  10.2 us
    all_to_all x1, starting transfers between devices, per_device(): parts = lax.all_to_all(sums, ('gx', 'gy'), 0, 0, tiled=True)  6.87 us
    all_to_all x1, waiting for transfers between devices, per_device(): parts = lax.all_to_all(sums, ('gx', 'gy'), 0, 0, tiled=True)  6.44 us
    pallas_call x1, Pallas kernels, per_device(): call(inner_kernel, (rows,) * 2 + (field,) * 5 + (edge,) * 2 + (shape(4 *...  2.78 us
    pallas_call x1, Pallas kernels, per_device(): call(pack_kernel, (shape(nodes, LANES), shape(nx * ny, LANES), face), in_...  1.56 us
    pallas_call x1, Pallas kernels, per_device(): call(outer_kernel, (shape(nodes, LANES), shape(nodes, LANES), shape(ny, L...  1.51 us
    pallas_call x1, Pallas kernels, per_device(): call(finish_kernel, (whole, whole), out_specs=(hbm, hbm), scratch_shapes=...  1.21 us
    ppermute x4, waiting for transfers between devices, swap(): return lax.ppermute(array, axis, pairs)  0.87 us
  transfers between devices with their start and end apart: 5, of which 2 were waited for; matrix products, arithmetic and copies ran while one was open for 0% of the time, Pallas kernels for 11%

profile of v11, /device:TPU:0, one launch (start us, length us, event | category | flops | bytes accessed | tf_op | source)
XLA Modules:
  0.0 33.2 jit_solution(10191458918369032518)
XLA Ops:
  0.6 1.6 %shard_map.41 = (f32[1024,128]{1,0:T(8,128)S(1)}, f32[128,128]{1,0:T(8,128)S(1)}, f32[240,128]{1,0:T(8,128)S(1)}) custom-call(f32[8,16,768]{2,1,0:T(8,128)} %b_ref.1, f32[16,768]{1,0:T(8,128)} %d_hbm.1), custom_call_target="tpu_custom_call" | custom-call | tf_op jit(solution)/shard_map/pallas_call | solution.py:628
  2.2 0.7 %collective-permute-start = (f32[240,128]{1,0:T(8,128)S(1)}, f32[240,128]{1,0:T(8,128)S(1)}, u32[]{:S(2)}, u32[]{:S(2)}) collective-permute-start(f32[240,128]{1,0:T(8,128)S(1)} %get-tuple-element.27), channel_id=1, source_target_pairs={{1,2},{2,1},{3,4},{4,3},{5,6},{6,5},{9,10},{10,9},{11,12},{12,11},... | collective-permute-start | bytes 368648 | tf_op jit(solution)/shard_map/ppermute | solution.py:604
  2.9 0.1 shard_map.43
  3.0 4.4 %collective-permute-start.1 = (f32[240,128]{1,0:T(8,128)S(1)}, f32[240,128]{1,0:T(8,128)S(1)}, u32[]{:S(2)}, u32[]{:S(2)}) collective-permute-start(f32[240,128]{1,0:T(8,128)S(1)} %shard_map.43), channel_id=1, source_target_pairs={{0,1},{1,0},{2,3},{3,2},{4,5},{5,4},{6,7},{7,6},{8,9},{9,8},{10,11... | collective-permute-start | bytes 368648 | tf_op jit(solution)/shard_map/ppermute | solution.py:604
  7.3 0.0 collective-permute-done.y_ref.y2_ref
  7.3 0.1 shard_map.42.t2_ref
  7.5 0.9 %collective-permute-done.1.y1_ref = f32[240,128]{1,0:T(8,128)S(1)} collective-permute-done((f32[240,128]{1,0:T(8,128)S(1)}, f32[240,128]{1,0:T(8,128)S(1)}, u32[]{:S(2)}, u32[]{:S(2)}) %collective-permute-start.1) | collective-permute-done | bytes 122912 | tf_op jit(solution)/shard_map/ppermute | solution.py:604
  8.3 0.2 shard_map.44
  8.5 0.7 %collective-permute-start.3 = (f32[192,128]{1,0:T(8,128)S(1)}, f32[192,128]{1,0:T(8,128)S(1)}, u32[]{:S(2)}, u32[]{:S(2)}) collective-permute-start(f32[192,128]{1,0:T(8,128)S(1)} %get-tuple-element.30), channel_id=1, source_target_pairs={{8,16},{16,8},{9,17},{17,9},{10,18},{18,10},{11,19},{19,11},{12,20... | collective-permute-start | bytes 294920 | tf_op jit(solution)/shard_map/ppermute | solution.py:604
  9.2 4.5 %collective-permute-start.2 = (f32[192,128]{1,0:T(8,128)S(1)}, f32[192,128]{1,0:T(8,128)S(1)}, u32[]{:S(2)}, u32[]{:S(2)}) collective-permute-start(f32[192,128]{1,0:T(8,128)S(1)} %get-tuple-element.29), channel_id=1, source_target_pairs={{0,8},{8,0},{16,24},{24,16},{1,9},{9,1},{17,25},{25,17},{2,10},{10... | collective-permute-start | bytes 294920 | tf_op jit(solution)/shard_map/ppermute | solution.py:604
  13.6 2.8 %shard_map.46 = (f32[320,128]{1,0:T(8,128)S(1)}, f32[320,128]{1,0:T(8,128)S(1)}, f32[1920,128]{1,0:T(8,128)S(1)}, f32[1920,128]{1,0:T(8,128)S(1)}, f32[1920,128]...) custom-call(f32[1024,128]{1,0:T(8,128)S(1)} %get-tuple-element.25.bt, ...), custom_call_target="tpu_custom_call" | custom-call | tf_op jit(solution)/shard_map/pallas_call | solution.py:653
  16.4 0.0 collective-permute-done.3.x_ref.x2_ref
  16.4 0.1 shard_map.45.t2_ref
  16.5 0.0 collective-permute-done.2.x1_ref
  16.5 1.5 %shard_map.47 = (f32[1024,128]{1,0:T(8,128)S(1)}, f32[1024,128]{1,0:T(8,128)S(1)}, f32[8,128]{1,0:T(8,128)S(1)}, f32[32,1,128]{2,1,0:T(1,128)}) custom-call(f32[256,128]{1,0:T(8,128)S(1)} %get-tuple-element.28.dens_ref, f32[192,128]{1,0:T(8,128)S(1)} %collective-permute-done.2.x1_ref, f32[192,128]{1,0:T(8,128)S(1)} %collective-permute-done.3.x_ref.x2_ref, ...), custom_call_target="tpu_custom_call" | custom-call | tf_op jit(solution)/shard_map/pallas_call | solution.py:657
  18.0 6.9 %all-to-all-start = ((f32[32,1,128]{2,1,0:T(1,128)}), f32[32,1,128]{2,1,0:T(1,128)S(1)}, u32[]{:S(2)}, u32[]{:S(2)}) async-start(f32[32,1,128]{2,1,0:T(1,128)} %get-tuple-element.41), calls=%async_computation | async-start | bytes 32768 | tf_op jit(solution)/shard_map/all_to_all | solution.py:671
  24.9 0.0 copy-start
  24.9 0.6 %shard_map.48 = (f32[8,16,768]{2,1,0:T(8,128)S(1)}, f32[8,16,768]{2,1,0:T(8,128)S(1)}, f32[16,768]{1,0:T(8,128)S(1)}) custom-call(f32[1024,128]{1,0:T(8,128)S(1)} %get-tuple-element.42.q_ref, f32[1024,128]{1,0:T(8,128)S(1)} %get-tuple-element.43.v_ref, f32[320,128]{1,0:T(8,128)S(1)} %get-tuple-element.32.invx1.inv1_ref, f32[8,128]{1,0:T(8,128)S(1)} %get-tuple-element.44.inv2_ref), custom_call_target="tpu_custom_call" | custom-call | tf_op jit(solution)/shard_map/pallas_call | solution.py:673
  25.5 6.4 %all-to-all-done.parts_ref = f32[32,1,128]{2,1,0:T(1,128)S(1)} async-done(((f32[32,1,128]{2,1,0:T(1,128)}), f32[32,1,128]{2,1,0:T(1,128)S(1)}, u32[]{:S(2)}, u32[]{:S(2)}) %all-to-all-start) | async-done | bytes 16416 | tf_op jit(solution)/shard_map/all_to_all | solution.py:671
  32.0 0.0 copy-done
  32.0 1.2 %shard_map.49 = (f32[8,16,768]{2,1,0:T(8,128)}, f32[8,16,768]{2,1,0:T(8,128)}) custom-call(f32[32,1,128]{2,1,0:T(1,128)S(1)} %all-to-all-done.parts_ref, f32[8,16,768]{2,1,0:T(8,128)S(1)} %copy-done, f32[8,16,768]{2,1,0:T(8,128)S(1)} %get-tuple-element.45.q_ref, f32[8,16,768]{2,1,0:T(8,128)S(1)} %get-tuple-element.46.v_ref, ...), custom_call_target="tpu_custom_call" | custom-call | tf_op jit(solution)/shard_map/pallas_call | solution.py:676
Async XLA Ops:
  2.2 5.1 %collective-permute-start = (f32[240,128]{1,0:T(8,128)S(1)}, f32[240,128]{1,0:T(8,128)S(1)}, u32[]{:S(2)}, u32[]{:S(2)}) collective-permute-start(f32[240,128]{1,0:T(8,128)S(1)} %get-tuple-element.27), channel_id=1, source_target_pairs={{1,2},{2,1},{3,4},{4,3},{5,6},{6,5},{9,10},{10,9},{11,12},{12,11},... | collective-permute-start | bytes 368648 | tf_op jit(solution)/shard_map/ppermute | solution.py:604
  3.0 5.3 %collective-permute-start.1 = (f32[240,128]{1,0:T(8,128)S(1)}, f32[240,128]{1,0:T(8,128)S(1)}, u32[]{:S(2)}, u32[]{:S(2)}) collective-permute-start(f32[240,128]{1,0:T(8,128)S(1)} %shard_map.43), channel_id=1, source_target_pairs={{0,1},{1,0},{2,3},{3,2},{4,5},{5,4},{6,7},{7,6},{8,9},{9,8},{10,11... | collective-permute-start | bytes 368648 | tf_op jit(solution)/shard_map/ppermute | solution.py:604
  8.5 7.9 %collective-permute-start.3 = (f32[192,128]{1,0:T(8,128)S(1)}, f32[192,128]{1,0:T(8,128)S(1)}, u32[]{:S(2)}, u32[]{:S(2)}) collective-permute-start(f32[192,128]{1,0:T(8,128)S(1)} %get-tuple-element.30), channel_id=1, source_target_pairs={{8,16},{16,8},{9,17},{17,9},{10,18},{18,10},{11,19},{19,11},{12,20... | collective-permute-start | bytes 294920 | tf_op jit(solution)/shard_map/ppermute | solution.py:604
  9.2 7.4 %collective-permute-start.2 = (f32[192,128]{1,0:T(8,128)S(1)}, f32[192,128]{1,0:T(8,128)S(1)}, u32[]{:S(2)}, u32[]{:S(2)}) collective-permute-start(f32[192,128]{1,0:T(8,128)S(1)} %get-tuple-element.29), channel_id=1, source_target_pairs={{0,8},{8,0},{16,24},{24,16},{1,9},{9,1},{17,25},{25,17},{2,10},{10... | collective-permute-start | bytes 294920 | tf_op jit(solution)/shard_map/ppermute | solution.py:604
  18.0 13.9 %all-to-all-start = ((f32[32,1,128]{2,1,0:T(1,128)}), f32[32,1,128]{2,1,0:T(1,128)S(1)}, u32[]{:S(2)}, u32[]{:S(2)}) async-start(f32[32,1,128]{2,1,0:T(1,128)} %get-tuple-element.41), calls=%async_computation | async-start | bytes 32768 | tf_op jit(solution)/shard_map/all_to_all | solution.py:671
  24.9 7.1 %copy-start = (f32[8,16,768]{2,1,0:T(8,128)S(1)}, f32[8,16,768]{2,1,0:T(8,128)}, u32[]{:S(2)}) copy-start(f32[8,16,768]{2,1,0:T(8,128)} %b_ref.1) | copy-start | bytes 1179652

commit v12 on v11

--- a/solution.py
+++ b/solution.py
@@ -83,8 +83,9 @@
 
 
 class Sizes:
-    def __init__(self, loads, nx, ny):
+    def __init__(self, loads, nx, ny, count_x, count_y):
         self.loads, self.nx, self.ny = loads, nx, ny
+        self.count_x, self.count_y = count_x, count_y
         self.mx, self.my = nx + 4, ny + 4
         self.pitch = -(-(ny + 6) // SUB) * SUB
         self.y_dens = packed_count(2 * nx) * loads
@@ -140,6 +141,13 @@
 
 def is_even(axis):
     return lax.rem(lax.axis_index(axis), 2) == 0
+
+
+def is_alone(axis, count, start):
+    place = lax.axis_index(axis)
+    last = (count - start) % 2
+    alone = place < start
+    return jnp.logical_or(alone, place == count - 1) if last else alone
 
 
 def pick(even, if_even, if_odd):
@@ -224,11 +232,14 @@
         dens_ref[at + 3 : at + 3 + ny, :] = dt_ref[x * ny : (x + 1) * ny, :]
         dens_ref[at + ny + 6 : at + pitch, :] = jnp.zeros((pitch - ny - 6, LANES), jnp.float32)
     for side, ref in enumerate((y1_ref, y2_ref)):
+        alone = is_alone("gy", s.count_y, side)
         for dy in range(3):
             for x0 in range(0, nx, SUB):
                 at = s.y_dens + dy * nx + x0
                 to = x0 * pitch + yd[side] + dy
-                dens_ref[pl.ds(to, SUB, stride=pitch), :] = ref[at : at + SUB, :]
+                dens_ref[pl.ds(to, SUB, stride=pitch), :] = jnp.where(
+                    alone, 0.0, ref[at : at + SUB, :]
+                )
     inner, edge = Tiles(bt_ref, ny, loads), Tiles(edge_ref, my, loads)
     far = Tiles(t2_ref, 2, loads)
     batch = Batch()
@@ -442,8 +453,9 @@
             lambda i, tile: [(Tiles(near_t, my, loads), (i // my, i % my), tile)],
         )
         far_t[...] = t2_ref[...]
-        near_d[...] = x1_ref[s.x_dens :, :]
-        far_d[...] = x2_ref[s.x_dens :, :]
+        for into, ref, start in ((near_d, x1_ref, 0), (far_d, x2_ref, 1)):
+            alone = is_alone("gx", s.count_x, start)
+            into[...] = jnp.where(alone, 0.0, ref[s.x_dens :, :])
 
     @pl.when(even_x)
     def _():
@@ -598,16 +610,20 @@
 
 
 def swap(array, axis, start):
-    pairs = []
-    for i in range(start, lax.axis_size(axis) - 1, 2):
-        pairs += [(i, i + 1), (i + 1, i)]
-    return lax.ppermute(array, axis, pairs)
+    count = lax.axis_size(axis)
+    target = list(range(count))
+    for i in range(start, count - 1, 2):
+        target[i], target[i + 1] = i + 1, i
+    ends = [i for i in range(count) if target[i] == i]
+    if len(ends) == 2:
+        target[ends[0]], target[ends[1]] = ends[1], ends[0]
+    return lax.ppermute(array, axis, list(enumerate(target)))
 
 
 def per_device(heat_source, density):
     loads, nx, flat = heat_source.shape
     ny = flat // NZ
-    s = Sizes(loads, nx, ny)
+    s = Sizes(loads, nx, ny, lax.axis_size("gx"), lax.axis_size("gy"))
     nodes = nx * ny * loads
     devices = lax.axis_size("gx") * lax.axis_size("gy")
 

time: 33.4 us -> 33 us (0.988)
  starting transfers between devices: 17 us -> 13 us
  waiting for transfers between devices: 7.31 us -> 11 us
    ppermute x4, waiting for transfers between devices: 0.87 us -> 4.6 us  [swap(): return lax.ppermute(array, axis, list(enumerate(target)))]
    all_to_all x1, starting transfers between devices: 6.87 us -> 4.34 us  [per_device(): parts = lax.all_to_all(sums, ('gx', 'gy'), 0, 0, tiled=True)]
    ppermute x4, starting transfers between devices: 10.2 us -> 8.62 us  [swap(): return lax.ppermute(array, axis, list(enumerate(target)))]
  transfers between devices with their start and end apart: 5 -> 5, of which waited for: 2 -> 3; matrix products, arithmetic and copies ran while one was open for 0% -> 0% of each run, Pallas kernels for 11% -> 11%
where the time goes in v12:
time: 33 us; the launch traced here: 32.8 us
  starting transfers between devices  13 us (39%)
  waiting for transfers between devices  11 us (33%)
  Pallas kernels  8.11 us (25%)
  between operations  0.72 us (2%)
    ppermute x4, starting transfers between devices, swap(): return lax.ppermute(array, axis, list(enumerate(target)))  8.62 us
    all_to_all x1, waiting for transfers between devices, per_device(): parts = lax.all_to_all(sums, ('gx', 'gy'), 0, 0, tiled=True)  6.44 us
    ppermute x4, waiting for transfers between devices, swap(): return lax.ppermute(array, axis, list(enumerate(target)))  4.6 us
    all_to_all x1, starting transfers between devices, per_device(): parts = lax.all_to_all(sums, ('gx', 'gy'), 0, 0, tiled=True)  4.34 us
    pallas_call x1, Pallas kernels, per_device(): call(inner_kernel, (rows,) * 2 + (field,) * 5 + (edge,) * 2 + (shape(4 *...  2.78 us
    pallas_call x1, Pallas kernels, per_device(): call(pack_kernel, (shape(nodes, LANES), shape(nx * ny, LANES), face), in_...  1.56 us
    pallas_call x1, Pallas kernels, per_device(): call(outer_kernel, (shape(nodes, LANES), shape(nodes, LANES), shape(ny, L...  1.49 us
    pallas_call x1, Pallas kernels, per_device(): call(finish_kernel, (whole, whole), out_specs=(hbm, hbm), scratch_shapes=...  1.21 us
  transfers between devices with their start and end apart: 5, of which 3 were waited for; matrix products, arithmetic and copies ran while one was open for 0% of the time, Pallas kernels for 11%

profile of v12, /device:TPU:0, one launch (start us, length us, event | category | flops | bytes accessed | tf_op | source)
XLA Modules:
  0.0 32.8 jit_solution(3475991342847863950)
XLA Ops:
  0.6 1.6 %shard_map.41 = (f32[1024,128]{1,0:T(8,128)S(1)}, f32[128,128]{1,0:T(8,128)S(1)}, f32[240,128]{1,0:T(8,128)S(1)}) custom-call(f32[8,16,768]{2,1,0:T(8,128)} %b_ref.1, f32[16,768]{1,0:T(8,128)} %d_hbm.1), custom_call_target="tpu_custom_call" | custom-call | tf_op jit(solution)/shard_map/pallas_call | solution.py:644
  2.2 3.4 %collective-permute-start = (f32[240,128]{1,0:T(8,128)S(1)}, f32[240,128]{1,0:T(8,128)S(1)}, u32[]{:S(2)}, u32[]{:S(2)}) collective-permute-start(f32[240,128]{1,0:T(8,128)S(1)} %get-tuple-element.27), channel_id=1, source_target_pairs={{0,7},{1,2},{2,1},{3,4},{4,3},{5,6},{6,5},{7,0},{8,15},{9,10},{10,... | collective-permute-start | bytes 368648 | tf_op jit(solution)/shard_map/ppermute | solution.py:620
  5.6 0.1 shard_map.43
  5.7 0.1 collective-permute-start.1
  5.8 2.9 %collective-permute-done.y_ref.y2_ref = f32[240,128]{1,0:T(8,128)S(1)} collective-permute-done((f32[240,128]{1,0:T(8,128)S(1)}, f32[240,128]{1,0:T(8,128)S(1)}, u32[]{:S(2)}, u32[]{:S(2)}) %collective-permute-start) | collective-permute-done | bytes 122912 | tf_op jit(solution)/shard_map/ppermute | solution.py:620
  8.6 0.1 shard_map.42.t2_ref
  8.8 0.0 collective-permute-done.1.y1_ref
  8.8 0.2 shard_map.44
  8.9 5.1 %collective-permute-start.3 = (f32[192,128]{1,0:T(8,128)S(1)}, f32[192,128]{1,0:T(8,128)S(1)}, u32[]{:S(2)}, u32[]{:S(2)}) collective-permute-start(f32[192,128]{1,0:T(8,128)S(1)} %get-tuple-element.30), channel_id=1, source_target_pairs={{0,24},{8,16},{16,8},{24,0},{1,25},{9,17},{17,9},{25,1},{2,26},{10... | collective-permute-start | bytes 294920 | tf_op jit(solution)/shard_map/ppermute | solution.py:620
  14.1 0.0 collective-permute-start.2
  14.1 2.8 %shard_map.46 = (f32[320,128]{1,0:T(8,128)S(1)}, f32[320,128]{1,0:T(8,128)S(1)}, f32[1920,128]{1,0:T(8,128)S(1)}, f32[1920,128]{1,0:T(8,128)S(1)}, f32[1920,128]...) custom-call(f32[1024,128]{1,0:T(8,128)S(1)} %get-tuple-element.25.bt, ...), custom_call_target="tpu_custom_call" | custom-call | tf_op jit(solution)/shard_map/pallas_call | solution.py:669
  16.9 0.0 collective-permute-done.3.x_ref.x2_ref
  16.9 0.1 shard_map.45.t2_ref
  17.0 1.7 %collective-permute-done.2.x1_ref = f32[192,128]{1,0:T(8,128)S(1)} collective-permute-done((f32[192,128]{1,0:T(8,128)S(1)}, f32[192,128]{1,0:T(8,128)S(1)}, u32[]{:S(2)}, u32[]{:S(2)}) %collective-permute-start.2) | collective-permute-done | bytes 98336 | tf_op jit(solution)/shard_map/ppermute | solution.py:620
  18.7 1.5 %shard_map.47 = (f32[1024,128]{1,0:T(8,128)S(1)}, f32[1024,128]{1,0:T(8,128)S(1)}, f32[8,128]{1,0:T(8,128)S(1)}, f32[32,1,128]{2,1,0:T(1,128)}) custom-call(f32[256,128]{1,0:T(8,128)S(1)} %get-tuple-element.28.dens_ref, f32[192,128]{1,0:T(8,128)S(1)} %collective-permute-done.2.x1_ref, f32[192,128]{1,0:T(8,128)S(1)} %collective-permute-done.3.x_ref.x2_ref, ...), custom_call_target="tpu_custom_call" | custom-call | tf_op jit(solution)/shard_map/pallas_call | solution.py:673
  20.2 4.3 %all-to-all-start = ((f32[32,1,128]{2,1,0:T(1,128)}), f32[32,1,128]{2,1,0:T(1,128)S(1)}, u32[]{:S(2)}, u32[]{:S(2)}) async-start(f32[32,1,128]{2,1,0:T(1,128)} %get-tuple-element.41), calls=%async_computation | async-start | bytes 32768 | tf_op jit(solution)/shard_map/all_to_all | solution.py:687
  24.5 0.0 copy-start
  24.6 0.6 %shard_map.48 = (f32[8,16,768]{2,1,0:T(8,128)S(1)}, f32[8,16,768]{2,1,0:T(8,128)S(1)}, f32[16,768]{1,0:T(8,128)S(1)}) custom-call(f32[1024,128]{1,0:T(8,128)S(1)} %get-tuple-element.42.q_ref, f32[1024,128]{1,0:T(8,128)S(1)} %get-tuple-element.43.v_ref, f32[320,128]{1,0:T(8,128)S(1)} %get-tuple-element.32.invx1.inv1_ref, f32[8,128]{1,0:T(8,128)S(1)} %get-tuple-element.44.inv2_ref), custom_call_target="tpu_custom_call" | custom-call | tf_op jit(solution)/shard_map/pallas_call | solution.py:689
  25.2 6.4 %all-to-all-done.parts_ref = f32[32,1,128]{2,1,0:T(1,128)S(1)} async-done(((f32[32,1,128]{2,1,0:T(1,128)}), f32[32,1,128]{2,1,0:T(1,128)S(1)}, u32[]{:S(2)}, u32[]{:S(2)}) %all-to-all-start) | async-done | bytes 16416 | tf_op jit(solution)/shard_map/all_to_all | solution.py:687
  31.6 0.0 copy-done
  31.6 1.2 %shard_map.49 = (f32[8,16,768]{2,1,0:T(8,128)}, f32[8,16,768]{2,1,0:T(8,128)}) custom-call(f32[32,1,128]{2,1,0:T(1,128)S(1)} %all-to-all-done.parts_ref, f32[8,16,768]{2,1,0:T(8,128)S(1)} %copy-done, f32[8,16,768]{2,1,0:T(8,128)S(1)} %get-tuple-element.45.q_ref, f32[8,16,768]{2,1,0:T(8,128)S(1)} %get-tuple-element.46.v_ref, ...), custom_call_target="tpu_custom_call" | custom-call | tf_op jit(solution)/shard_map/pallas_call | solution.py:692
Async XLA Ops:
  2.2 6.4 %collective-permute-start = (f32[240,128]{1,0:T(8,128)S(1)}, f32[240,128]{1,0:T(8,128)S(1)}, u32[]{:S(2)}, u32[]{:S(2)}) collective-permute-start(f32[240,128]{1,0:T(8,128)S(1)} %get-tuple-element.27), channel_id=1, source_target_pairs={{0,7},{1,2},{2,1},{3,4},{4,3},{5,6},{6,5},{7,0},{8,15},{9,10},{10,... | collective-permute-start | bytes 368648 | tf_op jit(solution)/shard_map/ppermute | solution.py:620
  5.7 3.1 %collective-permute-start.1 = (f32[240,128]{1,0:T(8,128)S(1)}, f32[240,128]{1,0:T(8,128)S(1)}, u32[]{:S(2)}, u32[]{:S(2)}) collective-permute-start(f32[240,128]{1,0:T(8,128)S(1)} %shard_map.43), channel_id=1, source_target_pairs={{0,1},{1,0},{2,3},{3,2},{4,5},{5,4},{6,7},{7,6},{8,9},{9,8},{10,11... | collective-permute-start | bytes 368648 | tf_op jit(solution)/shard_map/ppermute | solution.py:620
  8.9 7.9 %collective-permute-start.3 = (f32[192,128]{1,0:T(8,128)S(1)}, f32[192,128]{1,0:T(8,128)S(1)}, u32[]{:S(2)}, u32[]{:S(2)}) collective-permute-start(f32[192,128]{1,0:T(8,128)S(1)} %get-tuple-element.30), channel_id=1, source_target_pairs={{0,24},{8,16},{16,8},{24,0},{1,25},{9,17},{17,9},{25,1},{2,26},{10... | collective-permute-start | bytes 294920 | tf_op jit(solution)/shard_map/ppermute | solution.py:620
  14.1 4.6 %collective-permute-start.2 = (f32[192,128]{1,0:T(8,128)S(1)}, f32[192,128]{1,0:T(8,128)S(1)}, u32[]{:S(2)}, u32[]{:S(2)}) collective-permute-start(f32[192,128]{1,0:T(8,128)S(1)} %get-tuple-element.29), channel_id=1, source_target_pairs={{0,8},{8,0},{16,24},{24,16},{1,9},{9,1},{17,25},{25,17},{2,10},{10... | collective-permute-start | bytes 294920 | tf_op jit(solution)/shard_map/ppermute | solution.py:620
  20.2 11.4 %all-to-all-start = ((f32[32,1,128]{2,1,0:T(1,128)}), f32[32,1,128]{2,1,0:T(1,128)S(1)}, u32[]{:S(2)}, u32[]{:S(2)}) async-start(f32[32,1,128]{2,1,0:T(1,128)} %get-tuple-element.41), calls=%async_computation | async-start | bytes 32768 | tf_op jit(solution)/shard_map/all_to_all | solution.py:687
  24.5 7.1 %copy-start = (f32[8,16,768]{2,1,0:T(8,128)S(1)}, f32[8,16,768]{2,1,0:T(8,128)}, u32[]{:S(2)}) copy-start(f32[8,16,768]{2,1,0:T(8,128)} %b_ref.1) | copy-start | bytes 1179652

commit v13 on v12

--- a/solution.py
+++ b/solution.py
@@ -2,6 +2,7 @@
 
 import jax
 import jax.numpy as jnp
+import numpy as np
 from jax import lax
 from jax.experimental import pallas as pl
 from jax.experimental.pallas import tpu as pltpu
@@ -610,14 +611,18 @@
 
 
 def swap(array, axis, start):
-    count = lax.axis_size(axis)
-    target = list(range(count))
-    for i in range(start, count - 1, 2):
-        target[i], target[i + 1] = i + 1, i
-    ends = [i for i in range(count) if target[i] == i]
-    if len(ends) == 2:
-        target[ends[0]], target[ends[1]] = ends[1], ends[0]
-    return lax.ppermute(array, axis, list(enumerate(target)))
+    counts = {name: lax.axis_size(name) for name in ("gx", "gy")}
+    other = "gy" if axis == "gx" else "gx"
+    pairs = []
+    for at in np.ndindex(counts["gx"], counts["gy"]):
+        place = dict(zip(("gx", "gy"), at))
+        partner = place[axis] + (1 if (place[axis] - start) % 2 == 0 else -1)
+        if 0 <= partner < counts[axis]:
+            place[axis] = partner
+        elif place[other] ^ 1 < counts[other]:
+            place[other] ^= 1
+        pairs.append((at[0] * counts["gy"] + at[1], place["gx"] * counts["gy"] + place["gy"]))
+    return lax.ppermute(array, ("gx", "gy"), pairs)
 
 
 def per_device(heat_source, density):

time: 33 us -> 30.7 us (0.930)
  waiting for transfers between devices: 11 us -> 9.11 us
  starting transfers between devices: 13 us -> 12.5 us
    ppermute x4, waiting for transfers between devices: 4.6 us -> 2.67 us  [swap(): return lax.ppermute(array, ('gx', 'gy'), pairs)]
    ppermute x4, starting transfers between devices: 8.62 us -> 6.85 us  [swap(): return lax.ppermute(array, ('gx', 'gy'), pairs)]
    all_to_all x1, starting transfers between devices: 4.34 us -> 5.7 us  [per_device(): parts = lax.all_to_all(sums, ('gx', 'gy'), 0, 0, tiled=True)]
  transfers between devices with their start and end apart: 5 -> 5, of which waited for: 3 -> 2; matrix products, arithmetic and copies ran while one was open for 0% -> 0% of each run, Pallas kernels for 11% -> 12%
where the time goes in v13:
time: 30.7 us; the launch traced here: 30.5 us
  starting transfers between devices  12.5 us (41%)
  waiting for transfers between devices  9.11 us (30%)
  Pallas kernels  8.13 us (26%)
  between operations  0.72 us (2%)
    ppermute x4, starting transfers between devices, swap(): return lax.ppermute(array, ('gx', 'gy'), pairs)  6.85 us
    all_to_all x1, waiting for transfers between devices, per_device(): parts = lax.all_to_all(sums, ('gx', 'gy'), 0, 0, tiled=True)  6.44 us
    all_to_all x1, starting transfers between devices, per_device(): parts = lax.all_to_all(sums, ('gx', 'gy'), 0, 0, tiled=True)  5.7 us
    pallas_call x1, Pallas kernels, per_device(): call(inner_kernel, (rows,) * 2 + (field,) * 5 + (edge,) * 2 + (shape(4 *...  2.78 us
    ppermute x4, waiting for transfers between devices, swap(): return lax.ppermute(array, ('gx', 'gy'), pairs)  2.67 us
    pallas_call x1, Pallas kernels, per_device(): call(pack_kernel, (shape(nodes, LANES), shape(nx * ny, LANES), face), in_...  1.56 us
    pallas_call x1, Pallas kernels, per_device(): call(outer_kernel, (shape(nodes, LANES), shape(nodes, LANES), shape(ny, L...  1.51 us
    pallas_call x1, Pallas kernels, per_device(): call(finish_kernel, (whole, whole), out_specs=(hbm, hbm), scratch_shapes=...  1.21 us
  transfers between devices with their start and end apart: 5, of which 2 were waited for; matrix products, arithmetic and copies ran while one was open for 0% of the time, Pallas kernels for 12%

profile of v13, /device:TPU:0, one launch (start us, length us, event | category | flops | bytes accessed | tf_op | source)
XLA Modules:
  0.0 30.5 jit_solution(15246505546563285690)
XLA Ops:
  0.6 1.6 %shard_map.41 = (f32[1024,128]{1,0:T(8,128)S(1)}, f32[128,128]{1,0:T(8,128)S(1)}, f32[240,128]{1,0:T(8,128)S(1)}) custom-call(f32[8,16,768]{2,1,0:T(8,128)} %b_ref.1, f32[16,768]{1,0:T(8,128)} %d_hbm.1), custom_call_target="tpu_custom_call" | custom-call | tf_op jit(solution)/shard_map/pallas_call | solution.py:649
  2.2 3.1 %collective-permute-start = (f32[240,128]{1,0:T(8,128)S(1)}, f32[240,128]{1,0:T(8,128)S(1)}, u32[]{:S(2)}, u32[]{:S(2)}) collective-permute-start(f32[240,128]{1,0:T(8,128)S(1)} %get-tuple-element.27), channel_id=1, source_target_pairs={{0,8},{1,2},{2,1},{3,4},{4,3},{5,6},{6,5},{7,15},{8,0},{9,10},{10,... | collective-permute-start | bytes 368648 | tf_op jit(solution)/shard_map/ppermute | solution.py:625
  5.3 0.1 shard_map.43
  5.4 0.1 collective-permute-start.1
  5.5 2.7 %collective-permute-done.y_ref.y2_ref = f32[240,128]{1,0:T(8,128)S(1)} collective-permute-done((f32[240,128]{1,0:T(8,128)S(1)}, f32[240,128]{1,0:T(8,128)S(1)}, u32[]{:S(2)}, u32[]{:S(2)}) %collective-permute-start) | collective-permute-done | bytes 122912 | tf_op jit(solution)/shard_map/ppermute | solution.py:625
  8.1 0.1 shard_map.42.t2_ref
  8.3 0.0 collective-permute-done.1.y1_ref
  8.3 0.2 shard_map.44
  8.4 0.2 collective-permute-start.3
  8.7 3.4 %collective-permute-start.2 = (f32[192,128]{1,0:T(8,128)S(1)}, f32[192,128]{1,0:T(8,128)S(1)}, u32[]{:S(2)}, u32[]{:S(2)}) collective-permute-start(f32[192,128]{1,0:T(8,128)S(1)} %get-tuple-element.29), channel_id=1, source_target_pairs={{0,8},{1,9},{2,10},{3,11},{4,12},{5,13},{6,14},{7,15},{8,0},{9,1},... | collective-permute-start | bytes 294920 | tf_op jit(solution)/shard_map/ppermute | solution.py:625
  12.1 2.8 %shard_map.46 = (f32[320,128]{1,0:T(8,128)S(1)}, f32[320,128]{1,0:T(8,128)S(1)}, f32[1920,128]{1,0:T(8,128)S(1)}, f32[1920,128]{1,0:T(8,128)S(1)}, f32[1920,128]...) custom-call(f32[1024,128]{1,0:T(8,128)S(1)} %get-tuple-element.25.bt, ...), custom_call_target="tpu_custom_call" | custom-call | tf_op jit(solution)/shard_map/pallas_call | solution.py:674
  14.9 0.0 collective-permute-done.3.x_ref.x2_ref
  14.9 0.1 shard_map.45.t2_ref
  15.0 0.0 collective-permute-done.2.x1_ref
  15.0 1.5 %shard_map.47 = (f32[1024,128]{1,0:T(8,128)S(1)}, f32[1024,128]{1,0:T(8,128)S(1)}, f32[8,128]{1,0:T(8,128)S(1)}, f32[32,1,128]{2,1,0:T(1,128)}) custom-call(f32[256,128]{1,0:T(8,128)S(1)} %get-tuple-element.28.dens_ref, f32[192,128]{1,0:T(8,128)S(1)} %collective-permute-done.2.x1_ref, f32[192,128]{1,0:T(8,128)S(1)} %collective-permute-done.3.x_ref.x2_ref, ...), custom_call_target="tpu_custom_call" | custom-call | tf_op jit(solution)/shard_map/pallas_call | solution.py:678
  16.5 5.7 %all-to-all-start = ((f32[32,1,128]{2,1,0:T(1,128)}), f32[32,1,128]{2,1,0:T(1,128)S(1)}, u32[]{:S(2)}, u32[]{:S(2)}) async-start(f32[32,1,128]{2,1,0:T(1,128)} %get-tuple-element.41), calls=%async_computation | async-start | bytes 32768 | tf_op jit(solution)/shard_map/all_to_all | solution.py:692
  22.2 0.0 copy-start
  22.2 0.6 %shard_map.48 = (f32[8,16,768]{2,1,0:T(8,128)S(1)}, f32[8,16,768]{2,1,0:T(8,128)S(1)}, f32[16,768]{1,0:T(8,128)S(1)}) custom-call(f32[1024,128]{1,0:T(8,128)S(1)} %get-tuple-element.42.q_ref, f32[1024,128]{1,0:T(8,128)S(1)} %get-tuple-element.43.v_ref, f32[320,128]{1,0:T(8,128)S(1)} %get-tuple-element.32.invx1.inv1_ref, f32[8,128]{1,0:T(8,128)S(1)} %get-tuple-element.44.inv2_ref), custom_call_target="tpu_custom_call" | custom-call | tf_op jit(solution)/shard_map/pallas_call | solution.py:694
  22.9 6.4 %all-to-all-done.parts_ref = f32[32,1,128]{2,1,0:T(1,128)S(1)} async-done(((f32[32,1,128]{2,1,0:T(1,128)}), f32[32,1,128]{2,1,0:T(1,128)S(1)}, u32[]{:S(2)}, u32[]{:S(2)}) %all-to-all-start) | async-done | bytes 16416 | tf_op jit(solution)/shard_map/all_to_all | solution.py:692
  29.3 0.0 copy-done
  29.3 1.2 %shard_map.49 = (f32[8,16,768]{2,1,0:T(8,128)}, f32[8,16,768]{2,1,0:T(8,128)}) custom-call(f32[32,1,128]{2,1,0:T(1,128)S(1)} %all-to-all-done.parts_ref, f32[8,16,768]{2,1,0:T(8,128)S(1)} %copy-done, f32[8,16,768]{2,1,0:T(8,128)S(1)} %get-tuple-element.45.q_ref, f32[8,16,768]{2,1,0:T(8,128)S(1)} %get-tuple-element.46.v_ref, ...), custom_call_target="tpu_custom_call" | custom-call | tf_op jit(solution)/shard_map/pallas_call | solution.py:697
Async XLA Ops:
  2.2 5.9 %collective-permute-start = (f32[240,128]{1,0:T(8,128)S(1)}, f32[240,128]{1,0:T(8,128)S(1)}, u32[]{:S(2)}, u32[]{:S(2)}) collective-permute-start(f32[240,128]{1,0:T(8,128)S(1)} %get-tuple-element.27), channel_id=1, source_target_pairs={{0,8},{1,2},{2,1},{3,4},{4,3},{5,6},{6,5},{7,15},{8,0},{9,10},{10,... | collective-permute-start | bytes 368648 | tf_op jit(solution)/shard_map/ppermute | solution.py:625
  5.4 2.9 %collective-permute-start.1 = (f32[240,128]{1,0:T(8,128)S(1)}, f32[240,128]{1,0:T(8,128)S(1)}, u32[]{:S(2)}, u32[]{:S(2)}) collective-permute-start(f32[240,128]{1,0:T(8,128)S(1)} %shard_map.43), channel_id=1, source_target_pairs={{0,1},{1,0},{2,3},{3,2},{4,5},{5,4},{6,7},{7,6},{8,9},{9,8},{10,11... | collective-permute-start | bytes 368648 | tf_op jit(solution)/shard_map/ppermute | solution.py:625
  8.4 6.4 %collective-permute-start.3 = (f32[192,128]{1,0:T(8,128)S(1)}, f32[192,128]{1,0:T(8,128)S(1)}, u32[]{:S(2)}, u32[]{:S(2)}) collective-permute-start(f32[192,128]{1,0:T(8,128)S(1)} %get-tuple-element.30), channel_id=1, source_target_pairs={{0,1},{1,0},{2,3},{3,2},{4,5},{5,4},{6,7},{7,6},{8,16},{9,17},{10,... | collective-permute-start | bytes 294920 | tf_op jit(solution)/shard_map/ppermute | solution.py:625
  8.7 6.3 %collective-permute-start.2 = (f32[192,128]{1,0:T(8,128)S(1)}, f32[192,128]{1,0:T(8,128)S(1)}, u32[]{:S(2)}, u32[]{:S(2)}) collective-permute-start(f32[192,128]{1,0:T(8,128)S(1)} %get-tuple-element.29), channel_id=1, source_target_pairs={{0,8},{1,9},{2,10},{3,11},{4,12},{5,13},{6,14},{7,15},{8,0},{9,1},... | collective-permute-start | bytes 294920 | tf_op jit(solution)/shard_map/ppermute | solution.py:625
  16.5 12.8 %all-to-all-start = ((f32[32,1,128]{2,1,0:T(1,128)}), f32[32,1,128]{2,1,0:T(1,128)S(1)}, u32[]{:S(2)}, u32[]{:S(2)}) async-start(f32[32,1,128]{2,1,0:T(1,128)} %get-tuple-element.41), calls=%async_computation | async-start | bytes 32768 | tf_op jit(solution)/shard_map/all_to_all | solution.py:692
  22.2 7.1 %copy-start = (f32[8,16,768]{2,1,0:T(8,128)S(1)}, f32[8,16,768]{2,1,0:T(8,128)}, u32[]{:S(2)}) copy-start(f32[8,16,768]{2,1,0:T(8,128)} %b_ref.1) | copy-start | bytes 1179652

commit v14 on v13

--- a/solution.py
+++ b/solution.py
@@ -91,8 +91,10 @@
         self.pitch = -(-(ny + 6) // SUB) * SUB
         self.y_dens = packed_count(2 * nx) * loads
         self.y_rows = self.y_dens + 3 * nx
-        self.x_dens = packed_count(2 * self.my) * loads
-        self.x_rows = self.x_dens + 3 * self.pitch
+        self.x_dens = packed_count(2 * ny) * loads
+        self.x_rows = self.x_dens + 3 * ny
+        self.c_dens = packed_count(8) * loads
+        self.c_rows = self.c_dens + -(-18 // SUB) * SUB
 
 
 class Tiles:
@@ -190,8 +192,20 @@
     pack_face(s, jnp.logical_not(is_even("gy")), bt_ref, dt_ref, y2_ref)
 
 
-def pack_near_kernel(s, bt_ref, dt_ref, y1_ref):
+def pack_rest_kernel(s, bt_ref, dt_ref, y1_ref, x1_ref, x2_ref):
+    even_x = is_even("gx")
+    pack_x_face(s, jnp.logical_not(even_x), bt_ref, dt_ref, x2_ref)
+    pack_x_face(s, even_x, bt_ref, dt_ref, x1_ref)
     pack_face(s, is_even("gy"), bt_ref, dt_ref, y1_ref)
+
+
+def pack_x_face(s, upper, bt_ref, dt_ref, out_ref):
+    loads, nx, ny = s.loads, s.nx, s.ny
+    tiles = Tiles(bt_ref, ny, loads)
+    x0 = pick(upper, nx - 2, 0)
+    pack_tiles(out_ref, 0, loads, 2 * ny, lambda i: tiles[x0 + i // ny, i % ny])
+    rows = pl.ds(pl.multiple_of(pick(upper, nx - 3, 0) * ny, SUB), 3 * ny)
+    out_ref[s.x_dens :, :] = dt_ref[rows, :]
 
 
 def pack_face(s, upper, bt_ref, dt_ref, out_ref):
@@ -216,49 +230,53 @@
     )
 
 
-def open_x_kernel(s, x_ref, t_ref):
-    tiles = Tiles(t_ref, s.my, s.loads)
-    unpack_tiles(
-        x_ref, 0, s.loads, 2 * s.my, lambda i, tile: [(tiles, (i // s.my, i % s.my), tile)]
-    )
-
-
-def pack_x_kernel(s, bt_ref, dt_ref, y2_ref, t2_ref, y1_ref, dens_ref, x1_ref, x2_ref, edge_ref):
-    loads, nx, ny, my, pitch = s.loads, s.nx, s.ny, s.my, s.pitch
-    even_x, even_y = is_even("gx"), is_even("gy")
-    ys = (pick(even_y, ny + 2, 0), pick(even_y, 0, ny + 2))
+def corner_kernel(s, x1_ref, x2_ref, xt_ref, c1_ref, c2_ref):
+    loads, ny = s.loads, s.ny
+    tiles = Tiles(xt_ref, ny, loads)
+    for side, ref in enumerate((x1_ref, x2_ref)):
+        unpack_tiles(
+            ref, 0, loads, 2 * ny,
+            lambda i, tile: [(tiles, (2 * side + i // ny, i % ny), tile)],
+        )
+    even_y = is_even("gy")
+    for out_ref, upper in ((c2_ref, jnp.logical_not(even_y)), (c1_ref, even_y)):
+        y0 = pick(upper, ny - 2, 0)
+        pack_tiles(out_ref, 0, loads, 8, lambda i: tiles[i // 2, y0 + i % 2])
+        y0 = pick(upper, ny - 3, 0)
+        batch, at = Batch(18), s.c_dens
+        for ref in (x1_ref, x2_ref):
+            for t in range(3):
+                for dy in range(3):
+                    row = ref[pl.ds(s.x_dens + t * ny + y0 + dy, 1), :]
+                    batch.add(out_ref, (slice(at, at + 1), slice(None)), row)
+                    at += 1
+        batch.flush()
+        out_ref[at:, :] = jnp.zeros((s.c_rows - at, LANES), jnp.float32)
+
+
+def join_density(s, dt_ref, y1_ref, y2_ref, dens_ref):
+    nx, ny, pitch = s.nx, s.ny, s.pitch
+    even_y = is_even("gy")
     yd = (pick(even_y, ny + 3, 0), pick(even_y, 0, ny + 3))
+    batch = Batch(16)
     for x in range(nx):
         at = x * pitch
-        dens_ref[at + 3 : at + 3 + ny, :] = dt_ref[x * ny : (x + 1) * ny, :]
-        dens_ref[at + ny + 6 : at + pitch, :] = jnp.zeros((pitch - ny - 6, LANES), jnp.float32)
+        batch.add(
+            dens_ref, (slice(at + 3, at + 3 + ny), slice(None)), dt_ref[x * ny : (x + 1) * ny, :]
+        )
+    batch.flush()
     for side, ref in enumerate((y1_ref, y2_ref)):
         alone = is_alone("gy", s.count_y, side)
         for dy in range(3):
             for x0 in range(0, nx, SUB):
                 at = s.y_dens + dy * nx + x0
                 to = x0 * pitch + yd[side] + dy
-                dens_ref[pl.ds(to, SUB, stride=pitch), :] = jnp.where(
-                    alone, 0.0, ref[at : at + SUB, :]
+                batch.add(
+                    dens_ref,
+                    (pl.ds(to, SUB, stride=pitch), slice(None)),
+                    jnp.where(alone, 0.0, ref[at : at + SUB, :]),
                 )
-    inner, edge = Tiles(bt_ref, ny, loads), Tiles(edge_ref, my, loads)
-    far = Tiles(t2_ref, 2, loads)
-    batch = Batch()
-    for place, x in enumerate((0, 1, nx - 2, nx - 1)):
-        for y in range(ny):
-            batch.add(edge, (place, y + 2), inner[x, y])
-        for dy in range(2):
-            tile = unpack_tile(
-                lambda t: y1_ref[t * loads : (t + 1) * loads, :], 2 * x + dy, loads
-            )
-            batch.add(edge, (place, ys[0] + dy), tile)
-            batch.add(edge, (place, ys[1] + dy), far[x, dy])
-    batch.flush()
-    for ref, upper in ((x1_ref, even_x), (x2_ref, jnp.logical_not(even_x))):
-        place = pick(upper, 2, 0)
-        pack_tiles(ref, 0, loads, 2 * my, lambda i: edge[place + i // my, i % my])
-        rows = pl.ds(pl.multiple_of(pick(upper, nx - 3, 0) * pitch, SUB), 3 * pitch)
-        ref[s.x_dens :, :] = dens_ref[rows, :]
+    batch.flush()
 
 
 def conduct_of(dens):
@@ -375,14 +393,15 @@
 
 
 def inner_kernel(
-    s, bt_ref, dens_ref, y1_ref, t2_ref,
-    cond, invx, bx, zx, qx, wx, vx, carry1, carry2, sums_ref,
+    s, bt_ref, dt_ref, y1_ref, y2_ref, t2_ref,
+    dens_ref, cond, invx, bx, zx, qx, wx, vx, carry1, carry2, sums_ref,
 ):
     loads, nx, ny, my, pitch = s.loads, s.nx, s.ny, s.my, s.pitch
     bx, zx, qx, wx, vx, carry1, carry2 = (
         Tiles(ref, my, loads) for ref in (bx, zx, qx, wx, vx, carry1, carry2)
     )
     cond, invx = Rows(cond, pitch, loads), Rows(invx, pitch, loads)
+    join_density(s, dt_ref, y1_ref, y2_ref, dens_ref)
     even_y = is_even("gy")
     ys = (pick(even_y, ny + 2, 0), pick(even_y, 0, ny + 2))
     before = None
@@ -438,7 +457,7 @@
 
 
 def outer_kernel(
-    s, dens_ref, x1_ref, x2_ref, t2_ref,
+    s, dens_ref, x1_ref, x2_ref, xt_ref, c1_ref, c2_ref,
     cond1, invx1, bx1, zx1, qx1, wx1, vx1, carry1, carry2, sums1,
     q_out, v_out, inv_out, sums_ref,
     low_ref, high_ref, low_d, high_d, cond2, invx2, bx2, zx2, qx2, wx2, vx2, carry3,
@@ -446,17 +465,38 @@
     loads, nx, ny, mx, my, pitch = s.loads, s.nx, s.ny, s.mx, s.my, s.pitch
     even_x = is_even("gx")
 
+    even_y = is_even("gy")
+    ys = (pick(even_y, ny + 2, 0), pick(even_y, 0, ny + 2))
+    yd = (pick(even_y, ny + 3, 0), pick(even_y, 0, ny + 3))
+
     def take(near, far):
-        near_t, near_d = near
-        far_t, far_d = far
-        unpack_tiles(
-            x1_ref, 0, loads, 2 * my,
-            lambda i, tile: [(Tiles(near_t, my, loads), (i // my, i % my), tile)],
-        )
-        far_t[...] = t2_ref[...]
-        for into, ref, start in ((near_d, x1_ref, 0), (far_d, x2_ref, 1)):
-            alone = is_alone("gx", s.count_x, start)
-            into[...] = jnp.where(alone, 0.0, ref[s.x_dens :, :])
+        faces = Tiles(xt_ref, ny, loads)
+        for side, (ref, (tiles_ref, into)) in enumerate(((x1_ref, near), (x2_ref, far))):
+            tiles = Tiles(tiles_ref, my, loads)
+            alone_x = is_alone("gx", s.count_x, side)
+            batch = Batch(18)
+            for dx in range(2):
+                for y in range(ny):
+                    batch.add(tiles, (dx, y + 2), faces[2 * side + dx, y])
+            for t in range(3):
+                at = s.x_dens + t * ny
+                rows = jnp.where(alone_x, 0.0, ref[at : at + ny, :])
+                to = t * pitch + 3
+                batch.add(into, (slice(to, to + ny), slice(None)), rows)
+            batch.flush()
+            for end, corner in enumerate((c1_ref, c2_ref)):
+                alone = jnp.logical_or(alone_x, is_alone("gy", s.count_y, end))
+                for i in range(4):
+                    tile = unpack_tile(
+                        lambda t: corner[t * loads : (t + 1) * loads, :], 4 * side + i, loads
+                    )
+                    batch.add(tiles, (i // 2, ys[end] + i % 2), tile)
+                for i in range(9):
+                    at = s.c_dens + 9 * side + i
+                    row = jnp.where(alone, 0.0, corner[at : at + 1, :])
+                    to = i // 3 * pitch + yd[end] + i % 3
+                    batch.add(into, (pl.ds(to, 1), slice(None)), row)
+            batch.flush()
 
     @pl.when(even_x)
     def _():
@@ -660,21 +700,24 @@
         pltpu.with_memory_space_constraint(density, pltpu.HBM),
     )
     y2 = swap(y2, "gy", 1)
-    y1 = swap(call(pack_near_kernel, face)(bt, dt), "gy", 0)
+    x_face, corner = shape(s.x_rows, LANES), shape(s.c_rows, LANES)
+    y1, x1, x2 = call(pack_rest_kernel, (face, x_face, x_face))(bt, dt)
+    x2, y1, x1 = swap(x2, "gx", 1), swap(y1, "gy", 0), swap(x1, "gx", 0)
     t2 = call(open_y_kernel, shape(2 * nx * loads, LANES))(y2)
-    dens, x1, x2 = call(
-        pack_x_kernel,
-        (shape(nx * s.pitch, LANES), shape(s.x_rows, LANES), shape(s.x_rows, LANES)),
-        scratch_shapes=[scratch(4 * s.my * loads, LANES)],
-    )(bt, dt, y2, t2, y1)
-    x1, x2 = swap(x1, "gx", 0), swap(x2, "gx", 1)
+    xt, c1, c2 = call(corner_kernel, (shape(4 * ny * loads, LANES), corner, corner))(x1, x2)
+    xt, dt = lax.optimization_barrier((xt, dt))
+    c2, c1 = swap(c2, "gy", 1), swap(c1, "gy", 0)
     plane = s.my * loads
     rows, field = shape(s.mx * s.pitch, LANES), shape(s.mx * plane, LANES)
     edge = shape(2 * plane, LANES)
-    cond, inv_1, bx, zx, q_1, w_1, v_1, carry1, carry2, sums = call(
-        inner_kernel, (rows,) * 2 + (field,) * 5 + (edge,) * 2 + (shape(4 * loads, LANES),)
-    )(bt, dens, y1, t2)
-    xt2 = call(open_x_kernel, shape(2 * plane, LANES))(x2)
+    dens, cond, inv_1, bx, zx, q_1, w_1, v_1, carry1, carry2, sums = call(
+        inner_kernel,
+        (shape(nx * s.pitch, LANES),)
+        + (rows,) * 2
+        + (field,) * 5
+        + (edge,) * 2
+        + (shape(4 * loads, LANES),),
+    )(bt, dt, y1, y2, t2)
     q_t, v_t, inv_2, sums = call(
         outer_kernel,
         (
@@ -688,7 +731,7 @@
         + [scratch(5 * s.pitch, LANES)] * 2
         + [scratch(5 * plane, LANES)] * 5
         + [scratch(2 * plane, LANES)],
-    )(dens, x1, x2, xt2, cond, inv_1, bx, zx, q_1, w_1, v_1, carry1, carry2, sums)
+    )(dens, x1, x2, xt, c1, c2, cond, inv_1, bx, zx, q_1, w_1, v_1, carry1, carry2, sums)
     parts = lax.all_to_all(sums, ("gx", "gy"), 0, 0, tiled=True)
     whole = shape(loads, nx, flat)
     image, again, inverse = call(unpack_kernel, (whole, whole, shape(nx, flat)))(

time: 30.7 us -> 29.9 us (0.974)
  starting transfers between devices: 12.5 us -> 11.7 us
    all_to_all x1, starting transfers between devices: 5.7 us -> 4.28 us  [per_device(): parts = lax.all_to_all(sums, ('gx', 'gy'), 0, 0, tiled=True)]
    ppermute x4 -> x6, starting transfers between devices: 6.85 us -> 7.42 us  [swap(): return lax.ppermute(array, ('gx', 'gy'), pairs)]
    ppermute x4 -> x6, waiting for transfers between devices: 2.67 us -> 2.84 us  [swap(): return lax.ppermute(array, ('gx', 'gy'), pairs)]
    pallas_call x4 -> x3, Pallas kernels: 3.13 us -> 3.07 us  [the longest x1 2.79 us: per_device(): call(inner_kernel, (shape(nx * s.pitch, LANES),) + (rows,) * 2 + (field,)...]
  transfers between devices with their start and end apart: 5 -> 7, of which waited for: 2 -> 2; matrix products, arithmetic and copies ran while one was open for 0% -> 0% of each run, Pallas kernels for 12% -> 13%
where the time goes in v14:
time: 29.9 us; the launch traced here: 29.7 us
  starting transfers between devices  11.7 us (39%)
  waiting for transfers between devices  9.28 us (31%)
  Pallas kernels  8.02 us (27%)
  between operations  0.71 us (2%)
    ppermute x6, starting transfers between devices, swap(): return lax.ppermute(array, ('gx', 'gy'), pairs)  7.42 us
    all_to_all x1, waiting for transfers between devices, per_device(): parts = lax.all_to_all(sums, ('gx', 'gy'), 0, 0, tiled=True)  6.44 us
    all_to_all x1, starting transfers between devices, per_device(): parts = lax.all_to_all(sums, ('gx', 'gy'), 0, 0, tiled=True)  4.28 us
    ppermute x6, waiting for transfers between devices, swap(): return lax.ppermute(array, ('gx', 'gy'), pairs)  2.84 us
    pallas_call x1, Pallas kernels, per_device(): call(inner_kernel, (shape(nx * s.pitch, LANES),) + (rows,) * 2 + (field,)...  2.79 us
    pallas_call x1, Pallas kernels, per_device(): call(pack_kernel, (shape(nodes, LANES), shape(nx * ny, LANES), face), in_...  1.56 us
    pallas_call x1, Pallas kernels, per_device(): call(outer_kernel, (shape(nodes, LANES), shape(nodes, LANES), shape(ny, L...  1.45 us
    pallas_call x1, Pallas kernels, per_device(): call(finish_kernel, (whole, whole), out_specs=(hbm, hbm), scratch_shapes=...  1.21 us
  transfers between devices with their start and end apart: 7, of which 2 were waited for; matrix products, arithmetic and copies ran while one was open for 0% of the time, Pallas kernels for 13%

profile of v14, /device:TPU:0, one launch (start us, length us, event | category | flops | bytes accessed | tf_op | source)
XLA Modules:
  0.0 29.7 jit_solution(13217069044550088632)
XLA Ops:
  0.6 1.6 %shard_map.41 = (f32[1024,128]{1,0:T(8,128)S(1)}, f32[128,128]{1,0:T(8,128)S(1)}, f32[240,128]{1,0:T(8,128)S(1)}) custom-call(f32[8,16,768]{2,1,0:T(8,128)} %b_ref.1, f32[16,768]{1,0:T(8,128)} %d_hbm.1), custom_call_target="tpu_custom_call" | custom-call | tf_op jit(solution)/shard_map/pallas_call | solution.py:689
  2.2 3.1 %collective-permute-start.3 = (f32[240,128]{1,0:T(8,128)S(1)}, f32[240,128]{1,0:T(8,128)S(1)}, u32[]{:S(2)}, u32[]{:S(2)}) collective-permute-start(f32[240,128]{1,0:T(8,128)S(1)} %get-tuple-element.38), channel_id=1, source_target_pairs={{0,8},{1,2},{2,1},{3,4},{4,3},{5,6},{6,5},{7,15},{8,0},{9,10},{10,... | collective-permute-start | bytes 368648 | tf_op jit(solution)/shard_map/ppermute | solution.py:665
  5.3 0.1 shard_map.42
  5.4 0.1 collective-permute-start.2
  5.5 1.6 %collective-permute-start = (f32[120,128]{1,0:T(8,128)S(1)}, f32[120,128]{1,0:T(8,128)S(1)}, u32[]{:S(2)}, u32[]{:S(2)}) collective-permute-start(f32[120,128]{1,0:T(8,128)S(1)} %get-tuple-element.33), channel_id=1, source_target_pairs={{0,8},{1,9},{2,10},{3,11},{4,12},{5,13},{6,14},{7,15},{8,0},{9,1},... | collective-permute-start | bytes 184328 | tf_op jit(solution)/shard_map/ppermute | solution.py:665
  7.1 0.0 collective-permute-start.1
  7.1 2.8 %collective-permute-done.x1_ref = f32[120,128]{1,0:T(8,128)S(1)} collective-permute-done((f32[120,128]{1,0:T(8,128)S(1)}, f32[120,128]{1,0:T(8,128)S(1)}, u32[]{:S(2)}, u32[]{:S(2)}) %collective-permute-start) | collective-permute-done | bytes 61472 | tf_op jit(solution)/shard_map/ppermute | solution.py:665
  9.9 0.0 collective-permute-done.1.x2_ref
  9.9 0.2 shard_map.43
  10.1 0.1 collective-permute-start.4
  10.2 2.6 %collective-permute-start.5 = (f32[72,128]{1,0:T(8,128)S(1)}, f32[72,128]{1,0:T(8,128)S(1)}, u32[]{:S(2)}, u32[]{:S(2)}) collective-permute-start(f32[72,128]{1,0:T(8,128)S(1)} %get-tuple-element.42), channel_id=1, source_target_pairs={{0,8},{1,2},{2,1},{3,4},{4,3},{5,6},{6,5},{7,15},{8,0},{9,10},{10,... | collective-permute-start | bytes 110600 | tf_op jit(solution)/shard_map/ppermute | solution.py:665
  12.7 0.0 collective-permute-done.3.y_ref.y2_ref
  12.8 0.1 shard_map.44.t2_ref
  12.9 0.0 collective-permute-done.2.y1_ref
  12.9 2.8 %shard_map.45 = (f32[256,128]{1,0:T(8,128)S(1)}, f32[320,128]{1,0:T(8,128)S(1)}, f32[320,128]{1,0:T(8,128)S(1)}, f32[1920,128]{1,0:T(8,128)S(1)}, f32[1920,128]{...) custom-call(f32[1024,128]{1,0:T(8,128)S(1)} %get-tuple-element.31.bt, ...), custom_call_target="tpu_custom_call" | custom-call | tf_op jit(solution)/shard_map/pallas_call | solution.py:713
  15.7 0.0 collective-permute-done.4.c1_ref
  15.7 0.0 collective-permute-done.5.c2_ref
  15.7 1.5 %shard_map.46 = (f32[1024,128]{1,0:T(8,128)S(1)}, f32[1024,128]{1,0:T(8,128)S(1)}, f32[8,128]{1,0:T(8,128)S(1)}, f32[32,1,128]{2,1,0:T(1,128)}) custom-call(f32[256,128]{1,0:T(8,128)S(1)} %get-tuple-element.39.dens_ref, f32[120,128]{1,0:T(8,128)S(1)} %collective-permute-done.x1_ref, f32[120,128]{1,0:T(8,128)S(1)} %collective-permute-done.1.x2_ref, ...), custom_call_target="tpu_custom_call" | custom-call | tf_op jit(solution)/shard_map/pallas_call | solution.py:721
  17.1 4.3 %all-to-all-start = ((f32[32,1,128]{2,1,0:T(1,128)}), f32[32,1,128]{2,1,0:T(1,128)S(1)}, u32[]{:S(2)}, u32[]{:S(2)}) async-start(f32[32,1,128]{2,1,0:T(1,128)} %get-tuple-element.53), calls=%async_computation | async-start | bytes 32768 | tf_op jit(solution)/shard_map/all_to_all | solution.py:735
  21.4 0.0 copy-start
  21.4 0.6 %shard_map.47 = (f32[8,16,768]{2,1,0:T(8,128)S(1)}, f32[8,16,768]{2,1,0:T(8,128)S(1)}, f32[16,768]{1,0:T(8,128)S(1)}) custom-call(f32[1024,128]{1,0:T(8,128)S(1)} %get-tuple-element.54.q_ref, f32[1024,128]{1,0:T(8,128)S(1)} %get-tuple-element.55.v_ref, f32[320,128]{1,0:T(8,128)S(1)} %get-tuple-element.44.invx1.inv1_ref, f32[8,128]{1,0:T(8,128)S(1)} %get-tuple-element.56.inv2_ref), custom_call_target="tpu_custom_call" | custom-call | tf_op jit(solution)/shard_map/pallas_call | solution.py:737
  22.1 6.4 %all-to-all-done.parts_ref = f32[32,1,128]{2,1,0:T(1,128)S(1)} async-done(((f32[32,1,128]{2,1,0:T(1,128)}), f32[32,1,128]{2,1,0:T(1,128)S(1)}, u32[]{:S(2)}, u32[]{:S(2)}) %all-to-all-start) | async-done | bytes 16416 | tf_op jit(solution)/shard_map/all_to_all | solution.py:735
  28.5 0.0 copy-done
  28.5 1.2 %shard_map.48 = (f32[8,16,768]{2,1,0:T(8,128)}, f32[8,16,768]{2,1,0:T(8,128)}) custom-call(f32[32,1,128]{2,1,0:T(1,128)S(1)} %all-to-all-done.parts_ref, f32[8,16,768]{2,1,0:T(8,128)S(1)} %copy-done, f32[8,16,768]{2,1,0:T(8,128)S(1)} %get-tuple-element.57.q_ref, f32[8,16,768]{2,1,0:T(8,128)S(1)} %get-tuple-element.58.v_ref, ...), custom_call_target="tpu_custom_call" | custom-call | tf_op jit(solution)/shard_map/pallas_call | solution.py:740
Async XLA Ops:
  2.2 10.6 %collective-permute-start.3 = (f32[240,128]{1,0:T(8,128)S(1)}, f32[240,128]{1,0:T(8,128)S(1)}, u32[]{:S(2)}, u32[]{:S(2)}) collective-permute-start(f32[240,128]{1,0:T(8,128)S(1)} %get-tuple-element.38), channel_id=1, source_target_pairs={{0,8},{1,2},{2,1},{3,4},{4,3},{5,6},{6,5},{7,15},{8,0},{9,10},{10,... | collective-permute-start | bytes 368648 | tf_op jit(solution)/shard_map/ppermute | solution.py:665
  5.4 7.5 %collective-permute-start.2 = (f32[240,128]{1,0:T(8,128)S(1)}, f32[240,128]{1,0:T(8,128)S(1)}, u32[]{:S(2)}, u32[]{:S(2)}) collective-permute-start(f32[240,128]{1,0:T(8,128)S(1)} %get-tuple-element.37), channel_id=1, source_target_pairs={{0,1},{1,0},{2,3},{3,2},{4,5},{5,4},{6,7},{7,6},{8,9},{9,8},{10,11... | collective-permute-start | bytes 368648 | tf_op jit(solution)/shard_map/ppermute | solution.py:665
  5.5 4.4 %collective-permute-start = (f32[120,128]{1,0:T(8,128)S(1)}, f32[120,128]{1,0:T(8,128)S(1)}, u32[]{:S(2)}, u32[]{:S(2)}) collective-permute-start(f32[120,128]{1,0:T(8,128)S(1)} %get-tuple-element.33), channel_id=1, source_target_pairs={{0,8},{1,9},{2,10},{3,11},{4,12},{5,13},{6,14},{7,15},{8,0},{9,1},... | collective-permute-start | bytes 184328 | tf_op jit(solution)/shard_map/ppermute | solution.py:665
  7.1 2.8 %collective-permute-start.1 = (f32[120,128]{1,0:T(8,128)S(1)}, f32[120,128]{1,0:T(8,128)S(1)}, u32[]{:S(2)}, u32[]{:S(2)}) collective-permute-start(f32[120,128]{1,0:T(8,128)S(1)} %get-tuple-element.34), channel_id=1, source_target_pairs={{0,1},{1,0},{2,3},{3,2},{4,5},{5,4},{6,7},{7,6},{8,16},{9,17},{10,... | collective-permute-start | bytes 184328 | tf_op jit(solution)/shard_map/ppermute | solution.py:665
  10.1 5.6 %collective-permute-start.4 = (f32[72,128]{1,0:T(8,128)S(1)}, f32[72,128]{1,0:T(8,128)S(1)}, u32[]{:S(2)}, u32[]{:S(2)}) collective-permute-start(f32[72,128]{1,0:T(8,128)S(1)} %get-tuple-element.41), channel_id=1, source_target_pairs={{0,1},{1,0},{2,3},{3,2},{4,5},{5,4},{6,7},{7,6},{8,9},{9,8},{10,11... | collective-permute-start | bytes 110600 | tf_op jit(solution)/shard_map/ppermute | solution.py:665
  10.2 5.5 %collective-permute-start.5 = (f32[72,128]{1,0:T(8,128)S(1)}, f32[72,128]{1,0:T(8,128)S(1)}, u32[]{:S(2)}, u32[]{:S(2)}) collective-permute-start(f32[72,128]{1,0:T(8,128)S(1)} %get-tuple-element.42), channel_id=1, source_target_pairs={{0,8},{1,2},{2,1},{3,4},{4,3},{5,6},{6,5},{7,15},{8,0},{9,10},{10,... | collective-permute-start | bytes 110600 | tf_op jit(solution)/shard_map/ppermute | solution.py:665
  17.1 11.4 %all-to-all-start = ((f32[32,1,128]{2,1,0:T(1,128)}), f32[32,1,128]{2,1,0:T(1,128)S(1)}, u32[]{:S(2)}, u32[]{:S(2)}) async-start(f32[32,1,128]{2,1,0:T(1,128)} %get-tuple-element.53), calls=%async_computation | async-start | bytes 32768 | tf_op jit(solution)/shard_map/all_to_all | solution.py:735
  21.4 7.1 %copy-start = (f32[8,16,768]{2,1,0:T(8,128)S(1)}, f32[8,16,768]{2,1,0:T(8,128)}, u32[]{:S(2)}) copy-start(f32[8,16,768]{2,1,0:T(8,128)} %b_ref.1) | copy-start | bytes 1179652

commit v15 on v14

--- a/solution.py
+++ b/solution.py
@@ -573,8 +573,7 @@
     for place, part in enumerate(sums):
         total = jnp.sum(part, axis=1, keepdims=True)
         packed = packed + jnp.where(lane == place * loads + load, total, 0.0)
-    row = jnp.sum(packed, axis=0, keepdims=True)
-    sums_ref[...] = jnp.broadcast_to(row[None], sums_ref.shape)
+    sums_ref[...] = jnp.sum(packed, axis=0, keepdims=True)
 
 
 def again_planes(nx):
@@ -612,9 +611,10 @@
         )
 
 
-def finish_kernel(s, parts_ref, b_ref, q_ref, v_ref, inv_ref, x_hbm, r_hbm, x_ref, r_ref, sems):
+def finish_kernel(s, *refs):
+    *parts, b_ref, q_ref, v_ref, inv_ref, x_hbm, r_hbm, x_ref, r_ref, sems = refs
     loads = s.loads
-    totals = jnp.sum(parts_ref[...], axis=0)
+    totals = functools.reduce(jnp.add, [ref[...] for ref in parts])
 
     def part(place):
         return pltpu.roll(totals, (LANES - place * loads) % LANES, 1) if place else totals
@@ -650,6 +650,32 @@
         copy.wait()
 
 
+def radices(length):
+    found = []
+    while length > 1:
+        small = [f for f in range(2, 9) if length % f == 0]
+        factor = max(small) if small else length
+        found.append(factor)
+        length //= factor
+    return found
+
+
+def sum_rounds(row, axis):
+    length, stride, rows = lax.axis_size(axis), 1, [row]
+    for factor in radices(length):
+        row = functools.reduce(jnp.add, rows)
+        rows = [row]
+        for step in range(1, factor):
+            pairs = []
+            for i in range(length):
+                digit = i // stride % factor
+                to = digit ^ step if factor & (factor - 1) == 0 else (digit + step) % factor
+                pairs.append((i, i + (to - digit) * stride))
+            rows.append(lax.ppermute(row, axis, pairs))
+        stride *= factor
+    return rows
+
+
 def swap(array, axis, start):
     counts = {name: lax.axis_size(name) for name in ("gx", "gy")}
     other = "gy" if axis == "gx" else "gx"
@@ -670,7 +696,6 @@
     ny = flat // NZ
     s = Sizes(loads, nx, ny, lax.axis_size("gx"), lax.axis_size("gy"))
     nodes = nx * ny * loads
-    devices = lax.axis_size("gx") * lax.axis_size("gy")
 
     def shape(*dims):
         return jax.ShapeDtypeStruct(dims, jnp.float32)
@@ -724,7 +749,7 @@
             shape(nodes, LANES),
             shape(nodes, LANES),
             shape(ny, LANES),
-            shape(devices, 1, LANES),
+            shape(1, LANES),
         ),
         scratch_shapes=[scratch(2 * plane, LANES)] * 2
         + [scratch(3 * s.pitch, LANES)] * 2
@@ -732,7 +757,7 @@
         + [scratch(5 * plane, LANES)] * 5
         + [scratch(2 * plane, LANES)],
     )(dens, x1, x2, xt, c1, c2, cond, inv_1, bx, zx, q_1, w_1, v_1, carry1, carry2, sums)
-    parts = lax.all_to_all(sums, ("gx", "gy"), 0, 0, tiled=True)
+    parts = sum_rounds(functools.reduce(jnp.add, sum_rounds(sums, "gy")), "gx")
     whole = shape(loads, nx, flat)
     image, again, inverse = call(unpack_kernel, (whole, whole, shape(nx, flat)))(
         q_t, v_t, inv_1, inv_2
@@ -746,7 +771,7 @@
             scratch(loads, nx, flat),
             pltpu.SemaphoreType.DMA((2, loads)),
         ],
-    )(parts, heat_source, image, again, inverse)
+    )(*parts, heat_source, image, again, inverse)
 
 
 def solution(mesh):

time: 29.9 us -> 34.2 us (1.14)
  starting transfers between devices: 11.7 us -> 17.9 us
  waiting for transfers between devices: 9.28 us -> 7.9 us
  Pallas kernels: 8.02 us -> 7.45 us
    ppermute x0 -> x10, starting transfers between devices: none -> 10.5 us  [sum_rounds(): rows.append(lax.ppermute(row, axis, pairs))]
    all_to_all x1 -> x0, waiting for transfers between devices: 6.44 us -> none  [per_device(): parts = lax.all_to_all(sums, ('gx', 'gy'), 0, 0, tiled=True)]
    ppermute x0 -> x10, waiting for transfers between devices: none -> 5.06 us  [sum_rounds(): rows.append(lax.ppermute(row, axis, pairs))]
    all_to_all x1 -> x0, starting transfers between devices: 4.28 us -> none  [per_device(): parts = lax.all_to_all(sums, ('gx', 'gy'), 0, 0, tiled=True)]
    pallas_call x1, Pallas kernels: 1.45 us -> 0.83 us  [per_device(): call(outer_kernel, (shape(nodes, LANES), shape(nodes, LANES), shape(ny, L...]
  transfers between devices with their start and end apart: 7 -> 16, of which waited for: 2 -> 5; matrix products, arithmetic and copies ran while one was open for 0% -> 0% of each run, Pallas kernels for 13% -> 11%
where the time goes in v15:
time: 34.2 us; the launch traced here: 34 us
  starting transfers between devices  17.9 us (52%)
  waiting for transfers between devices  7.9 us (23%)
  Pallas kernels  7.45 us (22%)
  between operations  0.72 us (2%)
    ppermute x10, starting transfers between devices, sum_rounds(): rows.append(lax.ppermute(row, axis, pairs))  10.5 us
    ppermute x6, starting transfers between devices, swap(): return lax.ppermute(array, ('gx', 'gy'), pairs)  7.42 us
    ppermute x10, waiting for transfers between devices, sum_rounds(): rows.append(lax.ppermute(row, axis, pairs))  5.06 us
    ppermute x6, waiting for transfers between devices, swap(): return lax.ppermute(array, ('gx', 'gy'), pairs)  2.84 us
    pallas_call x1, Pallas kernels, per_device(): call(inner_kernel, (shape(nx * s.pitch, LANES),) + (rows,) * 2 + (field,)...  2.79 us
    pallas_call x1, Pallas kernels, per_device(): call(pack_kernel, (shape(nodes, LANES), shape(nx * ny, LANES), face), in_...  1.56 us
    pallas_call x1, Pallas kernels, per_device(): call(finish_kernel, (whole, whole), out_specs=(hbm, hbm), scratch_shapes=...  1.26 us
    pallas_call x1, Pallas kernels, per_device(): call(outer_kernel, (shape(nodes, LANES), shape(nodes, LANES), shape(ny, L...  0.83 us
  transfers between devices with their start and end apart: 16, of which 5 were waited for; matrix products, arithmetic and copies ran while one was open for 0% of the time, Pallas kernels for 11%

profile of v15, /device:TPU:0, one launch (start us, length us, event | category | flops | bytes accessed | tf_op | source)
XLA Modules:
  0.0 34.0 jit_solution(2610241011119056688)
XLA Ops:
  0.6 1.6 %shard_map.41 = (f32[1024,128]{1,0:T(8,128)S(1)}, f32[128,128]{1,0:T(8,128)S(1)}, f32[240,128]{1,0:T(8,128)S(1)}) custom-call(f32[8,16,768]{2,1,0:T(8,128)} %refs_4_.1, f32[16,768]{1,0:T(8,128)} %d_hbm.1), custom_call_target="tpu_custom_call" | custom-call | tf_op jit(solution)/shard_map/pallas_call | solution.py:714
  2.2 3.1 %collective-permute-start.3 = (f32[240,128]{1,0:T(8,128)S(1)}, f32[240,128]{1,0:T(8,128)S(1)}, u32[]{:S(2)}, u32[]{:S(2)}) collective-permute-start(f32[240,128]{1,0:T(8,128)S(1)} %get-tuple-element.38), channel_id=1, source_target_pairs={{0,8},{1,2},{2,1},{3,4},{4,3},{5,6},{6,5},{7,15},{8,0},{9,10},{10,... | collective-permute-start | bytes 368648 | tf_op jit(solution)/shard_map/ppermute | solution.py:691
  5.3 0.1 shard_map.42
  5.4 0.1 collective-permute-start.2
  5.5 1.6 %collective-permute-start = (f32[120,128]{1,0:T(8,128)S(1)}, f32[120,128]{1,0:T(8,128)S(1)}, u32[]{:S(2)}, u32[]{:S(2)}) collective-permute-start(f32[120,128]{1,0:T(8,128)S(1)} %get-tuple-element.33), channel_id=1, source_target_pairs={{0,8},{1,9},{2,10},{3,11},{4,12},{5,13},{6,14},{7,15},{8,0},{9,1},... | collective-permute-start | bytes 184328 | tf_op jit(solution)/shard_map/ppermute | solution.py:691
  7.1 0.0 collective-permute-start.1
  7.1 2.8 %collective-permute-done.x1_ref = f32[120,128]{1,0:T(8,128)S(1)} collective-permute-done((f32[120,128]{1,0:T(8,128)S(1)}, f32[120,128]{1,0:T(8,128)S(1)}, u32[]{:S(2)}, u32[]{:S(2)}) %collective-permute-start) | collective-permute-done | bytes 61472 | tf_op jit(solution)/shard_map/ppermute | solution.py:691
  9.9 0.0 collective-permute-done.1.x2_ref
  9.9 0.2 shard_map.43
  10.1 0.1 collective-permute-start.4
  10.2 2.6 %collective-permute-start.5 = (f32[72,128]{1,0:T(8,128)S(1)}, f32[72,128]{1,0:T(8,128)S(1)}, u32[]{:S(2)}, u32[]{:S(2)}) collective-permute-start(f32[72,128]{1,0:T(8,128)S(1)} %get-tuple-element.42), channel_id=1, source_target_pairs={{0,8},{1,2},{2,1},{3,4},{4,3},{5,6},{6,5},{7,15},{8,0},{9,10},{10,... | collective-permute-start | bytes 110600 | tf_op jit(solution)/shard_map/ppermute | solution.py:691
  12.8 0.1 shard_map.44.t2_ref
  12.9 0.0 collective-permute-done.2.y1_ref
  12.9 2.8 %shard_map.45 = (f32[256,128]{1,0:T(8,128)S(1)}, f32[320,128]{1,0:T(8,128)S(1)}, f32[320,128]{1,0:T(8,128)S(1)}, f32[1920,128]{1,0:T(8,128)S(1)}, f32[1920,128]{...) custom-call(f32[1024,128]{1,0:T(8,128)S(1)} %get-tuple-element.31.bt, ...), custom_call_target="tpu_custom_call" | custom-call | tf_op jit(solution)/shard_map/pallas_call | solution.py:738
  15.7 0.8 %shard_map.46 = (f32[1024,128]{1,0:T(8,128)S(1)}, f32[1024,128]{1,0:T(8,128)S(1)}, f32[8,128]{1,0:T(8,128)S(1)}, f32[1,128]{1,0:T(1,128)S(1)}) custom-call(f32[256,128]{1,0:T(8,128)S(1)} %get-tuple-element.39.dens_ref, f32[120,128]{1,0:T(8,128)S(1)} %collective-permute-done.x1_ref, f32[120,128]{1,0:T(8,128)S(1)} %collective-permute-done.1.x2_ref, ...), custom_call_target="tpu_custom_call" | custom-call | tf_op jit(solution)/shard_map/pallas_call | solution.py:746
  16.5 1.1 %collective-permute-start.12 = (f32[1,128]{1,0:T(1,128)S(1)}, f32[1,128]{1,0:T(1,128)S(1)}, u32[]{:S(2)}, u32[]{:S(2)}) collective-permute-start(f32[1,128]{1,0:T(1,128)S(1)} %get-tuple-element.53), channel_id=1, source_target_pairs={{0,7},{1,6},{2,5},{3,4},{4,3},{5,2},{6,1},{7,0},{8,15},{9,14},{10,... | collective-permute-start | bytes 1544 | tf_op jit(solution)/shard_map/ppermute | solution.py:674
  17.6 0.4 %collective-permute-start.11 = (f32[1,128]{1,0:T(1,128)S(1)}, f32[1,128]{1,0:T(1,128)S(1)}, u32[]{:S(2)}, u32[]{:S(2)}) collective-permute-start(f32[1,128]{1,0:T(1,128)S(1)} %get-tuple-element.53), channel_id=1, source_target_pairs={{0,6},{1,7},{2,4},{3,5},{4,2},{5,3},{6,0},{7,1},{8,14},{9,15},{10,... | collective-permute-start | bytes 1544 | tf_op jit(solution)/shard_map/ppermute | solution.py:674
  18.0 1.3 %collective-permute-start.10 = (f32[1,128]{1,0:T(1,128)S(1)}, f32[1,128]{1,0:T(1,128)S(1)}, u32[]{:S(2)}, u32[]{:S(2)}) collective-permute-start(f32[1,128]{1,0:T(1,128)S(1)} %get-tuple-element.53), channel_id=1, source_target_pairs={{0,5},{1,4},{2,7},{3,6},{4,1},{5,0},{6,3},{7,2},{8,13},{9,12},{10,... | collective-permute-start | bytes 1544 | tf_op jit(solution)/shard_map/ppermute | solution.py:674
  19.3 1.7 %collective-permute-start.9 = (f32[1,128]{1,0:T(1,128)S(1)}, f32[1,128]{1,0:T(1,128)S(1)}, u32[]{:S(2)}, u32[]{:S(2)}) collective-permute-start(f32[1,128]{1,0:T(1,128)S(1)} %get-tuple-element.53), channel_id=1, source_target_pairs={{0,4},{1,5},{2,6},{3,7},{4,0},{5,1},{6,2},{7,3},{8,12},{9,13},{10,... | collective-permute-start | bytes 1544 | tf_op jit(solution)/shard_map/ppermute | solution.py:674
  21.0 0.1 collective-permute-start.8
  21.1 0.4 %collective-permute-start.7 = (f32[1,128]{1,0:T(1,128)S(1)}, f32[1,128]{1,0:T(1,128)S(1)}, u32[]{:S(2)}, u32[]{:S(2)}) collective-permute-start(f32[1,128]{1,0:T(1,128)S(1)} %get-tuple-element.53), channel_id=1, source_target_pairs={{0,2},{1,3},{2,0},{3,1},{4,6},{5,7},{6,4},{7,5},{8,10},{9,11},{10,... | collective-permute-start | bytes 1544 | tf_op jit(solution)/shard_map/ppermute | solution.py:674
  21.5 0.6 %collective-permute-done.11 = f32[1,128]{1,0:T(1,128)S(1)} collective-permute-done((f32[1,128]{1,0:T(1,128)S(1)}, f32[1,128]{1,0:T(1,128)S(1)}, u32[]{:S(2)}, u32[]{:S(2)}) %collective-permute-start.11) | collective-permute-done | bytes 544 | tf_op jit(solution)/shard_map/ppermute | solution.py:674
  22.1 0.8 %collective-permute-start.6 = (f32[1,128]{1,0:T(1,128)S(1)}, f32[1,128]{1,0:T(1,128)S(1)}, u32[]{:S(2)}, u32[]{:S(2)}) collective-permute-start(f32[1,128]{1,0:T(1,128)S(1)} %get-tuple-element.53), channel_id=1, source_target_pairs={{0,1},{1,0},{2,3},{3,2},{4,5},{5,4},{6,7},{7,6},{8,9},{9,8},{10,11... | collective-permute-start | bytes 1544 | tf_op jit(solution)/shard_map/ppermute | solution.py:674
  22.8 0.0 collective-permute-done.9
  22.8 1.1 %collective-permute-done.8 = f32[1,128]{1,0:T(1,128)S(1)} collective-permute-done((f32[1,128]{1,0:T(1,128)S(1)}, f32[1,128]{1,0:T(1,128)S(1)}, u32[]{:S(2)}, u32[]{:S(2)}) %collective-permute-start.8) | collective-permute-done | bytes 544 | tf_op jit(solution)/shard_map/ppermute | solution.py:674
  23.9 0.7 %collective-permute-done.7 = f32[1,128]{1,0:T(1,128)S(1)} collective-permute-done((f32[1,128]{1,0:T(1,128)S(1)}, f32[1,128]{1,0:T(1,128)S(1)}, u32[]{:S(2)}, u32[]{:S(2)}) %collective-permute-start.7) | collective-permute-done | bytes 544 | tf_op jit(solution)/shard_map/ppermute | solution.py:674
  24.7 3.7 %collective-permute-start.15 = (f32[1,128]{1,0:T(1,128)S(1)}, f32[1,128]{1,0:T(1,128)S(1)}, u32[]{:S(2)}, u32[]{:S(2)}) collective-permute-start(f32[1,128]{1,0:T(1,128)S(1)} %add_add_fusion.refs_0_), channel_id=1, source_target_pairs={{0,24},{8,16},{16,8},{24,0},{1,25},{9,17},{17,9},{25,1},{2,26},{10... | collective-permute-start | bytes 1544 | tf_op jit(solution)/shard_map/ppermute | solution.py:674
  28.3 0.6 %collective-permute-start.14 = (f32[1,128]{1,0:T(1,128)S(1)}, f32[1,128]{1,0:T(1,128)S(1)}, u32[]{:S(2)}, u32[]{:S(2)}) collective-permute-start(f32[1,128]{1,0:T(1,128)S(1)} %add_add_fusion.refs_0_), channel_id=1, source_target_pairs={{0,16},{8,24},{16,0},{24,8},{1,17},{9,25},{17,1},{25,9},{2,18},{10... | collective-permute-start | bytes 1544 | tf_op jit(solution)/shard_map/ppermute | solution.py:674
  29.0 0.5 %collective-permute-start.13 = (f32[1,128]{1,0:T(1,128)S(1)}, f32[1,128]{1,0:T(1,128)S(1)}, u32[]{:S(2)}, u32[]{:S(2)}) collective-permute-start(f32[1,128]{1,0:T(1,128)S(1)} %add_add_fusion.refs_0_), channel_id=1, source_target_pairs={{0,8},{8,0},{16,24},{24,16},{1,9},{9,1},{17,25},{25,17},{2,10},{10... | collective-permute-start | bytes 1544 | tf_op jit(solution)/shard_map/ppermute | solution.py:674
  29.5 0.6 %shard_map.47 = (f32[8,16,768]{2,1,0:T(8,128)S(1)}, f32[8,16,768]{2,1,0:T(8,128)S(1)}, f32[16,768]{1,0:T(8,128)S(1)}) custom-call(f32[1024,128]{1,0:T(8,128)S(1)} %get-tuple-element.54.q_ref, f32[1024,128]{1,0:T(8,128)S(1)} %get-tuple-element.55.v_ref, f32[320,128]{1,0:T(8,128)S(1)} %get-tuple-element.44.invx1.inv1_ref, f32[8,128]{1,0:T(8,128)S(1)} %get-tuple-element.56.inv2_ref), custom_call_target="tpu_custom_call" | custom-call | tf_op jit(solution)/shard_map/pallas_call | solution.py:762
  30.1 2.7 %collective-permute-done.14.refs_2_ = f32[1,128]{1,0:T(1,128)S(1)} collective-permute-done((f32[1,128]{1,0:T(1,128)S(1)}, f32[1,128]{1,0:T(1,128)S(1)}, u32[]{:S(2)}, u32[]{:S(2)}) %collective-permute-start.14) | collective-permute-done | bytes 544 | tf_op jit(solution)/shard_map/ppermute | solution.py:674
  32.8 1.3 %shard_map.48 = (f32[8,16,768]{2,1,0:T(8,128)}, f32[8,16,768]{2,1,0:T(8,128)}) custom-call(f32[1,128]{1,0:T(1,128)S(1)} %add_add_fusion.refs_0_, f32[1,128]{1,0:T(1,128)S(1)} %collective-permute-done.13.refs_1_, f32[1,128]{1,0:T(1,128)S(1)} %collective-permute-done.14.refs_2_, f32[1,128]{1,0:T(1,128)S(1)} %collective-permute-done.15.refs_3_, ...), custom_call_target="tpu_custom_call" | custom-call | tf_op jit(solution)/shard_map/pallas_call | solution.py:765
  (11 shorter events, 0.0 us)
Async XLA Ops:
  2.2 10.6 %collective-permute-start.3 = (f32[240,128]{1,0:T(8,128)S(1)}, f32[240,128]{1,0:T(8,128)S(1)}, u32[]{:S(2)}, u32[]{:S(2)}) collective-permute-start(f32[240,128]{1,0:T(8,128)S(1)} %get-tuple-element.38), channel_id=1, source_target_pairs={{0,8},{1,2},{2,1},{3,4},{4,3},{5,6},{6,5},{7,15},{8,0},{9,10},{10,... | collective-permute-start | bytes 368648 | tf_op jit(solution)/shard_map/ppermute | solution.py:691
  5.4 7.5 %collective-permute-start.2 = (f32[240,128]{1,0:T(8,128)S(1)}, f32[240,128]{1,0:T(8,128)S(1)}, u32[]{:S(2)}, u32[]{:S(2)}) collective-permute-start(f32[240,128]{1,0:T(8,128)S(1)} %get-tuple-element.37), channel_id=1, source_target_pairs={{0,1},{1,0},{2,3},{3,2},{4,5},{5,4},{6,7},{7,6},{8,9},{9,8},{10,11... | collective-permute-start | bytes 368648 | tf_op jit(solution)/shard_map/ppermute | solution.py:691
  5.5 4.4 %collective-permute-start = (f32[120,128]{1,0:T(8,128)S(1)}, f32[120,128]{1,0:T(8,128)S(1)}, u32[]{:S(2)}, u32[]{:S(2)}) collective-permute-start(f32[120,128]{1,0:T(8,128)S(1)} %get-tuple-element.33), channel_id=1, source_target_pairs={{0,8},{1,9},{2,10},{3,11},{4,12},{5,13},{6,14},{7,15},{8,0},{9,1},... | collective-permute-start | bytes 184328 | tf_op jit(solution)/shard_map/ppermute | solution.py:691
  7.1 2.8 %collective-permute-start.1 = (f32[120,128]{1,0:T(8,128)S(1)}, f32[120,128]{1,0:T(8,128)S(1)}, u32[]{:S(2)}, u32[]{:S(2)}) collective-permute-start(f32[120,128]{1,0:T(8,128)S(1)} %get-tuple-element.34), channel_id=1, source_target_pairs={{0,1},{1,0},{2,3},{3,2},{4,5},{5,4},{6,7},{7,6},{8,16},{9,17},{10,... | collective-permute-start | bytes 184328 | tf_op jit(solution)/shard_map/ppermute | solution.py:691
  10.1 5.6 %collective-permute-start.4 = (f32[72,128]{1,0:T(8,128)S(1)}, f32[72,128]{1,0:T(8,128)S(1)}, u32[]{:S(2)}, u32[]{:S(2)}) collective-permute-start(f32[72,128]{1,0:T(8,128)S(1)} %get-tuple-element.41), channel_id=1, source_target_pairs={{0,1},{1,0},{2,3},{3,2},{4,5},{5,4},{6,7},{7,6},{8,9},{9,8},{10,11... | collective-permute-start | bytes 110600 | tf_op jit(solution)/shard_map/ppermute | solution.py:691
  10.2 5.5 %collective-permute-start.5 = (f32[72,128]{1,0:T(8,128)S(1)}, f32[72,128]{1,0:T(8,128)S(1)}, u32[]{:S(2)}, u32[]{:S(2)}) collective-permute-start(f32[72,128]{1,0:T(8,128)S(1)} %get-tuple-element.42), channel_id=1, source_target_pairs={{0,8},{1,2},{2,1},{3,4},{4,3},{5,6},{6,5},{7,15},{8,0},{9,10},{10,... | collective-permute-start | bytes 110600 | tf_op jit(solution)/shard_map/ppermute | solution.py:691
  16.5 4.6 %collective-permute-start.12 = (f32[1,128]{1,0:T(1,128)S(1)}, f32[1,128]{1,0:T(1,128)S(1)}, u32[]{:S(2)}, u32[]{:S(2)}) collective-permute-start(f32[1,128]{1,0:T(1,128)S(1)} %get-tuple-element.53), channel_id=1, source_target_pairs={{0,7},{1,6},{2,5},{3,4},{4,3},{5,2},{6,1},{7,0},{8,15},{9,14},{10,... | collective-permute-start | bytes 1544 | tf_op jit(solution)/shard_map/ppermute | solution.py:674
  17.6 4.4 %collective-permute-start.11 = (f32[1,128]{1,0:T(1,128)S(1)}, f32[1,128]{1,0:T(1,128)S(1)}, u32[]{:S(2)}, u32[]{:S(2)}) collective-permute-start(f32[1,128]{1,0:T(1,128)S(1)} %get-tuple-element.53), channel_id=1, source_target_pairs={{0,6},{1,7},{2,4},{3,5},{4,2},{5,3},{6,0},{7,1},{8,14},{9,15},{10,... | collective-permute-start | bytes 1544 | tf_op jit(solution)/shard_map/ppermute | solution.py:674
  18.0 4.8 %collective-permute-start.10 = (f32[1,128]{1,0:T(1,128)S(1)}, f32[1,128]{1,0:T(1,128)S(1)}, u32[]{:S(2)}, u32[]{:S(2)}) collective-permute-start(f32[1,128]{1,0:T(1,128)S(1)} %get-tuple-element.53), channel_id=1, source_target_pairs={{0,5},{1,4},{2,7},{3,6},{4,1},{5,0},{6,3},{7,2},{8,13},{9,12},{10,... | collective-permute-start | bytes 1544 | tf_op jit(solution)/shard_map/ppermute | solution.py:674
  19.3 3.5 %collective-permute-start.9 = (f32[1,128]{1,0:T(1,128)S(1)}, f32[1,128]{1,0:T(1,128)S(1)}, u32[]{:S(2)}, u32[]{:S(2)}) collective-permute-start(f32[1,128]{1,0:T(1,128)S(1)} %get-tuple-element.53), channel_id=1, source_target_pairs={{0,4},{1,5},{2,6},{3,7},{4,0},{5,1},{6,2},{7,3},{8,12},{9,13},{10,... | collective-permute-start | bytes 1544 | tf_op jit(solution)/shard_map/ppermute | solution.py:674
  21.0 3.0 %collective-permute-start.8 = (f32[1,128]{1,0:T(1,128)S(1)}, f32[1,128]{1,0:T(1,128)S(1)}, u32[]{:S(2)}, u32[]{:S(2)}) collective-permute-start(f32[1,128]{1,0:T(1,128)S(1)} %get-tuple-element.53), channel_id=1, source_target_pairs={{0,3},{1,2},{2,1},{3,0},{4,7},{5,6},{6,5},{7,4},{8,11},{9,10},{10,... | collective-permute-start | bytes 1544 | tf_op jit(solution)/shard_map/ppermute | solution.py:674
  21.1 3.5 %collective-permute-start.7 = (f32[1,128]{1,0:T(1,128)S(1)}, f32[1,128]{1,0:T(1,128)S(1)}, u32[]{:S(2)}, u32[]{:S(2)}) collective-permute-start(f32[1,128]{1,0:T(1,128)S(1)} %get-tuple-element.53), channel_id=1, source_target_pairs={{0,2},{1,3},{2,0},{3,1},{4,6},{5,7},{6,4},{7,5},{8,10},{9,11},{10,... | collective-permute-start | bytes 1544 | tf_op jit(solution)/shard_map/ppermute | solution.py:674
  22.1 2.6 %collective-permute-start.6 = (f32[1,128]{1,0:T(1,128)S(1)}, f32[1,128]{1,0:T(1,128)S(1)}, u32[]{:S(2)}, u32[]{:S(2)}) collective-permute-start(f32[1,128]{1,0:T(1,128)S(1)} %get-tuple-element.53), channel_id=1, source_target_pairs={{0,1},{1,0},{2,3},{3,2},{4,5},{5,4},{6,7},{7,6},{8,9},{9,8},{10,11... | collective-permute-start | bytes 1544 | tf_op jit(solution)/shard_map/ppermute | solution.py:674
  24.7 5.4 %collective-permute-start.15 = (f32[1,128]{1,0:T(1,128)S(1)}, f32[1,128]{1,0:T(1,128)S(1)}, u32[]{:S(2)}, u32[]{:S(2)}) collective-permute-start(f32[1,128]{1,0:T(1,128)S(1)} %add_add_fusion.refs_0_), channel_id=1, source_target_pairs={{0,24},{8,16},{16,8},{24,0},{1,25},{9,17},{17,9},{25,1},{2,26},{10... | collective-permute-start | bytes 1544 | tf_op jit(solution)/shard_map/ppermute | solution.py:674
  28.3 4.4 %collective-permute-start.14 = (f32[1,128]{1,0:T(1,128)S(1)}, f32[1,128]{1,0:T(1,128)S(1)}, u32[]{:S(2)}, u32[]{:S(2)}) collective-permute-start(f32[1,128]{1,0:T(1,128)S(1)} %add_add_fusion.refs_0_), channel_id=1, source_target_pairs={{0,16},{8,24},{16,0},{24,8},{1,17},{9,25},{17,1},{25,9},{2,18},{10... | collective-permute-start | bytes 1544 | tf_op jit(solution)/shard_map/ppermute | solution.py:674
  29.0 3.8 %collective-permute-start.13 = (f32[1,128]{1,0:T(1,128)S(1)}, f32[1,128]{1,0:T(1,128)S(1)}, u32[]{:S(2)}, u32[]{:S(2)}) collective-permute-start(f32[1,128]{1,0:T(1,128)S(1)} %add_add_fusion.refs_0_), channel_id=1, source_target_pairs={{0,8},{8,0},{16,24},{24,16},{1,9},{9,1},{17,25},{25,17},{2,10},{10... | collective-permute-start | bytes 1544 | tf_op jit(solution)/shard_map/ppermute | solution.py:674
  29.5 3.3 %copy-start = (f32[8,16,768]{2,1,0:T(8,128)S(1)}, f32[8,16,768]{2,1,0:T(8,128)}, u32[]{:S(2)}) copy-start(f32[8,16,768]{2,1,0:T(8,128)} %refs_4_.1) | copy-start | bytes 1179652

commit v16 on v14

--- a/solution.py
+++ b/solution.py
@@ -230,18 +230,21 @@
     )
 
 
-def corner_kernel(s, x1_ref, x2_ref, xt_ref, c1_ref, c2_ref):
+def open_x_kernel(s, x_ref, t_ref):
+    tiles = Tiles(t_ref, s.ny, s.loads)
+    unpack_tiles(
+        x_ref, 0, s.loads, 2 * s.ny, lambda i, tile: [(tiles, (i // s.ny, i % s.ny), tile)]
+    )
+
+
+def corner_kernel(s, x2_ref, t2_ref, x1_ref, t1_ref, c1_ref, c2_ref):
     loads, ny = s.loads, s.ny
-    tiles = Tiles(xt_ref, ny, loads)
-    for side, ref in enumerate((x1_ref, x2_ref)):
-        unpack_tiles(
-            ref, 0, loads, 2 * ny,
-            lambda i, tile: [(tiles, (2 * side + i // ny, i % ny), tile)],
-        )
+    open_x_kernel(s, x1_ref, t1_ref)
+    halves = Tiles(t1_ref, ny, loads), Tiles(t2_ref, ny, loads)
     even_y = is_even("gy")
     for out_ref, upper in ((c2_ref, jnp.logical_not(even_y)), (c1_ref, even_y)):
         y0 = pick(upper, ny - 2, 0)
-        pack_tiles(out_ref, 0, loads, 8, lambda i: tiles[i // 2, y0 + i % 2])
+        pack_tiles(out_ref, 0, loads, 8, lambda i: halves[i // 4][i // 2 % 2, y0 + i % 2])
         y0 = pick(upper, ny - 3, 0)
         batch, at = Batch(18), s.c_dens
         for ref in (x1_ref, x2_ref):
@@ -392,14 +395,12 @@
     return state
 
 
-def inner_kernel(
+def image_kernel(
     s, bt_ref, dt_ref, y1_ref, y2_ref, t2_ref,
-    dens_ref, cond, invx, bx, zx, qx, wx, vx, carry1, carry2, sums_ref,
+    dens_ref, cond, invx, bx, zx, qx, wx, carry1,
 ):
     loads, nx, ny, my, pitch = s.loads, s.nx, s.ny, s.my, s.pitch
-    bx, zx, qx, wx, vx, carry1, carry2 = (
-        Tiles(ref, my, loads) for ref in (bx, zx, qx, wx, vx, carry1, carry2)
-    )
+    bx, zx, qx, wx, carry1 = (Tiles(ref, my, loads) for ref in (bx, zx, qx, wx, carry1))
     cond, invx = Rows(cond, pitch, loads), Rows(invx, pitch, loads)
     join_density(s, dt_ref, y1_ref, y2_ref, dens_ref)
     even_y = is_even("gy")
@@ -443,6 +444,12 @@
         return state
 
     over_planes(4, nx + 1, first, 0)
+
+
+def again_kernel(s, cond, bx, zx, qx, wx, vx, carry2, sums_ref):
+    loads, nx, my = s.loads, s.nx, s.my
+    bx, zx, qx, wx, vx, carry2 = (Tiles(ref, my, loads) for ref in (bx, zx, qx, wx, vx, carry2))
+    cond = Rows(cond, s.pitch, loads)
     element_planes(cond, carry2, 4, 1, 1, my - 3, wx, None)
 
     def second(a, count, sums):
@@ -457,7 +464,7 @@
 
 
 def outer_kernel(
-    s, dens_ref, x1_ref, x2_ref, xt_ref, c1_ref, c2_ref,
+    s, dens_ref, x1_ref, x2_ref, t1_ref, t2_ref, c1_ref, c2_ref,
     cond1, invx1, bx1, zx1, qx1, wx1, vx1, carry1, carry2, sums1,
     q_out, v_out, inv_out, sums_ref,
     low_ref, high_ref, low_d, high_d, cond2, invx2, bx2, zx2, qx2, wx2, vx2, carry3,
@@ -470,14 +477,14 @@
     yd = (pick(even_y, ny + 3, 0), pick(even_y, 0, ny + 3))
 
     def take(near, far):
-        faces = Tiles(xt_ref, ny, loads)
-        for side, (ref, (tiles_ref, into)) in enumerate(((x1_ref, near), (x2_ref, far))):
-            tiles = Tiles(tiles_ref, my, loads)
+        faces = (x1_ref, t1_ref, near), (x2_ref, t2_ref, far)
+        for side, (ref, face_ref, (tiles_ref, into)) in enumerate(faces):
+            face, tiles = Tiles(face_ref, ny, loads), Tiles(tiles_ref, my, loads)
             alone_x = is_alone("gx", s.count_x, side)
             batch = Batch(18)
             for dx in range(2):
                 for y in range(ny):
-                    batch.add(tiles, (dx, y + 2), faces[2 * side + dx, y])
+                    batch.add(tiles, (dx, y + 2), face[dx, y])
             for t in range(3):
                 at = s.x_dens + t * ny
                 rows = jnp.where(alone_x, 0.0, ref[at : at + ny, :])
@@ -704,20 +711,20 @@
     y1, x1, x2 = call(pack_rest_kernel, (face, x_face, x_face))(bt, dt)
     x2, y1, x1 = swap(x2, "gx", 1), swap(y1, "gy", 0), swap(x1, "gx", 0)
     t2 = call(open_y_kernel, shape(2 * nx * loads, LANES))(y2)
-    xt, c1, c2 = call(corner_kernel, (shape(4 * ny * loads, LANES), corner, corner))(x1, x2)
-    xt, dt = lax.optimization_barrier((xt, dt))
-    c2, c1 = swap(c2, "gy", 1), swap(c1, "gy", 0)
     plane = s.my * loads
     rows, field = shape(s.mx * s.pitch, LANES), shape(s.mx * plane, LANES)
     edge = shape(2 * plane, LANES)
-    dens, cond, inv_1, bx, zx, q_1, w_1, v_1, carry1, carry2, sums = call(
-        inner_kernel,
-        (shape(nx * s.pitch, LANES),)
-        + (rows,) * 2
-        + (field,) * 5
-        + (edge,) * 2
-        + (shape(4 * loads, LANES),),
+    dens, cond, inv_1, bx, zx, q_1, w_1, carry1 = call(
+        image_kernel, (shape(nx * s.pitch, LANES),) + (rows,) * 2 + (field,) * 4 + (edge,)
     )(bt, dt, y1, y2, t2)
+    xt = shape(2 * ny * loads, LANES)
+    x2, w_1 = lax.optimization_barrier((x2, w_1))
+    xt2 = call(open_x_kernel, xt)(x2)
+    xt1, c1, c2 = call(corner_kernel, (xt, corner, corner))(x2, xt2, x1)
+    c2, c1 = swap(c2, "gy", 1), swap(c1, "gy", 0)
+    v_1, carry2, sums = call(again_kernel, (field, edge, shape(4 * loads, LANES)))(
+        cond, bx, zx, q_1, w_1
+    )
     q_t, v_t, inv_2, sums = call(
         outer_kernel,
         (
@@ -726,12 +733,13 @@
             shape(ny, LANES),
             shape(devices, 1, LANES),
         ),
+        out_specs=(pl.BlockSpec(memory_space=pltpu.VMEM),) * 4,
         scratch_shapes=[scratch(2 * plane, LANES)] * 2
         + [scratch(3 * s.pitch, LANES)] * 2
         + [scratch(5 * s.pitch, LANES)] * 2
         + [scratch(5 * plane, LANES)] * 5
         + [scratch(2 * plane, LANES)],
-    )(dens, x1, x2, xt, c1, c2, cond, inv_1, bx, zx, q_1, w_1, v_1, carry1, carry2, sums)
+    )(dens, x1, x2, xt1, xt2, c1, c2, cond, inv_1, bx, zx, q_1, w_1, v_1, carry1, carry2, sums)
     parts = lax.all_to_all(sums, ("gx", "gy"), 0, 0, tiled=True)
     whole = shape(loads, nx, flat)
     image, again, inverse = call(unpack_kernel, (whole, whole, shape(nx, flat)))(

time: 29.9 us -> 30.9 us (1.033)
  starting transfers between devices: 11.7 us -> 14.1 us
  waiting for transfers between devices: 9.28 us -> 7.71 us
    ppermute x6, waiting for transfers between devices: 2.84 us -> 1.27 us  [swap(): return lax.ppermute(array, ('gx', 'gy'), pairs)]
    all_to_all x1, starting transfers between devices: 4.28 us -> 5.74 us  [per_device(): parts = lax.all_to_all(sums, ('gx', 'gy'), 0, 0, tiled=True)]
    ppermute x6, starting transfers between devices: 7.42 us -> 8.4 us  [swap(): return lax.ppermute(array, ('gx', 'gy'), pairs)]
    pallas_call x2 -> x4, Pallas kernels: 2.96 us -> 3.13 us  [the longest x1 1.69 us: per_device(): call(image_kernel, (shape(nx * s.pitch, LANES),) + (rows,) * 2 + (field,)...]
  transfers between devices with their start and end apart: 7 -> 7, of which waited for: 2 -> 3; matrix products, arithmetic and copies ran while one was open for 0% -> 0% of each run, Pallas kernels for 13% -> 12%
where the time goes in v16:
time: 30.9 us; the launch traced here: 30.8 us
  starting transfers between devices  14.1 us (46%)
  Pallas kernels  8.19 us (27%)
  waiting for transfers between devices  7.71 us (25%)
  between operations  0.73 us (2%)
    ppermute x6, starting transfers between devices, swap(): return lax.ppermute(array, ('gx', 'gy'), pairs)  8.4 us
    all_to_all x1, waiting for transfers between devices, per_device(): parts = lax.all_to_all(sums, ('gx', 'gy'), 0, 0, tiled=True)  6.44 us
    all_to_all x1, starting transfers between devices, per_device(): parts = lax.all_to_all(sums, ('gx', 'gy'), 0, 0, tiled=True)  5.74 us
    pallas_call x1, Pallas kernels, per_device(): call(image_kernel, (shape(nx * s.pitch, LANES),) + (rows,) * 2 + (field,)...  1.69 us
    pallas_call x1, Pallas kernels, per_device(): call(pack_kernel, (shape(nodes, LANES), shape(nx * ny, LANES), face), in_...  1.56 us
    pallas_call x1, Pallas kernels, per_device(): call(outer_kernel, (shape(nodes, LANES), shape(nodes, LANES), shape(ny, L...  1.44 us
    ppermute x6, waiting for transfers between devices, swap(): return lax.ppermute(array, ('gx', 'gy'), pairs)  1.27 us
    pallas_call x1, Pallas kernels, per_device(): call(finish_kernel, (whole, whole), out_specs=(hbm, hbm), scratch_shapes=...  1.21 us
  transfers between devices with their start and end apart: 7, of which 3 were waited for; matrix products, arithmetic and copies ran while one was open for 0% of the time, Pallas kernels for 12%

profile of v16, /device:TPU:0, one launch (start us, length us, event | category | flops | bytes accessed | tf_op | source)
XLA Modules:
  0.0 30.8 jit_solution(5989660193165025079)
XLA Ops:
  0.6 1.6 %shard_map.41 = (f32[1024,128]{1,0:T(8,128)S(1)}, f32[128,128]{1,0:T(8,128)S(1)}, f32[240,128]{1,0:T(8,128)S(1)}) custom-call(f32[8,16,768]{2,1,0:T(8,128)} %b_ref.1, f32[16,768]{1,0:T(8,128)} %d_hbm.1), custom_call_target="tpu_custom_call" | custom-call | tf_op jit(solution)/shard_map/pallas_call | solution.py:696
  2.2 3.1 %collective-permute-start.1 = (f32[240,128]{1,0:T(8,128)S(1)}, f32[240,128]{1,0:T(8,128)S(1)}, u32[]{:S(2)}, u32[]{:S(2)}) collective-permute-start(f32[240,128]{1,0:T(8,128)S(1)} %get-tuple-element.34), channel_id=1, source_target_pairs={{0,8},{1,2},{2,1},{3,4},{4,3},{5,6},{6,5},{7,15},{8,0},{9,10},{10,... | collective-permute-start | bytes 368648 | tf_op jit(solution)/shard_map/ppermute | solution.py:672
  5.3 0.1 shard_map.42
  5.4 0.1 collective-permute-start
  5.5 0.5 %collective-permute-start.3 = (f32[120,128]{1,0:T(8,128)S(1)}, f32[120,128]{1,0:T(8,128)S(1)}, u32[]{:S(2)}, u32[]{:S(2)}) collective-permute-start(f32[120,128]{1,0:T(8,128)S(1)} %get-tuple-element.37), channel_id=1, source_target_pairs={{0,1},{1,0},{2,3},{3,2},{4,5},{5,4},{6,7},{7,6},{8,16},{9,17},{10,... | collective-permute-start | bytes 184328 | tf_op jit(solution)/shard_map/ppermute | solution.py:672
  6.0 2.7 %collective-permute-start.2 = (f32[120,128]{1,0:T(8,128)S(1)}, f32[120,128]{1,0:T(8,128)S(1)}, u32[]{:S(2)}, u32[]{:S(2)}) collective-permute-start(f32[120,128]{1,0:T(8,128)S(1)} %get-tuple-element.36), channel_id=1, source_target_pairs={{0,8},{1,9},{2,10},{3,11},{4,12},{5,13},{6,14},{7,15},{8,0},{9,1},... | collective-permute-start | bytes 184328 | tf_op jit(solution)/shard_map/ppermute | solution.py:672
  8.7 0.0 collective-permute-done.1.y_ref.y2_ref
  8.7 0.1 shard_map.43.t2_ref
  8.8 0.0 collective-permute-done.y1_ref
  8.8 1.7 %shard_map.44 = (f32[256,128]{1,0:T(8,128)S(1)}, f32[320,128]{1,0:T(8,128)S(1)}, f32[320,128]{1,0:T(8,128)S(1)}, f32[1920,128]{1,0:T(8,128)S(1)}, f32[1920,128]{...) custom-call(f32[1024,128]{1,0:T(8,128)S(1)} %get-tuple-element.31.bt_ref, ...), custom_call_target="tpu_custom_call" | custom-call | tf_op jit(solution)/shard_map/pallas_call | solution.py:717
  10.5 0.0 collective-permute-done.3.x_ref.x2_ref
  10.5 0.1 shard_map.45.t2_ref
  10.6 0.4 %collective-permute-done.2.x1_ref = f32[120,128]{1,0:T(8,128)S(1)} collective-permute-done((f32[120,128]{1,0:T(8,128)S(1)}, f32[120,128]{1,0:T(8,128)S(1)}, u32[]{:S(2)}, u32[]{:S(2)}) %collective-permute-start.2) | collective-permute-done | bytes 61472 | tf_op jit(solution)/shard_map/ppermute | solution.py:672
  11.0 0.2 shard_map.46
  11.2 0.1 collective-permute-start.4
  11.3 2.0 %collective-permute-start.5 = (f32[72,128]{1,0:T(8,128)S(1)}, f32[72,128]{1,0:T(8,128)S(1)}, u32[]{:S(2)}, u32[]{:S(2)}) collective-permute-start(f32[72,128]{1,0:T(8,128)S(1)} %get-tuple-element.42), channel_id=1, source_target_pairs={{0,8},{1,2},{2,1},{3,4},{4,3},{5,6},{6,5},{7,15},{8,0},{9,10},{10,... | collective-permute-start | bytes 110600 | tf_op jit(solution)/shard_map/ppermute | solution.py:672
  13.2 1.2 %shard_map.47 = (f32[1920,128]{1,0:T(8,128)S(1)}, f32[192,128]{1,0:T(8,128)S(1)}, f32[32,128]{1,0:T(8,128)S(1)}) custom-call(f32[320,128]{1,0:T(8,128)S(1)} %get-tuple-element.43.cond.cond1, f32[1920,128]{1,0:T(8,128)S(1)} %get-tuple-element.45.bx.bx1, f32[1920,128]{1,0:T(8,128)S(1)} %get-tuple-element.46.zx.zx1, f32[1920,128]{1,0:T(8,128)S(1)} %get-tuple-element.47.qx.qx1, ...), custom_call_target="tpu_custom_call" | custom-call | tf_op jit(solution)/shard_map/pallas_call | solution.py:725
  14.4 0.0 collective-permute-done.4.c1_ref
  14.4 0.8 %collective-permute-done.5.c2_ref = f32[72,128]{1,0:T(8,128)S(1)} collective-permute-done((f32[72,128]{1,0:T(8,128)S(1)}, f32[72,128]{1,0:T(8,128)S(1)}, u32[]{:S(2)}, u32[]{:S(2)}) %collective-permute-start.5) | collective-permute-done | bytes 36896 | tf_op jit(solution)/shard_map/ppermute | solution.py:672
  15.3 1.4 %shard_map.48 = (f32[1024,128]{1,0:T(8,128)S(1)}, f32[1024,128]{1,0:T(8,128)S(1)}, f32[8,128]{1,0:T(8,128)S(1)}, f32[32,1,128]{2,1,0:T(1,128)}) custom-call(f32[256,128]{1,0:T(8,128)S(1)} %get-tuple-element.35.dens_ref, f32[120,128]{1,0:T(8,128)S(1)} %collective-permute-done.2.x1_ref, f32[120,128]{1,0:T(8,128)S(1)} %collective-permute-done.3.x_ref.x2_ref, ...), custom_call_target="tpu_custom_call" | custom-call | tf_op jit(solution)/shard_map/pallas_call | solution.py:728
  16.7 5.7 %all-to-all-start = ((f32[32,1,128]{2,1,0:T(1,128)}), f32[32,1,128]{2,1,0:T(1,128)S(1)}, u32[]{:S(2)}, u32[]{:S(2)}) async-start(f32[32,1,128]{2,1,0:T(1,128)} %get-tuple-element.53), calls=%async_computation | async-start | bytes 32768 | tf_op jit(solution)/shard_map/all_to_all | solution.py:743
  22.5 0.0 copy-start
  22.5 0.6 %shard_map.49 = (f32[8,16,768]{2,1,0:T(8,128)S(1)}, f32[8,16,768]{2,1,0:T(8,128)S(1)}, f32[16,768]{1,0:T(8,128)S(1)}) custom-call(f32[1024,128]{1,0:T(8,128)S(1)} %get-tuple-element.54.q_ref, f32[1024,128]{1,0:T(8,128)S(1)} %get-tuple-element.55.v_ref, f32[320,128]{1,0:T(8,128)S(1)} %get-tuple-element.44.invx1.inv1_ref, f32[8,128]{1,0:T(8,128)S(1)} %get-tuple-element.56.inv2_ref), custom_call_target="tpu_custom_call" | custom-call | tf_op jit(solution)/shard_map/pallas_call | solution.py:745
  23.1 6.4 %all-to-all-done.parts_ref = f32[32,1,128]{2,1,0:T(1,128)S(1)} async-done(((f32[32,1,128]{2,1,0:T(1,128)}), f32[32,1,128]{2,1,0:T(1,128)S(1)}, u32[]{:S(2)}, u32[]{:S(2)}) %all-to-all-start) | async-done | bytes 16416 | tf_op jit(solution)/shard_map/all_to_all | solution.py:743
  29.5 0.0 copy-done
  29.6 1.2 %shard_map.50 = (f32[8,16,768]{2,1,0:T(8,128)}, f32[8,16,768]{2,1,0:T(8,128)}) custom-call(f32[32,1,128]{2,1,0:T(1,128)S(1)} %all-to-all-done.parts_ref, f32[8,16,768]{2,1,0:T(8,128)S(1)} %copy-done, f32[8,16,768]{2,1,0:T(8,128)S(1)} %get-tuple-element.57.q_ref, f32[8,16,768]{2,1,0:T(8,128)S(1)} %get-tuple-element.58.v_ref, ...), custom_call_target="tpu_custom_call" | custom-call | tf_op jit(solution)/shard_map/pallas_call | solution.py:748
Async XLA Ops:
  2.2 6.5 %collective-permute-start.1 = (f32[240,128]{1,0:T(8,128)S(1)}, f32[240,128]{1,0:T(8,128)S(1)}, u32[]{:S(2)}, u32[]{:S(2)}) collective-permute-start(f32[240,128]{1,0:T(8,128)S(1)} %get-tuple-element.34), channel_id=1, source_target_pairs={{0,8},{1,2},{2,1},{3,4},{4,3},{5,6},{6,5},{7,15},{8,0},{9,10},{10,... | collective-permute-start | bytes 368648 | tf_op jit(solution)/shard_map/ppermute | solution.py:672
  5.4 3.4 %collective-permute-start = (f32[240,128]{1,0:T(8,128)S(1)}, f32[240,128]{1,0:T(8,128)S(1)}, u32[]{:S(2)}, u32[]{:S(2)}) collective-permute-start(f32[240,128]{1,0:T(8,128)S(1)} %get-tuple-element.33), channel_id=1, source_target_pairs={{0,1},{1,0},{2,3},{3,2},{4,5},{5,4},{6,7},{7,6},{8,9},{9,8},{10,11... | collective-permute-start | bytes 368648 | tf_op jit(solution)/shard_map/ppermute | solution.py:672
  5.5 5.0 %collective-permute-start.3 = (f32[120,128]{1,0:T(8,128)S(1)}, f32[120,128]{1,0:T(8,128)S(1)}, u32[]{:S(2)}, u32[]{:S(2)}) collective-permute-start(f32[120,128]{1,0:T(8,128)S(1)} %get-tuple-element.37), channel_id=1, source_target_pairs={{0,1},{1,0},{2,3},{3,2},{4,5},{5,4},{6,7},{7,6},{8,16},{9,17},{10,... | collective-permute-start | bytes 184328 | tf_op jit(solution)/shard_map/ppermute | solution.py:672
  6.0 5.1 %collective-permute-start.2 = (f32[120,128]{1,0:T(8,128)S(1)}, f32[120,128]{1,0:T(8,128)S(1)}, u32[]{:S(2)}, u32[]{:S(2)}) collective-permute-start(f32[120,128]{1,0:T(8,128)S(1)} %get-tuple-element.36), channel_id=1, source_target_pairs={{0,8},{1,9},{2,10},{3,11},{4,12},{5,13},{6,14},{7,15},{8,0},{9,1},... | collective-permute-start | bytes 184328 | tf_op jit(solution)/shard_map/ppermute | solution.py:672
  11.2 3.2 %collective-permute-start.4 = (f32[72,128]{1,0:T(8,128)S(1)}, f32[72,128]{1,0:T(8,128)S(1)}, u32[]{:S(2)}, u32[]{:S(2)}) collective-permute-start(f32[72,128]{1,0:T(8,128)S(1)} %get-tuple-element.41), channel_id=1, source_target_pairs={{0,1},{1,0},{2,3},{3,2},{4,5},{5,4},{6,7},{7,6},{8,9},{9,8},{10,11... | collective-permute-start | bytes 110600 | tf_op jit(solution)/shard_map/ppermute | solution.py:672
  11.3 4.0 %collective-permute-start.5 = (f32[72,128]{1,0:T(8,128)S(1)}, f32[72,128]{1,0:T(8,128)S(1)}, u32[]{:S(2)}, u32[]{:S(2)}) collective-permute-start(f32[72,128]{1,0:T(8,128)S(1)} %get-tuple-element.42), channel_id=1, source_target_pairs={{0,8},{1,2},{2,1},{3,4},{4,3},{5,6},{6,5},{7,15},{8,0},{9,10},{10,... | collective-permute-start | bytes 110600 | tf_op jit(solution)/shard_map/ppermute | solution.py:672
  16.7 12.8 %all-to-all-start = ((f32[32,1,128]{2,1,0:T(1,128)}), f32[32,1,128]{2,1,0:T(1,128)S(1)}, u32[]{:S(2)}, u32[]{:S(2)}) async-start(f32[32,1,128]{2,1,0:T(1,128)} %get-tuple-element.53), calls=%async_computation | async-start | bytes 32768 | tf_op jit(solution)/shard_map/all_to_all | solution.py:743
  22.5 7.1 %copy-start = (f32[8,16,768]{2,1,0:T(8,128)S(1)}, f32[8,16,768]{2,1,0:T(8,128)}, u32[]{:S(2)}) copy-start(f32[8,16,768]{2,1,0:T(8,128)} %b_ref.1) | copy-start | bytes 1179652

commit v17 on v16

--- a/solution.py
+++ b/solution.py
@@ -369,8 +369,9 @@
 
 
 class Second:
-    def __init__(self, bx, zx, qx, vx, sums):
-        self.bx, self.zx, self.qx, self.vx, self.sums = bx, zx, qx, vx, sums
+    def __init__(self, bx, zx, qx, q_out, v_out, sums):
+        self.bx, self.zx, self.qx, self.sums = bx, zx, qx, sums
+        self.q_out, self.v_out = q_out, v_out
 
     def fetch(self, x, y):
         return self.bx[x, y], self.zx[x, y], self.qx[x, y]
@@ -384,7 +385,8 @@
         sums[1] = sums[1] + source * change
         sums[2] = sums[2] + (source - image) * change
         sums[3] = sums[3] + (image - again) * change
-        return [(self.vx, (x, y), again)]
+        at = x - 2, y - 2
+        return [(self.q_out, at, image), (self.v_out, at, again)]
 
 
 def over_planes(start, stop, body, state):
@@ -395,12 +397,15 @@
     return state
 
 
-def image_kernel(
+def inner_kernel(
     s, bt_ref, dt_ref, y1_ref, y2_ref, t2_ref,
-    dens_ref, cond, invx, bx, zx, qx, wx, carry1,
+    dens_ref, cond, invx, bx, zx, qx, wx, q_out, v_out, carry1, carry2, sums_ref,
 ):
     loads, nx, ny, my, pitch = s.loads, s.nx, s.ny, s.my, s.pitch
-    bx, zx, qx, wx, carry1 = (Tiles(ref, my, loads) for ref in (bx, zx, qx, wx, carry1))
+    bx, zx, qx, wx, carry1, carry2 = (
+        Tiles(ref, my, loads) for ref in (bx, zx, qx, wx, carry1, carry2)
+    )
+    q_out, v_out = Tiles(q_out, ny, loads), Tiles(v_out, ny, loads)
     cond, invx = Rows(cond, pitch, loads), Rows(invx, pitch, loads)
     join_density(s, dt_ref, y1_ref, y2_ref, dens_ref)
     even_y = is_even("gy")
@@ -444,17 +449,12 @@
         return state
 
     over_planes(4, nx + 1, first, 0)
-
-
-def again_kernel(s, cond, bx, zx, qx, wx, vx, carry2, sums_ref):
-    loads, nx, my = s.loads, s.nx, s.my
-    bx, zx, qx, wx, vx, carry2 = (Tiles(ref, my, loads) for ref in (bx, zx, qx, wx, vx, carry2))
-    cond = Rows(cond, s.pitch, loads)
     element_planes(cond, carry2, 4, 1, 1, my - 3, wx, None)
 
     def second(a, count, sums):
         sums = list(sums)
-        element_planes(cond, carry2, a, count, 1, my - 3, wx, Second(bx, zx, qx, vx, sums))
+        emitter = Second(bx, zx, qx, q_out, v_out, sums)
+        element_planes(cond, carry2, a, count, 1, my - 3, wx, emitter)
         return tuple(sums)
 
     zero = jnp.zeros((loads, LANES), jnp.float32)
@@ -465,9 +465,9 @@
 
 def outer_kernel(
     s, dens_ref, x1_ref, x2_ref, t1_ref, t2_ref, c1_ref, c2_ref,
-    cond1, invx1, bx1, zx1, qx1, wx1, vx1, carry1, carry2, sums1,
+    cond1, invx1, bx1, zx1, qx1, wx1, carry1, carry2, sums1,
     q_out, v_out, inv_out, sums_ref,
-    low_ref, high_ref, low_d, high_d, cond2, invx2, bx2, zx2, qx2, wx2, vx2, carry3,
+    low_ref, high_ref, low_d, high_d, cond2, invx2, bx2, zx2, qx2, wx2, carry3,
 ):
     loads, nx, ny, mx, my, pitch = s.loads, s.nx, s.ny, s.mx, s.my, s.pitch
     even_x = is_even("gx")
@@ -525,7 +525,8 @@
     cond, invx = joined_rows(cond2, cond1, outside), joined_rows(invx2, invx1, scaled_own)
     bx, zx = joined(bx2, bx1, outside), joined(zx2, zx1, scaled_own)
     qx, wx = joined(qx2, qx1, image_own), joined(wx2, wx1, image_own)
-    vx = joined(vx2, vx1, again_planes(nx))
+    own = [x - 2 for x in outer_planes(nx)]
+    q_out, v_out = (Joined(Tiles(ref, ny, loads), None, own) for ref in (q_out, v_out))
     carry1, carry2, carry3 = (Tiles(ref, my, loads) for ref in (carry1, carry2, carry3))
 
     def conduct(ref, x):
@@ -561,19 +562,11 @@
     element_planes(cond, carry3, 3, 1, 0, my - 1, zx, emitter, keep=False)
     element_planes(cond, carry1, nx + 1, 2, 0, my - 1, zx, emitter, keep=False)
     sums = [sums1[place * loads : (place + 1) * loads, :] for place in range(4)]
-    emitter = Second(bx, zx, qx, vx, sums)
+    emitter = Second(bx, zx, qx, q_out, v_out, sums)
     element_planes(cond, carry3, 1, 1, 1, my - 3, wx, None)
     element_planes(cond, carry3, 2, 2, 1, my - 3, wx, emitter)
     element_planes(cond, carry3, 4, 1, 1, my - 3, wx, emitter, keep=False)
     element_planes(cond, carry2, nx, 2, 1, my - 3, wx, emitter, keep=False)
-    for field, out in ((qx, q_out), (vx, v_out)):
-        out = Tiles(out, ny, loads)
-        batch = Batch()
-        for x in range(nx):
-            for y in range(ny):
-                batch.add(out, (x, y), field[x + 2, y + 2])
-        batch.flush()
-
     lane = lane_ids(loads)
     load = lax.broadcasted_iota(jnp.int32, (loads, LANES), 0)
     packed = jnp.zeros((loads, LANES), jnp.float32)
@@ -584,12 +577,26 @@
     sums_ref[...] = jnp.broadcast_to(row[None], sums_ref.shape)
 
 
-def again_planes(nx):
+def outer_planes(nx):
     return (2, 3, 4, nx, nx + 1)
 
 
-def unpack_kernel(s, q_ref, v_ref, inv1_ref, inv2_ref, qo_ref, vo_ref, io_ref):
+def unpack_kernel(
+    s, q1_ref, q2_ref, v1_ref, v2_ref, inv1_ref, inv2_ref, qo_ref, vo_ref, io_ref, q_ref, v_ref
+):
     loads, nx, ny = s.loads, s.nx, s.ny
+    batch = Batch()
+    planes = outer_planes(nx)
+    for first, second, whole in ((q1_ref, q2_ref, q_ref), (v1_ref, v2_ref, v_ref)):
+        first, second = Tiles(first, ny, loads), Tiles(second, ny, loads)
+        whole = Tiles(whole, ny, loads)
+        for x in range(nx):
+            for y in range(ny):
+                if x + 2 in planes:
+                    batch.add(whole, (x, y), second[planes.index(x + 2), y])
+                else:
+                    batch.add(whole, (x, y), first[x, y])
+    batch.flush()
     batch = Batch()
     for x0 in range(0, nx, SUB):
         for ref, out in ((q_ref, qo_ref), (v_ref, vo_ref)):
@@ -711,40 +718,41 @@
     y1, x1, x2 = call(pack_rest_kernel, (face, x_face, x_face))(bt, dt)
     x2, y1, x1 = swap(x2, "gx", 1), swap(y1, "gy", 0), swap(x1, "gx", 0)
     t2 = call(open_y_kernel, shape(2 * nx * loads, LANES))(y2)
+    xt = shape(2 * ny * loads, LANES)
+    xt2 = call(open_x_kernel, xt)(x2)
+    xt1, c1, c2 = call(corner_kernel, (xt, corner, corner))(x2, xt2, x1)
+    xt1, dt = lax.optimization_barrier((xt1, dt))
+    c2, c1 = swap(c2, "gy", 1), swap(c1, "gy", 0)
     plane = s.my * loads
     rows, field = shape(s.mx * s.pitch, LANES), shape(s.mx * plane, LANES)
     edge = shape(2 * plane, LANES)
-    dens, cond, inv_1, bx, zx, q_1, w_1, carry1 = call(
-        image_kernel, (shape(nx * s.pitch, LANES),) + (rows,) * 2 + (field,) * 4 + (edge,)
+    inside = shape(nodes, LANES)
+    dens, cond, inv_1, bx, zx, q_x, w_x, q_1, v_1, carry1, carry2, sums = call(
+        inner_kernel,
+        (shape(nx * s.pitch, LANES),)
+        + (rows,) * 2
+        + (field,) * 4
+        + (inside,) * 2
+        + (edge,) * 2
+        + (shape(4 * loads, LANES),),
     )(bt, dt, y1, y2, t2)
-    xt = shape(2 * ny * loads, LANES)
-    x2, w_1 = lax.optimization_barrier((x2, w_1))
-    xt2 = call(open_x_kernel, xt)(x2)
-    xt1, c1, c2 = call(corner_kernel, (xt, corner, corner))(x2, xt2, x1)
-    c2, c1 = swap(c2, "gy", 1), swap(c1, "gy", 0)
-    v_1, carry2, sums = call(again_kernel, (field, edge, shape(4 * loads, LANES)))(
-        cond, bx, zx, q_1, w_1
-    )
-    q_t, v_t, inv_2, sums = call(
+    ends = shape(len(outer_planes(nx)) * ny * loads, LANES)
+    q_2, v_2, inv_2, sums = call(
         outer_kernel,
-        (
-            shape(nodes, LANES),
-            shape(nodes, LANES),
-            shape(ny, LANES),
-            shape(devices, 1, LANES),
-        ),
-        out_specs=(pl.BlockSpec(memory_space=pltpu.VMEM),) * 4,
+        (ends, ends, shape(ny, LANES), shape(devices, 1, LANES)),
         scratch_shapes=[scratch(2 * plane, LANES)] * 2
         + [scratch(3 * s.pitch, LANES)] * 2
         + [scratch(5 * s.pitch, LANES)] * 2
-        + [scratch(5 * plane, LANES)] * 5
+        + [scratch(5 * plane, LANES)] * 4
         + [scratch(2 * plane, LANES)],
-    )(dens, x1, x2, xt1, xt2, c1, c2, cond, inv_1, bx, zx, q_1, w_1, v_1, carry1, carry2, sums)
+    )(dens, x1, x2, xt1, xt2, c1, c2, cond, inv_1, bx, zx, q_x, w_x, carry1, carry2, sums)
     parts = lax.all_to_all(sums, ("gx", "gy"), 0, 0, tiled=True)
     whole = shape(loads, nx, flat)
-    image, again, inverse = call(unpack_kernel, (whole, whole, shape(nx, flat)))(
-        q_t, v_t, inv_1, inv_2
-    )
+    image, again, inverse = call(
+        unpack_kernel,
+        (whole, whole, shape(nx, flat)),
+        scratch_shapes=[scratch(nodes, LANES)] * 2,
+    )(q_1, q_2, v_1, v_2, inv_1, inv_2)
     return call(
         finish_kernel,
         (whole, whole),

time: 30.9 us -> 29.5 us (0.955)
  starting transfers between devices: 14.1 us -> 11.8 us
  waiting for transfers between devices: 7.71 us -> 8.57 us
    all_to_all x1, starting transfers between devices: 5.74 us -> 3.44 us  [per_device(): parts = lax.all_to_all(sums, ('gx', 'gy'), 0, 0, tiled=True)]
    ppermute x6, waiting for transfers between devices: 1.27 us -> 2.25 us  [swap(): return lax.ppermute(array, ('gx', 'gy'), pairs)]
    pallas_call x4 -> x3, Pallas kernels: 4.95 us -> 4.96 us  [the longest x1 2.78 us: per_device(): call(inner_kernel, (shape(nx * s.pitch, LANES),) + (rows,) * 2 + (field,)...]
  transfers between devices with their start and end apart: 7 -> 7, of which waited for: 3 -> 2; matrix products, arithmetic and copies ran while one was open for 0% -> 0% of each run, Pallas kernels for 12% -> 14%
where the time goes in v17:
time: 29.5 us; the launch traced here: 29.3 us
  starting transfers between devices  11.8 us (40%)
  waiting for transfers between devices  8.57 us (29%)
  Pallas kernels  8.19 us (28%)
  between operations  0.72 us (2%)
    ppermute x6, starting transfers between devices, swap(): return lax.ppermute(array, ('gx', 'gy'), pairs)  8.4 us
    all_to_all x1, waiting for transfers between devices, per_device(): parts = lax.all_to_all(sums, ('gx', 'gy'), 0, 0, tiled=True)  6.32 us
    all_to_all x1, starting transfers between devices, per_device(): parts = lax.all_to_all(sums, ('gx', 'gy'), 0, 0, tiled=True)  3.44 us
    pallas_call x1, Pallas kernels, per_device(): call(inner_kernel, (shape(nx * s.pitch, LANES),) + (rows,) * 2 + (field,)...  2.78 us
    ppermute x6, waiting for transfers between devices, swap(): return lax.ppermute(array, ('gx', 'gy'), pairs)  2.25 us
    pallas_call x1, Pallas kernels, per_device(): call(pack_kernel, (shape(nodes, LANES), shape(nx * ny, LANES), face), in_...  1.56 us
    pallas_call x1, Pallas kernels, per_device(): call(outer_kernel, (ends, ends, shape(ny, LANES), shape(devices, 1, LANES...  1.44 us
    pallas_call x1, Pallas kernels, per_device(): call(finish_kernel, (whole, whole), out_specs=(hbm, hbm), scratch_shapes=...  1.21 us
  transfers between devices with their start and end apart: 7, of which 2 were waited for; matrix products, arithmetic and copies ran while one was open for 0% of the time, Pallas kernels for 14%

profile of v17, /device:TPU:0, one launch (start us, length us, event | category | flops | bytes accessed | tf_op | source)
XLA Modules:
  0.0 29.3 jit_solution(548257940934956159)
XLA Ops:
  0.6 1.6 %shard_map.41 = (f32[1024,128]{1,0:T(8,128)S(1)}, f32[128,128]{1,0:T(8,128)S(1)}, f32[240,128]{1,0:T(8,128)S(1)}) custom-call(f32[8,16,768]{2,1,0:T(8,128)} %b_ref.1, f32[16,768]{1,0:T(8,128)} %d_hbm.1), custom_call_target="tpu_custom_call" | custom-call | tf_op jit(solution)/shard_map/pallas_call | solution.py:703
  2.2 3.1 %collective-permute-start.3 = (f32[240,128]{1,0:T(8,128)S(1)}, f32[240,128]{1,0:T(8,128)S(1)}, u32[]{:S(2)}, u32[]{:S(2)}) collective-permute-start(f32[240,128]{1,0:T(8,128)S(1)} %get-tuple-element.39), channel_id=1, source_target_pairs={{0,8},{1,2},{2,1},{3,4},{4,3},{5,6},{6,5},{7,15},{8,0},{9,10},{10,... | collective-permute-start | bytes 368648 | tf_op jit(solution)/shard_map/ppermute | solution.py:679
  5.3 0.1 shard_map.42
  5.4 0.1 collective-permute-start.2
  5.5 0.5 %collective-permute-start = (f32[120,128]{1,0:T(8,128)S(1)}, f32[120,128]{1,0:T(8,128)S(1)}, u32[]{:S(2)}, u32[]{:S(2)}) collective-permute-start(f32[120,128]{1,0:T(8,128)S(1)} %get-tuple-element.34), channel_id=1, source_target_pairs={{0,1},{1,0},{2,3},{3,2},{4,5},{5,4},{6,7},{7,6},{8,16},{9,17},{10,... | collective-permute-start | bytes 184328 | tf_op jit(solution)/shard_map/ppermute | solution.py:679
  6.0 2.7 %collective-permute-start.1 = (f32[120,128]{1,0:T(8,128)S(1)}, f32[120,128]{1,0:T(8,128)S(1)}, u32[]{:S(2)}, u32[]{:S(2)}) collective-permute-start(f32[120,128]{1,0:T(8,128)S(1)} %get-tuple-element.35), channel_id=1, source_target_pairs={{0,8},{1,9},{2,10},{3,11},{4,12},{5,13},{6,14},{7,15},{8,0},{9,1},... | collective-permute-start | bytes 184328 | tf_op jit(solution)/shard_map/ppermute | solution.py:679
  8.7 0.0 collective-permute-done.x_ref.x2_ref
  8.7 0.1 shard_map.43.t2_ref
  8.8 2.2 %collective-permute-done.1.x1_ref = f32[120,128]{1,0:T(8,128)S(1)} collective-permute-done((f32[120,128]{1,0:T(8,128)S(1)}, f32[120,128]{1,0:T(8,128)S(1)}, u32[]{:S(2)}, u32[]{:S(2)}) %collective-permute-start.1) | collective-permute-done | bytes 61472 | tf_op jit(solution)/shard_map/ppermute | solution.py:679
  11.0 0.2 shard_map.44
  11.2 0.1 collective-permute-start.4
  11.3 2.0 %collective-permute-start.5 = (f32[72,128]{1,0:T(8,128)S(1)}, f32[72,128]{1,0:T(8,128)S(1)}, u32[]{:S(2)}, u32[]{:S(2)}) collective-permute-start(f32[72,128]{1,0:T(8,128)S(1)} %get-tuple-element.43), channel_id=1, source_target_pairs={{0,8},{1,2},{2,1},{3,4},{4,3},{5,6},{6,5},{7,15},{8,0},{9,10},{10,... | collective-permute-start | bytes 110600 | tf_op jit(solution)/shard_map/ppermute | solution.py:679
  13.2 0.0 collective-permute-done.3.y_ref.y2_ref
  13.2 0.1 shard_map.45.t2_ref
  13.3 0.0 collective-permute-done.2.y1_ref
  13.3 2.8 %shard_map.46 = (f32[256,128]{1,0:T(8,128)S(1)}, f32[320,128]{1,0:T(8,128)S(1)}, f32[320,128]{1,0:T(8,128)S(1)}, f32[1920,128]{1,0:T(8,128)S(1)}, f32[1920,128]{...) custom-call(f32[1024,128]{1,0:T(8,128)S(1)} %get-tuple-element.32.bt, ...), custom_call_target="tpu_custom_call" | custom-call | tf_op jit(solution)/shard_map/pallas_call | solution.py:730
  16.1 0.0 collective-permute-done.4.c1_ref
  16.1 0.0 collective-permute-done.5.c2_ref
  16.1 1.4 %shard_map.47 = (f32[320,128]{1,0:T(8,128)S(1)}, f32[320,128]{1,0:T(8,128)S(1)}, f32[8,128]{1,0:T(8,128)S(1)}, f32[32,1,128]{2,1,0:T(1,128)}) custom-call(f32[256,128]{1,0:T(8,128)S(1)} %get-tuple-element.40.dens_ref, f32[120,128]{1,0:T(8,128)S(1)} %collective-permute-done.1.x1_ref, f32[120,128]{1,0:T(8,128)S(1)} %collective-permute-done.x_ref.x2_ref, ...), custom_call_target="tpu_custom_call" | custom-call | tf_op jit(solution)/shard_map/pallas_call | solution.py:740
  17.6 3.4 %all-to-all-start = ((f32[32,1,128]{2,1,0:T(1,128)}), f32[32,1,128]{2,1,0:T(1,128)S(1)}, u32[]{:S(2)}, u32[]{:S(2)}) async-start(f32[32,1,128]{2,1,0:T(1,128)} %get-tuple-element.53), calls=%async_computation | async-start | bytes 32768 | tf_op jit(solution)/shard_map/all_to_all | solution.py:749
  21.0 0.0 copy-start
  21.0 0.7 %shard_map.48 = (f32[8,16,768]{2,1,0:T(8,128)S(1)}, f32[8,16,768]{2,1,0:T(8,128)S(1)}, f32[16,768]{1,0:T(8,128)S(1)}) custom-call(f32[1024,128]{1,0:T(8,128)S(1)} %get-tuple-element.54.q1_ref, f32[320,128]{1,0:T(8,128)S(1)} %get-tuple-element.55.q2_ref, f32[1024,128]{1,0:T(8,128)S(1)} %get-tuple-element.56.v1_ref, f32[320,128]{1,0:T(8,128)S(1)} %get-tuple-element.57.v2_ref, ...), custom_call_target="tpu_custom_call" | custom-call | tf_op jit(solution)/shard_map/pallas_call | solution.py:751
  21.8 6.3 %all-to-all-done.parts_ref = f32[32,1,128]{2,1,0:T(1,128)S(1)} async-done(((f32[32,1,128]{2,1,0:T(1,128)}), f32[32,1,128]{2,1,0:T(1,128)S(1)}, u32[]{:S(2)}, u32[]{:S(2)}) %all-to-all-start) | async-done | bytes 16416 | tf_op jit(solution)/shard_map/all_to_all | solution.py:749
  28.1 0.0 copy-done
  28.1 1.2 %shard_map.49 = (f32[8,16,768]{2,1,0:T(8,128)}, f32[8,16,768]{2,1,0:T(8,128)}) custom-call(f32[32,1,128]{2,1,0:T(1,128)S(1)} %all-to-all-done.parts_ref, f32[8,16,768]{2,1,0:T(8,128)S(1)} %copy-done, f32[8,16,768]{2,1,0:T(8,128)S(1)} %get-tuple-element.59.q_ref, f32[8,16,768]{2,1,0:T(8,128)S(1)} %get-tuple-element.60.v_ref, ...), custom_call_target="tpu_custom_call" | custom-call | tf_op jit(solution)/shard_map/pallas_call | solution.py:756
Async XLA Ops:
  2.2 11.0 %collective-permute-start.3 = (f32[240,128]{1,0:T(8,128)S(1)}, f32[240,128]{1,0:T(8,128)S(1)}, u32[]{:S(2)}, u32[]{:S(2)}) collective-permute-start(f32[240,128]{1,0:T(8,128)S(1)} %get-tuple-element.39), channel_id=1, source_target_pairs={{0,8},{1,2},{2,1},{3,4},{4,3},{5,6},{6,5},{7,15},{8,0},{9,10},{10,... | collective-permute-start | bytes 368648 | tf_op jit(solution)/shard_map/ppermute | solution.py:679
  5.4 7.9 %collective-permute-start.2 = (f32[240,128]{1,0:T(8,128)S(1)}, f32[240,128]{1,0:T(8,128)S(1)}, u32[]{:S(2)}, u32[]{:S(2)}) collective-permute-start(f32[240,128]{1,0:T(8,128)S(1)} %get-tuple-element.38), channel_id=1, source_target_pairs={{0,1},{1,0},{2,3},{3,2},{4,5},{5,4},{6,7},{7,6},{8,9},{9,8},{10,11... | collective-permute-start | bytes 368648 | tf_op jit(solution)/shard_map/ppermute | solution.py:679
  5.5 3.2 %collective-permute-start = (f32[120,128]{1,0:T(8,128)S(1)}, f32[120,128]{1,0:T(8,128)S(1)}, u32[]{:S(2)}, u32[]{:S(2)}) collective-permute-start(f32[120,128]{1,0:T(8,128)S(1)} %get-tuple-element.34), channel_id=1, source_target_pairs={{0,1},{1,0},{2,3},{3,2},{4,5},{5,4},{6,7},{7,6},{8,16},{9,17},{10,... | collective-permute-start | bytes 184328 | tf_op jit(solution)/shard_map/ppermute | solution.py:679
  6.0 5.1 %collective-permute-start.1 = (f32[120,128]{1,0:T(8,128)S(1)}, f32[120,128]{1,0:T(8,128)S(1)}, u32[]{:S(2)}, u32[]{:S(2)}) collective-permute-start(f32[120,128]{1,0:T(8,128)S(1)} %get-tuple-element.35), channel_id=1, source_target_pairs={{0,8},{1,9},{2,10},{3,11},{4,12},{5,13},{6,14},{7,15},{8,0},{9,1},... | collective-permute-start | bytes 184328 | tf_op jit(solution)/shard_map/ppermute | solution.py:679
  11.2 4.9 %collective-permute-start.4 = (f32[72,128]{1,0:T(8,128)S(1)}, f32[72,128]{1,0:T(8,128)S(1)}, u32[]{:S(2)}, u32[]{:S(2)}) collective-permute-start(f32[72,128]{1,0:T(8,128)S(1)} %get-tuple-element.42), channel_id=1, source_target_pairs={{0,1},{1,0},{2,3},{3,2},{4,5},{5,4},{6,7},{7,6},{8,9},{9,8},{10,11... | collective-permute-start | bytes 110600 | tf_op jit(solution)/shard_map/ppermute | solution.py:679
  11.3 4.9 %collective-permute-start.5 = (f32[72,128]{1,0:T(8,128)S(1)}, f32[72,128]{1,0:T(8,128)S(1)}, u32[]{:S(2)}, u32[]{:S(2)}) collective-permute-start(f32[72,128]{1,0:T(8,128)S(1)} %get-tuple-element.43), channel_id=1, source_target_pairs={{0,8},{1,2},{2,1},{3,4},{4,3},{5,6},{6,5},{7,15},{8,0},{9,10},{10,... | collective-permute-start | bytes 110600 | tf_op jit(solution)/shard_map/ppermute | solution.py:679
  17.6 10.5 %all-to-all-start = ((f32[32,1,128]{2,1,0:T(1,128)}), f32[32,1,128]{2,1,0:T(1,128)S(1)}, u32[]{:S(2)}, u32[]{:S(2)}) async-start(f32[32,1,128]{2,1,0:T(1,128)} %get-tuple-element.53), calls=%async_computation | async-start | bytes 32768 | tf_op jit(solution)/shard_map/all_to_all | solution.py:749
  21.0 7.1 %copy-start = (f32[8,16,768]{2,1,0:T(8,128)S(1)}, f32[8,16,768]{2,1,0:T(8,128)}, u32[]{:S(2)}) copy-start(f32[8,16,768]{2,1,0:T(8,128)} %b_ref.1) | copy-start | bytes 1179652

commit v18 on v17

--- a/solution.py
+++ b/solution.py
@@ -157,7 +157,7 @@
     return jnp.where(even, if_even, if_odd)
 
 
-def pack_kernel(s, b_hbm, d_hbm, bt_ref, dt_ref, y2_ref, b_ref, d_ref, sems):
+def pack_kernel(s, b_hbm, d_hbm, bt_ref, dt_ref, x1_ref, x2_ref, b_ref, d_ref, sems):
     loads, nx, ny = s.loads, s.nx, s.ny
     d_copy = pltpu.make_async_copy(d_hbm, d_ref, sems.at[0])
     d_copy.start()
@@ -189,14 +189,15 @@
                 rows = pl.ds((x0 * ny + y) * loads + load, SUB, stride=ny * loads)
                 batch.add(bt_ref, (rows, slice(None)), tile)
         batch.flush()
-    pack_face(s, jnp.logical_not(is_even("gy")), bt_ref, dt_ref, y2_ref)
-
-
-def pack_rest_kernel(s, bt_ref, dt_ref, y1_ref, x1_ref, x2_ref):
     even_x = is_even("gx")
     pack_x_face(s, jnp.logical_not(even_x), bt_ref, dt_ref, x2_ref)
     pack_x_face(s, even_x, bt_ref, dt_ref, x1_ref)
-    pack_face(s, is_even("gy"), bt_ref, dt_ref, y1_ref)
+
+
+def pack_y_kernel(s, bt_ref, dt_ref, y1_ref, y2_ref):
+    even_y = is_even("gy")
+    pack_y_face(s, jnp.logical_not(even_y), bt_ref, dt_ref, y2_ref)
+    pack_y_face(s, even_y, bt_ref, dt_ref, y1_ref)
 
 
 def pack_x_face(s, upper, bt_ref, dt_ref, out_ref):
@@ -208,7 +209,7 @@
     out_ref[s.x_dens :, :] = dt_ref[rows, :]
 
 
-def pack_face(s, upper, bt_ref, dt_ref, out_ref):
+def pack_y_face(s, upper, bt_ref, dt_ref, out_ref):
     loads, nx, ny = s.loads, s.nx, s.ny
     tiles = Tiles(bt_ref, ny, loads)
     y0 = pick(upper, ny - 2, 0)
@@ -699,10 +700,10 @@
         )
 
     hbm = pl.BlockSpec(memory_space=pltpu.HBM)
-    face = shape(s.y_rows, LANES)
-    bt, dt, y2 = call(
+    y_face, x_face, corner = (shape(rows, LANES) for rows in (s.y_rows, s.x_rows, s.c_rows))
+    bt, dt, x1, x2 = call(
         pack_kernel,
-        (shape(nodes, LANES), shape(nx * ny, LANES), face),
+        (shape(nodes, LANES), shape(nx * ny, LANES), x_face, x_face),
         in_specs=[hbm, hbm],
         scratch_shapes=[
             scratch(loads, nx, flat),
@@ -713,14 +714,17 @@
         pltpu.with_memory_space_constraint(heat_source, pltpu.HBM),
         pltpu.with_memory_space_constraint(density, pltpu.HBM),
     )
-    y2 = swap(y2, "gy", 1)
-    x_face, corner = shape(s.x_rows, LANES), shape(s.c_rows, LANES)
-    y1, x1, x2 = call(pack_rest_kernel, (face, x_face, x_face))(bt, dt)
-    x2, y1, x1 = swap(x2, "gx", 1), swap(y1, "gy", 0), swap(x1, "gx", 0)
+    x2, x1 = swap(x2, "gx", 1), swap(x1, "gx", 0)
+    y1, y2 = call(pack_y_kernel, (y_face, y_face))(bt, dt)
+    y2, y1 = swap(y2, "gy", 1), swap(y1, "gy", 0)
     t2 = call(open_y_kernel, shape(2 * nx * loads, LANES))(y2)
     xt = shape(2 * ny * loads, LANES)
     xt2 = call(open_x_kernel, xt)(x2)
-    xt1, c1, c2 = call(corner_kernel, (xt, corner, corner))(x2, xt2, x1)
+    xt1, c1, c2 = call(
+        corner_kernel,
+        (xt, corner, corner),
+        cost_estimate=pl.CostEstimate(flops=2 * 10**9, transcendentals=0, bytes_accessed=0),
+    )(x2, xt2, x1)
     xt1, dt = lax.optimization_barrier((xt1, dt))
     c2, c1 = swap(c2, "gy", 1), swap(c1, "gy", 0)
     plane = s.my * loads

time: 29.5 us -> 28.8 us (0.976)
  starting transfers between devices: 11.8 us -> 10.9 us
    ppermute x6, starting transfers between devices: 8.4 us -> 6.95 us  [swap(): return lax.ppermute(array, ('gx', 'gy'), pairs)]
    all_to_all x1, starting transfers between devices: 3.44 us -> 3.97 us  [per_device(): parts = lax.all_to_all(sums, ('gx', 'gy'), 0, 0, tiled=True)]
  transfers between devices with their start and end apart: 7 -> 7, of which waited for: 2 -> 3; matrix products, arithmetic and copies ran while one was open for 0% -> 0% of each run, Pallas kernels for 14% -> 14%
where the time goes in v18:
time: 28.8 us; the launch traced here: 28.7 us
  starting transfers between devices  10.9 us (38%)
  waiting for transfers between devices  8.79 us (31%)
  Pallas kernels  8.21 us (29%)
  between operations  0.75 us (3%)
    ppermute x6, starting transfers between devices, swap(): return lax.ppermute(array, ('gx', 'gy'), pairs)  6.95 us
    all_to_all x1, waiting for transfers between devices, per_device(): parts = lax.all_to_all(sums, ('gx', 'gy'), 0, 0, tiled=True)  6.32 us
    all_to_all x1, starting transfers between devices, per_device(): parts = lax.all_to_all(sums, ('gx', 'gy'), 0, 0, tiled=True)  3.97 us
    pallas_call x1, Pallas kernels, per_device(): call(inner_kernel, (shape(nx * s.pitch, LANES),) + (rows,) * 2 + (field,)...  2.78 us
    ppermute x6, waiting for transfers between devices, swap(): return lax.ppermute(array, ('gx', 'gy'), pairs)  2.46 us
    pallas_call x1, Pallas kernels, per_device(): call(pack_kernel, (shape(nodes, LANES), shape(nx * ny, LANES), x_face, x_...  1.58 us
    pallas_call x1, Pallas kernels, per_device(): call(outer_kernel, (ends, ends, shape(ny, LANES), shape(devices, 1, LANES...  1.45 us
    pallas_call x1, Pallas kernels, per_device(): call(finish_kernel, (whole, whole), out_specs=(hbm, hbm), scratch_shapes=...  1.21 us
  transfers between devices with their start and end apart: 7, of which 3 were waited for; matrix products, arithmetic and copies ran while one was open for 0% of the time, Pallas kernels for 14%

profile of v18, /device:TPU:0, one launch (start us, length us, event | category | flops | bytes accessed | tf_op | source)
XLA Modules:
  0.0 28.7 jit_solution(771621239983543982)
XLA Ops:
  0.6 1.6 %shard_map.41 = (f32[1024,128]{1,0:T(8,128)S(1)}, f32[128,128]{1,0:T(8,128)S(1)}, f32[120,128]{1,0:T(8,128)S(1)}, f32[120,128]{1,0:T(8,128)S(1)}) custom-call(f32[8,16,768]{2,1,0:T(8,128)} %b_ref.1, f32[16,768]{1,0:T(8,128)} %d_hbm.1), custom_call_target="tpu_custom_call" | custom-call | tf_op jit(solution)/shard_map/pallas_call | solution.py:704
  2.2 0.5 %collective-permute-start = (f32[120,128]{1,0:T(8,128)S(1)}, f32[120,128]{1,0:T(8,128)S(1)}, u32[]{:S(2)}, u32[]{:S(2)}) collective-permute-start(f32[120,128]{1,0:T(8,128)S(1)} %get-tuple-element.33), channel_id=1, source_target_pairs={{0,1},{1,0},{2,3},{3,2},{4,5},{5,4},{6,7},{7,6},{8,16},{9,17},{10,... | collective-permute-start | bytes 184328 | tf_op jit(solution)/shard_map/ppermute | solution.py:680
  2.7 4.1 %collective-permute-start.1 = (f32[120,128]{1,0:T(8,128)S(1)}, f32[120,128]{1,0:T(8,128)S(1)}, u32[]{:S(2)}, u32[]{:S(2)}) collective-permute-start(f32[120,128]{1,0:T(8,128)S(1)} %get-tuple-element.34), channel_id=1, source_target_pairs={{0,8},{1,9},{2,10},{3,11},{4,12},{5,13},{6,14},{7,15},{8,0},{9,1},... | collective-permute-start | bytes 184328 | tf_op jit(solution)/shard_map/ppermute | solution.py:680
  6.9 0.1 shard_map.44
  7.0 0.1 collective-permute-start.2
  7.1 0.1 collective-permute-start.3
  7.2 0.0 collective-permute-done.x_ref.x2_ref
  7.2 0.1 shard_map.42.t2_ref
  7.3 1.8 %collective-permute-done.1.x1_ref = f32[120,128]{1,0:T(8,128)S(1)} collective-permute-done((f32[120,128]{1,0:T(8,128)S(1)}, f32[120,128]{1,0:T(8,128)S(1)}, u32[]{:S(2)}, u32[]{:S(2)}) %collective-permute-start.1) | collective-permute-done | bytes 61472 | tf_op jit(solution)/shard_map/ppermute | solution.py:680
  9.1 0.2 shard_map.43
  9.2 0.1 collective-permute-start.4
  9.3 2.1 %collective-permute-start.5 = (f32[72,128]{1,0:T(8,128)S(1)}, f32[72,128]{1,0:T(8,128)S(1)}, u32[]{:S(2)}, u32[]{:S(2)}) collective-permute-start(f32[72,128]{1,0:T(8,128)S(1)} %get-tuple-element.43), channel_id=1, source_target_pairs={{0,8},{1,2},{2,1},{3,4},{4,3},{5,6},{6,5},{7,15},{8,0},{9,10},{10,... | collective-permute-start | bytes 110600 | tf_op jit(solution)/shard_map/ppermute | solution.py:680
  11.4 0.6 %collective-permute-done.3.y_ref.y2_ref = f32[240,128]{1,0:T(8,128)S(1)} collective-permute-done((f32[240,128]{1,0:T(8,128)S(1)}, f32[240,128]{1,0:T(8,128)S(1)}, u32[]{:S(2)}, u32[]{:S(2)}) %collective-permute-start.3) | collective-permute-done | bytes 122912 | tf_op jit(solution)/shard_map/ppermute | solution.py:680
  12.0 0.1 shard_map.45.t2_ref
  12.1 0.0 collective-permute-done.2.y1_ref
  12.2 2.8 %shard_map.46 = (f32[256,128]{1,0:T(8,128)S(1)}, f32[320,128]{1,0:T(8,128)S(1)}, f32[320,128]{1,0:T(8,128)S(1)}, f32[1920,128]{1,0:T(8,128)S(1)}, f32[1920,128]{...) custom-call(f32[1024,128]{1,0:T(8,128)S(1)} %get-tuple-element.32.bt, ...), custom_call_target="tpu_custom_call" | custom-call | tf_op jit(solution)/shard_map/pallas_call | solution.py:734
  14.9 0.0 collective-permute-done.4.c1_ref
  14.9 0.0 collective-permute-done.5.c2_ref
  15.0 1.4 %shard_map.47 = (f32[320,128]{1,0:T(8,128)S(1)}, f32[320,128]{1,0:T(8,128)S(1)}, f32[8,128]{1,0:T(8,128)S(1)}, f32[32,1,128]{2,1,0:T(1,128)}) custom-call(f32[256,128]{1,0:T(8,128)S(1)} %get-tuple-element.40.dens_ref, f32[120,128]{1,0:T(8,128)S(1)} %collective-permute-done.1.x1_ref, f32[120,128]{1,0:T(8,128)S(1)} %collective-permute-done.x_ref.x2_ref, ...), custom_call_target="tpu_custom_call" | custom-call | tf_op jit(solution)/shard_map/pallas_call | solution.py:744
  16.4 4.0 %all-to-all-start = ((f32[32,1,128]{2,1,0:T(1,128)}), f32[32,1,128]{2,1,0:T(1,128)S(1)}, u32[]{:S(2)}, u32[]{:S(2)}) async-start(f32[32,1,128]{2,1,0:T(1,128)} %get-tuple-element.53), calls=%async_computation | async-start | bytes 32768 | tf_op jit(solution)/shard_map/all_to_all | solution.py:753
  20.4 0.0 copy-start
  20.4 0.7 %shard_map.48 = (f32[8,16,768]{2,1,0:T(8,128)S(1)}, f32[8,16,768]{2,1,0:T(8,128)S(1)}, f32[16,768]{1,0:T(8,128)S(1)}) custom-call(f32[1024,128]{1,0:T(8,128)S(1)} %get-tuple-element.54.q1_ref, f32[320,128]{1,0:T(8,128)S(1)} %get-tuple-element.55.q2_ref, f32[1024,128]{1,0:T(8,128)S(1)} %get-tuple-element.56.v1_ref, f32[320,128]{1,0:T(8,128)S(1)} %get-tuple-element.57.v2_ref, ...), custom_call_target="tpu_custom_call" | custom-call | tf_op jit(solution)/shard_map/pallas_call | solution.py:755
  21.1 6.3 %all-to-all-done.parts_ref = f32[32,1,128]{2,1,0:T(1,128)S(1)} async-done(((f32[32,1,128]{2,1,0:T(1,128)}), f32[32,1,128]{2,1,0:T(1,128)S(1)}, u32[]{:S(2)}, u32[]{:S(2)}) %all-to-all-start) | async-done | bytes 16416 | tf_op jit(solution)/shard_map/all_to_all | solution.py:753
  27.5 0.0 copy-done
  27.5 1.2 %shard_map.49 = (f32[8,16,768]{2,1,0:T(8,128)}, f32[8,16,768]{2,1,0:T(8,128)}) custom-call(f32[32,1,128]{2,1,0:T(1,128)S(1)} %all-to-all-done.parts_ref, f32[8,16,768]{2,1,0:T(8,128)S(1)} %copy-done, f32[8,16,768]{2,1,0:T(8,128)S(1)} %get-tuple-element.59.q_ref, f32[8,16,768]{2,1,0:T(8,128)S(1)} %get-tuple-element.60.v_ref, ...), custom_call_target="tpu_custom_call" | custom-call | tf_op jit(solution)/shard_map/pallas_call | solution.py:760
Async XLA Ops:
  2.2 5.0 %collective-permute-start = (f32[120,128]{1,0:T(8,128)S(1)}, f32[120,128]{1,0:T(8,128)S(1)}, u32[]{:S(2)}, u32[]{:S(2)}) collective-permute-start(f32[120,128]{1,0:T(8,128)S(1)} %get-tuple-element.33), channel_id=1, source_target_pairs={{0,1},{1,0},{2,3},{3,2},{4,5},{5,4},{6,7},{7,6},{8,16},{9,17},{10,... | collective-permute-start | bytes 184328 | tf_op jit(solution)/shard_map/ppermute | solution.py:680
  2.7 6.3 %collective-permute-start.1 = (f32[120,128]{1,0:T(8,128)S(1)}, f32[120,128]{1,0:T(8,128)S(1)}, u32[]{:S(2)}, u32[]{:S(2)}) collective-permute-start(f32[120,128]{1,0:T(8,128)S(1)} %get-tuple-element.34), channel_id=1, source_target_pairs={{0,8},{1,9},{2,10},{3,11},{4,12},{5,13},{6,14},{7,15},{8,0},{9,1},... | collective-permute-start | bytes 184328 | tf_op jit(solution)/shard_map/ppermute | solution.py:680
  7.0 5.1 %collective-permute-start.2 = (f32[240,128]{1,0:T(8,128)S(1)}, f32[240,128]{1,0:T(8,128)S(1)}, u32[]{:S(2)}, u32[]{:S(2)}) collective-permute-start(f32[240,128]{1,0:T(8,128)S(1)} %get-tuple-element.38), channel_id=1, source_target_pairs={{0,1},{1,0},{2,3},{3,2},{4,5},{5,4},{6,7},{7,6},{8,9},{9,8},{10,11... | collective-permute-start | bytes 368648 | tf_op jit(solution)/shard_map/ppermute | solution.py:680
  7.1 4.9 %collective-permute-start.3 = (f32[240,128]{1,0:T(8,128)S(1)}, f32[240,128]{1,0:T(8,128)S(1)}, u32[]{:S(2)}, u32[]{:S(2)}) collective-permute-start(f32[240,128]{1,0:T(8,128)S(1)} %get-tuple-element.39), channel_id=1, source_target_pairs={{0,8},{1,2},{2,1},{3,4},{4,3},{5,6},{6,5},{7,15},{8,0},{9,10},{10,... | collective-permute-start | bytes 368648 | tf_op jit(solution)/shard_map/ppermute | solution.py:680
  9.2 5.7 %collective-permute-start.4 = (f32[72,128]{1,0:T(8,128)S(1)}, f32[72,128]{1,0:T(8,128)S(1)}, u32[]{:S(2)}, u32[]{:S(2)}) collective-permute-start(f32[72,128]{1,0:T(8,128)S(1)} %get-tuple-element.42), channel_id=1, source_target_pairs={{0,1},{1,0},{2,3},{3,2},{4,5},{5,4},{6,7},{7,6},{8,9},{9,8},{10,11... | collective-permute-start | bytes 110600 | tf_op jit(solution)/shard_map/ppermute | solution.py:680
  9.3 5.6 %collective-permute-start.5 = (f32[72,128]{1,0:T(8,128)S(1)}, f32[72,128]{1,0:T(8,128)S(1)}, u32[]{:S(2)}, u32[]{:S(2)}) collective-permute-start(f32[72,128]{1,0:T(8,128)S(1)} %get-tuple-element.43), channel_id=1, source_target_pairs={{0,8},{1,2},{2,1},{3,4},{4,3},{5,6},{6,5},{7,15},{8,0},{9,10},{10,... | collective-permute-start | bytes 110600 | tf_op jit(solution)/shard_map/ppermute | solution.py:680
  16.4 11.1 %all-to-all-start = ((f32[32,1,128]{2,1,0:T(1,128)}), f32[32,1,128]{2,1,0:T(1,128)S(1)}, u32[]{:S(2)}, u32[]{:S(2)}) async-start(f32[32,1,128]{2,1,0:T(1,128)} %get-tuple-element.53), calls=%async_computation | async-start | bytes 32768 | tf_op jit(solution)/shard_map/all_to_all | solution.py:753
  20.4 7.1 %copy-start = (f32[8,16,768]{2,1,0:T(8,128)S(1)}, f32[8,16,768]{2,1,0:T(8,128)}, u32[]{:S(2)}) copy-start(f32[8,16,768]{2,1,0:T(8,128)} %b_ref.1) | copy-start | bytes 1179652

commit v19 on v18

--- a/solution.py
+++ b/solution.py
@@ -142,6 +142,19 @@
         self.first.put(self.own.index(x), values)
 
 
+class Inside:
+    def __init__(self, inner, own, outer):
+        self.inner, self.own, self.outer = inner, own, outer
+
+    def __getitem__(self, at):
+        if at[1] in self.own:
+            return self.inner[at[0] - 2, at[1] - 2]
+        return self.outer[at]
+
+    def __setitem__(self, at, tile):
+        self.outer[at] = tile
+
+
 def is_even(axis):
     return lax.rem(lax.axis_index(axis), 2) == 0
 
@@ -157,16 +170,17 @@
     return jnp.where(even, if_even, if_odd)
 
 
-def pack_kernel(s, b_hbm, d_hbm, bt_ref, dt_ref, x1_ref, x2_ref, b_ref, d_ref, sems):
+def pack_x_kernel(s, b_hbm, d_hbm, b_ref, dt_ref, x1_ref, x2_ref, d_ref, sems):
     loads, nx, ny = s.loads, s.nx, s.ny
-    d_copy = pltpu.make_async_copy(d_hbm, d_ref, sems.at[0])
+    blocks = packed_count(ny)
+    d_copy = pltpu.make_async_copy(d_hbm, d_ref, sems.at[blocks])
     d_copy.start()
-    parts = 2 if loads % 2 == 0 else 1
-    each = loads // parts
     copies = []
-    for part in range(parts):
-        some = pl.ds(part * each, each)
-        copies.append(pltpu.make_async_copy(b_hbm.at[some], b_ref.at[some], sems.at[part + 1]))
+    for block in range(blocks):
+        lanes = pl.ds(block * LANES, LANES)
+        copies.append(
+            pltpu.make_async_copy(b_hbm.at[:, lanes], b_ref.at[block], sems.at[block])
+        )
         copies[-1].start()
     d_copy.wait()
     batch = Batch(16)
@@ -177,36 +191,39 @@
             )
             batch.add(dt_ref, (pl.ds(x0 * ny + y, SUB, stride=ny), slice(None)), tile)
     batch.flush()
+    even_x = is_even("gx")
+    for ref, upper in ((x2_ref, jnp.logical_not(even_x)), (x1_ref, even_x)):
+        rows = pl.ds(pl.multiple_of(pick(upper, nx - 3, 0) * ny, SUB), 3 * ny)
+        ref[s.x_dens :, :] = dt_ref[rows, :]
+    for copy in copies:
+        copy.wait()
+    batch = Batch()
+    for ref, upper in ((x2_ref, jnp.logical_not(even_x)), (x1_ref, even_x)):
+        x0 = pick(upper, nx - 2, 0)
+        for dx in range(2):
+            for block in range(blocks):
+                tile = b_ref[block, pl.ds(x0 + dx, loads, stride=nx), :]
+                at = (dx * blocks + block) * loads
+                batch.add(ref, (slice(at, at + loads), slice(None)), tile)
+    batch.flush()
+
+
+def pack_y_kernel(s, b_ref, dt_ref, bt_ref, y1_ref, y2_ref):
+    loads, nx, ny = s.loads, s.nx, s.ny
+    batch = Batch(16)
     for load in range(loads):
-        if load % each == 0:
-            copies[load // each].wait()
-        batch = Batch(16)
         for x0 in range(0, nx, SUB):
+            at = load * nx + x0
             for y in range(ny):
                 tile = unpack_tile(
-                    lambda t: b_ref[load, x0 : x0 + SUB, t * LANES : (t + 1) * LANES], y, SUB
+                    lambda t: b_ref[t, at : at + SUB, :], y, SUB
                 )
                 rows = pl.ds((x0 * ny + y) * loads + load, SUB, stride=ny * loads)
                 batch.add(bt_ref, (rows, slice(None)), tile)
-        batch.flush()
-    even_x = is_even("gx")
-    pack_x_face(s, jnp.logical_not(even_x), bt_ref, dt_ref, x2_ref)
-    pack_x_face(s, even_x, bt_ref, dt_ref, x1_ref)
-
-
-def pack_y_kernel(s, bt_ref, dt_ref, y1_ref, y2_ref):
+    batch.flush()
     even_y = is_even("gy")
     pack_y_face(s, jnp.logical_not(even_y), bt_ref, dt_ref, y2_ref)
     pack_y_face(s, even_y, bt_ref, dt_ref, y1_ref)
-
-
-def pack_x_face(s, upper, bt_ref, dt_ref, out_ref):
-    loads, nx, ny = s.loads, s.nx, s.ny
-    tiles = Tiles(bt_ref, ny, loads)
-    x0 = pick(upper, nx - 2, 0)
-    pack_tiles(out_ref, 0, loads, 2 * ny, lambda i: tiles[x0 + i // ny, i % ny])
-    rows = pl.ds(pl.multiple_of(pick(upper, nx - 3, 0) * ny, SUB), 3 * ny)
-    out_ref[s.x_dens :, :] = dt_ref[rows, :]
 
 
 def pack_y_face(s, upper, bt_ref, dt_ref, out_ref):
@@ -398,8 +415,36 @@
     return state
 
 
+def inside_fields(s, bt_ref, zt_ref, bx, zx):
+    brick = (Tiles(ref, s.ny, s.loads) for ref in (bt_ref, zt_ref))
+    starts = (2, 3)
+    return tuple(
+        Inside(inner, range(start, s.ny + 2), outer)
+        for inner, start, outer in zip(brick, starts, (bx, zx))
+    )
+
+
+def scale_kernel(s, bt_ref, dt_ref, zt_ref, inv_ref):
+    loads, nx, ny = s.loads, s.nx, s.ny
+    inner, scaled = Tiles(bt_ref, ny, loads), Tiles(zt_ref, ny, loads)
+    inverse = Rows(inv_ref, ny, loads)
+    before = conduct_of(dt_ref[0:ny, :])
+    for x in range(1, nx):
+        after = conduct_of(dt_ref[x * ny : (x + 1) * ny, :])
+        pair = before + after
+        pair = pair[: ny - 1] + pair[1:]
+        total = 4.0 * (pair + pltpu.roll(pair, 1, 1))
+        inverse.put(x, jnp.where(after[1:] > 0.0, 1.0 / total, 0.0))
+        before = after
+    batch = Batch(16)
+    for x in range(1, nx):
+        for y in range(1, ny):
+            batch.add(scaled, (x, y), inner[x, y] * inverse[x, y - 1])
+    batch.flush()
+
+
 def inner_kernel(
-    s, bt_ref, dt_ref, y1_ref, y2_ref, t2_ref,
+    s, bt_ref, zt_ref, dt_ref, y1_ref, y2_ref, t1_ref,
     dens_ref, cond, invx, bx, zx, qx, wx, q_out, v_out, carry1, carry2, sums_ref,
 ):
     loads, nx, ny, my, pitch = s.loads, s.nx, s.ny, s.my, s.pitch
@@ -419,27 +464,26 @@
             invx.put(x + 2, inverse_of(s, before, after))
         before = after
 
+    bx, zx = inside_fields(s, bt_ref, zt_ref, bx, zx)
+
     def stage(x, y, tile):
         stores = [(bx, (x + 2, y), tile)]
         if x:
             stores.append((zx, (x + 2, y), tile * invx[x + 2, y]))
         return stores
 
-    inner = Tiles(bt_ref, ny, loads)
     batch = Batch(16)
-    for x in range(nx):
-        for y in range(ny):
-            for store in stage(x, y + 2, inner[x, y]):
-                batch.add(*store)
+    for x in range(1, nx):
+        batch.add(zx, (x + 2, 2), bx[x + 2, 2] * invx[x + 2, 2])
     batch.flush()
     unpack_tiles(
-        y1_ref, 0, loads, 2 * nx, lambda i, tile: stage(i // 2, ys[0] + i % 2, tile)
-    )
-    far = Tiles(t2_ref, 2, loads)
+        y2_ref, 0, loads, 2 * nx, lambda i, tile: stage(i // 2, ys[1] + i % 2, tile)
+    )
+    near = Tiles(t1_ref, 2, loads)
     batch = Batch(16)
     for x in range(nx):
         for dy in range(2):
-            for store in stage(x, ys[1] + dy, far[x, dy]):
+            for store in stage(x, ys[0] + dy, near[x, dy]):
                 batch.add(*store)
     batch.flush()
 
@@ -465,7 +509,7 @@
 
 
 def outer_kernel(
-    s, dens_ref, x1_ref, x2_ref, t1_ref, t2_ref, c1_ref, c2_ref,
+    s, bt_ref, zt_ref, dens_ref, x1_ref, x2_ref, t1_ref, t2_ref, c1_ref, c2_ref,
     cond1, invx1, bx1, zx1, qx1, wx1, carry1, carry2, sums1,
     q_out, v_out, inv_out, sums_ref,
     low_ref, high_ref, low_d, high_d, cond2, invx2, bx2, zx2, qx2, wx2, carry3,
@@ -524,7 +568,11 @@
     scaled_own = outside + (2,)
     image_own = (1, 2, 3, nx + 1, nx + 2)
     cond, invx = joined_rows(cond2, cond1, outside), joined_rows(invx2, invx1, scaled_own)
-    bx, zx = joined(bx2, bx1, outside), joined(zx2, zx1, scaled_own)
+    bx1, zx1 = inside_fields(
+        s, bt_ref, zt_ref, Tiles(bx1, my, loads), Tiles(zx1, my, loads)
+    )
+    bx = Joined(Tiles(bx2, my, loads), bx1, outside)
+    zx = Joined(Tiles(zx2, my, loads), zx1, scaled_own)
     qx, wx = joined(qx2, qx1, image_own), joined(wx2, wx1, image_own)
     own = [x - 2 for x in outer_planes(nx)]
     q_out, v_out = (Joined(Tiles(ref, ny, loads), None, own) for ref in (q_out, v_out))
@@ -701,25 +749,25 @@
 
     hbm = pl.BlockSpec(memory_space=pltpu.HBM)
     y_face, x_face, corner = (shape(rows, LANES) for rows in (s.y_rows, s.x_rows, s.c_rows))
-    bt, dt, x1, x2 = call(
-        pack_kernel,
-        (shape(nodes, LANES), shape(nx * ny, LANES), x_face, x_face),
+    b, dt, x1, x2 = call(
+        pack_x_kernel,
+        (shape(packed_count(ny), loads * nx, LANES), shape(nx * ny, LANES), x_face, x_face),
         in_specs=[hbm, hbm],
-        scratch_shapes=[
-            scratch(loads, nx, flat),
-            scratch(nx, flat),
-            pltpu.SemaphoreType.DMA((3,)),
-        ],
+        scratch_shapes=[scratch(nx, flat), pltpu.SemaphoreType.DMA((packed_count(ny) + 1,))],
     )(
-        pltpu.with_memory_space_constraint(heat_source, pltpu.HBM),
+        pltpu.with_memory_space_constraint(heat_source.reshape(loads * nx, flat), pltpu.HBM),
         pltpu.with_memory_space_constraint(density, pltpu.HBM),
     )
     x2, x1 = swap(x2, "gx", 1), swap(x1, "gx", 0)
-    y1, y2 = call(pack_y_kernel, (y_face, y_face))(bt, dt)
+    bt, y1, y2 = call(pack_y_kernel, (shape(nodes, LANES), y_face, y_face))(b, dt)
     y2, y1 = swap(y2, "gy", 1), swap(y1, "gy", 0)
-    t2 = call(open_y_kernel, shape(2 * nx * loads, LANES))(y2)
+    t1 = call(open_y_kernel, shape(2 * nx * loads, LANES))(y1)
     xt = shape(2 * ny * loads, LANES)
     xt2 = call(open_x_kernel, xt)(x2)
+    xt2, dt_later = lax.optimization_barrier((xt2, dt))
+    zt = call(
+        scale_kernel, shape(nodes, LANES), scratch_shapes=[scratch(nx * ny, LANES)]
+    )(bt, dt_later)
     xt1, c1, c2 = call(
         corner_kernel,
         (xt, corner, corner),
@@ -739,7 +787,7 @@
         + (inside,) * 2
         + (edge,) * 2
         + (shape(4 * loads, LANES),),
-    )(bt, dt, y1, y2, t2)
+    )(bt, zt, dt, y1, y2, t1)
     ends = shape(len(outer_planes(nx)) * ny * loads, LANES)
     q_2, v_2, inv_2, sums = call(
         outer_kernel,
@@ -749,7 +797,7 @@
         + [scratch(5 * s.pitch, LANES)] * 2
         + [scratch(5 * plane, LANES)] * 4
         + [scratch(2 * plane, LANES)],
-    )(dens, x1, x2, xt1, xt2, c1, c2, cond, inv_1, bx, zx, q_x, w_x, carry1, carry2, sums)
+    )(bt, zt, dens, x1, x2, xt1, xt2, c1, c2, cond, inv_1, bx, zx, q_x, w_x, carry1, carry2, sums)
     parts = lax.all_to_all(sums, ("gx", "gy"), 0, 0, tiled=True)
     whole = shape(loads, nx, flat)
     image, again, inverse = call(

time: 28.8 us -> 28.6 us (level)
    pallas_call x3 -> x4, Pallas kernels: 1.8 us -> 1.88 us  [the longest x1 1.13 us: per_device(): call(pack_x_kernel, (shape(packed_count(ny), loads * nx, LANES), shape(nx...]
  transfers between devices with their start and end apart: 7 -> 7, of which waited for: 3 -> 3; matrix products, arithmetic and copies ran while one was open for 0% -> 0% of each run, Pallas kernels for 14% -> 16%
where the time goes in v19:
time: 28.6 us; the launch traced here: 28.4 us
  starting transfers between devices  10.9 us (38%)
  waiting for transfers between devices  8.52 us (30%)
  Pallas kernels  8.25 us (29%)
  between operations  0.74 us (3%)
    ppermute x6, starting transfers between devices, swap(): return lax.ppermute(array, ('gx', 'gy'), pairs)  6.96 us
    all_to_all x1, waiting for transfers between devices, per_device(): parts = lax.all_to_all(sums, ('gx', 'gy'), 0, 0, tiled=True)  6.32 us
    all_to_all x1, starting transfers between devices, per_device(): parts = lax.all_to_all(sums, ('gx', 'gy'), 0, 0, tiled=True)  3.97 us
    pallas_call x1, Pallas kernels, per_device(): call(inner_kernel, (shape(nx * s.pitch, LANES),) + (rows,) * 2 + (field,)...  2.73 us
    ppermute x6, waiting for transfers between devices, swap(): return lax.ppermute(array, ('gx', 'gy'), pairs)  2.2 us
    pallas_call x1, Pallas kernels, per_device(): call(outer_kernel, (ends, ends, shape(ny, LANES), shape(devices, 1, LANES...  1.45 us
    pallas_call x1, Pallas kernels, per_device(): call(finish_kernel, (whole, whole), out_specs=(hbm, hbm), scratch_shapes=...  1.21 us
    pallas_call x1, Pallas kernels, per_device(): call(pack_x_kernel, (shape(packed_count(ny), loads * nx, LANES), shape(nx...  1.13 us
  transfers between devices with their start and end apart: 7, of which 3 were waited for; matrix products, arithmetic and copies ran while one was open for 0% of the time, Pallas kernels for 16%

profile of v19, /device:TPU:0, one launch (start us, length us, event | category | flops | bytes accessed | tf_op | source)
XLA Modules:
  0.0 28.4 jit_solution(10593764555734010802)
XLA Ops:
  0.6 1.1 %shard_map.41 = (f32[6,128,128]{2,1,0:T(8,128)S(1)}, f32[128,128]{1,0:T(8,128)S(1)}, f32[120,128]{1,0:T(8,128)S(1)}, f32[120,128]{1,0:T(8,128)S(1)}) custom-call(f32[128,768]{1,0:T(8,128)} %bitcast.1, f32[16,768]{1,0:T(8,128)} %d_hbm.1), custom_call_target="tpu_custom_call" | custom-call | tf_op jit(solution)/shard_map/pallas_call | solution.py:752
  1.8 0.5 %collective-permute-start = (f32[120,128]{1,0:T(8,128)S(1)}, f32[120,128]{1,0:T(8,128)S(1)}, u32[]{:S(2)}, u32[]{:S(2)}) collective-permute-start(f32[120,128]{1,0:T(8,128)S(1)} %get-tuple-element.38), channel_id=1, source_target_pairs={{0,1},{1,0},{2,3},{3,2},{4,5},{5,4},{6,7},{7,6},{8,16},{9,17},{10,... | collective-permute-start | bytes 184328 | tf_op jit(solution)/shard_map/ppermute | solution.py:728
  2.3 4.1 %collective-permute-start.1 = (f32[120,128]{1,0:T(8,128)S(1)}, f32[120,128]{1,0:T(8,128)S(1)}, u32[]{:S(2)}, u32[]{:S(2)}) collective-permute-start(f32[120,128]{1,0:T(8,128)S(1)} %get-tuple-element.41), channel_id=1, source_target_pairs={{0,8},{1,9},{2,10},{3,11},{4,12},{5,13},{6,14},{7,15},{8,0},{9,1},... | collective-permute-start | bytes 184328 | tf_op jit(solution)/shard_map/ppermute | solution.py:728
  6.4 0.5 %shard_map.42 = (f32[1024,128]{1,0:T(8,128)S(1)}, f32[240,128]{1,0:T(8,128)S(1)}, f32[240,128]{1,0:T(8,128)S(1)}) custom-call(f32[6,128,128]{2,1,0:T(8,128)S(1)} %get-tuple-element.35.b_ref, f32[128,128]{1,0:T(8,128)S(1)} %get-tuple-element.43.dt_ref), custom_call_target="tpu_custom_call" | custom-call | tf_op jit(solution)/shard_map/pallas_call | solution.py:762
  6.9 0.1 collective-permute-start.2
  7.0 0.1 collective-permute-start.3
  7.1 0.0 collective-permute-done.x_ref.x2_ref
  7.1 0.1 shard_map.43.t2_ref
  7.2 1.4 %collective-permute-done.1.x1_ref = f32[120,128]{1,0:T(8,128)S(1)} collective-permute-done((f32[120,128]{1,0:T(8,128)S(1)}, f32[120,128]{1,0:T(8,128)S(1)}, u32[]{:S(2)}, u32[]{:S(2)}) %collective-permute-start.1) | collective-permute-done | bytes 61472 | tf_op jit(solution)/shard_map/ppermute | solution.py:728
  8.6 0.2 shard_map.45
  8.8 0.2 collective-permute-start.4
  9.0 1.9 %collective-permute-start.5 = (f32[72,128]{1,0:T(8,128)S(1)}, f32[72,128]{1,0:T(8,128)S(1)}, u32[]{:S(2)}, u32[]{:S(2)}) collective-permute-start(f32[72,128]{1,0:T(8,128)S(1)} %get-tuple-element.49), channel_id=1, source_target_pairs={{0,8},{1,2},{2,1},{3,4},{4,3},{5,6},{6,5},{7,15},{8,0},{9,10},{10,... | collective-permute-start | bytes 110600 | tf_op jit(solution)/shard_map/ppermute | solution.py:728
  10.9 0.1 shard_map.44.zt_ref
  11.1 0.0 collective-permute-done.2.y_ref.y1_ref
  11.1 0.1 shard_map.46.t1_ref
  11.2 0.8 %collective-permute-done.3.y2_ref = f32[240,128]{1,0:T(8,128)S(1)} collective-permute-done((f32[240,128]{1,0:T(8,128)S(1)}, f32[240,128]{1,0:T(8,128)S(1)}, u32[]{:S(2)}, u32[]{:S(2)}) %collective-permute-start.3) | collective-permute-done | bytes 122912 | tf_op jit(solution)/shard_map/ppermute | solution.py:728
  12.0 2.7 %shard_map.47 = (f32[256,128]{1,0:T(8,128)S(1)}, f32[320,128]{1,0:T(8,128)S(1)}, f32[320,128]{1,0:T(8,128)S(1)}, f32[1920,128]{1,0:T(8,128)S(1)}, f32[1920,128]{...) custom-call(f32[1024,128]{1,0:T(8,128)S(1)} %get-tuple-element.37.bt, ...), custom_call_target="tpu_custom_call" | custom-call | tf_op jit(solution)/shard_map/pallas_call | solution.py:782
  14.7 0.0 collective-permute-done.4.c1_ref
  14.7 0.0 collective-permute-done.5.c2_ref
  14.7 1.5 %shard_map.48 = (f32[320,128]{1,0:T(8,128)S(1)}, f32[320,128]{1,0:T(8,128)S(1)}, f32[8,128]{1,0:T(8,128)S(1)}, f32[32,1,128]{2,1,0:T(1,128)}) custom-call(f32[1024,128]{1,0:T(8,128)S(1)} %get-tuple-element.37.bt_ref, f32[1024,128]{1,0:T(8,128)S(1)} %shard_map.44.zt_ref, f32[256,128]{1,0:T(8,128)S(1)} %get-tuple-element.46.dens_ref, ...), custom_call_target="tpu_custom_call" | custom-call | tf_op jit(solution)/shard_map/pallas_call | solution.py:792
  16.2 4.0 %all-to-all-start = ((f32[32,1,128]{2,1,0:T(1,128)}), f32[32,1,128]{2,1,0:T(1,128)S(1)}, u32[]{:S(2)}, u32[]{:S(2)}) async-start(f32[32,1,128]{2,1,0:T(1,128)} %get-tuple-element.59), calls=%async_computation | async-start | bytes 32768 | tf_op jit(solution)/shard_map/all_to_all | solution.py:801
  20.2 0.0 copy-start
  20.2 0.7 %shard_map.49 = (f32[8,16,768]{2,1,0:T(8,128)S(1)}, f32[8,16,768]{2,1,0:T(8,128)S(1)}, f32[16,768]{1,0:T(8,128)S(1)}) custom-call(f32[1024,128]{1,0:T(8,128)S(1)} %get-tuple-element.60.q1_ref, f32[320,128]{1,0:T(8,128)S(1)} %get-tuple-element.61.q2_ref, f32[1024,128]{1,0:T(8,128)S(1)} %get-tuple-element.62.v1_ref, f32[320,128]{1,0:T(8,128)S(1)} %get-tuple-element.63.v2_ref, ...), custom_call_target="tpu_custom_call" | custom-call | tf_op jit(solution)/shard_map/pallas_call | solution.py:803
  20.9 6.3 %all-to-all-done.parts_ref = f32[32,1,128]{2,1,0:T(1,128)S(1)} async-done(((f32[32,1,128]{2,1,0:T(1,128)}), f32[32,1,128]{2,1,0:T(1,128)S(1)}, u32[]{:S(2)}, u32[]{:S(2)}) %all-to-all-start) | async-done | bytes 16416 | tf_op jit(solution)/shard_map/all_to_all | solution.py:801
  27.2 0.0 copy-done
  27.2 1.2 %shard_map.50 = (f32[8,16,768]{2,1,0:T(8,128)}, f32[8,16,768]{2,1,0:T(8,128)}) custom-call(f32[32,1,128]{2,1,0:T(1,128)S(1)} %all-to-all-done.parts_ref, f32[8,16,768]{2,1,0:T(8,128)S(1)} %copy-done, f32[8,16,768]{2,1,0:T(8,128)S(1)} %get-tuple-element.65.q_ref, f32[8,16,768]{2,1,0:T(8,128)S(1)} %get-tuple-element.66.v_ref, ...), custom_call_target="tpu_custom_call" | custom-call | tf_op jit(solution)/shard_map/pallas_call | solution.py:808
Async XLA Ops:
  1.8 5.3 %collective-permute-start = (f32[120,128]{1,0:T(8,128)S(1)}, f32[120,128]{1,0:T(8,128)S(1)}, u32[]{:S(2)}, u32[]{:S(2)}) collective-permute-start(f32[120,128]{1,0:T(8,128)S(1)} %get-tuple-element.38), channel_id=1, source_target_pairs={{0,1},{1,0},{2,3},{3,2},{4,5},{5,4},{6,7},{7,6},{8,16},{9,17},{10,... | collective-permute-start | bytes 184328 | tf_op jit(solution)/shard_map/ppermute | solution.py:728
  2.3 6.3 %collective-permute-start.1 = (f32[120,128]{1,0:T(8,128)S(1)}, f32[120,128]{1,0:T(8,128)S(1)}, u32[]{:S(2)}, u32[]{:S(2)}) collective-permute-start(f32[120,128]{1,0:T(8,128)S(1)} %get-tuple-element.41), channel_id=1, source_target_pairs={{0,8},{1,9},{2,10},{3,11},{4,12},{5,13},{6,14},{7,15},{8,0},{9,1},... | collective-permute-start | bytes 184328 | tf_op jit(solution)/shard_map/ppermute | solution.py:728
  6.9 4.1 %collective-permute-start.2 = (f32[240,128]{1,0:T(8,128)S(1)}, f32[240,128]{1,0:T(8,128)S(1)}, u32[]{:S(2)}, u32[]{:S(2)}) collective-permute-start(f32[240,128]{1,0:T(8,128)S(1)} %get-tuple-element.44), channel_id=1, source_target_pairs={{0,1},{1,0},{2,3},{3,2},{4,5},{5,4},{6,7},{7,6},{8,9},{9,8},{10,11... | collective-permute-start | bytes 368648 | tf_op jit(solution)/shard_map/ppermute | solution.py:728
  7.0 4.9 %collective-permute-start.3 = (f32[240,128]{1,0:T(8,128)S(1)}, f32[240,128]{1,0:T(8,128)S(1)}, u32[]{:S(2)}, u32[]{:S(2)}) collective-permute-start(f32[240,128]{1,0:T(8,128)S(1)} %get-tuple-element.45), channel_id=1, source_target_pairs={{0,8},{1,2},{2,1},{3,4},{4,3},{5,6},{6,5},{7,15},{8,0},{9,10},{10,... | collective-permute-start | bytes 368648 | tf_op jit(solution)/shard_map/ppermute | solution.py:728
  8.8 5.9 %collective-permute-start.4 = (f32[72,128]{1,0:T(8,128)S(1)}, f32[72,128]{1,0:T(8,128)S(1)}, u32[]{:S(2)}, u32[]{:S(2)}) collective-permute-start(f32[72,128]{1,0:T(8,128)S(1)} %get-tuple-element.48), channel_id=1, source_target_pairs={{0,1},{1,0},{2,3},{3,2},{4,5},{5,4},{6,7},{7,6},{8,9},{9,8},{10,11... | collective-permute-start | bytes 110600 | tf_op jit(solution)/shard_map/ppermute | solution.py:728
  9.0 5.7 %collective-permute-start.5 = (f32[72,128]{1,0:T(8,128)S(1)}, f32[72,128]{1,0:T(8,128)S(1)}, u32[]{:S(2)}, u32[]{:S(2)}) collective-permute-start(f32[72,128]{1,0:T(8,128)S(1)} %get-tuple-element.49), channel_id=1, source_target_pairs={{0,8},{1,2},{2,1},{3,4},{4,3},{5,6},{6,5},{7,15},{8,0},{9,10},{10,... | collective-permute-start | bytes 110600 | tf_op jit(solution)/shard_map/ppermute | solution.py:728
  16.2 11.1 %all-to-all-start = ((f32[32,1,128]{2,1,0:T(1,128)}), f32[32,1,128]{2,1,0:T(1,128)S(1)}, u32[]{:S(2)}, u32[]{:S(2)}) async-start(f32[32,1,128]{2,1,0:T(1,128)} %get-tuple-element.59), calls=%async_computation | async-start | bytes 32768 | tf_op jit(solution)/shard_map/all_to_all | solution.py:801
  20.2 7.1 %copy-start = (f32[8,16,768]{2,1,0:T(8,128)S(1)}, f32[8,16,768]{2,1,0:T(8,128)}, u32[]{:S(2)}) copy-start(f32[8,16,768]{2,1,0:T(8,128)} %b_ref.1) | copy-start | bytes 1179652

commit v20 on v19

--- a/solution.py
+++ b/solution.py
@@ -93,8 +93,8 @@
         self.y_rows = self.y_dens + 3 * nx
         self.x_dens = packed_count(2 * ny) * loads
         self.x_rows = self.x_dens + 3 * ny
-        self.c_dens = packed_count(8) * loads
-        self.c_rows = self.c_dens + -(-18 // SUB) * SUB
+        self.c_dens = packed_count(4) * loads
+        self.c_rows = self.c_dens + -(-9 // SUB) * SUB
 
 
 class Tiles:
@@ -170,17 +170,16 @@
     return jnp.where(even, if_even, if_odd)
 
 
-def pack_x_kernel(s, b_hbm, d_hbm, b_ref, dt_ref, x1_ref, x2_ref, d_ref, sems):
+def pack_kernel(s, b_hbm, d_hbm, bt_ref, dt_ref, y2_ref, b_ref, d_ref, sems):
     loads, nx, ny = s.loads, s.nx, s.ny
-    blocks = packed_count(ny)
-    d_copy = pltpu.make_async_copy(d_hbm, d_ref, sems.at[blocks])
+    d_copy = pltpu.make_async_copy(d_hbm, d_ref, sems.at[0])
     d_copy.start()
+    parts = 2 if loads % 2 == 0 else 1
+    each = loads // parts
     copies = []
-    for block in range(blocks):
-        lanes = pl.ds(block * LANES, LANES)
-        copies.append(
-            pltpu.make_async_copy(b_hbm.at[:, lanes], b_ref.at[block], sems.at[block])
-        )
+    for part in range(parts):
+        some = pl.ds(part * each, each)
+        copies.append(pltpu.make_async_copy(b_hbm.at[some], b_ref.at[some], sems.at[part + 1]))
         copies[-1].start()
     d_copy.wait()
     batch = Batch(16)
@@ -191,39 +190,52 @@
             )
             batch.add(dt_ref, (pl.ds(x0 * ny + y, SUB, stride=ny), slice(None)), tile)
     batch.flush()
-    even_x = is_even("gx")
-    for ref, upper in ((x2_ref, jnp.logical_not(even_x)), (x1_ref, even_x)):
-        rows = pl.ds(pl.multiple_of(pick(upper, nx - 3, 0) * ny, SUB), 3 * ny)
-        ref[s.x_dens :, :] = dt_ref[rows, :]
-    for copy in copies:
-        copy.wait()
-    batch = Batch()
-    for ref, upper in ((x2_ref, jnp.logical_not(even_x)), (x1_ref, even_x)):
-        x0 = pick(upper, nx - 2, 0)
-        for dx in range(2):
-            for block in range(blocks):
-                tile = b_ref[block, pl.ds(x0 + dx, loads, stride=nx), :]
-                at = (dx * blocks + block) * loads
-                batch.add(ref, (slice(at, at + loads), slice(None)), tile)
-    batch.flush()
-
-
-def pack_y_kernel(s, b_ref, dt_ref, bt_ref, y1_ref, y2_ref):
-    loads, nx, ny = s.loads, s.nx, s.ny
-    batch = Batch(16)
     for load in range(loads):
+        if load % each == 0:
+            copies[load // each].wait()
+        batch = Batch(16)
         for x0 in range(0, nx, SUB):
-            at = load * nx + x0
             for y in range(ny):
                 tile = unpack_tile(
-                    lambda t: b_ref[t, at : at + SUB, :], y, SUB
+                    lambda t: b_ref[load, x0 : x0 + SUB, t * LANES : (t + 1) * LANES], y, SUB
                 )
                 rows = pl.ds((x0 * ny + y) * loads + load, SUB, stride=ny * loads)
                 batch.add(bt_ref, (rows, slice(None)), tile)
-    batch.flush()
-    even_y = is_even("gy")
-    pack_y_face(s, jnp.logical_not(even_y), bt_ref, dt_ref, y2_ref)
+        batch.flush()
+    pack_y_face(s, jnp.logical_not(is_even("gy")), bt_ref, dt_ref, y2_ref)
+
+
+def pack_rest_kernel(s, bt_ref, dt_ref, y1_ref, x1_ref, x2_ref, *corners):
+    even_x, even_y = is_even("gx"), is_even("gy")
+    upper_x, upper_y = ((even, jnp.logical_not(even)) for even in (even_x, even_y))
     pack_y_face(s, even_y, bt_ref, dt_ref, y1_ref)
+    pack_x_face(s, upper_x[1], bt_ref, dt_ref, x2_ref)
+    pack_x_face(s, upper_x[0], bt_ref, dt_ref, x1_ref)
+    for place, ref in enumerate(corners):
+        pack_corner(s, upper_x[place // 2], upper_y[place % 2], bt_ref, dt_ref, ref)
+
+
+def pack_corner(s, upper_x, upper_y, bt_ref, dt_ref, out_ref):
+    loads, nx, ny = s.loads, s.nx, s.ny
+    tiles = Tiles(bt_ref, ny, loads)
+    x0, y0 = pick(upper_x, nx - 2, 0), pick(upper_y, ny - 2, 0)
+    pack_tiles(out_ref, 0, loads, 4, lambda i: tiles[x0 + i // 2, y0 + i % 2])
+    x0, y0 = pick(upper_x, nx - 3, 0), pick(upper_y, ny - 3, 0)
+    batch = Batch()
+    for i in range(9):
+        row = dt_ref[pl.ds((x0 + i // 3) * ny + y0 + i % 3, 1), :]
+        batch.add(out_ref, (slice(s.c_dens + i, s.c_dens + i + 1), slice(None)), row)
+    batch.flush()
+    out_ref[s.c_dens + 9 :, :] = jnp.zeros((s.c_rows - s.c_dens - 9, LANES), jnp.float32)
+
+
+def pack_x_face(s, upper, bt_ref, dt_ref, out_ref):
+    loads, nx, ny = s.loads, s.nx, s.ny
+    tiles = Tiles(bt_ref, ny, loads)
+    x0 = pick(upper, nx - 2, 0)
+    pack_tiles(out_ref, 0, loads, 2 * ny, lambda i: tiles[x0 + i // ny, i % ny])
+    rows = pl.ds(pl.multiple_of(pick(upper, nx - 3, 0) * ny, SUB), 3 * ny)
+    out_ref[s.x_dens :, :] = dt_ref[rows, :]
 
 
 def pack_y_face(s, upper, bt_ref, dt_ref, out_ref):
@@ -248,31 +260,13 @@
     )
 
 
-def open_x_kernel(s, x_ref, t_ref):
-    tiles = Tiles(t_ref, s.ny, s.loads)
-    unpack_tiles(
-        x_ref, 0, s.loads, 2 * s.ny, lambda i, tile: [(tiles, (i // s.ny, i % s.ny), tile)]
-    )
-
-
-def corner_kernel(s, x2_ref, t2_ref, x1_ref, t1_ref, c1_ref, c2_ref):
-    loads, ny = s.loads, s.ny
-    open_x_kernel(s, x1_ref, t1_ref)
-    halves = Tiles(t1_ref, ny, loads), Tiles(t2_ref, ny, loads)
-    even_y = is_even("gy")
-    for out_ref, upper in ((c2_ref, jnp.logical_not(even_y)), (c1_ref, even_y)):
-        y0 = pick(upper, ny - 2, 0)
-        pack_tiles(out_ref, 0, loads, 8, lambda i: halves[i // 4][i // 2 % 2, y0 + i % 2])
-        y0 = pick(upper, ny - 3, 0)
-        batch, at = Batch(18), s.c_dens
-        for ref in (x1_ref, x2_ref):
-            for t in range(3):
-                for dy in range(3):
-                    row = ref[pl.ds(s.x_dens + t * ny + y0 + dy, 1), :]
-                    batch.add(out_ref, (slice(at, at + 1), slice(None)), row)
-                    at += 1
-        batch.flush()
-        out_ref[at:, :] = jnp.zeros((s.c_rows - at, LANES), jnp.float32)
+def open_x_kernel(s, x1_ref, x2_ref, t1_ref, t2_ref):
+    for x_ref, t_ref in ((x1_ref, t1_ref), (x2_ref, t2_ref)):
+        tiles = Tiles(t_ref, s.ny, s.loads)
+        unpack_tiles(
+            x_ref, 0, s.loads, 2 * s.ny,
+            lambda i, tile: [(tiles, (i // s.ny, i % s.ny), tile)],
+        )
 
 
 def join_density(s, dt_ref, y1_ref, y2_ref, dens_ref):
@@ -509,7 +503,8 @@
 
 
 def outer_kernel(
-    s, bt_ref, zt_ref, dens_ref, x1_ref, x2_ref, t1_ref, t2_ref, c1_ref, c2_ref,
+    s, bt_ref, zt_ref, dens_ref, x1_ref, x2_ref, t1_ref, t2_ref,
+    c11_ref, c12_ref, c21_ref, c22_ref,
     cond1, invx1, bx1, zx1, qx1, wx1, carry1, carry2, sums1,
     q_out, v_out, inv_out, sums_ref,
     low_ref, high_ref, low_d, high_d, cond2, invx2, bx2, zx2, qx2, wx2, carry3,
@@ -536,15 +531,16 @@
                 to = t * pitch + 3
                 batch.add(into, (slice(to, to + ny), slice(None)), rows)
             batch.flush()
-            for end, corner in enumerate((c1_ref, c2_ref)):
+            corners = ((c11_ref, c12_ref), (c21_ref, c22_ref))[side]
+            for end, corner in enumerate(corners):
                 alone = jnp.logical_or(alone_x, is_alone("gy", s.count_y, end))
                 for i in range(4):
                     tile = unpack_tile(
-                        lambda t: corner[t * loads : (t + 1) * loads, :], 4 * side + i, loads
+                        lambda t: corner[t * loads : (t + 1) * loads, :], i, loads
                     )
                     batch.add(tiles, (i // 2, ys[end] + i % 2), tile)
                 for i in range(9):
-                    at = s.c_dens + 9 * side + i
+                    at = s.c_dens + i
                     row = jnp.where(alone, 0.0, corner[at : at + 1, :])
                     to = i // 3 * pitch + yd[end] + i % 3
                     batch.add(into, (pl.ds(to, 1), slice(None)), row)
@@ -713,18 +709,31 @@
         copy.wait()
 
 
-def swap(array, axis, start):
-    counts = {name: lax.axis_size(name) for name in ("gx", "gy")}
-    other = "gy" if axis == "gx" else "gx"
+def swap(array, start_x=None, start_y=None):
+    count_x, count_y = lax.axis_size("gx"), lax.axis_size("gy")
+
+    def partner(place, start, count):
+        if start is None:
+            return place
+        to = place + (1 if (place - start) % 2 == 0 else -1)
+        return to if 0 <= to < count else None
+
     pairs = []
-    for at in np.ndindex(counts["gx"], counts["gy"]):
-        place = dict(zip(("gx", "gy"), at))
-        partner = place[axis] + (1 if (place[axis] - start) % 2 == 0 else -1)
-        if 0 <= partner < counts[axis]:
-            place[axis] = partner
-        elif place[other] ^ 1 < counts[other]:
-            place[other] ^= 1
-        pairs.append((at[0] * counts["gy"] + at[1], place["gx"] * counts["gy"] + place["gy"]))
+    for x, y in np.ndindex(count_x, count_y):
+        to_x, to_y = partner(x, start_x, count_x), partner(y, start_y, count_y)
+        if to_x is None and to_y is None:
+            to_x, to_y = x, y
+            if partner(count_x - 1 - x, start_x, count_x) is None:
+                to_x = count_x - 1 - x
+        elif to_x is None:
+            to_x = x
+            if start_y is None and y ^ 1 < count_y:
+                to_y = y ^ 1
+        elif to_y is None:
+            to_y = y
+            if start_x is None and x ^ 1 < count_x:
+                to_x = x ^ 1
+        pairs.append((x * count_y + y, to_x * count_y + to_y))
     return lax.ppermute(array, ("gx", "gy"), pairs)
 
 
@@ -749,32 +758,29 @@
 
     hbm = pl.BlockSpec(memory_space=pltpu.HBM)
     y_face, x_face, corner = (shape(rows, LANES) for rows in (s.y_rows, s.x_rows, s.c_rows))
-    b, dt, x1, x2 = call(
-        pack_x_kernel,
-        (shape(packed_count(ny), loads * nx, LANES), shape(nx * ny, LANES), x_face, x_face),
+    bt, dt, y2 = call(
+        pack_kernel,
+        (shape(nodes, LANES), shape(nx * ny, LANES), y_face),
         in_specs=[hbm, hbm],
-        scratch_shapes=[scratch(nx, flat), pltpu.SemaphoreType.DMA((packed_count(ny) + 1,))],
+        scratch_shapes=[
+            scratch(loads, nx, flat),
+            scratch(nx, flat),
+            pltpu.SemaphoreType.DMA((3,)),
+        ],
     )(
-        pltpu.with_memory_space_constraint(heat_source.reshape(loads * nx, flat), pltpu.HBM),
+        pltpu.with_memory_space_constraint(heat_source, pltpu.HBM),
         pltpu.with_memory_space_constraint(density, pltpu.HBM),
     )
-    x2, x1 = swap(x2, "gx", 1), swap(x1, "gx", 0)
-    bt, y1, y2 = call(pack_y_kernel, (shape(nodes, LANES), y_face, y_face))(b, dt)
-    y2, y1 = swap(y2, "gy", 1), swap(y1, "gy", 0)
+    y2 = swap(y2, start_y=1)
+    y1, x1, x2, *corners = call(pack_rest_kernel, (y_face, x_face, x_face) + (corner,) * 4)(bt, dt)
+    y1, x2, x1 = swap(y1, start_y=0), swap(x2, start_x=1), swap(x1, start_x=0)
+    corners = [swap(part, place // 2, place % 2) for place, part in enumerate(corners)]
     t1 = call(open_y_kernel, shape(2 * nx * loads, LANES))(y1)
-    xt = shape(2 * ny * loads, LANES)
-    xt2 = call(open_x_kernel, xt)(x2)
-    xt2, dt_later = lax.optimization_barrier((xt2, dt))
     zt = call(
         scale_kernel, shape(nodes, LANES), scratch_shapes=[scratch(nx * ny, LANES)]
-    )(bt, dt_later)
-    xt1, c1, c2 = call(
-        corner_kernel,
-        (xt, corner, corner),
-        cost_estimate=pl.CostEstimate(flops=2 * 10**9, transcendentals=0, bytes_accessed=0),
-    )(x2, xt2, x1)
-    xt1, dt = lax.optimization_barrier((xt1, dt))
-    c2, c1 = swap(c2, "gy", 1), swap(c1, "gy", 0)
+    )(bt, dt)
+    xt = shape(2 * ny * loads, LANES)
+    xt1, xt2 = call(open_x_kernel, (xt, xt))(x1, x2)
     plane = s.my * loads
     rows, field = shape(s.mx * s.pitch, LANES), shape(s.mx * plane, LANES)
     edge = shape(2 * plane, LANES)
@@ -797,7 +803,7 @@
         + [scratch(5 * s.pitch, LANES)] * 2
         + [scratch(5 * plane, LANES)] * 4
         + [scratch(2 * plane, LANES)],
-    )(bt, zt, dens, x1, x2, xt1, xt2, c1, c2, cond, inv_1, bx, zx, q_x, w_x, carry1, carry2, sums)
+    )(bt, zt, dens, x1, x2, xt1, xt2, *corners, cond, inv_1, bx, zx, q_x, w_x, carry1, carry2, sums)
     parts = lax.all_to_all(sums, ("gx", "gy"), 0, 0, tiled=True)
     whole = shape(loads, nx, flat)
     image, again, inverse = call(

time: 28.6 us -> 31.3 us (1.094)
  starting transfers between devices: 10.9 us -> 15.4 us
  waiting for transfers between devices: 8.52 us -> 6.76 us
    ppermute x6 -> x8, starting transfers between devices: 6.96 us -> 11.7 us  [swap(): return lax.ppermute(array, ('gx', 'gy'), pairs)]
    ppermute x6 -> x8, waiting for transfers between devices: 2.2 us -> 0.43 us  [swap(): return lax.ppermute(array, ('gx', 'gy'), pairs)]
    pallas_call x4 -> x3, Pallas kernels: 1.88 us -> 1.81 us  [the longest x1 1.56 us: per_device(): call(pack_kernel, (shape(nodes, LANES), shape(nx * ny, LANES), y_face), i...]
  transfers between devices with their start and end apart: 7 -> 9, of which waited for: 3 -> 2; matrix products, arithmetic and copies ran while one was open for 0% -> 0% of each run, Pallas kernels for 16% -> 12%
where the time goes in v20:
time: 31.3 us; the launch traced here: 31.1 us
  starting transfers between devices  15.4 us (49%)
  Pallas kernels  8.2 us (26%)
  waiting for transfers between devices  6.76 us (22%)
  between operations  0.73 us (2%)
    ppermute x8, starting transfers between devices, swap(): return lax.ppermute(array, ('gx', 'gy'), pairs)  11.7 us
    all_to_all x1, waiting for transfers between devices, per_device(): parts = lax.all_to_all(sums, ('gx', 'gy'), 0, 0, tiled=True)  6.32 us
    all_to_all x1, starting transfers between devices, per_device(): parts = lax.all_to_all(sums, ('gx', 'gy'), 0, 0, tiled=True)  3.7 us
    pallas_call x1, Pallas kernels, per_device(): call(inner_kernel, (shape(nx * s.pitch, LANES),) + (rows,) * 2 + (field,)...  2.74 us
    pallas_call x1, Pallas kernels, per_device(): call(pack_kernel, (shape(nodes, LANES), shape(nx * ny, LANES), y_face), i...  1.56 us
    pallas_call x1, Pallas kernels, per_device(): call(outer_kernel, (ends, ends, shape(ny, LANES), shape(devices, 1, LANES...  1.46 us
    pallas_call x1, Pallas kernels, per_device(): call(finish_kernel, (whole, whole), out_specs=(hbm, hbm), scratch_shapes=...  1.21 us
    pallas_call x1, Pallas kernels, per_device(): call(unpack_kernel, (whole, whole, shape(nx, flat)), scratch_shapes=[scra...  0.73 us
  transfers between devices with their start and end apart: 9, of which 2 were waited for; matrix products, arithmetic and copies ran while one was open for 0% of the time, Pallas kernels for 12%

profile of v20, /device:TPU:0, one launch (start us, length us, event | category | flops | bytes accessed | tf_op | source)
XLA Modules:
  0.0 31.1 jit_solution(12704700906756234730)
XLA Ops:
  0.6 1.6 %shard_map.41 = (f32[1024,128]{1,0:T(8,128)S(1)}, f32[128,128]{1,0:T(8,128)S(1)}, f32[240,128]{1,0:T(8,128)S(1)}) custom-call(f32[8,16,768]{2,1,0:T(8,128)} %b_ref.1, f32[16,768]{1,0:T(8,128)} %d_hbm.1), custom_call_target="tpu_custom_call" | custom-call | tf_op jit(solution)/shard_map/pallas_call | solution.py:761
  2.2 0.1 shard_map.43
  2.4 0.5 %collective-permute-start = (f32[240,128]{1,0:T(8,128)S(1)}, f32[240,128]{1,0:T(8,128)S(1)}, u32[]{:S(2)}, u32[]{:S(2)}) collective-permute-start(f32[240,128]{1,0:T(8,128)S(1)} %get-tuple-element.35), channel_id=1, source_target_pairs={{0,1},{1,0},{2,3},{3,2},{4,5},{5,4},{6,7},{7,6},{8,9},{9,8},{10,11... | collective-permute-start | bytes 368648 | tf_op jit(solution)/shard_map/ppermute | solution.py:737
  2.9 2.6 %collective-permute-start.1 = (f32[240,128]{1,0:T(8,128)S(1)}, f32[240,128]{1,0:T(8,128)S(1)}, u32[]{:S(2)}, u32[]{:S(2)}) collective-permute-start(f32[240,128]{1,0:T(8,128)S(1)} %get-tuple-element.36), channel_id=1, source_target_pairs={{0,8},{1,2},{2,1},{3,4},{4,3},{5,6},{6,5},{7,15},{8,0},{9,10},{10,... | collective-permute-start | bytes 368648 | tf_op jit(solution)/shard_map/ppermute | solution.py:737
  5.5 0.1 collective-permute-start.2
  5.6 1.2 %collective-permute-start.3 = (f32[120,128]{1,0:T(8,128)S(1)}, f32[120,128]{1,0:T(8,128)S(1)}, u32[]{:S(2)}, u32[]{:S(2)}) collective-permute-start(f32[120,128]{1,0:T(8,128)S(1)} %get-tuple-element.39), channel_id=1, source_target_pairs={{0,1},{1,0},{2,3},{3,2},{4,5},{5,4},{6,7},{7,6},{8,16},{9,17},{10,... | collective-permute-start | bytes 184328 | tf_op jit(solution)/shard_map/ppermute | solution.py:737
  6.8 2.5 %collective-permute-start.4 = (f32[40,128]{1,0:T(8,128)S(1)}, f32[40,128]{1,0:T(8,128)S(1)}, u32[]{:S(2)}, u32[]{:S(2)}) collective-permute-start(f32[40,128]{1,0:T(8,128)S(1)} %get-tuple-element.42), channel_id=1, source_target_pairs={{0,9},{1,8},{2,11},{3,10},{4,13},{5,12},{6,15},{7,14},{8,1},{9,0},... | collective-permute-start | bytes 61448 | tf_op jit(solution)/shard_map/ppermute | solution.py:737
  9.3 0.4 %collective-permute-done.2.x1_ref = f32[120,128]{1,0:T(8,128)S(1)} collective-permute-done((f32[120,128]{1,0:T(8,128)S(1)}, f32[120,128]{1,0:T(8,128)S(1)}, u32[]{:S(2)}, u32[]{:S(2)}) %collective-permute-start.2) | collective-permute-done | bytes 61472 | tf_op jit(solution)/shard_map/ppermute | solution.py:737
  9.7 2.0 %collective-permute-start.5 = (f32[40,128]{1,0:T(8,128)S(1)}, f32[40,128]{1,0:T(8,128)S(1)}, u32[]{:S(2)}, u32[]{:S(2)}) collective-permute-start(f32[40,128]{1,0:T(8,128)S(1)} %get-tuple-element.43), channel_id=1, source_target_pairs={{0,8},{1,10},{2,9},{3,12},{4,11},{5,14},{6,13},{7,15},{8,0},{9,2},... | collective-permute-start | bytes 61448 | tf_op jit(solution)/shard_map/ppermute | solution.py:737
  11.7 0.0 collective-permute-done.3.x2_ref
  11.7 0.2 collective-permute-start.6
  12.0 0.0 collective-permute-done.y_ref.y1_ref
  12.0 2.5 %collective-permute-start.7 = (f32[40,128]{1,0:T(8,128)S(1)}, f32[40,128]{1,0:T(8,128)S(1)}, u32[]{:S(2)}, u32[]{:S(2)}) collective-permute-start(f32[40,128]{1,0:T(8,128)S(1)} %get-tuple-element.45), channel_id=1, source_target_pairs={{0,24},{1,2},{2,1},{3,4},{4,3},{5,6},{6,5},{7,31},{8,16},{9,18},{1... | collective-permute-start | bytes 61448 | tf_op jit(solution)/shard_map/ppermute | solution.py:737
  14.5 0.1 shard_map.42.zt_ref
  14.6 0.1 shard_map.46
  14.7 0.1 shard_map.44.t1_ref
  14.9 0.0 collective-permute-done.1.y2_ref
  14.9 2.7 %shard_map.45 = (f32[256,128]{1,0:T(8,128)S(1)}, f32[320,128]{1,0:T(8,128)S(1)}, f32[320,128]{1,0:T(8,128)S(1)}, f32[1920,128]{1,0:T(8,128)S(1)}, f32[1920,128]{...) custom-call(f32[1024,128]{1,0:T(8,128)S(1)} %get-tuple-element.33.bt, ...), custom_call_target="tpu_custom_call" | custom-call | tf_op jit(solution)/shard_map/pallas_call | solution.py:788
  17.6 0.0 collective-permute-done.4.c11_ref
  17.6 0.0 collective-permute-done.5.c12_ref
  17.6 0.0 collective-permute-done.6.c21_ref
  17.6 0.0 collective-permute-done.7.c22_ref
  17.7 1.5 %shard_map.47 = (f32[320,128]{1,0:T(8,128)S(1)}, f32[320,128]{1,0:T(8,128)S(1)}, f32[8,128]{1,0:T(8,128)S(1)}, f32[32,1,128]{2,1,0:T(1,128)}) custom-call(f32[1024,128]{1,0:T(8,128)S(1)} %get-tuple-element.33.bt_ref, f32[1024,128]{1,0:T(8,128)S(1)} %shard_map.42.zt_ref, f32[256,128]{1,0:T(8,128)S(1)} %get-tuple-element.37.dens_ref, ...), custom_call_target="tpu_custom_call" | custom-call | tf_op jit(solution)/shard_map/pallas_call | solution.py:798
  19.1 3.7 %all-to-all-start = ((f32[32,1,128]{2,1,0:T(1,128)}), f32[32,1,128]{2,1,0:T(1,128)S(1)}, u32[]{:S(2)}, u32[]{:S(2)}) async-start(f32[32,1,128]{2,1,0:T(1,128)} %get-tuple-element.55), calls=%async_computation | async-start | bytes 32768 | tf_op jit(solution)/shard_map/all_to_all | solution.py:807
  22.8 0.0 copy-start
  22.8 0.7 %shard_map.48 = (f32[8,16,768]{2,1,0:T(8,128)S(1)}, f32[8,16,768]{2,1,0:T(8,128)S(1)}, f32[16,768]{1,0:T(8,128)S(1)}) custom-call(f32[1024,128]{1,0:T(8,128)S(1)} %get-tuple-element.56.q1_ref, f32[320,128]{1,0:T(8,128)S(1)} %get-tuple-element.57.q2_ref, f32[1024,128]{1,0:T(8,128)S(1)} %get-tuple-element.58.v1_ref, f32[320,128]{1,0:T(8,128)S(1)} %get-tuple-element.59.v2_ref, ...), custom_call_target="tpu_custom_call" | custom-call | tf_op jit(solution)/shard_map/pallas_call | solution.py:809
  23.6 6.3 %all-to-all-done.parts_ref = f32[32,1,128]{2,1,0:T(1,128)S(1)} async-done(((f32[32,1,128]{2,1,0:T(1,128)}), f32[32,1,128]{2,1,0:T(1,128)S(1)}, u32[]{:S(2)}, u32[]{:S(2)}) %all-to-all-start) | async-done | bytes 16416 | tf_op jit(solution)/shard_map/all_to_all | solution.py:807
  29.9 0.0 copy-done
  29.9 1.2 %shard_map.49 = (f32[8,16,768]{2,1,0:T(8,128)}, f32[8,16,768]{2,1,0:T(8,128)}) custom-call(f32[32,1,128]{2,1,0:T(1,128)S(1)} %all-to-all-done.parts_ref, f32[8,16,768]{2,1,0:T(8,128)S(1)} %copy-done, f32[8,16,768]{2,1,0:T(8,128)S(1)} %get-tuple-element.61.q_ref, f32[8,16,768]{2,1,0:T(8,128)S(1)} %get-tuple-element.62.v_ref, ...), custom_call_target="tpu_custom_call" | custom-call | tf_op jit(solution)/shard_map/pallas_call | solution.py:814
Async XLA Ops:
  2.4 9.6 %collective-permute-start = (f32[240,128]{1,0:T(8,128)S(1)}, f32[240,128]{1,0:T(8,128)S(1)}, u32[]{:S(2)}, u32[]{:S(2)}) collective-permute-start(f32[240,128]{1,0:T(8,128)S(1)} %get-tuple-element.35), channel_id=1, source_target_pairs={{0,1},{1,0},{2,3},{3,2},{4,5},{5,4},{6,7},{7,6},{8,9},{9,8},{10,11... | collective-permute-start | bytes 368648 | tf_op jit(solution)/shard_map/ppermute | solution.py:737
  2.9 12.0 %collective-permute-start.1 = (f32[240,128]{1,0:T(8,128)S(1)}, f32[240,128]{1,0:T(8,128)S(1)}, u32[]{:S(2)}, u32[]{:S(2)}) collective-permute-start(f32[240,128]{1,0:T(8,128)S(1)} %get-tuple-element.36), channel_id=1, source_target_pairs={{0,8},{1,2},{2,1},{3,4},{4,3},{5,6},{6,5},{7,15},{8,0},{9,10},{10,... | collective-permute-start | bytes 368648 | tf_op jit(solution)/shard_map/ppermute | solution.py:737
  5.5 4.2 %collective-permute-start.2 = (f32[120,128]{1,0:T(8,128)S(1)}, f32[120,128]{1,0:T(8,128)S(1)}, u32[]{:S(2)}, u32[]{:S(2)}) collective-permute-start(f32[120,128]{1,0:T(8,128)S(1)} %get-tuple-element.38), channel_id=1, source_target_pairs={{0,8},{1,9},{2,10},{3,11},{4,12},{5,13},{6,14},{7,15},{8,0},{9,1},... | collective-permute-start | bytes 184328 | tf_op jit(solution)/shard_map/ppermute | solution.py:737
  5.6 6.1 %collective-permute-start.3 = (f32[120,128]{1,0:T(8,128)S(1)}, f32[120,128]{1,0:T(8,128)S(1)}, u32[]{:S(2)}, u32[]{:S(2)}) collective-permute-start(f32[120,128]{1,0:T(8,128)S(1)} %get-tuple-element.39), channel_id=1, source_target_pairs={{0,1},{1,0},{2,3},{3,2},{4,5},{5,4},{6,7},{7,6},{8,16},{9,17},{10,... | collective-permute-start | bytes 184328 | tf_op jit(solution)/shard_map/ppermute | solution.py:737
  6.8 10.8 %collective-permute-start.4 = (f32[40,128]{1,0:T(8,128)S(1)}, f32[40,128]{1,0:T(8,128)S(1)}, u32[]{:S(2)}, u32[]{:S(2)}) collective-permute-start(f32[40,128]{1,0:T(8,128)S(1)} %get-tuple-element.42), channel_id=1, source_target_pairs={{0,9},{1,8},{2,11},{3,10},{4,13},{5,12},{6,15},{7,14},{8,1},{9,0},... | collective-permute-start | bytes 61448 | tf_op jit(solution)/shard_map/ppermute | solution.py:737
  9.7 7.9 %collective-permute-start.5 = (f32[40,128]{1,0:T(8,128)S(1)}, f32[40,128]{1,0:T(8,128)S(1)}, u32[]{:S(2)}, u32[]{:S(2)}) collective-permute-start(f32[40,128]{1,0:T(8,128)S(1)} %get-tuple-element.43), channel_id=1, source_target_pairs={{0,8},{1,10},{2,9},{3,12},{4,11},{5,14},{6,13},{7,15},{8,0},{9,2},... | collective-permute-start | bytes 61448 | tf_op jit(solution)/shard_map/ppermute | solution.py:737
  11.7 5.9 %collective-permute-start.6 = (f32[40,128]{1,0:T(8,128)S(1)}, f32[40,128]{1,0:T(8,128)S(1)}, u32[]{:S(2)}, u32[]{:S(2)}) collective-permute-start(f32[40,128]{1,0:T(8,128)S(1)} %get-tuple-element.44), channel_id=1, source_target_pairs={{0,1},{1,0},{2,3},{3,2},{4,5},{5,4},{6,7},{7,6},{8,17},{9,16},{10,... | collective-permute-start | bytes 61448 | tf_op jit(solution)/shard_map/ppermute | solution.py:737
  12.0 5.7 %collective-permute-start.7 = (f32[40,128]{1,0:T(8,128)S(1)}, f32[40,128]{1,0:T(8,128)S(1)}, u32[]{:S(2)}, u32[]{:S(2)}) collective-permute-start(f32[40,128]{1,0:T(8,128)S(1)} %get-tuple-element.45), channel_id=1, source_target_pairs={{0,24},{1,2},{2,1},{3,4},{4,3},{5,6},{6,5},{7,31},{8,16},{9,18},{1... | collective-permute-start | bytes 61448 | tf_op jit(solution)/shard_map/ppermute | solution.py:737
  19.1 10.8 %all-to-all-start = ((f32[32,1,128]{2,1,0:T(1,128)}), f32[32,1,128]{2,1,0:T(1,128)S(1)}, u32[]{:S(2)}, u32[]{:S(2)}) async-start(f32[32,1,128]{2,1,0:T(1,128)} %get-tuple-element.55), calls=%async_computation | async-start | bytes 32768 | tf_op jit(solution)/shard_map/all_to_all | solution.py:807
  22.8 7.1 %copy-start = (f32[8,16,768]{2,1,0:T(8,128)S(1)}, f32[8,16,768]{2,1,0:T(8,128)}, u32[]{:S(2)}) copy-start(f32[8,16,768]{2,1,0:T(8,128)} %b_ref.1) | copy-start | bytes 1179652

commit v21 on v19

--- a/solution.py
+++ b/solution.py
@@ -317,10 +317,10 @@
     return pltpu.roll(tile, LANES - 1, 1)
 
 
-def element_planes(cond, carry, a, count, y0, columns, field, emitter, keep=True):
+def element_planes(cond, carry, a, count, y0, columns, field, field_up, emitter, keep=True):
     def loads_of(step):
         y = y0 + step
-        right = [field[a + u, y + 1] for u in range(count + 1)]
+        right = [(field[a + u, y + 1], field_up[a + u, y + 1]) for u in range(count + 1)]
         conduct = [cond[a + u, y] for u in range(count)]
         above = extra = None
         if step and emitter:
@@ -328,7 +328,7 @@
             extra = [emitter.fetch(a + u, y) for u in range(count)]
         return right, conduct, above, extra
 
-    left = [(tile, up(tile)) for tile in [field[a + u, y0] for u in range(count + 1)]]
+    left = [(field[a + u, y0], field_up[a + u, y0]) for u in range(count + 1)]
     ahead = loads_of(0)
     old, waiting = [None] * count, []
     for step in range(columns):
@@ -340,7 +340,6 @@
             for into, at, tile in waiting.pop(0):
                 into[at] = tile
         stores = []
-        right = [(tile, up(tile)) for tile in right]
         for u in range(count):
             (p0, p0s), (p1, p1s) = left[u], left[u + 1]
             (r0, r0s), (r1, r1s) = right[u], right[u + 1]
@@ -374,8 +373,8 @@
 
 
 class First:
-    def __init__(self, bx, invx, qx, wx):
-        self.bx, self.invx, self.qx, self.wx = bx, invx, qx, wx
+    def __init__(self, bx, invx, qx, wx, wu):
+        self.bx, self.invx, self.qx, self.wx, self.wu = bx, invx, qx, wx, wu
 
     def fetch(self, x, y):
         return self.bx[x, y], self.invx[x, y]
@@ -383,7 +382,9 @@
     def finish(self, x, y, node, total, extra):
         source, inverse = extra
         image = 1.25 * source - total
-        return [(self.qx, (x, y), image), (self.wx, (x, y), image * inverse)]
+        weighted = image * inverse
+        at = x, y
+        return [(self.qx, at, image), (self.wx, at, weighted), (self.wu, at, up(weighted))]
 
 
 class Second:
@@ -415,18 +416,18 @@
     return state
 
 
-def inside_fields(s, bt_ref, zt_ref, bx, zx):
-    brick = (Tiles(ref, s.ny, s.loads) for ref in (bt_ref, zt_ref))
-    starts = (2, 3)
+def inside_fields(s, bt_ref, zt_ref, ut_ref, bx, zx, zu):
+    brick = (Tiles(ref, s.ny, s.loads) for ref in (bt_ref, zt_ref, ut_ref))
+    starts = (2, 3, 3)
     return tuple(
         Inside(inner, range(start, s.ny + 2), outer)
-        for inner, start, outer in zip(brick, starts, (bx, zx))
-    )
-
-
-def scale_kernel(s, bt_ref, dt_ref, zt_ref, inv_ref):
+        for inner, start, outer in zip(brick, starts, (bx, zx, zu))
+    )
+
+
+def scale_kernel(s, bt_ref, dt_ref, zt_ref, ut_ref, inv_ref):
     loads, nx, ny = s.loads, s.nx, s.ny
-    inner, scaled = Tiles(bt_ref, ny, loads), Tiles(zt_ref, ny, loads)
+    inner, scaled, shifted = (Tiles(ref, ny, loads) for ref in (bt_ref, zt_ref, ut_ref))
     inverse = Rows(inv_ref, ny, loads)
     before = conduct_of(dt_ref[0:ny, :])
     for x in range(1, nx):
@@ -439,17 +440,19 @@
     batch = Batch(16)
     for x in range(1, nx):
         for y in range(1, ny):
-            batch.add(scaled, (x, y), inner[x, y] * inverse[x, y - 1])
+            tile = inner[x, y] * inverse[x, y - 1]
+            batch.add(scaled, (x, y), tile)
+            batch.add(shifted, (x, y), up(tile))
     batch.flush()
 
 
 def inner_kernel(
-    s, bt_ref, zt_ref, dt_ref, y1_ref, y2_ref, t1_ref,
-    dens_ref, cond, invx, bx, zx, qx, wx, q_out, v_out, carry1, carry2, sums_ref,
+    s, bt_ref, zt_ref, ut_ref, dt_ref, y1_ref, y2_ref, t1_ref,
+    dens_ref, cond, invx, bx, zx, zu, qx, wx, wu, q_out, v_out, carry1, carry2, sums_ref,
 ):
     loads, nx, ny, my, pitch = s.loads, s.nx, s.ny, s.my, s.pitch
-    bx, zx, qx, wx, carry1, carry2 = (
-        Tiles(ref, my, loads) for ref in (bx, zx, qx, wx, carry1, carry2)
+    bx, zx, zu, qx, wx, wu, carry1, carry2 = (
+        Tiles(ref, my, loads) for ref in (bx, zx, zu, qx, wx, wu, carry1, carry2)
     )
     q_out, v_out = Tiles(q_out, ny, loads), Tiles(v_out, ny, loads)
     cond, invx = Rows(cond, pitch, loads), Rows(invx, pitch, loads)
@@ -464,17 +467,20 @@
             invx.put(x + 2, inverse_of(s, before, after))
         before = after
 
-    bx, zx = inside_fields(s, bt_ref, zt_ref, bx, zx)
+    bx, zx, zu = inside_fields(s, bt_ref, zt_ref, ut_ref, bx, zx, zu)
 
     def stage(x, y, tile):
         stores = [(bx, (x + 2, y), tile)]
         if x:
-            stores.append((zx, (x + 2, y), tile * invx[x + 2, y]))
+            scaled = tile * invx[x + 2, y]
+            stores += [(zx, (x + 2, y), scaled), (zu, (x + 2, y), up(scaled))]
         return stores
 
     batch = Batch(16)
     for x in range(1, nx):
-        batch.add(zx, (x + 2, 2), bx[x + 2, 2] * invx[x + 2, 2])
+        scaled = bx[x + 2, 2] * invx[x + 2, 2]
+        batch.add(zx, (x + 2, 2), scaled)
+        batch.add(zu, (x + 2, 2), up(scaled))
     batch.flush()
     unpack_tiles(
         y2_ref, 0, loads, 2 * nx, lambda i, tile: stage(i // 2, ys[1] + i % 2, tile)
@@ -487,19 +493,20 @@
                 batch.add(*store)
     batch.flush()
 
-    element_planes(cond, carry1, 3, 1, 0, my - 1, zx, None)
+    element_planes(cond, carry1, 3, 1, 0, my - 1, zx, zu, None)
 
     def first(a, count, state):
-        element_planes(cond, carry1, a, count, 0, my - 1, zx, First(bx, invx, qx, wx))
+        emitter = First(bx, invx, qx, wx, wu)
+        element_planes(cond, carry1, a, count, 0, my - 1, zx, zu, emitter)
         return state
 
     over_planes(4, nx + 1, first, 0)
-    element_planes(cond, carry2, 4, 1, 1, my - 3, wx, None)
+    element_planes(cond, carry2, 4, 1, 1, my - 3, wx, wu, None)
 
     def second(a, count, sums):
         sums = list(sums)
         emitter = Second(bx, zx, qx, q_out, v_out, sums)
-        element_planes(cond, carry2, a, count, 1, my - 3, wx, emitter)
+        element_planes(cond, carry2, a, count, 1, my - 3, wx, wu, emitter)
         return tuple(sums)
 
     zero = jnp.zeros((loads, LANES), jnp.float32)
@@ -509,10 +516,10 @@
 
 
 def outer_kernel(
-    s, bt_ref, zt_ref, dens_ref, x1_ref, x2_ref, t1_ref, t2_ref, c1_ref, c2_ref,
-    cond1, invx1, bx1, zx1, qx1, wx1, carry1, carry2, sums1,
+    s, bt_ref, zt_ref, ut_ref, dens_ref, x1_ref, x2_ref, t1_ref, t2_ref, c1_ref, c2_ref,
+    cond1, invx1, bx1, zx1, zu1, qx1, wx1, wu1, carry1, carry2, sums1,
     q_out, v_out, inv_out, sums_ref,
-    low_ref, high_ref, low_d, high_d, cond2, invx2, bx2, zx2, qx2, wx2, carry3,
+    low_ref, high_ref, low_d, high_d, cond2, invx2, bx2, zx2, zu2, qx2, wx2, wu2, carry3,
 ):
     loads, nx, ny, mx, my, pitch = s.loads, s.nx, s.ny, s.mx, s.my, s.pitch
     even_x = is_even("gx")
@@ -568,12 +575,14 @@
     scaled_own = outside + (2,)
     image_own = (1, 2, 3, nx + 1, nx + 2)
     cond, invx = joined_rows(cond2, cond1, outside), joined_rows(invx2, invx1, scaled_own)
-    bx1, zx1 = inside_fields(
-        s, bt_ref, zt_ref, Tiles(bx1, my, loads), Tiles(zx1, my, loads)
+    bx1, zx1, zu1 = inside_fields(
+        s, bt_ref, zt_ref, ut_ref, *(Tiles(ref, my, loads) for ref in (bx1, zx1, zu1))
     )
     bx = Joined(Tiles(bx2, my, loads), bx1, outside)
     zx = Joined(Tiles(zx2, my, loads), zx1, scaled_own)
+    zu = Joined(Tiles(zu2, my, loads), zu1, scaled_own)
     qx, wx = joined(qx2, qx1, image_own), joined(wx2, wx1, image_own)
+    wu = joined(wu2, wu1, image_own)
     own = [x - 2 for x in outer_planes(nx)]
     q_out, v_out = (Joined(Tiles(ref, ny, loads), None, own) for ref in (q_out, v_out))
     carry1, carry2, carry3 = (Tiles(ref, my, loads) for ref in (carry1, carry2, carry3))
@@ -600,22 +609,26 @@
             for y in range(my):
                 tile = tiles[dx, y]
                 batch.add(bx, (x0 + dx, y), tile)
-                batch.add(zx, (x0 + dx, y), tile * invx[x0 + dx, y])
+                scaled = tile * invx[x0 + dx, y]
+                batch.add(zx, (x0 + dx, y), scaled)
+                batch.add(zu, (x0 + dx, y), up(scaled))
     for y in range(my):
-        batch.add(zx, (2, y), bx[2, y] * invx[2, y])
-    batch.flush()
-
-    emitter = First(bx, invx, qx, wx)
-    element_planes(cond, carry3, 0, 1, 0, my - 1, zx, None)
-    element_planes(cond, carry3, 1, 2, 0, my - 1, zx, emitter)
-    element_planes(cond, carry3, 3, 1, 0, my - 1, zx, emitter, keep=False)
-    element_planes(cond, carry1, nx + 1, 2, 0, my - 1, zx, emitter, keep=False)
+        scaled = bx[2, y] * invx[2, y]
+        batch.add(zx, (2, y), scaled)
+        batch.add(zu, (2, y), up(scaled))
+    batch.flush()
+
+    emitter = First(bx, invx, qx, wx, wu)
+    element_planes(cond, carry3, 0, 1, 0, my - 1, zx, zu, None)
+    element_planes(cond, carry3, 1, 2, 0, my - 1, zx, zu, emitter)
+    element_planes(cond, carry3, 3, 1, 0, my - 1, zx, zu, emitter, keep=False)
+    element_planes(cond, carry1, nx + 1, 2, 0, my - 1, zx, zu, emitter, keep=False)
     sums = [sums1[place * loads : (place + 1) * loads, :] for place in range(4)]
     emitter = Second(bx, zx, qx, q_out, v_out, sums)
-    element_planes(cond, carry3, 1, 1, 1, my - 3, wx, None)
-    element_planes(cond, carry3, 2, 2, 1, my - 3, wx, emitter)
-    element_planes(cond, carry3, 4, 1, 1, my - 3, wx, emitter, keep=False)
-    element_planes(cond, carry2, nx, 2, 1, my - 3, wx, emitter, keep=False)
+    element_planes(cond, carry3, 1, 1, 1, my - 3, wx, wu, None)
+    element_planes(cond, carry3, 2, 2, 1, my - 3, wx, wu, emitter)
+    element_planes(cond, carry3, 4, 1, 1, my - 3, wx, wu, emitter, keep=False)
+    element_planes(cond, carry2, nx, 2, 1, my - 3, wx, wu, emitter, keep=False)
     lane = lane_ids(loads)
     load = lax.broadcasted_iota(jnp.int32, (loads, LANES), 0)
     packed = jnp.zeros((loads, LANES), jnp.float32)
@@ -765,8 +778,9 @@
     xt = shape(2 * ny * loads, LANES)
     xt2 = call(open_x_kernel, xt)(x2)
     xt2, dt_later = lax.optimization_barrier((xt2, dt))
-    zt = call(
-        scale_kernel, shape(nodes, LANES), scratch_shapes=[scratch(nx * ny, LANES)]
+    inside = shape(nodes, LANES)
+    zt, ut = call(
+        scale_kernel, (inside, inside), scratch_shapes=[scratch(nx * ny, LANES)]
     )(bt, dt_later)
     xt1, c1, c2 = call(
         corner_kernel,
@@ -778,16 +792,15 @@
     plane = s.my * loads
     rows, field = shape(s.mx * s.pitch, LANES), shape(s.mx * plane, LANES)
     edge = shape(2 * plane, LANES)
-    inside = shape(nodes, LANES)
-    dens, cond, inv_1, bx, zx, q_x, w_x, q_1, v_1, carry1, carry2, sums = call(
+    dens, cond, inv_1, bx, zx, zu, q_x, w_x, w_u, q_1, v_1, carry1, carry2, sums = call(
         inner_kernel,
         (shape(nx * s.pitch, LANES),)
         + (rows,) * 2
-        + (field,) * 4
+        + (field,) * 6
         + (inside,) * 2
         + (edge,) * 2
         + (shape(4 * loads, LANES),),
-    )(bt, zt, dt, y1, y2, t1)
+    )(bt, zt, ut, dt, y1, y2, t1)
     ends = shape(len(outer_planes(nx)) * ny * loads, LANES)
     q_2, v_2, inv_2, sums = call(
         outer_kernel,
@@ -795,9 +808,9 @@
         scratch_shapes=[scratch(2 * plane, LANES)] * 2
         + [scratch(3 * s.pitch, LANES)] * 2
         + [scratch(5 * s.pitch, LANES)] * 2
-        + [scratch(5 * plane, LANES)] * 4
+        + [scratch(5 * plane, LANES)] * 6
         + [scratch(2 * plane, LANES)],
-    )(bt, zt, dens, x1, x2, xt1, xt2, c1, c2, cond, inv_1, bx, zx, q_x, w_x, carry1, carry2, sums)
+    )(bt, zt, ut, dens, x1, x2, xt1, xt2, c1, c2, cond, inv_1, bx, zx, zu, q_x, w_x, w_u, carry1, carry2, sums)
     parts = lax.all_to_all(sums, ("gx", "gy"), 0, 0, tiled=True)
     whole = shape(loads, nx, flat)
     image, again, inverse = call(

time: 28.6 us -> 28.3 us (0.990)
    pallas_call x1, Pallas kernels: 2.73 us -> 2.4 us  [per_device(): call(inner_kernel, (shape(nx * s.pitch, LANES),) + (rows,) * 2 + (field,)...]
  transfers between devices with their start and end apart: 7 -> 7, of which waited for: 3 -> 3; matrix products, arithmetic and copies ran while one was open for 0% -> 0% of each run, Pallas kernels for 16% -> 15%
where the time goes in v21:
time: 28.3 us; the launch traced here: 28.1 us
  starting transfers between devices  10.9 us (39%)
  waiting for transfers between devices  8.39 us (30%)
  Pallas kernels  8.03 us (28%)
  between operations  0.74 us (3%)
    ppermute x6, starting transfers between devices, swap(): return lax.ppermute(array, ('gx', 'gy'), pairs)  6.96 us
    all_to_all x1, waiting for transfers between devices, per_device(): parts = lax.all_to_all(sums, ('gx', 'gy'), 0, 0, tiled=True)  6.32 us
    all_to_all x1, starting transfers between devices, per_device(): parts = lax.all_to_all(sums, ('gx', 'gy'), 0, 0, tiled=True)  3.97 us
    pallas_call x1, Pallas kernels, per_device(): call(inner_kernel, (shape(nx * s.pitch, LANES),) + (rows,) * 2 + (field,)...  2.4 us
    ppermute x6, waiting for transfers between devices, swap(): return lax.ppermute(array, ('gx', 'gy'), pairs)  2.06 us
    pallas_call x1, Pallas kernels, per_device(): call(outer_kernel, (ends, ends, shape(ny, LANES), shape(devices, 1, LANES...  1.44 us
    pallas_call x1, Pallas kernels, per_device(): call(finish_kernel, (whole, whole), out_specs=(hbm, hbm), scratch_shapes=...  1.21 us
    pallas_call x1, Pallas kernels, per_device(): call(pack_x_kernel, (shape(packed_count(ny), loads * nx, LANES), shape(nx...  1.13 us
  transfers between devices with their start and end apart: 7, of which 3 were waited for; matrix products, arithmetic and copies ran while one was open for 0% of the time, Pallas kernels for 15%

profile of v21, /device:TPU:0, one launch (start us, length us, event | category | flops | bytes accessed | tf_op | source)
XLA Modules:
  0.0 28.1 jit_solution(16228498637892417787)
XLA Ops:
  0.6 1.1 %shard_map.41 = (f32[6,128,128]{2,1,0:T(8,128)S(1)}, f32[128,128]{1,0:T(8,128)S(1)}, f32[120,128]{1,0:T(8,128)S(1)}, f32[120,128]{1,0:T(8,128)S(1)}) custom-call(f32[128,768]{1,0:T(8,128)} %bitcast.1, f32[16,768]{1,0:T(8,128)} %d_hbm.1), custom_call_target="tpu_custom_call" | custom-call | tf_op jit(solution)/shard_map/pallas_call | solution.py:765
  1.8 0.5 %collective-permute-start = (f32[120,128]{1,0:T(8,128)S(1)}, f32[120,128]{1,0:T(8,128)S(1)}, u32[]{:S(2)}, u32[]{:S(2)}) collective-permute-start(f32[120,128]{1,0:T(8,128)S(1)} %get-tuple-element.42), channel_id=1, source_target_pairs={{0,1},{1,0},{2,3},{3,2},{4,5},{5,4},{6,7},{7,6},{8,16},{9,17},{10,... | collective-permute-start | bytes 184328 | tf_op jit(solution)/shard_map/ppermute | solution.py:741
  2.3 4.1 %collective-permute-start.1 = (f32[120,128]{1,0:T(8,128)S(1)}, f32[120,128]{1,0:T(8,128)S(1)}, u32[]{:S(2)}, u32[]{:S(2)}) collective-permute-start(f32[120,128]{1,0:T(8,128)S(1)} %get-tuple-element.47), channel_id=1, source_target_pairs={{0,8},{1,9},{2,10},{3,11},{4,12},{5,13},{6,14},{7,15},{8,0},{9,1},... | collective-permute-start | bytes 184328 | tf_op jit(solution)/shard_map/ppermute | solution.py:741
  6.4 0.5 %shard_map.42 = (f32[1024,128]{1,0:T(8,128)S(1)}, f32[240,128]{1,0:T(8,128)S(1)}, f32[240,128]{1,0:T(8,128)S(1)}) custom-call(f32[6,128,128]{2,1,0:T(8,128)S(1)} %get-tuple-element.39.b_ref, f32[128,128]{1,0:T(8,128)S(1)} %get-tuple-element.49.dt_ref), custom_call_target="tpu_custom_call" | custom-call | tf_op jit(solution)/shard_map/pallas_call | solution.py:775
  6.9 0.1 collective-permute-start.2
  7.0 0.1 collective-permute-start.3
  7.1 0.0 collective-permute-done.x_ref.x2_ref
  7.1 0.1 shard_map.43.t2_ref
  7.2 1.4 %collective-permute-done.1.x1_ref = f32[120,128]{1,0:T(8,128)S(1)} collective-permute-done((f32[120,128]{1,0:T(8,128)S(1)}, f32[120,128]{1,0:T(8,128)S(1)}, u32[]{:S(2)}, u32[]{:S(2)}) %collective-permute-start.1) | collective-permute-done | bytes 61472 | tf_op jit(solution)/shard_map/ppermute | solution.py:741
  8.6 0.2 shard_map.45
  8.8 0.2 collective-permute-start.4
  9.0 1.9 %collective-permute-start.5 = (f32[72,128]{1,0:T(8,128)S(1)}, f32[72,128]{1,0:T(8,128)S(1)}, u32[]{:S(2)}, u32[]{:S(2)}) collective-permute-start(f32[72,128]{1,0:T(8,128)S(1)} %get-tuple-element.55), channel_id=1, source_target_pairs={{0,8},{1,2},{2,1},{3,4},{4,3},{5,6},{6,5},{7,15},{8,0},{9,10},{10,... | collective-permute-start | bytes 110600 | tf_op jit(solution)/shard_map/ppermute | solution.py:741
  10.9 0.3 shard_map.44
  11.2 0.0 collective-permute-done.2.y_ref.y1_ref
  11.2 0.1 shard_map.46.t1_ref
  11.3 0.6 %collective-permute-done.3.y2_ref = f32[240,128]{1,0:T(8,128)S(1)} collective-permute-done((f32[240,128]{1,0:T(8,128)S(1)}, f32[240,128]{1,0:T(8,128)S(1)}, u32[]{:S(2)}, u32[]{:S(2)}) %collective-permute-start.3) | collective-permute-done | bytes 122912 | tf_op jit(solution)/shard_map/ppermute | solution.py:741
  12.0 2.4 %shard_map.47 = (f32[256,128]{1,0:T(8,128)S(1)}, f32[320,128]{1,0:T(8,128)S(1)}, f32[320,128]{1,0:T(8,128)S(1)}, f32[1920,128]{1,0:T(8,128)S(1)}, f32[1920,128]{...) custom-call(f32[1024,128]{1,0:T(8,128)S(1)} %get-tuple-element.41.bt, ...), custom_call_target="tpu_custom_call" | custom-call | tf_op jit(solution)/shard_map/pallas_call | solution.py:795
  14.4 0.0 collective-permute-done.4.c1_ref
  14.4 0.0 collective-permute-done.5.c2_ref
  14.4 1.4 %shard_map.48 = (f32[320,128]{1,0:T(8,128)S(1)}, f32[320,128]{1,0:T(8,128)S(1)}, f32[8,128]{1,0:T(8,128)S(1)}, f32[32,1,128]{2,1,0:T(1,128)}) custom-call(f32[1024,128]{1,0:T(8,128)S(1)} %get-tuple-element.41.bt_ref, f32[1024,128]{1,0:T(8,128)S(1)} %get-tuple-element.44.zt_ref, f32[1024,128]{1,0:T(8,128)S(1)} %get-tuple-element.45.ut_ref, ...), custom_call_target="tpu_custom_call" | custom-call | tf_op jit(solution)/shard_map/pallas_call | solution.py:805
  15.8 4.0 %all-to-all-start = ((f32[32,1,128]{2,1,0:T(1,128)}), f32[32,1,128]{2,1,0:T(1,128)S(1)}, u32[]{:S(2)}, u32[]{:S(2)}) async-start(f32[32,1,128]{2,1,0:T(1,128)} %get-tuple-element.67), calls=%async_computation | async-start | bytes 32768 | tf_op jit(solution)/shard_map/all_to_all | solution.py:814
  19.8 0.0 copy-start
  19.8 0.7 %shard_map.49 = (f32[8,16,768]{2,1,0:T(8,128)S(1)}, f32[8,16,768]{2,1,0:T(8,128)S(1)}, f32[16,768]{1,0:T(8,128)S(1)}) custom-call(f32[1024,128]{1,0:T(8,128)S(1)} %get-tuple-element.68.q1_ref, f32[320,128]{1,0:T(8,128)S(1)} %get-tuple-element.69.q2_ref, f32[1024,128]{1,0:T(8,128)S(1)} %get-tuple-element.70.v1_ref, f32[320,128]{1,0:T(8,128)S(1)} %get-tuple-element.71.v2_ref, ...), custom_call_target="tpu_custom_call" | custom-call | tf_op jit(solution)/shard_map/pallas_call | solution.py:816
  20.6 6.3 %all-to-all-done.parts_ref = f32[32,1,128]{2,1,0:T(1,128)S(1)} async-done(((f32[32,1,128]{2,1,0:T(1,128)}), f32[32,1,128]{2,1,0:T(1,128)S(1)}, u32[]{:S(2)}, u32[]{:S(2)}) %all-to-all-start) | async-done | bytes 16416 | tf_op jit(solution)/shard_map/all_to_all | solution.py:814
  26.9 0.0 copy-done
  26.9 1.2 %shard_map.50 = (f32[8,16,768]{2,1,0:T(8,128)}, f32[8,16,768]{2,1,0:T(8,128)}) custom-call(f32[32,1,128]{2,1,0:T(1,128)S(1)} %all-to-all-done.parts_ref, f32[8,16,768]{2,1,0:T(8,128)S(1)} %copy-done, f32[8,16,768]{2,1,0:T(8,128)S(1)} %get-tuple-element.73.q_ref, f32[8,16,768]{2,1,0:T(8,128)S(1)} %get-tuple-element.74.v_ref, ...), custom_call_target="tpu_custom_call" | custom-call | tf_op jit(solution)/shard_map/pallas_call | solution.py:821
Async XLA Ops:
  1.8 5.3 %collective-permute-start = (f32[120,128]{1,0:T(8,128)S(1)}, f32[120,128]{1,0:T(8,128)S(1)}, u32[]{:S(2)}, u32[]{:S(2)}) collective-permute-start(f32[120,128]{1,0:T(8,128)S(1)} %get-tuple-element.42), channel_id=1, source_target_pairs={{0,1},{1,0},{2,3},{3,2},{4,5},{5,4},{6,7},{7,6},{8,16},{9,17},{10,... | collective-permute-start | bytes 184328 | tf_op jit(solution)/shard_map/ppermute | solution.py:741
  2.3 6.3 %collective-permute-start.1 = (f32[120,128]{1,0:T(8,128)S(1)}, f32[120,128]{1,0:T(8,128)S(1)}, u32[]{:S(2)}, u32[]{:S(2)}) collective-permute-start(f32[120,128]{1,0:T(8,128)S(1)} %get-tuple-element.47), channel_id=1, source_target_pairs={{0,8},{1,9},{2,10},{3,11},{4,12},{5,13},{6,14},{7,15},{8,0},{9,1},... | collective-permute-start | bytes 184328 | tf_op jit(solution)/shard_map/ppermute | solution.py:741
  6.9 4.3 %collective-permute-start.2 = (f32[240,128]{1,0:T(8,128)S(1)}, f32[240,128]{1,0:T(8,128)S(1)}, u32[]{:S(2)}, u32[]{:S(2)}) collective-permute-start(f32[240,128]{1,0:T(8,128)S(1)} %get-tuple-element.50), channel_id=1, source_target_pairs={{0,1},{1,0},{2,3},{3,2},{4,5},{5,4},{6,7},{7,6},{8,9},{9,8},{10,11... | collective-permute-start | bytes 368648 | tf_op jit(solution)/shard_map/ppermute | solution.py:741
  7.0 4.9 %collective-permute-start.3 = (f32[240,128]{1,0:T(8,128)S(1)}, f32[240,128]{1,0:T(8,128)S(1)}, u32[]{:S(2)}, u32[]{:S(2)}) collective-permute-start(f32[240,128]{1,0:T(8,128)S(1)} %get-tuple-element.51), channel_id=1, source_target_pairs={{0,8},{1,2},{2,1},{3,4},{4,3},{5,6},{6,5},{7,15},{8,0},{9,10},{10,... | collective-permute-start | bytes 368648 | tf_op jit(solution)/shard_map/ppermute | solution.py:741
  8.8 5.6 %collective-permute-start.4 = (f32[72,128]{1,0:T(8,128)S(1)}, f32[72,128]{1,0:T(8,128)S(1)}, u32[]{:S(2)}, u32[]{:S(2)}) collective-permute-start(f32[72,128]{1,0:T(8,128)S(1)} %get-tuple-element.54), channel_id=1, source_target_pairs={{0,1},{1,0},{2,3},{3,2},{4,5},{5,4},{6,7},{7,6},{8,9},{9,8},{10,11... | collective-permute-start | bytes 110600 | tf_op jit(solution)/shard_map/ppermute | solution.py:741
  9.0 5.4 %collective-permute-start.5 = (f32[72,128]{1,0:T(8,128)S(1)}, f32[72,128]{1,0:T(8,128)S(1)}, u32[]{:S(2)}, u32[]{:S(2)}) collective-permute-start(f32[72,128]{1,0:T(8,128)S(1)} %get-tuple-element.55), channel_id=1, source_target_pairs={{0,8},{1,2},{2,1},{3,4},{4,3},{5,6},{6,5},{7,15},{8,0},{9,10},{10,... | collective-permute-start | bytes 110600 | tf_op jit(solution)/shard_map/ppermute | solution.py:741
  15.8 11.1 %all-to-all-start = ((f32[32,1,128]{2,1,0:T(1,128)}), f32[32,1,128]{2,1,0:T(1,128)S(1)}, u32[]{:S(2)}, u32[]{:S(2)}) async-start(f32[32,1,128]{2,1,0:T(1,128)} %get-tuple-element.67), calls=%async_computation | async-start | bytes 32768 | tf_op jit(solution)/shard_map/all_to_all | solution.py:814
  19.8 7.1 %copy-start = (f32[8,16,768]{2,1,0:T(8,128)S(1)}, f32[8,16,768]{2,1,0:T(8,128)}, u32[]{:S(2)}) copy-start(f32[8,16,768]{2,1,0:T(8,128)} %b_ref.1) | copy-start | bytes 1179652

commit v22 on v21

--- a/solution.py
+++ b/solution.py
@@ -140,6 +140,17 @@
 
     def put(self, x, values):
         self.first.put(self.own.index(x), values)
+
+
+class Halves:
+    def __init__(self, outer_ref, middle_ref, ny, loads):
+        self.edge = (0, 1, ny - 2, ny - 1)
+        self.outer, self.middle = Tiles(outer_ref, 4, loads), Tiles(middle_ref, ny - 4, loads)
+
+    def __getitem__(self, at):
+        if at[1] in self.edge:
+            return self.outer[at[0], self.edge.index(at[1])]
+        return self.middle[at[0], at[1] - 2]
 
 
 class Inside:
@@ -208,28 +219,30 @@
     batch.flush()
 
 
-def pack_y_kernel(s, b_ref, dt_ref, bt_ref, y1_ref, y2_ref):
-    loads, nx, ny = s.loads, s.nx, s.ny
+def lay_out(s, b_ref, columns, out_ref):
+    loads, nx, count = s.loads, s.nx, len(columns)
     batch = Batch(16)
     for load in range(loads):
         for x0 in range(0, nx, SUB):
             at = load * nx + x0
-            for y in range(ny):
-                tile = unpack_tile(
-                    lambda t: b_ref[t, at : at + SUB, :], y, SUB
-                )
-                rows = pl.ds((x0 * ny + y) * loads + load, SUB, stride=ny * loads)
-                batch.add(bt_ref, (rows, slice(None)), tile)
-    batch.flush()
+            for place, y in enumerate(columns):
+                tile = unpack_tile(lambda t: b_ref[t, at : at + SUB, :], y, SUB)
+                rows = pl.ds((x0 * count + place) * loads + load, SUB, stride=count * loads)
+                batch.add(out_ref, (rows, slice(None)), tile)
+    batch.flush()
+
+
+def pack_y_kernel(s, b_ref, dt_ref, be_ref, y1_ref, y2_ref):
+    lay_out(s, b_ref, (0, 1, s.ny - 2, s.ny - 1), be_ref)
     even_y = is_even("gy")
-    pack_y_face(s, jnp.logical_not(even_y), bt_ref, dt_ref, y2_ref)
-    pack_y_face(s, even_y, bt_ref, dt_ref, y1_ref)
-
-
-def pack_y_face(s, upper, bt_ref, dt_ref, out_ref):
+    pack_y_face(s, jnp.logical_not(even_y), be_ref, dt_ref, y2_ref)
+    pack_y_face(s, even_y, be_ref, dt_ref, y1_ref)
+
+
+def pack_y_face(s, upper, be_ref, dt_ref, out_ref):
     loads, nx, ny = s.loads, s.nx, s.ny
-    tiles = Tiles(bt_ref, ny, loads)
-    y0 = pick(upper, ny - 2, 0)
+    tiles = Tiles(be_ref, 4, loads)
+    y0 = pick(upper, 2, 0)
     pack_tiles(out_ref, 0, loads, 2 * nx, lambda i: tiles[i // 2, y0 + i % 2])
     y0 = pick(upper, ny - 3, 0)
     batch = Batch()
@@ -416,8 +429,9 @@
     return state
 
 
-def inside_fields(s, bt_ref, zt_ref, ut_ref, bx, zx, zu):
-    brick = (Tiles(ref, s.ny, s.loads) for ref in (bt_ref, zt_ref, ut_ref))
+def inside_fields(s, be_ref, bm_ref, zt_ref, ut_ref, bx, zx, zu):
+    brick = [Halves(be_ref, bm_ref, s.ny, s.loads)]
+    brick += [Tiles(ref, s.ny, s.loads) for ref in (zt_ref, ut_ref)]
     starts = (2, 3, 3)
     return tuple(
         Inside(inner, range(start, s.ny + 2), outer)
@@ -425,29 +439,41 @@
     )
 
 
-def scale_kernel(s, bt_ref, dt_ref, zt_ref, ut_ref, inv_ref):
+def scale_kernel(
+    s, b_ref, be_ref, dt_ref, bm_ref, zt_ref, ut_ref, ct_ref, it_ref, cond_ref, inv_ref
+):
     loads, nx, ny = s.loads, s.nx, s.ny
-    inner, scaled, shifted = (Tiles(ref, ny, loads) for ref in (bt_ref, zt_ref, ut_ref))
-    inverse = Rows(inv_ref, ny, loads)
-    before = conduct_of(dt_ref[0:ny, :])
-    for x in range(1, nx):
+    lay_out(s, b_ref, range(2, ny - 2), bm_ref)
+    inner = Halves(be_ref, bm_ref, ny, loads)
+    scaled, shifted, cond_t, inv_t = (
+        Tiles(ref, ny, loads) for ref in (zt_ref, ut_ref, ct_ref, it_ref)
+    )
+    cond, inverse = Rows(cond_ref, ny, loads), Rows(inv_ref, ny, loads)
+    before = None
+    for x in range(nx):
         after = conduct_of(dt_ref[x * ny : (x + 1) * ny, :])
-        pair = before + after
-        pair = pair[: ny - 1] + pair[1:]
-        total = 4.0 * (pair + pltpu.roll(pair, 1, 1))
-        inverse.put(x, jnp.where(after[1:] > 0.0, 1.0 / total, 0.0))
+        cond.put(x, after)
+        if x:
+            pair = before + after
+            pair = pair[: ny - 1] + pair[1:]
+            total = 4.0 * (pair + pltpu.roll(pair, 1, 1))
+            inverse.put(x, jnp.where(after[1:] > 0.0, 1.0 / total, 0.0))
         before = after
     batch = Batch(16)
-    for x in range(1, nx):
-        for y in range(1, ny):
-            tile = inner[x, y] * inverse[x, y - 1]
-            batch.add(scaled, (x, y), tile)
-            batch.add(shifted, (x, y), up(tile))
+    for x in range(nx):
+        for y in range(ny):
+            batch.add(cond_t, (x, y), cond[x, y])
+            if x and y:
+                row = inverse[x, y - 1]
+                tile = inner[x, y] * row
+                batch.add(inv_t, (x, y), row)
+                batch.add(scaled, (x, y), tile)
+                batch.add(shifted, (x, y), up(tile))
     batch.flush()
 
 
 def inner_kernel(
-    s, bt_ref, zt_ref, ut_ref, dt_ref, y1_ref, y2_ref, t1_ref,
+    s, be_ref, bm_ref, zt_ref, ut_ref, ct_ref, it_ref, dt_ref, y1_ref, y2_ref, t1_ref,
     dens_ref, cond, invx, bx, zx, zu, qx, wx, wu, q_out, v_out, carry1, carry2, sums_ref,
 ):
     loads, nx, ny, my, pitch = s.loads, s.nx, s.ny, s.my, s.pitch
@@ -467,7 +493,7 @@
             invx.put(x + 2, inverse_of(s, before, after))
         before = after
 
-    bx, zx, zu = inside_fields(s, bt_ref, zt_ref, ut_ref, bx, zx, zu)
+    bx, zx, zu = inside_fields(s, be_ref, bm_ref, zt_ref, ut_ref, bx, zx, zu)
 
     def stage(x, y, tile):
         stores = [(bx, (x + 2, y), tile)]
@@ -493,6 +519,8 @@
                 batch.add(*store)
     batch.flush()
 
+    cond = Inside(Tiles(ct_ref, ny, loads), range(2, ny + 2), cond)
+    invx = Inside(Tiles(it_ref, ny, loads), range(3, ny + 2), invx)
     element_planes(cond, carry1, 3, 1, 0, my - 1, zx, zu, None)
 
     def first(a, count, state):
@@ -516,7 +544,7 @@
 
 
 def outer_kernel(
-    s, bt_ref, zt_ref, ut_ref, dens_ref, x1_ref, x2_ref, t1_ref, t2_ref, c1_ref, c2_ref,
+    s, be_ref, bm_ref, zt_ref, ut_ref, dens_ref, x1_ref, x2_ref, t1_ref, t2_ref, c1_ref, c2_ref,
     cond1, invx1, bx1, zx1, zu1, qx1, wx1, wu1, carry1, carry2, sums1,
     q_out, v_out, inv_out, sums_ref,
     low_ref, high_ref, low_d, high_d, cond2, invx2, bx2, zx2, zu2, qx2, wx2, wu2, carry3,
@@ -576,7 +604,7 @@
     image_own = (1, 2, 3, nx + 1, nx + 2)
     cond, invx = joined_rows(cond2, cond1, outside), joined_rows(invx2, invx1, scaled_own)
     bx1, zx1, zu1 = inside_fields(
-        s, bt_ref, zt_ref, ut_ref, *(Tiles(ref, my, loads) for ref in (bx1, zx1, zu1))
+        s, be_ref, bm_ref, zt_ref, ut_ref, *(Tiles(ref, my, loads) for ref in (bx1, zx1, zu1))
     )
     bx = Joined(Tiles(bx2, my, loads), bx1, outside)
     zx = Joined(Tiles(zx2, my, loads), zx1, scaled_own)
@@ -772,16 +800,19 @@
         pltpu.with_memory_space_constraint(density, pltpu.HBM),
     )
     x2, x1 = swap(x2, "gx", 1), swap(x1, "gx", 0)
-    bt, y1, y2 = call(pack_y_kernel, (shape(nodes, LANES), y_face, y_face))(b, dt)
+    outer_columns = shape(nx * 4 * loads, LANES)
+    be, y1, y2 = call(pack_y_kernel, (outer_columns, y_face, y_face))(b, dt)
     y2, y1 = swap(y2, "gy", 1), swap(y1, "gy", 0)
     t1 = call(open_y_kernel, shape(2 * nx * loads, LANES))(y1)
     xt = shape(2 * ny * loads, LANES)
     xt2 = call(open_x_kernel, xt)(x2)
     xt2, dt_later = lax.optimization_barrier((xt2, dt))
     inside = shape(nodes, LANES)
-    zt, ut = call(
-        scale_kernel, (inside, inside), scratch_shapes=[scratch(nx * ny, LANES)]
-    )(bt, dt_later)
+    bm, zt, ut, ct, it = call(
+        scale_kernel,
+        (shape(nx * (ny - 4) * loads, LANES),) + (inside,) * 4,
+        scratch_shapes=[scratch(nx * ny, LANES)] * 2,
+    )(b, be, dt_later)
     xt1, c1, c2 = call(
         corner_kernel,
         (xt, corner, corner),
@@ -800,7 +831,7 @@
         + (inside,) * 2
         + (edge,) * 2
         + (shape(4 * loads, LANES),),
-    )(bt, zt, ut, dt, y1, y2, t1)
+    )(be, bm, zt, ut, ct, it, dt, y1, y2, t1)
     ends = shape(len(outer_planes(nx)) * ny * loads, LANES)
     q_2, v_2, inv_2, sums = call(
         outer_kernel,
@@ -810,7 +841,7 @@
         + [scratch(5 * s.pitch, LANES)] * 2
         + [scratch(5 * plane, LANES)] * 6
         + [scratch(2 * plane, LANES)],
-    )(bt, zt, ut, dens, x1, x2, xt1, xt2, c1, c2, cond, inv_1, bx, zx, zu, q_x, w_x, w_u, carry1, carry2, sums)
+    )(be, bm, zt, ut, dens, x1, x2, xt1, xt2, c1, c2, cond, inv_1, bx, zx, zu, q_x, w_x, w_u, carry1, carry2, sums)
     parts = lax.all_to_all(sums, ("gx", "gy"), 0, 0, tiled=True)
     whole = shape(loads, nx, flat)
     image, again, inverse = call(

time: 28.3 us -> 28.1 us (level)
  no operation moved by 1% of the time
where the time goes in v22:
time: 28.1 us; the launch traced here: 27.9 us
  starting transfers between devices  10.9 us (39%)
  waiting for transfers between devices  8.23 us (29%)
  Pallas kernels  8.03 us (29%)
  between operations  0.74 us (3%)
    ppermute x6, starting transfers between devices, swap(): return lax.ppermute(array, ('gx', 'gy'), pairs)  6.96 us
    all_to_all x1, waiting for transfers between devices, per_device(): parts = lax.all_to_all(sums, ('gx', 'gy'), 0, 0, tiled=True)  6.32 us
    all_to_all x1, starting transfers between devices, per_device(): parts = lax.all_to_all(sums, ('gx', 'gy'), 0, 0, tiled=True)  3.97 us
    pallas_call x1, Pallas kernels, per_device(): call(inner_kernel, (shape(nx * s.pitch, LANES),) + (rows,) * 2 + (field,)...  2.38 us
    ppermute x6, waiting for transfers between devices, swap(): return lax.ppermute(array, ('gx', 'gy'), pairs)  1.9 us
    pallas_call x1, Pallas kernels, per_device(): call(outer_kernel, (ends, ends, shape(ny, LANES), shape(devices, 1, LANES...  1.46 us
    pallas_call x1, Pallas kernels, per_device(): call(finish_kernel, (whole, whole), out_specs=(hbm, hbm), scratch_shapes=...  1.21 us
    pallas_call x1, Pallas kernels, per_device(): call(pack_x_kernel, (shape(packed_count(ny), loads * nx, LANES), shape(nx...  1.13 us
  transfers between devices with their start and end apart: 7, of which 3 were waited for; matrix products, arithmetic and copies ran while one was open for 0% of the time, Pallas kernels for 15%

profile of v22, /device:TPU:0, one launch (start us, length us, event | category | flops | bytes accessed | tf_op | source)
XLA Modules:
  0.0 27.9 jit_solution(18193690139934139892)
XLA Ops:
  0.6 1.1 %shard_map.41 = (f32[6,128,128]{2,1,0:T(8,128)S(1)}, f32[128,128]{1,0:T(8,128)S(1)}, f32[120,128]{1,0:T(8,128)S(1)}, f32[120,128]{1,0:T(8,128)S(1)}) custom-call(f32[128,768]{1,0:T(8,128)} %bitcast.1, f32[16,768]{1,0:T(8,128)} %d_hbm.1), custom_call_target="tpu_custom_call" | custom-call | tf_op jit(solution)/shard_map/pallas_call | solution.py:793
  1.8 0.5 %collective-permute-start = (f32[120,128]{1,0:T(8,128)S(1)}, f32[120,128]{1,0:T(8,128)S(1)}, u32[]{:S(2)}, u32[]{:S(2)}) collective-permute-start(f32[120,128]{1,0:T(8,128)S(1)} %get-tuple-element.45), channel_id=1, source_target_pairs={{0,1},{1,0},{2,3},{3,2},{4,5},{5,4},{6,7},{7,6},{8,16},{9,17},{10,... | collective-permute-start | bytes 184328 | tf_op jit(solution)/shard_map/ppermute | solution.py:769
  2.3 4.1 %collective-permute-start.1 = (f32[120,128]{1,0:T(8,128)S(1)}, f32[120,128]{1,0:T(8,128)S(1)}, u32[]{:S(2)}, u32[]{:S(2)}) collective-permute-start(f32[120,128]{1,0:T(8,128)S(1)} %get-tuple-element.53), channel_id=1, source_target_pairs={{0,8},{1,9},{2,10},{3,11},{4,12},{5,13},{6,14},{7,15},{8,0},{9,1},... | collective-permute-start | bytes 184328 | tf_op jit(solution)/shard_map/ppermute | solution.py:769
  6.4 0.3 %shard_map.42 = (f32[512,128]{1,0:T(8,128)S(1)}, f32[240,128]{1,0:T(8,128)S(1)}, f32[240,128]{1,0:T(8,128)S(1)}) custom-call(f32[6,128,128]{2,1,0:T(8,128)S(1)} %get-tuple-element.42.b_ref, f32[128,128]{1,0:T(8,128)S(1)} %get-tuple-element.55.dt_ref), custom_call_target="tpu_custom_call" | custom-call | tf_op jit(solution)/shard_map/pallas_call | solution.py:804
  6.8 0.1 collective-permute-start.2
  6.9 0.1 collective-permute-start.3
  6.9 0.0 collective-permute-done.x_ref.x2_ref
  7.0 0.1 shard_map.43.t2_ref
  7.0 1.6 %collective-permute-done.1.x1_ref = f32[120,128]{1,0:T(8,128)S(1)} collective-permute-done((f32[120,128]{1,0:T(8,128)S(1)}, f32[120,128]{1,0:T(8,128)S(1)}, u32[]{:S(2)}, u32[]{:S(2)}) %collective-permute-start.1) | collective-permute-done | bytes 61472 | tf_op jit(solution)/shard_map/ppermute | solution.py:769
  8.6 0.2 shard_map.45
  8.8 0.1 collective-permute-start.4
  8.9 2.1 %collective-permute-start.5 = (f32[72,128]{1,0:T(8,128)S(1)}, f32[72,128]{1,0:T(8,128)S(1)}, u32[]{:S(2)}, u32[]{:S(2)}) collective-permute-start(f32[72,128]{1,0:T(8,128)S(1)} %get-tuple-element.61), channel_id=1, source_target_pairs={{0,8},{1,2},{2,1},{3,4},{4,3},{5,6},{6,5},{7,15},{8,0},{9,10},{10,... | collective-permute-start | bytes 110600 | tf_op jit(solution)/shard_map/ppermute | solution.py:769
  10.9 0.4 %shard_map.44 = (f32[512,128]{1,0:T(8,128)S(1)}, f32[1024,128]{1,0:T(8,128)S(1)}, f32[1024,128]{1,0:T(8,128)S(1)}, f32[1024,128]{1,0:T(8,128)S(1)}, f32[1024,128]{1,0:T(8,128)S(1)}) custom-call(f32[6,128,128]{2,1,0:T(8,128)S(1)} %get-tuple-element.42.b_ref, f32[512,128]{1,0:T(8,128)S(1)} %get-tuple-element.44.be_ref, f32[128,128]{1,0:T(8,128)S(1)} %get-tuple-element.55.dt_ref), custom_call_target="tpu_custom_call" | custom-call | tf_op jit(solution)/shard_map/pallas_call | solution.py:811
  11.4 0.0 collective-permute-done.2.y_ref.y1_ref
  11.4 0.1 shard_map.46.t1_ref
  11.5 0.3 %collective-permute-done.3.y2_ref = f32[240,128]{1,0:T(8,128)S(1)} collective-permute-done((f32[240,128]{1,0:T(8,128)S(1)}, f32[240,128]{1,0:T(8,128)S(1)}, u32[]{:S(2)}, u32[]{:S(2)}) %collective-permute-start.3) | collective-permute-done | bytes 122912 | tf_op jit(solution)/shard_map/ppermute | solution.py:769
  11.8 2.4 %shard_map.47 = (f32[256,128]{1,0:T(8,128)S(1)}, f32[320,128]{1,0:T(8,128)S(1)}, f32[320,128]{1,0:T(8,128)S(1)}, f32[1920,128]{1,0:T(8,128)S(1)}, f32[1920,128]{...) custom-call(f32[512,128]{1,0:T(8,128)S(1)} %get-tuple-element.44.be_, ...), custom_call_target="tpu_custom_call" | custom-call | tf_op jit(solution)/shard_map/pallas_call | solution.py:826
  14.2 0.0 collective-permute-done.4.c1_ref
  14.2 0.0 collective-permute-done.5.c2_ref
  14.2 1.5 %shard_map.48 = (f32[320,128]{1,0:T(8,128)S(1)}, f32[320,128]{1,0:T(8,128)S(1)}, f32[8,128]{1,0:T(8,128)S(1)}, f32[32,1,128]{2,1,0:T(1,128)}) custom-call(f32[512,128]{1,0:T(8,128)S(1)} %get-tuple-element.44.be_ref, f32[512,128]{1,0:T(8,128)S(1)} %get-tuple-element.47.bm_ref, f32[1024,128]{1,0:T(8,128)S(1)} %get-tuple-element.48.zt_ref, ...), custom_call_target="tpu_custom_call" | custom-call | tf_op jit(solution)/shard_map/pallas_call | solution.py:836
  15.7 4.0 %all-to-all-start = ((f32[32,1,128]{2,1,0:T(1,128)}), f32[32,1,128]{2,1,0:T(1,128)S(1)}, u32[]{:S(2)}, u32[]{:S(2)}) async-start(f32[32,1,128]{2,1,0:T(1,128)} %get-tuple-element.73), calls=%async_computation | async-start | bytes 32768 | tf_op jit(solution)/shard_map/all_to_all | solution.py:845
  19.6 0.0 copy-start
  19.7 0.7 %shard_map.49 = (f32[8,16,768]{2,1,0:T(8,128)S(1)}, f32[8,16,768]{2,1,0:T(8,128)S(1)}, f32[16,768]{1,0:T(8,128)S(1)}) custom-call(f32[1024,128]{1,0:T(8,128)S(1)} %get-tuple-element.74.q1_ref, f32[320,128]{1,0:T(8,128)S(1)} %get-tuple-element.75.q2_ref, f32[1024,128]{1,0:T(8,128)S(1)} %get-tuple-element.76.v1_ref, f32[320,128]{1,0:T(8,128)S(1)} %get-tuple-element.77.v2_ref, ...), custom_call_target="tpu_custom_call" | custom-call | tf_op jit(solution)/shard_map/pallas_call | solution.py:847
  20.4 6.3 %all-to-all-done.parts_ref = f32[32,1,128]{2,1,0:T(1,128)S(1)} async-done(((f32[32,1,128]{2,1,0:T(1,128)}), f32[32,1,128]{2,1,0:T(1,128)S(1)}, u32[]{:S(2)}, u32[]{:S(2)}) %all-to-all-start) | async-done | bytes 16416 | tf_op jit(solution)/shard_map/all_to_all | solution.py:845
  26.7 0.0 copy-done
  26.7 1.2 %shard_map.50 = (f32[8,16,768]{2,1,0:T(8,128)}, f32[8,16,768]{2,1,0:T(8,128)}) custom-call(f32[32,1,128]{2,1,0:T(1,128)S(1)} %all-to-all-done.parts_ref, f32[8,16,768]{2,1,0:T(8,128)S(1)} %copy-done, f32[8,16,768]{2,1,0:T(8,128)S(1)} %get-tuple-element.79.q_ref, f32[8,16,768]{2,1,0:T(8,128)S(1)} %get-tuple-element.80.v_ref, ...), custom_call_target="tpu_custom_call" | custom-call | tf_op jit(solution)/shard_map/pallas_call | solution.py:852
Async XLA Ops:
  1.8 5.2 %collective-permute-start = (f32[120,128]{1,0:T(8,128)S(1)}, f32[120,128]{1,0:T(8,128)S(1)}, u32[]{:S(2)}, u32[]{:S(2)}) collective-permute-start(f32[120,128]{1,0:T(8,128)S(1)} %get-tuple-element.45), channel_id=1, source_target_pairs={{0,1},{1,0},{2,3},{3,2},{4,5},{5,4},{6,7},{7,6},{8,16},{9,17},{10,... | collective-permute-start | bytes 184328 | tf_op jit(solution)/shard_map/ppermute | solution.py:769
  2.3 6.3 %collective-permute-start.1 = (f32[120,128]{1,0:T(8,128)S(1)}, f32[120,128]{1,0:T(8,128)S(1)}, u32[]{:S(2)}, u32[]{:S(2)}) collective-permute-start(f32[120,128]{1,0:T(8,128)S(1)} %get-tuple-element.53), channel_id=1, source_target_pairs={{0,8},{1,9},{2,10},{3,11},{4,12},{5,13},{6,14},{7,15},{8,0},{9,1},... | collective-permute-start | bytes 184328 | tf_op jit(solution)/shard_map/ppermute | solution.py:769
  6.8 4.6 %collective-permute-start.2 = (f32[240,128]{1,0:T(8,128)S(1)}, f32[240,128]{1,0:T(8,128)S(1)}, u32[]{:S(2)}, u32[]{:S(2)}) collective-permute-start(f32[240,128]{1,0:T(8,128)S(1)} %get-tuple-element.56), channel_id=1, source_target_pairs={{0,1},{1,0},{2,3},{3,2},{4,5},{5,4},{6,7},{7,6},{8,9},{9,8},{10,11... | collective-permute-start | bytes 368648 | tf_op jit(solution)/shard_map/ppermute | solution.py:769
  6.9 4.9 %collective-permute-start.3 = (f32[240,128]{1,0:T(8,128)S(1)}, f32[240,128]{1,0:T(8,128)S(1)}, u32[]{:S(2)}, u32[]{:S(2)}) collective-permute-start(f32[240,128]{1,0:T(8,128)S(1)} %get-tuple-element.57), channel_id=1, source_target_pairs={{0,8},{1,2},{2,1},{3,4},{4,3},{5,6},{6,5},{7,15},{8,0},{9,10},{10,... | collective-permute-start | bytes 368648 | tf_op jit(solution)/shard_map/ppermute | solution.py:769
  8.8 5.4 %collective-permute-start.4 = (f32[72,128]{1,0:T(8,128)S(1)}, f32[72,128]{1,0:T(8,128)S(1)}, u32[]{:S(2)}, u32[]{:S(2)}) collective-permute-start(f32[72,128]{1,0:T(8,128)S(1)} %get-tuple-element.60), channel_id=1, source_target_pairs={{0,1},{1,0},{2,3},{3,2},{4,5},{5,4},{6,7},{7,6},{8,9},{9,8},{10,11... | collective-permute-start | bytes 110600 | tf_op jit(solution)/shard_map/ppermute | solution.py:769
  8.9 5.4 %collective-permute-start.5 = (f32[72,128]{1,0:T(8,128)S(1)}, f32[72,128]{1,0:T(8,128)S(1)}, u32[]{:S(2)}, u32[]{:S(2)}) collective-permute-start(f32[72,128]{1,0:T(8,128)S(1)} %get-tuple-element.61), channel_id=1, source_target_pairs={{0,8},{1,2},{2,1},{3,4},{4,3},{5,6},{6,5},{7,15},{8,0},{9,10},{10,... | collective-permute-start | bytes 110600 | tf_op jit(solution)/shard_map/ppermute | solution.py:769
  15.7 11.1 %all-to-all-start = ((f32[32,1,128]{2,1,0:T(1,128)}), f32[32,1,128]{2,1,0:T(1,128)S(1)}, u32[]{:S(2)}, u32[]{:S(2)}) async-start(f32[32,1,128]{2,1,0:T(1,128)} %get-tuple-element.73), calls=%async_computation | async-start | bytes 32768 | tf_op jit(solution)/shard_map/all_to_all | solution.py:845
  19.6 7.1 %copy-start = (f32[8,16,768]{2,1,0:T(8,128)S(1)}, f32[8,16,768]{2,1,0:T(8,128)}, u32[]{:S(2)}) copy-start(f32[8,16,768]{2,1,0:T(8,128)} %b_ref.1) | copy-start | bytes 1179652

commit v23 on v22

--- a/solution.py
+++ b/solution.py
@@ -232,11 +232,13 @@
     batch.flush()
 
 
-def pack_y_kernel(s, b_ref, dt_ref, be_ref, y1_ref, y2_ref):
+def pack_far_kernel(s, b_ref, dt_ref, be_ref, y2_ref):
     lay_out(s, b_ref, (0, 1, s.ny - 2, s.ny - 1), be_ref)
-    even_y = is_even("gy")
-    pack_y_face(s, jnp.logical_not(even_y), be_ref, dt_ref, y2_ref)
-    pack_y_face(s, even_y, be_ref, dt_ref, y1_ref)
+    pack_y_face(s, jnp.logical_not(is_even("gy")), be_ref, dt_ref, y2_ref)
+
+
+def pack_near_kernel(s, be_ref, dt_ref, y1_ref):
+    pack_y_face(s, is_even("gy"), be_ref, dt_ref, y1_ref)
 
 
 def pack_y_face(s, upper, be_ref, dt_ref, out_ref):
@@ -801,12 +803,13 @@
     )
     x2, x1 = swap(x2, "gx", 1), swap(x1, "gx", 0)
     outer_columns = shape(nx * 4 * loads, LANES)
-    be, y1, y2 = call(pack_y_kernel, (outer_columns, y_face, y_face))(b, dt)
-    y2, y1 = swap(y2, "gy", 1), swap(y1, "gy", 0)
-    t1 = call(open_y_kernel, shape(2 * nx * loads, LANES))(y1)
+    be, y2 = call(pack_far_kernel, (outer_columns, y_face))(b, dt)
+    y2 = swap(y2, "gy", 1)
     xt = shape(2 * ny * loads, LANES)
     xt2 = call(open_x_kernel, xt)(x2)
-    xt2, dt_later = lax.optimization_barrier((xt2, dt))
+    xt2, be_later, dt_later = lax.optimization_barrier((xt2, be, dt))
+    y1 = swap(call(pack_near_kernel, y_face)(be_later, dt_later), "gy", 0)
+    t1 = call(open_y_kernel, shape(2 * nx * loads, LANES))(y1)
     inside = shape(nodes, LANES)
     bm, zt, ut, ct, it = call(
         scale_kernel,

time: 28.1 us -> 28.2 us (level)
  waiting for transfers between devices: 8.23 us -> 6.55 us
  starting transfers between devices: 10.9 us -> 12.5 us
    ppermute x6, waiting for transfers between devices: 1.9 us -> 0.22 us  [swap(): return lax.ppermute(array, ('gx', 'gy'), pairs)]
    ppermute x6, starting transfers between devices: 6.96 us -> 8.46 us  [swap(): return lax.ppermute(array, ('gx', 'gy'), pairs)]
  transfers between devices with their start and end apart: 7 -> 7, of which waited for: 3 -> 2; matrix products, arithmetic and copies ran while one was open for 0% -> 0% of each run, Pallas kernels for 15% -> 16%
where the time goes in v23:
time: 28.2 us; the launch traced here: 28 us
  starting transfers between devices  12.5 us (44%)
  Pallas kernels  8.13 us (29%)
  waiting for transfers between devices  6.55 us (23%)
  between operations  0.74 us (3%)
    ppermute x6, starting transfers between devices, swap(): return lax.ppermute(array, ('gx', 'gy'), pairs)  8.46 us
    all_to_all x1, waiting for transfers between devices, per_device(): parts = lax.all_to_all(sums, ('gx', 'gy'), 0, 0, tiled=True)  6.32 us
    all_to_all x1, starting transfers between devices, per_device(): parts = lax.all_to_all(sums, ('gx', 'gy'), 0, 0, tiled=True)  4.08 us
    pallas_call x1, Pallas kernels, per_device(): call(inner_kernel, (shape(nx * s.pitch, LANES),) + (rows,) * 2 + (field,)...  2.41 us
    pallas_call x1, Pallas kernels, per_device(): call(outer_kernel, (ends, ends, shape(ny, LANES), shape(devices, 1, LANES...  1.44 us
    pallas_call x1, Pallas kernels, per_device(): call(finish_kernel, (whole, whole), out_specs=(hbm, hbm), scratch_shapes=...  1.21 us
    pallas_call x1, Pallas kernels, per_device(): call(pack_x_kernel, (shape(packed_count(ny), loads * nx, LANES), shape(nx...  1.13 us
    pallas_call x1, Pallas kernels, per_device(): call(unpack_kernel, (whole, whole, shape(nx, flat)), scratch_shapes=[scra...  0.73 us
  transfers between devices with their start and end apart: 7, of which 2 were waited for; matrix products, arithmetic and copies ran while one was open for 0% of the time, Pallas kernels for 16%

profile of v23, /device:TPU:0, one launch (start us, length us, event | category | flops | bytes accessed | tf_op | source)
XLA Modules:
  0.0 28.0 jit_solution(10689833452485312681)
XLA Ops:
  0.6 1.1 %shard_map.41 = (f32[6,128,128]{2,1,0:T(8,128)S(1)}, f32[128,128]{1,0:T(8,128)S(1)}, f32[120,128]{1,0:T(8,128)S(1)}, f32[120,128]{1,0:T(8,128)S(1)}) custom-call(f32[128,768]{1,0:T(8,128)} %bitcast.1, f32[16,768]{1,0:T(8,128)} %d_hbm.1), custom_call_target="tpu_custom_call" | custom-call | tf_op jit(solution)/shard_map/pallas_call | solution.py:795
  1.8 0.5 %collective-permute-start = (f32[120,128]{1,0:T(8,128)S(1)}, f32[120,128]{1,0:T(8,128)S(1)}, u32[]{:S(2)}, u32[]{:S(2)}) collective-permute-start(f32[120,128]{1,0:T(8,128)S(1)} %get-tuple-element.45), channel_id=1, source_target_pairs={{0,1},{1,0},{2,3},{3,2},{4,5},{5,4},{6,7},{7,6},{8,16},{9,17},{10,... | collective-permute-start | bytes 184328 | tf_op jit(solution)/shard_map/ppermute | solution.py:771
  2.3 4.1 %collective-permute-start.1 = (f32[120,128]{1,0:T(8,128)S(1)}, f32[120,128]{1,0:T(8,128)S(1)}, u32[]{:S(2)}, u32[]{:S(2)}) collective-permute-start(f32[120,128]{1,0:T(8,128)S(1)} %get-tuple-element.53), channel_id=1, source_target_pairs={{0,8},{1,9},{2,10},{3,11},{4,12},{5,13},{6,14},{7,15},{8,0},{9,1},... | collective-permute-start | bytes 184328 | tf_op jit(solution)/shard_map/ppermute | solution.py:771
  6.4 0.3 %shard_map.42 = (f32[512,128]{1,0:T(8,128)S(1)}, f32[240,128]{1,0:T(8,128)S(1)}) custom-call(f32[6,128,128]{2,1,0:T(8,128)S(1)} %get-tuple-element.42.b_ref, f32[128,128]{1,0:T(8,128)S(1)} %get-tuple-element.55.dt_ref), custom_call_target="tpu_custom_call" | custom-call | tf_op jit(solution)/shard_map/pallas_call | solution.py:806
  6.8 0.1 collective-permute-start.3
  6.8 0.0 collective-permute-done.x_ref.x2_ref
  6.9 0.1 shard_map.43.t2_ref
  6.9 0.1 shard_map.46
  7.1 1.7 %collective-permute-start.2 = (f32[240,128]{1,0:T(8,128)S(1)}, f32[240,128]{1,0:T(8,128)S(1)}, u32[]{:S(2)}, u32[]{:S(2)}) collective-permute-start(f32[240,128]{1,0:T(8,128)S(1)} %shard_map.46), channel_id=1, source_target_pairs={{0,1},{1,0},{2,3},{3,2},{4,5},{5,4},{6,7},{7,6},{8,9},{9,8},{10,11... | collective-permute-start | bytes 368648 | tf_op jit(solution)/shard_map/ppermute | solution.py:771
  8.7 0.0 collective-permute-done.1.x1_ref
  8.7 0.2 shard_map.45
  8.9 0.1 collective-permute-start.4
  8.9 2.0 %collective-permute-start.5 = (f32[72,128]{1,0:T(8,128)S(1)}, f32[72,128]{1,0:T(8,128)S(1)}, u32[]{:S(2)}, u32[]{:S(2)}) collective-permute-start(f32[72,128]{1,0:T(8,128)S(1)} %get-tuple-element.61), channel_id=1, source_target_pairs={{0,8},{1,2},{2,1},{3,4},{4,3},{5,6},{6,5},{7,15},{8,0},{9,10},{10,... | collective-permute-start | bytes 110600 | tf_op jit(solution)/shard_map/ppermute | solution.py:771
  10.9 0.4 %shard_map.44 = (f32[512,128]{1,0:T(8,128)S(1)}, f32[1024,128]{1,0:T(8,128)S(1)}, f32[1024,128]{1,0:T(8,128)S(1)}, f32[1024,128]{1,0:T(8,128)S(1)}, f32[1024,128]{1,0:T(8,128)S(1)}) custom-call(f32[6,128,128]{2,1,0:T(8,128)S(1)} %get-tuple-element.42.b_ref, f32[512,128]{1,0:T(8,128)S(1)} %get-tuple-element.56.be_ref, f32[128,128]{1,0:T(8,128)S(1)} %get-tuple-element.55.dt_ref), custom_call_target="tpu_custom_call" | custom-call | tf_op jit(solution)/shard_map/pallas_call | solution.py:814
  11.4 0.0 collective-permute-done.2.y_ref.y1_ref
  11.4 0.1 shard_map.47.t1_ref
  11.5 0.2 collective-permute-done.3.y2_ref
  11.7 2.4 %shard_map.48 = (f32[256,128]{1,0:T(8,128)S(1)}, f32[320,128]{1,0:T(8,128)S(1)}, f32[320,128]{1,0:T(8,128)S(1)}, f32[1920,128]{1,0:T(8,128)S(1)}, f32[1920,128]{...) custom-call(f32[512,128]{1,0:T(8,128)S(1)} %get-tuple-element.56.be_, ...), custom_call_target="tpu_custom_call" | custom-call | tf_op jit(solution)/shard_map/pallas_call | solution.py:829
  14.1 0.0 collective-permute-done.4.c1_ref
  14.1 0.0 collective-permute-done.5.c2_ref
  14.1 1.4 %shard_map.49 = (f32[320,128]{1,0:T(8,128)S(1)}, f32[320,128]{1,0:T(8,128)S(1)}, f32[8,128]{1,0:T(8,128)S(1)}, f32[32,1,128]{2,1,0:T(1,128)}) custom-call(f32[512,128]{1,0:T(8,128)S(1)} %get-tuple-element.56.be_ref, f32[512,128]{1,0:T(8,128)S(1)} %get-tuple-element.47.bm_ref, f32[1024,128]{1,0:T(8,128)S(1)} %get-tuple-element.48.zt_ref, ...), custom_call_target="tpu_custom_call" | custom-call | tf_op jit(solution)/shard_map/pallas_call | solution.py:839
  15.6 4.1 %all-to-all-start = ((f32[32,1,128]{2,1,0:T(1,128)}), f32[32,1,128]{2,1,0:T(1,128)S(1)}, u32[]{:S(2)}, u32[]{:S(2)}) async-start(f32[32,1,128]{2,1,0:T(1,128)} %get-tuple-element.73), calls=%async_computation | async-start | bytes 32768 | tf_op jit(solution)/shard_map/all_to_all | solution.py:848
  19.7 0.0 copy-start
  19.7 0.7 %shard_map.50 = (f32[8,16,768]{2,1,0:T(8,128)S(1)}, f32[8,16,768]{2,1,0:T(8,128)S(1)}, f32[16,768]{1,0:T(8,128)S(1)}) custom-call(f32[1024,128]{1,0:T(8,128)S(1)} %get-tuple-element.74.q1_ref, f32[320,128]{1,0:T(8,128)S(1)} %get-tuple-element.75.q2_ref, f32[1024,128]{1,0:T(8,128)S(1)} %get-tuple-element.76.v1_ref, f32[320,128]{1,0:T(8,128)S(1)} %get-tuple-element.77.v2_ref, ...), custom_call_target="tpu_custom_call" | custom-call | tf_op jit(solution)/shard_map/pallas_call | solution.py:850
  20.4 6.3 %all-to-all-done.parts_ref = f32[32,1,128]{2,1,0:T(1,128)S(1)} async-done(((f32[32,1,128]{2,1,0:T(1,128)}), f32[32,1,128]{2,1,0:T(1,128)S(1)}, u32[]{:S(2)}, u32[]{:S(2)}) %all-to-all-start) | async-done | bytes 16416 | tf_op jit(solution)/shard_map/all_to_all | solution.py:848
  26.8 0.0 copy-done
  26.8 1.2 %shard_map.51 = (f32[8,16,768]{2,1,0:T(8,128)}, f32[8,16,768]{2,1,0:T(8,128)}) custom-call(f32[32,1,128]{2,1,0:T(1,128)S(1)} %all-to-all-done.parts_ref, f32[8,16,768]{2,1,0:T(8,128)S(1)} %copy-done, f32[8,16,768]{2,1,0:T(8,128)S(1)} %get-tuple-element.79.q_ref, f32[8,16,768]{2,1,0:T(8,128)S(1)} %get-tuple-element.80.v_ref, ...), custom_call_target="tpu_custom_call" | custom-call | tf_op jit(solution)/shard_map/pallas_call | solution.py:855
Async XLA Ops:
  1.8 5.1 %collective-permute-start = (f32[120,128]{1,0:T(8,128)S(1)}, f32[120,128]{1,0:T(8,128)S(1)}, u32[]{:S(2)}, u32[]{:S(2)}) collective-permute-start(f32[120,128]{1,0:T(8,128)S(1)} %get-tuple-element.45), channel_id=1, source_target_pairs={{0,1},{1,0},{2,3},{3,2},{4,5},{5,4},{6,7},{7,6},{8,16},{9,17},{10,... | collective-permute-start | bytes 184328 | tf_op jit(solution)/shard_map/ppermute | solution.py:771
  2.3 6.4 %collective-permute-start.1 = (f32[120,128]{1,0:T(8,128)S(1)}, f32[120,128]{1,0:T(8,128)S(1)}, u32[]{:S(2)}, u32[]{:S(2)}) collective-permute-start(f32[120,128]{1,0:T(8,128)S(1)} %get-tuple-element.53), channel_id=1, source_target_pairs={{0,8},{1,9},{2,10},{3,11},{4,12},{5,13},{6,14},{7,15},{8,0},{9,1},... | collective-permute-start | bytes 184328 | tf_op jit(solution)/shard_map/ppermute | solution.py:771
  6.8 4.9 %collective-permute-start.3 = (f32[240,128]{1,0:T(8,128)S(1)}, f32[240,128]{1,0:T(8,128)S(1)}, u32[]{:S(2)}, u32[]{:S(2)}) collective-permute-start(f32[240,128]{1,0:T(8,128)S(1)} %get-tuple-element.57), channel_id=1, source_target_pairs={{0,8},{1,2},{2,1},{3,4},{4,3},{5,6},{6,5},{7,15},{8,0},{9,10},{10,... | collective-permute-start | bytes 368648 | tf_op jit(solution)/shard_map/ppermute | solution.py:771
  7.1 4.3 %collective-permute-start.2 = (f32[240,128]{1,0:T(8,128)S(1)}, f32[240,128]{1,0:T(8,128)S(1)}, u32[]{:S(2)}, u32[]{:S(2)}) collective-permute-start(f32[240,128]{1,0:T(8,128)S(1)} %shard_map.46), channel_id=1, source_target_pairs={{0,1},{1,0},{2,3},{3,2},{4,5},{5,4},{6,7},{7,6},{8,9},{9,8},{10,11... | collective-permute-start | bytes 368648 | tf_op jit(solution)/shard_map/ppermute | solution.py:771
  8.9 5.3 %collective-permute-start.4 = (f32[72,128]{1,0:T(8,128)S(1)}, f32[72,128]{1,0:T(8,128)S(1)}, u32[]{:S(2)}, u32[]{:S(2)}) collective-permute-start(f32[72,128]{1,0:T(8,128)S(1)} %get-tuple-element.60), channel_id=1, source_target_pairs={{0,1},{1,0},{2,3},{3,2},{4,5},{5,4},{6,7},{7,6},{8,9},{9,8},{10,11... | collective-permute-start | bytes 110600 | tf_op jit(solution)/shard_map/ppermute | solution.py:771
  8.9 5.2 %collective-permute-start.5 = (f32[72,128]{1,0:T(8,128)S(1)}, f32[72,128]{1,0:T(8,128)S(1)}, u32[]{:S(2)}, u32[]{:S(2)}) collective-permute-start(f32[72,128]{1,0:T(8,128)S(1)} %get-tuple-element.61), channel_id=1, source_target_pairs={{0,8},{1,2},{2,1},{3,4},{4,3},{5,6},{6,5},{7,15},{8,0},{9,10},{10,... | collective-permute-start | bytes 110600 | tf_op jit(solution)/shard_map/ppermute | solution.py:771
  15.6 11.2 %all-to-all-start = ((f32[32,1,128]{2,1,0:T(1,128)}), f32[32,1,128]{2,1,0:T(1,128)S(1)}, u32[]{:S(2)}, u32[]{:S(2)}) async-start(f32[32,1,128]{2,1,0:T(1,128)} %get-tuple-element.73), calls=%async_computation | async-start | bytes 32768 | tf_op jit(solution)/shard_map/all_to_all | solution.py:848
  19.7 7.1 %copy-start = (f32[8,16,768]{2,1,0:T(8,128)S(1)}, f32[8,16,768]{2,1,0:T(8,128)}, u32[]{:S(2)}) copy-start(f32[8,16,768]{2,1,0:T(8,128)} %b_ref.1) | copy-start | bytes 1179652

commit v24 on v23

--- a/solution.py
+++ b/solution.py
@@ -424,10 +424,10 @@
 
 
 def over_planes(start, stop, body, state):
-    pairs = (stop - start) // 2
-    state = lax.fori_loop(0, pairs, lambda i, st: body(start + 2 * i, 2, st), state)
-    if (stop - start) % 2:
-        state = body(stop - 1, 1, state)
+    groups, rest = (stop - start) // 3, (stop - start) % 3
+    state = lax.fori_loop(0, groups, lambda i, st: body(start + 3 * i, 3, st), state)
+    if rest:
+        state = body(stop - rest, rest, state)
     return state
 
 

time: 28.2 us -> 27.9 us (0.989)
  Pallas kernels: 8.13 us -> 7.68 us
    pallas_call x1, Pallas kernels: 2.41 us -> 1.97 us  [per_device(): call(inner_kernel, (shape(nx * s.pitch, LANES),) + (rows,) * 2 + (field,)...]
  transfers between devices with their start and end apart: 7 -> 7, of which waited for: 2 -> 2; matrix products, arithmetic and copies ran while one was open for 0% -> 0% of each run, Pallas kernels for 16% -> 14%
where the time goes in v24:
time: 27.9 us; the launch traced here: 27.7 us
  starting transfers between devices  12.7 us (46%)
  Pallas kernels  7.68 us (28%)
  waiting for transfers between devices  6.55 us (23%)
  between operations  0.74 us (3%)
    ppermute x6, starting transfers between devices, swap(): return lax.ppermute(array, ('gx', 'gy'), pairs)  8.46 us
    all_to_all x1, waiting for transfers between devices, per_device(): parts = lax.all_to_all(sums, ('gx', 'gy'), 0, 0, tiled=True)  6.32 us
    all_to_all x1, starting transfers between devices, per_device(): parts = lax.all_to_all(sums, ('gx', 'gy'), 0, 0, tiled=True)  4.24 us
    pallas_call x1, Pallas kernels, per_device(): call(inner_kernel, (shape(nx * s.pitch, LANES),) + (rows,) * 2 + (field,)...  1.97 us
    pallas_call x1, Pallas kernels, per_device(): call(outer_kernel, (ends, ends, shape(ny, LANES), shape(devices, 1, LANES...  1.44 us
    pallas_call x1, Pallas kernels, per_device(): call(finish_kernel, (whole, whole), out_specs=(hbm, hbm), scratch_shapes=...  1.21 us
    pallas_call x1, Pallas kernels, per_device(): call(pack_x_kernel, (shape(packed_count(ny), loads * nx, LANES), shape(nx...  1.13 us
    pallas_call x1, Pallas kernels, per_device(): call(unpack_kernel, (whole, whole, shape(nx, flat)), scratch_shapes=[scra...  0.73 us
  transfers between devices with their start and end apart: 7, of which 2 were waited for; matrix products, arithmetic and copies ran while one was open for 0% of the time, Pallas kernels for 14%

profile of v24, /device:TPU:0, one launch (start us, length us, event | category | flops | bytes accessed | tf_op | source)
XLA Modules:
  0.0 27.7 jit_solution(12878363489773408871)
XLA Ops:
  0.6 1.1 %shard_map.41 = (f32[6,128,128]{2,1,0:T(8,128)S(1)}, f32[128,128]{1,0:T(8,128)S(1)}, f32[120,128]{1,0:T(8,128)S(1)}, f32[120,128]{1,0:T(8,128)S(1)}) custom-call(f32[128,768]{1,0:T(8,128)} %bitcast.1, f32[16,768]{1,0:T(8,128)} %d_hbm.1), custom_call_target="tpu_custom_call" | custom-call | tf_op jit(solution)/shard_map/pallas_call | solution.py:795
  1.8 0.5 %collective-permute-start = (f32[120,128]{1,0:T(8,128)S(1)}, f32[120,128]{1,0:T(8,128)S(1)}, u32[]{:S(2)}, u32[]{:S(2)}) collective-permute-start(f32[120,128]{1,0:T(8,128)S(1)} %get-tuple-element.45), channel_id=1, source_target_pairs={{0,1},{1,0},{2,3},{3,2},{4,5},{5,4},{6,7},{7,6},{8,16},{9,17},{10,... | collective-permute-start | bytes 184328 | tf_op jit(solution)/shard_map/ppermute | solution.py:771
  2.3 4.1 %collective-permute-start.1 = (f32[120,128]{1,0:T(8,128)S(1)}, f32[120,128]{1,0:T(8,128)S(1)}, u32[]{:S(2)}, u32[]{:S(2)}) collective-permute-start(f32[120,128]{1,0:T(8,128)S(1)} %get-tuple-element.53), channel_id=1, source_target_pairs={{0,8},{1,9},{2,10},{3,11},{4,12},{5,13},{6,14},{7,15},{8,0},{9,1},... | collective-permute-start | bytes 184328 | tf_op jit(solution)/shard_map/ppermute | solution.py:771
  6.4 0.3 %shard_map.42 = (f32[512,128]{1,0:T(8,128)S(1)}, f32[240,128]{1,0:T(8,128)S(1)}) custom-call(f32[6,128,128]{2,1,0:T(8,128)S(1)} %get-tuple-element.42.b_ref, f32[128,128]{1,0:T(8,128)S(1)} %get-tuple-element.55.dt_ref), custom_call_target="tpu_custom_call" | custom-call | tf_op jit(solution)/shard_map/pallas_call | solution.py:806
  6.8 0.1 collective-permute-start.3
  6.8 0.0 collective-permute-done.x_ref.x2_ref
  6.9 0.1 shard_map.43.t2_ref
  6.9 0.1 shard_map.46
  7.1 1.7 %collective-permute-start.2 = (f32[240,128]{1,0:T(8,128)S(1)}, f32[240,128]{1,0:T(8,128)S(1)}, u32[]{:S(2)}, u32[]{:S(2)}) collective-permute-start(f32[240,128]{1,0:T(8,128)S(1)} %shard_map.46), channel_id=1, source_target_pairs={{0,1},{1,0},{2,3},{3,2},{4,5},{5,4},{6,7},{7,6},{8,9},{9,8},{10,11... | collective-permute-start | bytes 368648 | tf_op jit(solution)/shard_map/ppermute | solution.py:771
  8.7 0.0 collective-permute-done.1.x1_ref
  8.7 0.2 shard_map.45
  8.9 0.1 collective-permute-start.4
  8.9 2.0 %collective-permute-start.5 = (f32[72,128]{1,0:T(8,128)S(1)}, f32[72,128]{1,0:T(8,128)S(1)}, u32[]{:S(2)}, u32[]{:S(2)}) collective-permute-start(f32[72,128]{1,0:T(8,128)S(1)} %get-tuple-element.61), channel_id=1, source_target_pairs={{0,8},{1,2},{2,1},{3,4},{4,3},{5,6},{6,5},{7,15},{8,0},{9,10},{10,... | collective-permute-start | bytes 110600 | tf_op jit(solution)/shard_map/ppermute | solution.py:771
  10.9 0.4 %shard_map.44 = (f32[512,128]{1,0:T(8,128)S(1)}, f32[1024,128]{1,0:T(8,128)S(1)}, f32[1024,128]{1,0:T(8,128)S(1)}, f32[1024,128]{1,0:T(8,128)S(1)}, f32[1024,128]{1,0:T(8,128)S(1)}) custom-call(f32[6,128,128]{2,1,0:T(8,128)S(1)} %get-tuple-element.42.b_ref, f32[512,128]{1,0:T(8,128)S(1)} %get-tuple-element.56.be_ref, f32[128,128]{1,0:T(8,128)S(1)} %get-tuple-element.55.dt_ref), custom_call_target="tpu_custom_call" | custom-call | tf_op jit(solution)/shard_map/pallas_call | solution.py:814
  11.4 0.0 collective-permute-done.2.y_ref.y1_ref
  11.4 0.1 shard_map.47.t1_ref
  11.5 0.2 collective-permute-done.3.y2_ref
  11.7 2.0 %shard_map.48 = (f32[256,128]{1,0:T(8,128)S(1)}, f32[320,128]{1,0:T(8,128)S(1)}, f32[320,128]{1,0:T(8,128)S(1)}, f32[1920,128]{1,0:T(8,128)S(1)}, f32[1920,128]{...) custom-call(f32[512,128]{1,0:T(8,128)S(1)} %get-tuple-element.56.be_, ...), custom_call_target="tpu_custom_call" | custom-call | tf_op jit(solution)/shard_map/pallas_call | solution.py:829
  13.7 0.0 collective-permute-done.4.c1_ref
  13.7 0.0 collective-permute-done.5.c2_ref
  13.7 1.4 %shard_map.49 = (f32[320,128]{1,0:T(8,128)S(1)}, f32[320,128]{1,0:T(8,128)S(1)}, f32[8,128]{1,0:T(8,128)S(1)}, f32[32,1,128]{2,1,0:T(1,128)}) custom-call(f32[512,128]{1,0:T(8,128)S(1)} %get-tuple-element.56.be_ref, f32[512,128]{1,0:T(8,128)S(1)} %get-tuple-element.47.bm_ref, f32[1024,128]{1,0:T(8,128)S(1)} %get-tuple-element.48.zt_ref, ...), custom_call_target="tpu_custom_call" | custom-call | tf_op jit(solution)/shard_map/pallas_call | solution.py:839
  15.1 4.2 %all-to-all-start = ((f32[32,1,128]{2,1,0:T(1,128)}), f32[32,1,128]{2,1,0:T(1,128)S(1)}, u32[]{:S(2)}, u32[]{:S(2)}) async-start(f32[32,1,128]{2,1,0:T(1,128)} %get-tuple-element.73), calls=%async_computation | async-start | bytes 32768 | tf_op jit(solution)/shard_map/all_to_all | solution.py:848
  19.4 0.0 copy-start
  19.4 0.7 %shard_map.50 = (f32[8,16,768]{2,1,0:T(8,128)S(1)}, f32[8,16,768]{2,1,0:T(8,128)S(1)}, f32[16,768]{1,0:T(8,128)S(1)}) custom-call(f32[1024,128]{1,0:T(8,128)S(1)} %get-tuple-element.74.q1_ref, f32[320,128]{1,0:T(8,128)S(1)} %get-tuple-element.75.q2_ref, f32[1024,128]{1,0:T(8,128)S(1)} %get-tuple-element.76.v1_ref, f32[320,128]{1,0:T(8,128)S(1)} %get-tuple-element.77.v2_ref, ...), custom_call_target="tpu_custom_call" | custom-call | tf_op jit(solution)/shard_map/pallas_call | solution.py:850
  20.1 6.3 %all-to-all-done.parts_ref = f32[32,1,128]{2,1,0:T(1,128)S(1)} async-done(((f32[32,1,128]{2,1,0:T(1,128)}), f32[32,1,128]{2,1,0:T(1,128)S(1)}, u32[]{:S(2)}, u32[]{:S(2)}) %all-to-all-start) | async-done | bytes 16416 | tf_op jit(solution)/shard_map/all_to_all | solution.py:848
  26.5 0.0 copy-done
  26.5 1.2 %shard_map.51 = (f32[8,16,768]{2,1,0:T(8,128)}, f32[8,16,768]{2,1,0:T(8,128)}) custom-call(f32[32,1,128]{2,1,0:T(1,128)S(1)} %all-to-all-done.parts_ref, f32[8,16,768]{2,1,0:T(8,128)S(1)} %copy-done, f32[8,16,768]{2,1,0:T(8,128)S(1)} %get-tuple-element.79.q_ref, f32[8,16,768]{2,1,0:T(8,128)S(1)} %get-tuple-element.80.v_ref, ...), custom_call_target="tpu_custom_call" | custom-call | tf_op jit(solution)/shard_map/pallas_call | solution.py:855
Async XLA Ops:
  1.8 5.1 %collective-permute-start = (f32[120,128]{1,0:T(8,128)S(1)}, f32[120,128]{1,0:T(8,128)S(1)}, u32[]{:S(2)}, u32[]{:S(2)}) collective-permute-start(f32[120,128]{1,0:T(8,128)S(1)} %get-tuple-element.45), channel_id=1, source_target_pairs={{0,1},{1,0},{2,3},{3,2},{4,5},{5,4},{6,7},{7,6},{8,16},{9,17},{10,... | collective-permute-start | bytes 184328 | tf_op jit(solution)/shard_map/ppermute | solution.py:771
  2.3 6.4 %collective-permute-start.1 = (f32[120,128]{1,0:T(8,128)S(1)}, f32[120,128]{1,0:T(8,128)S(1)}, u32[]{:S(2)}, u32[]{:S(2)}) collective-permute-start(f32[120,128]{1,0:T(8,128)S(1)} %get-tuple-element.53), channel_id=1, source_target_pairs={{0,8},{1,9},{2,10},{3,11},{4,12},{5,13},{6,14},{7,15},{8,0},{9,1},... | collective-permute-start | bytes 184328 | tf_op jit(solution)/shard_map/ppermute | solution.py:771
  6.8 4.9 %collective-permute-start.3 = (f32[240,128]{1,0:T(8,128)S(1)}, f32[240,128]{1,0:T(8,128)S(1)}, u32[]{:S(2)}, u32[]{:S(2)}) collective-permute-start(f32[240,128]{1,0:T(8,128)S(1)} %get-tuple-element.57), channel_id=1, source_target_pairs={{0,8},{1,2},{2,1},{3,4},{4,3},{5,6},{6,5},{7,15},{8,0},{9,10},{10,... | collective-permute-start | bytes 368648 | tf_op jit(solution)/shard_map/ppermute | solution.py:771
  7.1 4.3 %collective-permute-start.2 = (f32[240,128]{1,0:T(8,128)S(1)}, f32[240,128]{1,0:T(8,128)S(1)}, u32[]{:S(2)}, u32[]{:S(2)}) collective-permute-start(f32[240,128]{1,0:T(8,128)S(1)} %shard_map.46), channel_id=1, source_target_pairs={{0,1},{1,0},{2,3},{3,2},{4,5},{5,4},{6,7},{7,6},{8,9},{9,8},{10,11... | collective-permute-start | bytes 368648 | tf_op jit(solution)/shard_map/ppermute | solution.py:771
  8.9 4.8 %collective-permute-start.4 = (f32[72,128]{1,0:T(8,128)S(1)}, f32[72,128]{1,0:T(8,128)S(1)}, u32[]{:S(2)}, u32[]{:S(2)}) collective-permute-start(f32[72,128]{1,0:T(8,128)S(1)} %get-tuple-element.60), channel_id=1, source_target_pairs={{0,1},{1,0},{2,3},{3,2},{4,5},{5,4},{6,7},{7,6},{8,9},{9,8},{10,11... | collective-permute-start | bytes 110600 | tf_op jit(solution)/shard_map/ppermute | solution.py:771
  8.9 4.8 %collective-permute-start.5 = (f32[72,128]{1,0:T(8,128)S(1)}, f32[72,128]{1,0:T(8,128)S(1)}, u32[]{:S(2)}, u32[]{:S(2)}) collective-permute-start(f32[72,128]{1,0:T(8,128)S(1)} %get-tuple-element.61), channel_id=1, source_target_pairs={{0,8},{1,2},{2,1},{3,4},{4,3},{5,6},{6,5},{7,15},{8,0},{9,10},{10,... | collective-permute-start | bytes 110600 | tf_op jit(solution)/shard_map/ppermute | solution.py:771
  15.1 11.3 %all-to-all-start = ((f32[32,1,128]{2,1,0:T(1,128)}), f32[32,1,128]{2,1,0:T(1,128)S(1)}, u32[]{:S(2)}, u32[]{:S(2)}) async-start(f32[32,1,128]{2,1,0:T(1,128)} %get-tuple-element.73), calls=%async_computation | async-start | bytes 32768 | tf_op jit(solution)/shard_map/all_to_all | solution.py:848
  19.4 7.1 %copy-start = (f32[8,16,768]{2,1,0:T(8,128)S(1)}, f32[8,16,768]{2,1,0:T(8,128)}, u32[]{:S(2)}) copy-start(f32[8,16,768]{2,1,0:T(8,128)} %b_ref.1) | copy-start | bytes 1179652

commit v25 on v24

--- a/solution.py
+++ b/solution.py
@@ -424,8 +424,8 @@
 
 
 def over_planes(start, stop, body, state):
-    groups, rest = (stop - start) // 3, (stop - start) % 3
-    state = lax.fori_loop(0, groups, lambda i, st: body(start + 3 * i, 3, st), state)
+    groups, rest = (stop - start) // 4, (stop - start) % 4
+    state = lax.fori_loop(0, groups, lambda i, st: body(start + 4 * i, 4, st), state)
     if rest:
         state = body(stop - rest, rest, state)
     return state
@@ -650,14 +650,12 @@
 
     emitter = First(bx, invx, qx, wx, wu)
     element_planes(cond, carry3, 0, 1, 0, my - 1, zx, zu, None)
-    element_planes(cond, carry3, 1, 2, 0, my - 1, zx, zu, emitter)
-    element_planes(cond, carry3, 3, 1, 0, my - 1, zx, zu, emitter, keep=False)
+    element_planes(cond, carry3, 1, 3, 0, my - 1, zx, zu, emitter, keep=False)
     element_planes(cond, carry1, nx + 1, 2, 0, my - 1, zx, zu, emitter, keep=False)
     sums = [sums1[place * loads : (place + 1) * loads, :] for place in range(4)]
     emitter = Second(bx, zx, qx, q_out, v_out, sums)
     element_planes(cond, carry3, 1, 1, 1, my - 3, wx, wu, None)
-    element_planes(cond, carry3, 2, 2, 1, my - 3, wx, wu, emitter)
-    element_planes(cond, carry3, 4, 1, 1, my - 3, wx, wu, emitter, keep=False)
+    element_planes(cond, carry3, 2, 3, 1, my - 3, wx, wu, emitter, keep=False)
     element_planes(cond, carry2, nx, 2, 1, my - 3, wx, wu, emitter, keep=False)
     lane = lane_ids(loads)
     load = lax.broadcasted_iota(jnp.int32, (loads, LANES), 0)

time: 27.9 us -> 27.9 us (level)
  no operation moved by 1% of the time
where the time goes in v25:
time: 27.9 us; the launch traced here: 27.7 us
  starting transfers between devices  12.8 us (46%)
  Pallas kernels  7.54 us (27%)
  waiting for transfers between devices  6.55 us (23%)
  between operations  0.74 us (3%)
    ppermute x6, starting transfers between devices, swap(): return lax.ppermute(array, ('gx', 'gy'), pairs)  8.46 us
    all_to_all x1, waiting for transfers between devices, per_device(): parts = lax.all_to_all(sums, ('gx', 'gy'), 0, 0, tiled=True)  6.32 us
    all_to_all x1, starting transfers between devices, per_device(): parts = lax.all_to_all(sums, ('gx', 'gy'), 0, 0, tiled=True)  4.38 us
    pallas_call x1, Pallas kernels, per_device(): call(inner_kernel, (shape(nx * s.pitch, LANES),) + (rows,) * 2 + (field,)...  1.82 us
    pallas_call x1, Pallas kernels, per_device(): call(outer_kernel, (ends, ends, shape(ny, LANES), shape(devices, 1, LANES...  1.44 us
    pallas_call x1, Pallas kernels, per_device(): call(finish_kernel, (whole, whole), out_specs=(hbm, hbm), scratch_shapes=...  1.21 us
    pallas_call x1, Pallas kernels, per_device(): call(pack_x_kernel, (shape(packed_count(ny), loads * nx, LANES), shape(nx...  1.13 us
    pallas_call x1, Pallas kernels, per_device(): call(unpack_kernel, (whole, whole, shape(nx, flat)), scratch_shapes=[scra...  0.73 us
  transfers between devices with their start and end apart: 7, of which 2 were waited for; matrix products, arithmetic and copies ran while one was open for 0% of the time, Pallas kernels for 14%

profile of v25, /device:TPU:0, one launch (start us, length us, event | category | flops | bytes accessed | tf_op | source)
XLA Modules:
  0.0 27.7 jit_solution(11086490779002867250)
XLA Ops:
  0.6 1.1 %shard_map.41 = (f32[6,128,128]{2,1,0:T(8,128)S(1)}, f32[128,128]{1,0:T(8,128)S(1)}, f32[120,128]{1,0:T(8,128)S(1)}, f32[120,128]{1,0:T(8,128)S(1)}) custom-call(f32[128,768]{1,0:T(8,128)} %bitcast.1, f32[16,768]{1,0:T(8,128)} %d_hbm.1), custom_call_target="tpu_custom_call" | custom-call | tf_op jit(solution)/shard_map/pallas_call | solution.py:793
  1.8 0.5 %collective-permute-start = (f32[120,128]{1,0:T(8,128)S(1)}, f32[120,128]{1,0:T(8,128)S(1)}, u32[]{:S(2)}, u32[]{:S(2)}) collective-permute-start(f32[120,128]{1,0:T(8,128)S(1)} %get-tuple-element.45), channel_id=1, source_target_pairs={{0,1},{1,0},{2,3},{3,2},{4,5},{5,4},{6,7},{7,6},{8,16},{9,17},{10,... | collective-permute-start | bytes 184328 | tf_op jit(solution)/shard_map/ppermute | solution.py:769
  2.3 4.1 %collective-permute-start.1 = (f32[120,128]{1,0:T(8,128)S(1)}, f32[120,128]{1,0:T(8,128)S(1)}, u32[]{:S(2)}, u32[]{:S(2)}) collective-permute-start(f32[120,128]{1,0:T(8,128)S(1)} %get-tuple-element.53), channel_id=1, source_target_pairs={{0,8},{1,9},{2,10},{3,11},{4,12},{5,13},{6,14},{7,15},{8,0},{9,1},... | collective-permute-start | bytes 184328 | tf_op jit(solution)/shard_map/ppermute | solution.py:769
  6.4 0.3 %shard_map.42 = (f32[512,128]{1,0:T(8,128)S(1)}, f32[240,128]{1,0:T(8,128)S(1)}) custom-call(f32[6,128,128]{2,1,0:T(8,128)S(1)} %get-tuple-element.42.b_ref, f32[128,128]{1,0:T(8,128)S(1)} %get-tuple-element.55.dt_ref), custom_call_target="tpu_custom_call" | custom-call | tf_op jit(solution)/shard_map/pallas_call | solution.py:804
  6.8 0.1 collective-permute-start.3
  6.8 0.0 collective-permute-done.x_ref.x2_ref
  6.9 0.1 shard_map.43.t2_ref
  6.9 0.1 shard_map.46
  7.1 1.7 %collective-permute-start.2 = (f32[240,128]{1,0:T(8,128)S(1)}, f32[240,128]{1,0:T(8,128)S(1)}, u32[]{:S(2)}, u32[]{:S(2)}) collective-permute-start(f32[240,128]{1,0:T(8,128)S(1)} %shard_map.46), channel_id=1, source_target_pairs={{0,1},{1,0},{2,3},{3,2},{4,5},{5,4},{6,7},{7,6},{8,9},{9,8},{10,11... | collective-permute-start | bytes 368648 | tf_op jit(solution)/shard_map/ppermute | solution.py:769
  8.7 0.0 collective-permute-done.1.x1_ref
  8.7 0.2 shard_map.45
  8.9 0.1 collective-permute-start.4
  8.9 2.0 %collective-permute-start.5 = (f32[72,128]{1,0:T(8,128)S(1)}, f32[72,128]{1,0:T(8,128)S(1)}, u32[]{:S(2)}, u32[]{:S(2)}) collective-permute-start(f32[72,128]{1,0:T(8,128)S(1)} %get-tuple-element.61), channel_id=1, source_target_pairs={{0,8},{1,2},{2,1},{3,4},{4,3},{5,6},{6,5},{7,15},{8,0},{9,10},{10,... | collective-permute-start | bytes 110600 | tf_op jit(solution)/shard_map/ppermute | solution.py:769
  10.9 0.4 %shard_map.44 = (f32[512,128]{1,0:T(8,128)S(1)}, f32[1024,128]{1,0:T(8,128)S(1)}, f32[1024,128]{1,0:T(8,128)S(1)}, f32[1024,128]{1,0:T(8,128)S(1)}, f32[1024,128]{1,0:T(8,128)S(1)}) custom-call(f32[6,128,128]{2,1,0:T(8,128)S(1)} %get-tuple-element.42.b_ref, f32[512,128]{1,0:T(8,128)S(1)} %get-tuple-element.56.be_ref, f32[128,128]{1,0:T(8,128)S(1)} %get-tuple-element.55.dt_ref), custom_call_target="tpu_custom_call" | custom-call | tf_op jit(solution)/shard_map/pallas_call | solution.py:812
  11.4 0.0 collective-permute-done.2.y_ref.y1_ref
  11.4 0.1 shard_map.47.t1_ref
  11.5 0.2 collective-permute-done.3.y2_ref
  11.7 1.8 %shard_map.48 = (f32[256,128]{1,0:T(8,128)S(1)}, f32[320,128]{1,0:T(8,128)S(1)}, f32[320,128]{1,0:T(8,128)S(1)}, f32[1920,128]{1,0:T(8,128)S(1)}, f32[1920,128]{...) custom-call(f32[512,128]{1,0:T(8,128)S(1)} %get-tuple-element.56.be_, ...), custom_call_target="tpu_custom_call" | custom-call | tf_op jit(solution)/shard_map/pallas_call | solution.py:827
  13.5 0.0 collective-permute-done.4.c1_ref
  13.5 0.0 collective-permute-done.5.c2_ref
  13.6 1.4 %shard_map.49 = (f32[320,128]{1,0:T(8,128)S(1)}, f32[320,128]{1,0:T(8,128)S(1)}, f32[8,128]{1,0:T(8,128)S(1)}, f32[32,1,128]{2,1,0:T(1,128)}) custom-call(f32[512,128]{1,0:T(8,128)S(1)} %get-tuple-element.56.be_ref, f32[512,128]{1,0:T(8,128)S(1)} %get-tuple-element.47.bm_ref, f32[1024,128]{1,0:T(8,128)S(1)} %get-tuple-element.48.zt_ref, ...), custom_call_target="tpu_custom_call" | custom-call | tf_op jit(solution)/shard_map/pallas_call | solution.py:837
  15.0 4.4 %all-to-all-start = ((f32[32,1,128]{2,1,0:T(1,128)}), f32[32,1,128]{2,1,0:T(1,128)S(1)}, u32[]{:S(2)}, u32[]{:S(2)}) async-start(f32[32,1,128]{2,1,0:T(1,128)} %get-tuple-element.73), calls=%async_computation | async-start | bytes 32768 | tf_op jit(solution)/shard_map/all_to_all | solution.py:846
  19.4 0.0 copy-start
  19.4 0.7 %shard_map.50 = (f32[8,16,768]{2,1,0:T(8,128)S(1)}, f32[8,16,768]{2,1,0:T(8,128)S(1)}, f32[16,768]{1,0:T(8,128)S(1)}) custom-call(f32[1024,128]{1,0:T(8,128)S(1)} %get-tuple-element.74.q1_ref, f32[320,128]{1,0:T(8,128)S(1)} %get-tuple-element.75.q2_ref, f32[1024,128]{1,0:T(8,128)S(1)} %get-tuple-element.76.v1_ref, f32[320,128]{1,0:T(8,128)S(1)} %get-tuple-element.77.v2_ref, ...), custom_call_target="tpu_custom_call" | custom-call | tf_op jit(solution)/shard_map/pallas_call | solution.py:848
  20.1 6.3 %all-to-all-done.parts_ref = f32[32,1,128]{2,1,0:T(1,128)S(1)} async-done(((f32[32,1,128]{2,1,0:T(1,128)}), f32[32,1,128]{2,1,0:T(1,128)S(1)}, u32[]{:S(2)}, u32[]{:S(2)}) %all-to-all-start) | async-done | bytes 16416 | tf_op jit(solution)/shard_map/all_to_all | solution.py:846
  26.5 0.0 copy-done
  26.5 1.2 %shard_map.51 = (f32[8,16,768]{2,1,0:T(8,128)}, f32[8,16,768]{2,1,0:T(8,128)}) custom-call(f32[32,1,128]{2,1,0:T(1,128)S(1)} %all-to-all-done.parts_ref, f32[8,16,768]{2,1,0:T(8,128)S(1)} %copy-done, f32[8,16,768]{2,1,0:T(8,128)S(1)} %get-tuple-element.79.q_ref, f32[8,16,768]{2,1,0:T(8,128)S(1)} %get-tuple-element.80.v_ref, ...), custom_call_target="tpu_custom_call" | custom-call | tf_op jit(solution)/shard_map/pallas_call | solution.py:853
Async XLA Ops:
  1.8 5.1 %collective-permute-start = (f32[120,128]{1,0:T(8,128)S(1)}, f32[120,128]{1,0:T(8,128)S(1)}, u32[]{:S(2)}, u32[]{:S(2)}) collective-permute-start(f32[120,128]{1,0:T(8,128)S(1)} %get-tuple-element.45), channel_id=1, source_target_pairs={{0,1},{1,0},{2,3},{3,2},{4,5},{5,4},{6,7},{7,6},{8,16},{9,17},{10,... | collective-permute-start | bytes 184328 | tf_op jit(solution)/shard_map/ppermute | solution.py:769
  2.3 6.4 %collective-permute-start.1 = (f32[120,128]{1,0:T(8,128)S(1)}, f32[120,128]{1,0:T(8,128)S(1)}, u32[]{:S(2)}, u32[]{:S(2)}) collective-permute-start(f32[120,128]{1,0:T(8,128)S(1)} %get-tuple-element.53), channel_id=1, source_target_pairs={{0,8},{1,9},{2,10},{3,11},{4,12},{5,13},{6,14},{7,15},{8,0},{9,1},... | collective-permute-start | bytes 184328 | tf_op jit(solution)/shard_map/ppermute | solution.py:769
  6.8 4.9 %collective-permute-start.3 = (f32[240,128]{1,0:T(8,128)S(1)}, f32[240,128]{1,0:T(8,128)S(1)}, u32[]{:S(2)}, u32[]{:S(2)}) collective-permute-start(f32[240,128]{1,0:T(8,128)S(1)} %get-tuple-element.57), channel_id=1, source_target_pairs={{0,8},{1,2},{2,1},{3,4},{4,3},{5,6},{6,5},{7,15},{8,0},{9,10},{10,... | collective-permute-start | bytes 368648 | tf_op jit(solution)/shard_map/ppermute | solution.py:769
  7.1 4.3 %collective-permute-start.2 = (f32[240,128]{1,0:T(8,128)S(1)}, f32[240,128]{1,0:T(8,128)S(1)}, u32[]{:S(2)}, u32[]{:S(2)}) collective-permute-start(f32[240,128]{1,0:T(8,128)S(1)} %shard_map.46), channel_id=1, source_target_pairs={{0,1},{1,0},{2,3},{3,2},{4,5},{5,4},{6,7},{7,6},{8,9},{9,8},{10,11... | collective-permute-start | bytes 368648 | tf_op jit(solution)/shard_map/ppermute | solution.py:769
  8.9 4.7 %collective-permute-start.4 = (f32[72,128]{1,0:T(8,128)S(1)}, f32[72,128]{1,0:T(8,128)S(1)}, u32[]{:S(2)}, u32[]{:S(2)}) collective-permute-start(f32[72,128]{1,0:T(8,128)S(1)} %get-tuple-element.60), channel_id=1, source_target_pairs={{0,1},{1,0},{2,3},{3,2},{4,5},{5,4},{6,7},{7,6},{8,9},{9,8},{10,11... | collective-permute-start | bytes 110600 | tf_op jit(solution)/shard_map/ppermute | solution.py:769
  8.9 4.6 %collective-permute-start.5 = (f32[72,128]{1,0:T(8,128)S(1)}, f32[72,128]{1,0:T(8,128)S(1)}, u32[]{:S(2)}, u32[]{:S(2)}) collective-permute-start(f32[72,128]{1,0:T(8,128)S(1)} %get-tuple-element.61), channel_id=1, source_target_pairs={{0,8},{1,2},{2,1},{3,4},{4,3},{5,6},{6,5},{7,15},{8,0},{9,10},{10,... | collective-permute-start | bytes 110600 | tf_op jit(solution)/shard_map/ppermute | solution.py:769
  15.0 11.5 %all-to-all-start = ((f32[32,1,128]{2,1,0:T(1,128)}), f32[32,1,128]{2,1,0:T(1,128)S(1)}, u32[]{:S(2)}, u32[]{:S(2)}) async-start(f32[32,1,128]{2,1,0:T(1,128)} %get-tuple-element.73), calls=%async_computation | async-start | bytes 32768 | tf_op jit(solution)/shard_map/all_to_all | solution.py:846
  19.4 7.1 %copy-start = (f32[8,16,768]{2,1,0:T(8,128)S(1)}, f32[8,16,768]{2,1,0:T(8,128)}, u32[]{:S(2)}) copy-start(f32[8,16,768]{2,1,0:T(8,128)} %b_ref.1) | copy-start | bytes 1179652

commit v26 on v25

--- a/solution.py
+++ b/solution.py
@@ -546,7 +546,7 @@
 
 
 def outer_kernel(
-    s, be_ref, bm_ref, zt_ref, ut_ref, dens_ref, x1_ref, x2_ref, t1_ref, t2_ref, c1_ref, c2_ref,
+    s, be_ref, bm_ref, zt_ref, ut_ref, dens_ref, x1_ref, x2_ref, t1_ref, t2_ref, c2_ref, c1_ref,
     cond1, invx1, bx1, zx1, zu1, qx1, wx1, wu1, carry1, carry2, sums1,
     q_out, v_out, inv_out, sums_ref,
     low_ref, high_ref, low_d, high_d, cond2, invx2, bx2, zx2, zu2, qx2, wx2, wu2, carry3,
@@ -820,7 +820,7 @@
         cost_estimate=pl.CostEstimate(flops=2 * 10**9, transcendentals=0, bytes_accessed=0),
     )(x2, xt2, x1)
     xt1, dt = lax.optimization_barrier((xt1, dt))
-    c2, c1 = swap(c2, "gy", 1), swap(c1, "gy", 0)
+    c1, c2 = swap(c1, "gy", 0), swap(c2, "gy", 1)
     plane = s.my * loads
     rows, field = shape(s.mx * s.pitch, LANES), shape(s.mx * plane, LANES)
     edge = shape(2 * plane, LANES)
@@ -842,7 +842,7 @@
         + [scratch(5 * s.pitch, LANES)] * 2
         + [scratch(5 * plane, LANES)] * 6
         + [scratch(2 * plane, LANES)],
-    )(be, bm, zt, ut, dens, x1, x2, xt1, xt2, c1, c2, cond, inv_1, bx, zx, zu, q_x, w_x, w_u, carry1, carry2, sums)
+    )(be, bm, zt, ut, dens, x1, x2, xt1, xt2, c2, c1, cond, inv_1, bx, zx, zu, q_x, w_x, w_u, carry1, carry2, sums)
     parts = lax.all_to_all(sums, ("gx", "gy"), 0, 0, tiled=True)
     whole = shape(loads, nx, flat)
     image, again, inverse = call(

time: 27.9 us -> 27.6 us (0.989)
  starting transfers between devices: 12.8 us -> 12.5 us
    all_to_all x1, starting transfers between devices: 4.38 us -> 4.08 us  [per_device(): parts = lax.all_to_all(sums, ('gx', 'gy'), 0, 0, tiled=True)]
where the time goes in v26:
time: 27.6 us; the launch traced here: 27.4 us
  starting transfers between devices  12.5 us (45%)
  Pallas kernels  7.53 us (27%)
  waiting for transfers between devices  6.62 us (24%)
  between operations  0.74 us (3%)
    ppermute x6, starting transfers between devices, swap(): return lax.ppermute(array, ('gx', 'gy'), pairs)  8.38 us
    all_to_all x1, waiting for transfers between devices, per_device(): parts = lax.all_to_all(sums, ('gx', 'gy'), 0, 0, tiled=True)  6.32 us
    all_to_all x1, starting transfers between devices, per_device(): parts = lax.all_to_all(sums, ('gx', 'gy'), 0, 0, tiled=True)  4.08 us
    pallas_call x1, Pallas kernels, per_device(): call(inner_kernel, (shape(nx * s.pitch, LANES),) + (rows,) * 2 + (field,)...  1.82 us
    pallas_call x1, Pallas kernels, per_device(): call(outer_kernel, (ends, ends, shape(ny, LANES), shape(devices, 1, LANES...  1.44 us
    pallas_call x1, Pallas kernels, per_device(): call(finish_kernel, (whole, whole), out_specs=(hbm, hbm), scratch_shapes=...  1.21 us
    pallas_call x1, Pallas kernels, per_device(): call(pack_x_kernel, (shape(packed_count(ny), loads * nx, LANES), shape(nx...  1.13 us
    pallas_call x1, Pallas kernels, per_device(): call(unpack_kernel, (whole, whole, shape(nx, flat)), scratch_shapes=[scra...  0.73 us
  transfers between devices with their start and end apart: 7, of which 2 were waited for; matrix products, arithmetic and copies ran while one was open for 0% of the time, Pallas kernels for 14%

profile of v26, /device:TPU:0, one launch (start us, length us, event | category | flops | bytes accessed | tf_op | source)
XLA Modules:
  0.0 27.4 jit_solution(15304267658857923666)
XLA Ops:
  0.6 1.1 %shard_map.41 = (f32[6,128,128]{2,1,0:T(8,128)S(1)}, f32[128,128]{1,0:T(8,128)S(1)}, f32[120,128]{1,0:T(8,128)S(1)}, f32[120,128]{1,0:T(8,128)S(1)}) custom-call(f32[128,768]{1,0:T(8,128)} %bitcast.1, f32[16,768]{1,0:T(8,128)} %d_hbm.1), custom_call_target="tpu_custom_call" | custom-call | tf_op jit(solution)/shard_map/pallas_call | solution.py:793
  1.8 0.5 %collective-permute-start = (f32[120,128]{1,0:T(8,128)S(1)}, f32[120,128]{1,0:T(8,128)S(1)}, u32[]{:S(2)}, u32[]{:S(2)}) collective-permute-start(f32[120,128]{1,0:T(8,128)S(1)} %get-tuple-element.45), channel_id=1, source_target_pairs={{0,1},{1,0},{2,3},{3,2},{4,5},{5,4},{6,7},{7,6},{8,16},{9,17},{10,... | collective-permute-start | bytes 184328 | tf_op jit(solution)/shard_map/ppermute | solution.py:769
  2.3 4.1 %collective-permute-start.1 = (f32[120,128]{1,0:T(8,128)S(1)}, f32[120,128]{1,0:T(8,128)S(1)}, u32[]{:S(2)}, u32[]{:S(2)}) collective-permute-start(f32[120,128]{1,0:T(8,128)S(1)} %get-tuple-element.53), channel_id=1, source_target_pairs={{0,8},{1,9},{2,10},{3,11},{4,12},{5,13},{6,14},{7,15},{8,0},{9,1},... | collective-permute-start | bytes 184328 | tf_op jit(solution)/shard_map/ppermute | solution.py:769
  6.4 0.3 %shard_map.42 = (f32[512,128]{1,0:T(8,128)S(1)}, f32[240,128]{1,0:T(8,128)S(1)}) custom-call(f32[6,128,128]{2,1,0:T(8,128)S(1)} %get-tuple-element.42.b_ref, f32[128,128]{1,0:T(8,128)S(1)} %get-tuple-element.55.dt_ref), custom_call_target="tpu_custom_call" | custom-call | tf_op jit(solution)/shard_map/pallas_call | solution.py:804
  6.8 0.1 collective-permute-start.3
  6.8 0.0 collective-permute-done.x_ref.x2_ref
  6.9 0.1 shard_map.43.t2_ref
  6.9 0.1 shard_map.46
  7.1 1.7 %collective-permute-start.2 = (f32[240,128]{1,0:T(8,128)S(1)}, f32[240,128]{1,0:T(8,128)S(1)}, u32[]{:S(2)}, u32[]{:S(2)}) collective-permute-start(f32[240,128]{1,0:T(8,128)S(1)} %shard_map.46), channel_id=1, source_target_pairs={{0,1},{1,0},{2,3},{3,2},{4,5},{5,4},{6,7},{7,6},{8,9},{9,8},{10,11... | collective-permute-start | bytes 368648 | tf_op jit(solution)/shard_map/ppermute | solution.py:769
  8.7 0.0 collective-permute-done.1.x1_ref
  8.7 0.2 shard_map.45
  8.9 2.0 %collective-permute-start.4 = (f32[72,128]{1,0:T(8,128)S(1)}, f32[72,128]{1,0:T(8,128)S(1)}, u32[]{:S(2)}, u32[]{:S(2)}) collective-permute-start(f32[72,128]{1,0:T(8,128)S(1)} %get-tuple-element.60), channel_id=1, source_target_pairs={{0,8},{1,2},{2,1},{3,4},{4,3},{5,6},{6,5},{7,15},{8,0},{9,10},{10,... | collective-permute-start | bytes 110600 | tf_op jit(solution)/shard_map/ppermute | solution.py:769
  10.9 0.0 collective-permute-start.5
  10.9 0.4 %shard_map.44 = (f32[512,128]{1,0:T(8,128)S(1)}, f32[1024,128]{1,0:T(8,128)S(1)}, f32[1024,128]{1,0:T(8,128)S(1)}, f32[1024,128]{1,0:T(8,128)S(1)}, f32[1024,128]{1,0:T(8,128)S(1)}) custom-call(f32[6,128,128]{2,1,0:T(8,128)S(1)} %get-tuple-element.42.b_ref, f32[512,128]{1,0:T(8,128)S(1)} %get-tuple-element.56.be_ref, f32[128,128]{1,0:T(8,128)S(1)} %get-tuple-element.55.dt_ref), custom_call_target="tpu_custom_call" | custom-call | tf_op jit(solution)/shard_map/pallas_call | solution.py:812
  11.3 0.0 collective-permute-done.2.y_ref.y1_ref
  11.3 0.1 shard_map.47.t1_ref
  11.4 0.3 %collective-permute-done.3.y2_ref = f32[240,128]{1,0:T(8,128)S(1)} collective-permute-done((f32[240,128]{1,0:T(8,128)S(1)}, f32[240,128]{1,0:T(8,128)S(1)}, u32[]{:S(2)}, u32[]{:S(2)}) %collective-permute-start.3) | collective-permute-done | bytes 122912 | tf_op jit(solution)/shard_map/ppermute | solution.py:769
  11.7 1.8 %shard_map.48 = (f32[256,128]{1,0:T(8,128)S(1)}, f32[320,128]{1,0:T(8,128)S(1)}, f32[320,128]{1,0:T(8,128)S(1)}, f32[1920,128]{1,0:T(8,128)S(1)}, f32[1920,128]{...) custom-call(f32[512,128]{1,0:T(8,128)S(1)} %get-tuple-element.56.be_, ...), custom_call_target="tpu_custom_call" | custom-call | tf_op jit(solution)/shard_map/pallas_call | solution.py:827
  13.5 0.0 collective-permute-done.4.c2_ref
  13.5 0.0 collective-permute-done.5.c1_ref
  13.6 1.4 %shard_map.49 = (f32[320,128]{1,0:T(8,128)S(1)}, f32[320,128]{1,0:T(8,128)S(1)}, f32[8,128]{1,0:T(8,128)S(1)}, f32[32,1,128]{2,1,0:T(1,128)}) custom-call(f32[512,128]{1,0:T(8,128)S(1)} %get-tuple-element.56.be_ref, f32[512,128]{1,0:T(8,128)S(1)} %get-tuple-element.47.bm_ref, f32[1024,128]{1,0:T(8,128)S(1)} %get-tuple-element.48.zt_ref, ...), custom_call_target="tpu_custom_call" | custom-call | tf_op jit(solution)/shard_map/pallas_call | solution.py:837
  15.0 4.1 %all-to-all-start = ((f32[32,1,128]{2,1,0:T(1,128)}), f32[32,1,128]{2,1,0:T(1,128)S(1)}, u32[]{:S(2)}, u32[]{:S(2)}) async-start(f32[32,1,128]{2,1,0:T(1,128)} %get-tuple-element.73), calls=%async_computation | async-start | bytes 32768 | tf_op jit(solution)/shard_map/all_to_all | solution.py:846
  19.1 0.0 copy-start
  19.1 0.7 %shard_map.50 = (f32[8,16,768]{2,1,0:T(8,128)S(1)}, f32[8,16,768]{2,1,0:T(8,128)S(1)}, f32[16,768]{1,0:T(8,128)S(1)}) custom-call(f32[1024,128]{1,0:T(8,128)S(1)} %get-tuple-element.74.q1_ref, f32[320,128]{1,0:T(8,128)S(1)} %get-tuple-element.75.q2_ref, f32[1024,128]{1,0:T(8,128)S(1)} %get-tuple-element.76.v1_ref, f32[320,128]{1,0:T(8,128)S(1)} %get-tuple-element.77.v2_ref, ...), custom_call_target="tpu_custom_call" | custom-call | tf_op jit(solution)/shard_map/pallas_call | solution.py:848
  19.8 6.3 %all-to-all-done.parts_ref = f32[32,1,128]{2,1,0:T(1,128)S(1)} async-done(((f32[32,1,128]{2,1,0:T(1,128)}), f32[32,1,128]{2,1,0:T(1,128)S(1)}, u32[]{:S(2)}, u32[]{:S(2)}) %all-to-all-start) | async-done | bytes 16416 | tf_op jit(solution)/shard_map/all_to_all | solution.py:846
  26.2 0.0 copy-done
  26.2 1.2 %shard_map.51 = (f32[8,16,768]{2,1,0:T(8,128)}, f32[8,16,768]{2,1,0:T(8,128)}) custom-call(f32[32,1,128]{2,1,0:T(1,128)S(1)} %all-to-all-done.parts_ref, f32[8,16,768]{2,1,0:T(8,128)S(1)} %copy-done, f32[8,16,768]{2,1,0:T(8,128)S(1)} %get-tuple-element.79.q_ref, f32[8,16,768]{2,1,0:T(8,128)S(1)} %get-tuple-element.80.v_ref, ...), custom_call_target="tpu_custom_call" | custom-call | tf_op jit(solution)/shard_map/pallas_call | solution.py:853
Async XLA Ops:
  1.8 5.1 %collective-permute-start = (f32[120,128]{1,0:T(8,128)S(1)}, f32[120,128]{1,0:T(8,128)S(1)}, u32[]{:S(2)}, u32[]{:S(2)}) collective-permute-start(f32[120,128]{1,0:T(8,128)S(1)} %get-tuple-element.45), channel_id=1, source_target_pairs={{0,1},{1,0},{2,3},{3,2},{4,5},{5,4},{6,7},{7,6},{8,16},{9,17},{10,... | collective-permute-start | bytes 184328 | tf_op jit(solution)/shard_map/ppermute | solution.py:769
  2.3 6.4 %collective-permute-start.1 = (f32[120,128]{1,0:T(8,128)S(1)}, f32[120,128]{1,0:T(8,128)S(1)}, u32[]{:S(2)}, u32[]{:S(2)}) collective-permute-start(f32[120,128]{1,0:T(8,128)S(1)} %get-tuple-element.53), channel_id=1, source_target_pairs={{0,8},{1,9},{2,10},{3,11},{4,12},{5,13},{6,14},{7,15},{8,0},{9,1},... | collective-permute-start | bytes 184328 | tf_op jit(solution)/shard_map/ppermute | solution.py:769
  6.8 4.9 %collective-permute-start.3 = (f32[240,128]{1,0:T(8,128)S(1)}, f32[240,128]{1,0:T(8,128)S(1)}, u32[]{:S(2)}, u32[]{:S(2)}) collective-permute-start(f32[240,128]{1,0:T(8,128)S(1)} %get-tuple-element.57), channel_id=1, source_target_pairs={{0,8},{1,2},{2,1},{3,4},{4,3},{5,6},{6,5},{7,15},{8,0},{9,10},{10,... | collective-permute-start | bytes 368648 | tf_op jit(solution)/shard_map/ppermute | solution.py:769
  7.1 4.2 %collective-permute-start.2 = (f32[240,128]{1,0:T(8,128)S(1)}, f32[240,128]{1,0:T(8,128)S(1)}, u32[]{:S(2)}, u32[]{:S(2)}) collective-permute-start(f32[240,128]{1,0:T(8,128)S(1)} %shard_map.46), channel_id=1, source_target_pairs={{0,1},{1,0},{2,3},{3,2},{4,5},{5,4},{6,7},{7,6},{8,9},{9,8},{10,11... | collective-permute-start | bytes 368648 | tf_op jit(solution)/shard_map/ppermute | solution.py:769
  8.9 4.7 %collective-permute-start.4 = (f32[72,128]{1,0:T(8,128)S(1)}, f32[72,128]{1,0:T(8,128)S(1)}, u32[]{:S(2)}, u32[]{:S(2)}) collective-permute-start(f32[72,128]{1,0:T(8,128)S(1)} %get-tuple-element.60), channel_id=1, source_target_pairs={{0,8},{1,2},{2,1},{3,4},{4,3},{5,6},{6,5},{7,15},{8,0},{9,10},{10,... | collective-permute-start | bytes 110600 | tf_op jit(solution)/shard_map/ppermute | solution.py:769
  10.9 2.7 %collective-permute-start.5 = (f32[72,128]{1,0:T(8,128)S(1)}, f32[72,128]{1,0:T(8,128)S(1)}, u32[]{:S(2)}, u32[]{:S(2)}) collective-permute-start(f32[72,128]{1,0:T(8,128)S(1)} %get-tuple-element.61), channel_id=1, source_target_pairs={{0,1},{1,0},{2,3},{3,2},{4,5},{5,4},{6,7},{7,6},{8,9},{9,8},{10,11... | collective-permute-start | bytes 110600 | tf_op jit(solution)/shard_map/ppermute | solution.py:769
  15.0 11.2 %all-to-all-start = ((f32[32,1,128]{2,1,0:T(1,128)}), f32[32,1,128]{2,1,0:T(1,128)S(1)}, u32[]{:S(2)}, u32[]{:S(2)}) async-start(f32[32,1,128]{2,1,0:T(1,128)} %get-tuple-element.73), calls=%async_computation | async-start | bytes 32768 | tf_op jit(solution)/shard_map/all_to_all | solution.py:846
  19.1 7.1 %copy-start = (f32[8,16,768]{2,1,0:T(8,128)S(1)}, f32[8,16,768]{2,1,0:T(8,128)}, u32[]{:S(2)}) copy-start(f32[8,16,768]{2,1,0:T(8,128)} %b_ref.1) | copy-start | bytes 1179652

commit v27 on v26

--- a/solution.py
+++ b/solution.py
@@ -425,6 +425,8 @@
 
 def over_planes(start, stop, body, state):
     groups, rest = (stop - start) // 4, (stop - start) % 4
+    if rest == 1 and groups:
+        groups, rest = groups - 1, 5
     state = lax.fori_loop(0, groups, lambda i, st: body(start + 4 * i, 4, st), state)
     if rest:
         state = body(stop - rest, rest, state)

time: 27.6 us -> 27.5 us (level)
  transfers between devices with their start and end apart: 7 -> 7, of which waited for: 2 -> 2; matrix products, arithmetic and copies ran while one was open for 0% -> 0% of each run, Pallas kernels for 14% -> 13%
where the time goes in v27:
time: 27.5 us; the launch traced here: 27.3 us
  starting transfers between devices  12.5 us (45%)
  Pallas kernels  7.4 us (27%)
  waiting for transfers between devices  6.62 us (24%)
  between operations  0.74 us (3%)
    ppermute x6, starting transfers between devices, swap(): return lax.ppermute(array, ('gx', 'gy'), pairs)  8.38 us
    all_to_all x1, waiting for transfers between devices, per_device(): parts = lax.all_to_all(sums, ('gx', 'gy'), 0, 0, tiled=True)  6.32 us
    all_to_all x1, starting transfers between devices, per_device(): parts = lax.all_to_all(sums, ('gx', 'gy'), 0, 0, tiled=True)  4.15 us
    pallas_call x1, Pallas kernels, per_device(): call(inner_kernel, (shape(nx * s.pitch, LANES),) + (rows,) * 2 + (field,)...  1.69 us
    pallas_call x1, Pallas kernels, per_device(): call(outer_kernel, (ends, ends, shape(ny, LANES), shape(devices, 1, LANES...  1.44 us
    pallas_call x1, Pallas kernels, per_device(): call(finish_kernel, (whole, whole), out_specs=(hbm, hbm), scratch_shapes=...  1.21 us
    pallas_call x1, Pallas kernels, per_device(): call(pack_x_kernel, (shape(packed_count(ny), loads * nx, LANES), shape(nx...  1.13 us
    pallas_call x1, Pallas kernels, per_device(): call(unpack_kernel, (whole, whole, shape(nx, flat)), scratch_shapes=[scra...  0.73 us
  transfers between devices with their start and end apart: 7, of which 2 were waited for; matrix products, arithmetic and copies ran while one was open for 0% of the time, Pallas kernels for 13%

profile of v27, /device:TPU:0, one launch (start us, length us, event | category | flops | bytes accessed | tf_op | source)
XLA Modules:
  0.0 27.3 jit_solution(5192263829392943834)
XLA Ops:
  0.6 1.1 %shard_map.41 = (f32[6,128,128]{2,1,0:T(8,128)S(1)}, f32[128,128]{1,0:T(8,128)S(1)}, f32[120,128]{1,0:T(8,128)S(1)}, f32[120,128]{1,0:T(8,128)S(1)}) custom-call(f32[128,768]{1,0:T(8,128)} %bitcast.1, f32[16,768]{1,0:T(8,128)} %d_hbm.1), custom_call_target="tpu_custom_call" | custom-call | tf_op jit(solution)/shard_map/pallas_call | solution.py:795
  1.8 0.5 %collective-permute-start = (f32[120,128]{1,0:T(8,128)S(1)}, f32[120,128]{1,0:T(8,128)S(1)}, u32[]{:S(2)}, u32[]{:S(2)}) collective-permute-start(f32[120,128]{1,0:T(8,128)S(1)} %get-tuple-element.45), channel_id=1, source_target_pairs={{0,1},{1,0},{2,3},{3,2},{4,5},{5,4},{6,7},{7,6},{8,16},{9,17},{10,... | collective-permute-start | bytes 184328 | tf_op jit(solution)/shard_map/ppermute | solution.py:771
  2.3 4.1 %collective-permute-start.1 = (f32[120,128]{1,0:T(8,128)S(1)}, f32[120,128]{1,0:T(8,128)S(1)}, u32[]{:S(2)}, u32[]{:S(2)}) collective-permute-start(f32[120,128]{1,0:T(8,128)S(1)} %get-tuple-element.53), channel_id=1, source_target_pairs={{0,8},{1,9},{2,10},{3,11},{4,12},{5,13},{6,14},{7,15},{8,0},{9,1},... | collective-permute-start | bytes 184328 | tf_op jit(solution)/shard_map/ppermute | solution.py:771
  6.4 0.3 %shard_map.42 = (f32[512,128]{1,0:T(8,128)S(1)}, f32[240,128]{1,0:T(8,128)S(1)}) custom-call(f32[6,128,128]{2,1,0:T(8,128)S(1)} %get-tuple-element.42.b_ref, f32[128,128]{1,0:T(8,128)S(1)} %get-tuple-element.55.dt_ref), custom_call_target="tpu_custom_call" | custom-call | tf_op jit(solution)/shard_map/pallas_call | solution.py:806
  6.8 0.1 collective-permute-start.3
  6.8 0.0 collective-permute-done.x_ref.x2_ref
  6.9 0.1 shard_map.43.t2_ref
  6.9 0.1 shard_map.46
  7.1 1.7 %collective-permute-start.2 = (f32[240,128]{1,0:T(8,128)S(1)}, f32[240,128]{1,0:T(8,128)S(1)}, u32[]{:S(2)}, u32[]{:S(2)}) collective-permute-start(f32[240,128]{1,0:T(8,128)S(1)} %shard_map.46), channel_id=1, source_target_pairs={{0,1},{1,0},{2,3},{3,2},{4,5},{5,4},{6,7},{7,6},{8,9},{9,8},{10,11... | collective-permute-start | bytes 368648 | tf_op jit(solution)/shard_map/ppermute | solution.py:771
  8.7 0.0 collective-permute-done.1.x1_ref
  8.7 0.2 shard_map.45
  8.9 2.0 %collective-permute-start.4 = (f32[72,128]{1,0:T(8,128)S(1)}, f32[72,128]{1,0:T(8,128)S(1)}, u32[]{:S(2)}, u32[]{:S(2)}) collective-permute-start(f32[72,128]{1,0:T(8,128)S(1)} %get-tuple-element.60), channel_id=1, source_target_pairs={{0,8},{1,2},{2,1},{3,4},{4,3},{5,6},{6,5},{7,15},{8,0},{9,10},{10,... | collective-permute-start | bytes 110600 | tf_op jit(solution)/shard_map/ppermute | solution.py:771
  10.9 0.0 collective-permute-start.5
  10.9 0.4 %shard_map.44 = (f32[512,128]{1,0:T(8,128)S(1)}, f32[1024,128]{1,0:T(8,128)S(1)}, f32[1024,128]{1,0:T(8,128)S(1)}, f32[1024,128]{1,0:T(8,128)S(1)}, f32[1024,128]{1,0:T(8,128)S(1)}) custom-call(f32[6,128,128]{2,1,0:T(8,128)S(1)} %get-tuple-element.42.b_ref, f32[512,128]{1,0:T(8,128)S(1)} %get-tuple-element.56.be_ref, f32[128,128]{1,0:T(8,128)S(1)} %get-tuple-element.55.dt_ref), custom_call_target="tpu_custom_call" | custom-call | tf_op jit(solution)/shard_map/pallas_call | solution.py:814
  11.3 0.0 collective-permute-done.2.y_ref.y1_ref
  11.3 0.1 shard_map.47.t1_ref
  11.4 0.3 %collective-permute-done.3.y2_ref = f32[240,128]{1,0:T(8,128)S(1)} collective-permute-done((f32[240,128]{1,0:T(8,128)S(1)}, f32[240,128]{1,0:T(8,128)S(1)}, u32[]{:S(2)}, u32[]{:S(2)}) %collective-permute-start.3) | collective-permute-done | bytes 122912 | tf_op jit(solution)/shard_map/ppermute | solution.py:771
  11.7 1.7 %shard_map.48 = (f32[256,128]{1,0:T(8,128)S(1)}, f32[320,128]{1,0:T(8,128)S(1)}, f32[320,128]{1,0:T(8,128)S(1)}, f32[1920,128]{1,0:T(8,128)S(1)}, f32[1920,128]{...) custom-call(f32[512,128]{1,0:T(8,128)S(1)} %get-tuple-element.56.be_, ...), custom_call_target="tpu_custom_call" | custom-call | tf_op jit(solution)/shard_map/pallas_call | solution.py:829
  13.4 0.0 collective-permute-done.4.c2_ref
  13.4 0.0 collective-permute-done.5.c1_ref
  13.4 1.4 %shard_map.49 = (f32[320,128]{1,0:T(8,128)S(1)}, f32[320,128]{1,0:T(8,128)S(1)}, f32[8,128]{1,0:T(8,128)S(1)}, f32[32,1,128]{2,1,0:T(1,128)}) custom-call(f32[512,128]{1,0:T(8,128)S(1)} %get-tuple-element.56.be_ref, f32[512,128]{1,0:T(8,128)S(1)} %get-tuple-element.47.bm_ref, f32[1024,128]{1,0:T(8,128)S(1)} %get-tuple-element.48.zt_ref, ...), custom_call_target="tpu_custom_call" | custom-call | tf_op jit(solution)/shard_map/pallas_call | solution.py:839
  14.9 4.2 %all-to-all-start = ((f32[32,1,128]{2,1,0:T(1,128)}), f32[32,1,128]{2,1,0:T(1,128)S(1)}, u32[]{:S(2)}, u32[]{:S(2)}) async-start(f32[32,1,128]{2,1,0:T(1,128)} %get-tuple-element.73), calls=%async_computation | async-start | bytes 32768 | tf_op jit(solution)/shard_map/all_to_all | solution.py:848
  19.0 0.0 copy-start
  19.0 0.7 %shard_map.50 = (f32[8,16,768]{2,1,0:T(8,128)S(1)}, f32[8,16,768]{2,1,0:T(8,128)S(1)}, f32[16,768]{1,0:T(8,128)S(1)}) custom-call(f32[1024,128]{1,0:T(8,128)S(1)} %get-tuple-element.74.q1_ref, f32[320,128]{1,0:T(8,128)S(1)} %get-tuple-element.75.q2_ref, f32[1024,128]{1,0:T(8,128)S(1)} %get-tuple-element.76.v1_ref, f32[320,128]{1,0:T(8,128)S(1)} %get-tuple-element.77.v2_ref, ...), custom_call_target="tpu_custom_call" | custom-call | tf_op jit(solution)/shard_map/pallas_call | solution.py:850
  19.8 6.3 %all-to-all-done.parts_ref = f32[32,1,128]{2,1,0:T(1,128)S(1)} async-done(((f32[32,1,128]{2,1,0:T(1,128)}), f32[32,1,128]{2,1,0:T(1,128)S(1)}, u32[]{:S(2)}, u32[]{:S(2)}) %all-to-all-start) | async-done | bytes 16416 | tf_op jit(solution)/shard_map/all_to_all | solution.py:848
  26.1 0.0 copy-done
  26.1 1.2 %shard_map.51 = (f32[8,16,768]{2,1,0:T(8,128)}, f32[8,16,768]{2,1,0:T(8,128)}) custom-call(f32[32,1,128]{2,1,0:T(1,128)S(1)} %all-to-all-done.parts_ref, f32[8,16,768]{2,1,0:T(8,128)S(1)} %copy-done, f32[8,16,768]{2,1,0:T(8,128)S(1)} %get-tuple-element.79.q_ref, f32[8,16,768]{2,1,0:T(8,128)S(1)} %get-tuple-element.80.v_ref, ...), custom_call_target="tpu_custom_call" | custom-call | tf_op jit(solution)/shard_map/pallas_call | solution.py:855
Async XLA Ops:
  1.8 5.1 %collective-permute-start = (f32[120,128]{1,0:T(8,128)S(1)}, f32[120,128]{1,0:T(8,128)S(1)}, u32[]{:S(2)}, u32[]{:S(2)}) collective-permute-start(f32[120,128]{1,0:T(8,128)S(1)} %get-tuple-element.45), channel_id=1, source_target_pairs={{0,1},{1,0},{2,3},{3,2},{4,5},{5,4},{6,7},{7,6},{8,16},{9,17},{10,... | collective-permute-start | bytes 184328 | tf_op jit(solution)/shard_map/ppermute | solution.py:771
  2.3 6.4 %collective-permute-start.1 = (f32[120,128]{1,0:T(8,128)S(1)}, f32[120,128]{1,0:T(8,128)S(1)}, u32[]{:S(2)}, u32[]{:S(2)}) collective-permute-start(f32[120,128]{1,0:T(8,128)S(1)} %get-tuple-element.53), channel_id=1, source_target_pairs={{0,8},{1,9},{2,10},{3,11},{4,12},{5,13},{6,14},{7,15},{8,0},{9,1},... | collective-permute-start | bytes 184328 | tf_op jit(solution)/shard_map/ppermute | solution.py:771
  6.8 4.9 %collective-permute-start.3 = (f32[240,128]{1,0:T(8,128)S(1)}, f32[240,128]{1,0:T(8,128)S(1)}, u32[]{:S(2)}, u32[]{:S(2)}) collective-permute-start(f32[240,128]{1,0:T(8,128)S(1)} %get-tuple-element.57), channel_id=1, source_target_pairs={{0,8},{1,2},{2,1},{3,4},{4,3},{5,6},{6,5},{7,15},{8,0},{9,10},{10,... | collective-permute-start | bytes 368648 | tf_op jit(solution)/shard_map/ppermute | solution.py:771
  7.1 4.2 %collective-permute-start.2 = (f32[240,128]{1,0:T(8,128)S(1)}, f32[240,128]{1,0:T(8,128)S(1)}, u32[]{:S(2)}, u32[]{:S(2)}) collective-permute-start(f32[240,128]{1,0:T(8,128)S(1)} %shard_map.46), channel_id=1, source_target_pairs={{0,1},{1,0},{2,3},{3,2},{4,5},{5,4},{6,7},{7,6},{8,9},{9,8},{10,11... | collective-permute-start | bytes 368648 | tf_op jit(solution)/shard_map/ppermute | solution.py:771
  8.9 4.5 %collective-permute-start.4 = (f32[72,128]{1,0:T(8,128)S(1)}, f32[72,128]{1,0:T(8,128)S(1)}, u32[]{:S(2)}, u32[]{:S(2)}) collective-permute-start(f32[72,128]{1,0:T(8,128)S(1)} %get-tuple-element.60), channel_id=1, source_target_pairs={{0,8},{1,2},{2,1},{3,4},{4,3},{5,6},{6,5},{7,15},{8,0},{9,10},{10,... | collective-permute-start | bytes 110600 | tf_op jit(solution)/shard_map/ppermute | solution.py:771
  10.9 2.6 %collective-permute-start.5 = (f32[72,128]{1,0:T(8,128)S(1)}, f32[72,128]{1,0:T(8,128)S(1)}, u32[]{:S(2)}, u32[]{:S(2)}) collective-permute-start(f32[72,128]{1,0:T(8,128)S(1)} %get-tuple-element.61), channel_id=1, source_target_pairs={{0,1},{1,0},{2,3},{3,2},{4,5},{5,4},{6,7},{7,6},{8,9},{9,8},{10,11... | collective-permute-start | bytes 110600 | tf_op jit(solution)/shard_map/ppermute | solution.py:771
  14.9 11.2 %all-to-all-start = ((f32[32,1,128]{2,1,0:T(1,128)}), f32[32,1,128]{2,1,0:T(1,128)S(1)}, u32[]{:S(2)}, u32[]{:S(2)}) async-start(f32[32,1,128]{2,1,0:T(1,128)} %get-tuple-element.73), calls=%async_computation | async-start | bytes 32768 | tf_op jit(solution)/shard_map/all_to_all | solution.py:848
  19.0 7.1 %copy-start = (f32[8,16,768]{2,1,0:T(8,128)S(1)}, f32[8,16,768]{2,1,0:T(8,128)}, u32[]{:S(2)}) copy-start(f32[8,16,768]{2,1,0:T(8,128)} %b_ref.1) | copy-start | bytes 1179652
